TPU v7x, 32 devices: a whole 2x2x4 slice. The times are simulated.
32 devices in a mesh: row: 8 (over z, core), col: 4 (over y, x).
Axes of the slice: x: 2, y: 2, z: 4, core: 2. Of those that a mesh axis runs over, the one named last changes fastest.
Arguments:
- momentum: float32 [4096, 6656], P('row', 'col'), may hold values from -20 to 20
- grad: bfloat16 [4096, 6656], P('row', 'col'), may hold values from -3 to 3
- basis: float32 [6656, 128], P('col'), may hold values from -0.078125 to 0.078125
Outputs:
- momentum_out: float32 [4096, 6656], P('row', 'col')
- left_out: float32 [2, 4096, 128], P(None, 'row')
- right_out: float32 [6656, 128], P('col')
All inputs are finite; a program needn't handle non-finite values.
Results may differ from a plain program's by a relative error of at most 0.0003.
Values sent between devices are 32-bit elements; how exact they have to be, the bound alone decides.
No kernel may reach another device: no remote copies, remote signals or barrier semaphores. Data moves between devices by JAX's collectives and lax.ppermute only.
A program may use at most 64 MiB of HBM per device.

v0:
```python
import jax
import jax.numpy as jnp
from jax import lax
from jax.experimental import pallas as pl
from jax.experimental.pallas import tpu as pltpu
from jax.sharding import PartitionSpec as P

ITERS = 2
HIGHEST = lax.Precision.HIGHEST
HIGH = lax.Precision.HIGH


def mm(a, b, dims, precision=HIGH):
    return lax.dot_general(a, b, ((dims[0], dims[1]), ((), ())), precision=precision)


def masks_of(axis):
    size = lax.axis_size(axis)
    masks = []
    mask = 1
    while mask < size:
        masks.append(mask)
        mask *= 2
    assert mask == size
    return masks


def swap(x, axis, mask):
    return lax.ppermute(x, axis, [(i, i ^ mask) for i in range(lax.axis_size(axis))])


def sum_whole(x, axis):
    for mask in masks_of(axis):
        x = x + swap(x, axis, mask)
    return x


def sum_halving(x, axis):
    place = lax.axis_index(axis)
    masks = masks_of(axis)
    for mask in masks:
        half = x.shape[0] // 2
        bit = (place // mask) % 2
        keep = lax.dynamic_slice_in_dim(x, bit * half, half)
        send = lax.dynamic_slice_in_dim(x, (1 - bit) * half, half)
        x = keep + swap(send, axis, mask)
    for mask in reversed(masks):
        bit = (place // mask) % 2
        other = swap(x, axis, mask)
        low = jnp.where(bit == 0, x, other)
        high = jnp.where(bit == 0, other, x)
        x = jnp.concatenate([low, high], axis=0)
    return x


def gram_of(x):
    return mm(x, x, ((0,), (0,)), HIGHEST)


def eliminate(full, first):
    rank = full.shape[1]
    sub = lax.broadcasted_iota(jnp.int32, (8, rank), 0)
    lane = lax.broadcasted_iota(jnp.int32, (8, rank), 1)
    rolled = pltpu.roll(full, lax.rem(rank - first, rank), 1)
    cols = [jnp.broadcast_to(rolled[:, j:j + 1], (8, rank)) for j in range(8)]
    for j in range(8):
        pivot = jnp.broadcast_to(cols[j][j:j + 1], (8, rank))
        mult = jnp.where(sub > j, cols[j] * (1.0 / pivot), 0.0)
        for k in range(j + 1, 8):
            cols[k] = cols[k] - mult * cols[k][j:j + 1]
        here = lane == first + j
        row = jnp.where(here[:1], 1.0, full[j:j + 1])
        rest = jnp.where(here & (sub > j), 0.0, full) - mult * row
        full = jnp.where(sub == j, row * lax.rsqrt(pivot), rest)
    return full

def factor_body(gram_ref, out_ref):
    rank = gram_ref.shape[0]
    out_ref[...] = gram_ref[...]
    row = lax.broadcasted_iota(jnp.int32, (rank, rank), 0)
    col = lax.broadcasted_iota(jnp.int32, (rank, rank), 1)

    def panel(p, carry):
        first = pl.multiple_of(p * 8, 8)
        done = eliminate(out_ref[pl.ds(first, 8), :], first)
        sub = lax.broadcasted_iota(jnp.int32, (8, rank), 0)
        lane = lax.broadcasted_iota(jnp.int32, (8, rank), 1)
        lower = jnp.where((lane > first + sub) & (lane < first + 8), 0.0, done)
        step = lax.dot_general(done, lower, (((0,), (0,)), ((), ())), precision=HIGHEST, preferred_element_type=jnp.float32)
        old = out_ref[...]
        old = jnp.where(row >= first + 8, jnp.where((col >= first) & (col < first + 8), 0.0, old) - step, old)
        out_ref[...] = old
        out_ref[pl.ds(first, 8), :] = done
        return carry

    lax.fori_loop(0, rank // 8, panel, 0)
    out_ref[...] = jnp.where(row >= col, out_ref[...], 0.0)

def factor(gram):
    return pl.pallas_call(
        factor_body,
        out_shape=jax.ShapeDtypeStruct(gram.shape, gram.dtype),
        in_specs=[pl.BlockSpec(memory_space=pltpu.VMEM)],
        out_specs=pl.BlockSpec(memory_space=pltpu.VMEM),
        name="factor",
        cost_estimate=pl.CostEstimate(flops=40_000_000, bytes_accessed=131072, transcendentals=0),
    )(gram)


def shards(momentum, grad, basis):
    work = momentum + grad.astype(jnp.float32)
    total_rows = momentum.shape[0] * lax.axis_size("row")
    total_cols = momentum.shape[1] * lax.axis_size("col")
    proj = sum_whole(mm(work, basis, ((1,), (0,))), "col")
    lefts = []
    rights = []
    for step in range(ITERS):
        gram_left = sum_whole(gram_of(proj), "row")
        partial = mm(work, proj, ((0,), (0,)))
        for left, right in zip(lefts, rights):
            partial = partial - 0.95 * mm(right, mm(left, proj, ((0,), (0,))), ((1,), (0,)))
        inv_left = factor(gram_left)
        left = mm(proj, inv_left, ((1,), (1,)), HIGHEST)
        right = mm(sum_halving(partial, "row"), inv_left, ((1,), (1,)), HIGHEST)
        lefts.append(left)
        rights.append(right)
        gram_right = sum_whole(gram_of(right), "col")
        inv_right = factor(gram_right)
        if step + 1 < ITERS:
            image = sum_whole(mm(work, right, ((1,), (0,))), "col")
            for other_left, other_right in zip(lefts[:-1], rights[:-1]):
                cross = sum_whole(mm(other_right, right, ((0,), (0,))), "col")
                image = image - 0.95 * mm(other_left, cross, ((1,), (0,)))
            image = image - 0.95 * mm(left, gram_right, ((1,), (0,)), HIGHEST)
            proj = mm(image, inv_right, ((1,), (1,)), HIGHEST)
    basis_out = mm(rights[-1], inv_right, ((1,), (1,)), HIGHEST)
    outer = mm(jnp.concatenate(lefts, axis=1), jnp.concatenate(rights, axis=1), ((1,), (1,)))
    return (
        work - 0.95 * outer,
        jnp.stack(lefts) * jnp.sqrt(jnp.float32(total_rows)),
        basis_out * jnp.sqrt(jnp.float32(total_cols)),
    )


def solution(mesh):
    in_specs = (P("row", "col"), P("row", "col"), P("col", None))
    out_specs = (P("row", "col"), P(None, "row", None), P("col", None))
    return jax.shard_map(shards, mesh=mesh, in_specs=in_specs, out_specs=out_specs, check_vma=False)
```

profile of v0, /device:TPU:0, one launch (start us, length us, event | category | flops | bytes accessed | tf_op | source)
XLA Modules:
  0.0 207.5 jit_solution(4748389348067358296)
XLA Ops:
  1.8 4.2 %fusion.22 = f32[512,128]{1,0:T(8,128)S(1)} fusion(f32[1664,128]{1,0:T(8,128)S(1)} %copy-done, f32[512,1664]{1,0:T(8,128)} %param.3, bf16[512,1664]{1,0:T(8,128)(2,1)} %param.4), kind=kOutput, calls=%fused_computation.57 | convolution fusion | flops 656015360 | bytes 6225920 | tf_op jit(solution)/shard_map/dot_general | solution.py:14
  6.0 3.0 %collective-permute-start = (f32[512,128]{1,0:T(8,128)S(1)}, f32[512,128]{1,0:T(8,128)S(1)}, u32[]{:S(2)}, u32[]{:S(2)}) collective-permute-start(f32[512,128]{1,0:T(8,128)S(1)} %fusion.22), channel_id=1, source_target_pairs={{0,1},{1,0},{2,3},{3,2},{4,5},{5,4},{6,7},{7,6},{8,9},{9,8},{10,11... | collective-permute-start | bytes 786440 | tf_op jit(solution)/shard_map/ppermute | solution.py:29
  9.0 6.3 %collective-permute-done = f32[512,128]{1,0:T(8,128)S(1)} collective-permute-done((f32[512,128]{1,0:T(8,128)S(1)}, f32[512,128]{1,0:T(8,128)S(1)}, u32[]{:S(2)}, u32[]{:S(2)}) %collective-permute-start) | collective-permute-done | bytes 262176 | tf_op jit(solution)/shard_map/ppermute | solution.py:29
  15.3 1.8 collective-permute-start.1
  17.1 5.7 %collective-permute-done.1 = f32[512,128]{1,0:T(8,128)S(1)} collective-permute-done((f32[512,128]{1,0:T(8,128)S(1)}, f32[512,128]{1,0:T(8,128)S(1)}, u32[]{:S(2)}, u32[]{:S(2)}) %collective-permute-start.1) | collective-permute-done | bytes 262176 | tf_op jit(solution)/shard_map/ppermute | solution.py:29
  22.9 4.9 %fusion.21 = f32[1664,128]{1,0:T(8,128)S(1)} fusion(f32[512,128]{1,0:T(8,128)S(1)} %add.111, f32[512,1664]{1,0:T(8,128)} %param.3, bf16[512,1664]{1,0:T(8,128)(2,1)S(1)} %copy-done.3), kind=kOutput, calls=%fused_computation.56 | convolution fusion | flops 656015360 | bytes 6225920 | tf_op jit(solution)/shard_map/dot_general | solution.py:14
  28.9 1.8 collective-permute-done.5
  33.5 5.9 %collective-permute-done.6 = f32[416,128]{1,0:T(8,128)} collective-permute-done((f32[416,128]{1,0:T(8,128)S(1)}, f32[416,128]{1,0:T(8,128)}, u32[]{:S(2)}, u32[]{:S(2)}) %collective-permute-start.6) | collective-permute-done | bytes 213024 | tf_op jit(solution)/shard_map/ppermute | solution.py:29
  40.4 2.6 %collective-permute-start.7 = (f32[208,128]{1,0:T(8,128)S(1)}, f32[208,128]{1,0:T(8,128)S(1)}, u32[]{:S(2)}, u32[]{:S(2)}) collective-permute-start(f32[208,128]{1,0:T(8,128)S(1)} %constant_dynamic-slice_fusion.3), channel_id=1, source_target_pairs={{0,16},{4,20},{8,24},{12,28},{16,0},{20,4},{24,8},{28,12},{1,17},{... | collective-permute-start | bytes 319496 | tf_op jit(solution)/shard_map/ppermute | solution.py:29
  43.0 4.8 %collective-permute-done.7 = f32[208,128]{1,0:T(8,128)S(1)} collective-permute-done((f32[208,128]{1,0:T(8,128)S(1)}, f32[208,128]{1,0:T(8,128)S(1)}, u32[]{:S(2)}, u32[]{:S(2)}) %collective-permute-start.7) | collective-permute-done | bytes 106528 | tf_op jit(solution)/shard_map/ppermute | solution.py:29
  48.7 6.5 %collective-permute-done.8 = f32[208,128]{1,0:T(8,128)S(1)} collective-permute-done((f32[208,128]{1,0:T(8,128)S(1)}, f32[208,128]{1,0:T(8,128)S(1)}, u32[]{:S(2)}, u32[]{:S(2)}) %collective-permute-start.8) | collective-permute-done | bytes 106528 | tf_op jit(solution)/shard_map/ppermute | solution.py:29
  55.3 5.9 %collective-permute-done.9 = f32[416,128]{1,0:T(8,128)} collective-permute-done((f32[416,128]{1,0:T(8,128)S(1)}, f32[416,128]{1,0:T(8,128)}, u32[]{:S(2)}, u32[]{:S(2)}) %collective-permute-start.9) | collective-permute-done | bytes 213024 | tf_op jit(solution)/shard_map/ppermute | solution.py:29
  65.4 4.1 %collective-permute-done.3 = f32[128,128]{1,0:T(8,128)S(1)} collective-permute-done((f32[128,128]{1,0:T(8,128)S(1)}, f32[128,128]{1,0:T(8,128)S(1)}, u32[]{:S(2)}, u32[]{:S(2)}) %collective-permute-start.3) | collective-permute-done | bytes 65568 | tf_op jit(solution)/shard_map/ppermute | solution.py:29
  69.5 1.9 collective-permute-start.4
  71.4 4.0 %collective-permute-done.4 = f32[128,128]{1,0:T(8,128)S(1)} collective-permute-done((f32[128,128]{1,0:T(8,128)S(1)}, f32[128,128]{1,0:T(8,128)S(1)}, u32[]{:S(2)}, u32[]{:S(2)}) %collective-permute-start.4) | collective-permute-done | bytes 65568 | tf_op jit(solution)/shard_map/ppermute | solution.py:29
  76.1 9.6 %factor.4 = f32[128,128]{1,0:T(8,128)} custom-call(f32[128,128]{1,0:T(8,128)} %add.114.gram_ref), custom_call_target="tpu_custom_call" | custom-call | flops 40000000 | bytes 131072 | tf_op jit(solution)/shard_map/factor/pallas_call | solution.py:100
  86.8 1.8 fusion.3
  93.4 5.0 %collective-permute-done.13 = f32[128,128]{1,0:T(8,128)S(1)} collective-permute-done((f32[128,128]{1,0:T(8,128)S(1)}, f32[128,128]{1,0:T(8,128)S(1)}, u32[]{:S(2)}, u32[]{:S(2)}) %collective-permute-start.13) | collective-permute-done | bytes 65568 | tf_op jit(solution)/shard_map/ppermute | solution.py:29
  104.1 9.6 %factor.5 = f32[128,128]{1,0:T(8,128)} custom-call(f32[128,128]{1,0:T(8,128)} %add.130.gram_ref), custom_call_target="tpu_custom_call" | custom-call | flops 40000000 | bytes 131072 | tf_op jit(solution)/shard_map/factor/pallas_call | solution.py:100
  119.0 2.9 %convolution_subtract_fusion = f32[1664,128]{1,0:T(8,128)S(1)} fusion(f32[1664,128]{1,0:T(8,128)S(1)} %convolution_multiply_fusion.1, f32[512,128]{1,0:T(8,128)S(1)} %fusion.14, f32[512,1664]{1,0:T(8,128)S(1)} %copy-done.2, bf16[512,1664]{1,0:T(8,128)(2,1)S(1)} %copy-done.3), kind=kOutput, calls=%fused_computation.2 | convolution fusion | flops 656228352 | bytes 7077888 | tf_op jit(solution)/shard_map/dot_general | solution.py:14
  124.3 7.0 %collective-permute-done.19 = f32[416,128]{1,0:T(8,128)S(1)} collective-permute-done((f32[416,128]{1,0:T(8,128)S(1)}, f32[416,128]{1,0:T(8,128)S(1)}, u32[]{:S(2)}, u32[]{:S(2)}) %collective-permute-start.19) | collective-permute-done | bytes 213024 | tf_op jit(solution)/shard_map/ppermute | solution.py:29
  133.0 5.8 %collective-permute-done.20 = f32[208,128]{1,0:T(8,128)S(1)} collective-permute-done((f32[208,128]{1,0:T(8,128)S(1)}, f32[208,128]{1,0:T(8,128)S(1)}, u32[]{:S(2)}, u32[]{:S(2)}) %collective-permute-start.20) | collective-permute-done | bytes 106528 | tf_op jit(solution)/shard_map/ppermute | solution.py:29
  138.8 7.7 %collective-permute-done.21 = f32[208,128]{1,0:T(8,128)S(1)} collective-permute-done((f32[208,128]{1,0:T(8,128)S(1)}, f32[208,128]{1,0:T(8,128)S(1)}, u32[]{:S(2)}, u32[]{:S(2)}) %collective-permute-start.21) | collective-permute-done | bytes 106528 | tf_op jit(solution)/shard_map/ppermute | solution.py:29
  147.3 6.1 %collective-permute-done.22 = f32[416,128]{1,0:T(8,128)S(1)} collective-permute-done((f32[416,128]{1,0:T(8,128)S(1)}, f32[416,128]{1,0:T(8,128)S(1)}, u32[]{:S(2)}, u32[]{:S(2)}) %collective-permute-start.22) | collective-permute-done | bytes 213024 | tf_op jit(solution)/shard_map/ppermute | solution.py:29
  155.3 4.2 %collective-permute-done.16 = f32[128,128]{1,0:T(8,128)S(1)} collective-permute-done((f32[128,128]{1,0:T(8,128)S(1)}, f32[128,128]{1,0:T(8,128)S(1)}, u32[]{:S(2)}, u32[]{:S(2)}) %collective-permute-start.16) | collective-permute-done | bytes 65568 | tf_op jit(solution)/shard_map/ppermute | solution.py:29
  159.6 5.7 %collective-permute-done.17 = f32[128,128]{1,0:T(8,128)S(1)} collective-permute-done((f32[128,128]{1,0:T(8,128)S(1)}, f32[128,128]{1,0:T(8,128)S(1)}, u32[]{:S(2)}, u32[]{:S(2)}) %collective-permute-start.17) | collective-permute-done | bytes 65568 | tf_op jit(solution)/shard_map/ppermute | solution.py:29
  166.0 9.8 %factor.6 = f32[128,128]{1,0:T(8,128)} custom-call(f32[128,128]{1,0:T(8,128)} %add.133.gram_ref), custom_call_target="tpu_custom_call" | custom-call | flops 40000000 | bytes 131072 | tf_op jit(solution)/shard_map/factor/pallas_call | solution.py:100
  178.5 1.8 fusion.7
  184.6 2.0 copy.6
  187.6 6.1 %multiply_subtract_fusion = f32[512,1664]{1,0:T(8,128)} fusion(f32[1664,128]{0,1:T(8,128)} %copy-done.4, f32[1664,128]{0,1:T(8,128)S(1)} %fusion.3, f32[512,128]{0,1:T(8,128)} %copy-done.10, f32[512,128]{0,1:T(8,128)} %fusion.24, f32[512,1664]{1,0:T(8,128)} %param.3, bf16[512,1664]{1,0:T(8,128)(2,1)S(1)} %copy-done.3), kind=kOutput, calls=%fused_computation | convolution fusion | flops 1312587776 | bytes 10747904 | tf_op jit(solution)/shard_map/dot_general | solution.py:14
  194.4 9.6 %factor.7 = f32[128,128]{1,0:T(8,128)} custom-call(f32[128,128]{1,0:T(8,128)} %add.138.gram_ref), custom_call_target="tpu_custom_call" | custom-call | flops 40000000 | bytes 131072 | tf_op jit(solution)/shard_map/factor/pallas_call | solution.py:100
  204.0 3.6 %convolution_multiply_fusion = f32[1664,128]{1,0:T(8,128)} fusion(f32[1664,128]{0,1:T(8,128)} %copy-done.4, f32[128,128]{1,0:T(8,128)} %factor.7), kind=kOutput, calls=%fused_computation.3 | convolution fusion | flops 327368704 | bytes 1769472 | tf_op jit(solution)/shard_map/dot_general | solution.py:14
  (107 shorter events, 44.7 us)
Async XLA Ops:
  1.8 21.1 %copy-start.3 = (bf16[512,1664]{1,0:T(8,128)(2,1)S(1)}, bf16[512,1664]{1,0:T(8,128)(2,1)}, u32[]{:S(2)}) copy-start(bf16[512,1664]{1,0:T(8,128)(2,1)} %param.4) | copy-start | bytes 5111812
  6.0 9.3 %collective-permute-start = (f32[512,128]{1,0:T(8,128)S(1)}, f32[512,128]{1,0:T(8,128)S(1)}, u32[]{:S(2)}, u32[]{:S(2)}) collective-permute-start(f32[512,128]{1,0:T(8,128)S(1)} %fusion.22), channel_id=1, source_target_pairs={{0,1},{1,0},{2,3},{3,2},{4,5},{5,4},{6,7},{7,6},{8,9},{9,8},{10,11... | collective-permute-start | bytes 786440 | tf_op jit(solution)/shard_map/ppermute | solution.py:29
  15.3 7.6 %collective-permute-start.1 = (f32[512,128]{1,0:T(8,128)S(1)}, f32[512,128]{1,0:T(8,128)S(1)}, u32[]{:S(2)}, u32[]{:S(2)}) collective-permute-start(f32[512,128]{1,0:T(8,128)S(1)} %add.110), channel_id=1, source_target_pairs={{0,2},{1,3},{2,0},{3,1},{4,6},{5,7},{6,4},{7,5},{8,10},{9,11},{10,... | collective-permute-start | bytes 786440 | tf_op jit(solution)/shard_map/ppermute | solution.py:29
  22.9 40.1 %copy-start.6 = (f32[512,128]{1,0:T(8,128)}, f32[512,128]{1,0:T(8,128)S(1)}, u32[]{:S(2)}) copy-start(f32[512,128]{1,0:T(8,128)S(1)} %add.111) | copy-start | bytes 786436
  28.8 2.0 collective-permute-start.5
  32.0 7.5 %collective-permute-start.6 = (f32[416,128]{1,0:T(8,128)S(1)}, f32[416,128]{1,0:T(8,128)}, u32[]{:S(2)}, u32[]{:S(2)}) collective-permute-start(f32[416,128]{1,0:T(8,128)S(1)} %constant_dynamic-slice_fusion.4), channel_id=1, source_target_pairs={{0,8},{4,12},{8,0},{12,4},{16,24},{20,28},{24,16},{28,20},{1,9},{5... | collective-permute-start | bytes 638984 | tf_op jit(solution)/shard_map/ppermute | solution.py:29
  40.4 7.4 %collective-permute-start.7 = (f32[208,128]{1,0:T(8,128)S(1)}, f32[208,128]{1,0:T(8,128)S(1)}, u32[]{:S(2)}, u32[]{:S(2)}) collective-permute-start(f32[208,128]{1,0:T(8,128)S(1)} %constant_dynamic-slice_fusion.3), channel_id=1, source_target_pairs={{0,16},{4,20},{8,24},{12,28},{16,0},{20,4},{24,8},{28,12},{1,17},{... | collective-permute-start | bytes 319496 | tf_op jit(solution)/shard_map/ppermute | solution.py:29
  47.9 7.3 %collective-permute-start.8 = (f32[208,128]{1,0:T(8,128)S(1)}, f32[208,128]{1,0:T(8,128)S(1)}, u32[]{:S(2)}, u32[]{:S(2)}) collective-permute-start(f32[208,128]{1,0:T(8,128)S(1)} %dynamic-slice_add_fusion.5), channel_id=1, source_target_pairs={{0,16},{4,20},{8,24},{12,28},{16,0},{20,4},{24,8},{28,12},{1,17},{... | collective-permute-start | bytes 319496 | tf_op jit(solution)/shard_map/ppermute | solution.py:29
  55.2 6.0 %collective-permute-start.9 = (f32[416,128]{1,0:T(8,128)S(1)}, f32[416,128]{1,0:T(8,128)}, u32[]{:S(2)}, u32[]{:S(2)}) collective-permute-start(f32[416,128]{1,0:T(8,128)S(1)} %pad_maximum_fusion.2), channel_id=1, source_target_pairs={{0,8},{4,12},{8,0},{12,4},{16,24},{20,28},{24,16},{28,20},{1,9},{5... | collective-permute-start | bytes 638984 | tf_op jit(solution)/shard_map/ppermute | solution.py:29
  63.0 22.7 %collective-permute-start.10 = (f32[832,128]{1,0:T(8,128)}, f32[832,128]{1,0:T(8,128)}, u32[]{:S(2)}, u32[]{:S(2)}) collective-permute-start(f32[832,128]{1,0:T(8,128)} %pad_maximum_fusion), channel_id=1, source_target_pairs={{0,4},{4,0},{8,12},{12,8},{16,20},{20,16},{24,28},{28,24},{1,5},{5... | collective-permute-start | bytes 1277960 | tf_op jit(solution)/shard_map/ppermute | solution.py:29
  63.6 1.5 collective-permute-start.2
  65.1 4.4 %collective-permute-start.3 = (f32[128,128]{1,0:T(8,128)S(1)}, f32[128,128]{1,0:T(8,128)S(1)}, u32[]{:S(2)}, u32[]{:S(2)}) collective-permute-start(f32[128,128]{1,0:T(8,128)S(1)} %add.112), channel_id=1, source_target_pairs={{0,8},{4,12},{8,0},{12,4},{16,24},{20,28},{24,16},{28,20},{1,9},{5... | collective-permute-start | bytes 196616 | tf_op jit(solution)/shard_map/ppermute | solution.py:29
  69.5 5.9 %collective-permute-start.4 = (f32[128,128]{1,0:T(8,128)S(1)}, f32[128,128]{1,0:T(8,128)S(1)}, u32[]{:S(2)}, u32[]{:S(2)}) collective-permute-start(f32[128,128]{1,0:T(8,128)S(1)} %add.113), channel_id=1, source_target_pairs={{0,16},{4,20},{8,24},{12,28},{16,0},{20,4},{24,8},{28,12},{1,17},{... | collective-permute-start | bytes 196616 | tf_op jit(solution)/shard_map/ppermute | solution.py:29
  88.7 12.6 %copy-start.7 = (f32[512,128]{1,0:T(8,128)S(1)}, f32[512,128]{1,0:T(8,128)}, u32[]{:S(2)}) copy-start(f32[512,128]{1,0:T(8,128)} %copy-done.6) | copy-start | bytes 786436
  88.7 12.6 %copy-start.13 = (f32[128,128]{1,0:T(8,128)S(1)}, f32[128,128]{1,0:T(8,128)}, u32[]{:S(2)}) copy-start(f32[128,128]{1,0:T(8,128)} %factor.4) | copy-start | bytes 196612
  90.3 9.7 %collective-permute-start.11 = (f32[512,128]{1,0:T(8,128)S(1)}, f32[512,128]{1,0:T(8,128)S(1)}, u32[]{:S(2)}, u32[]{:S(2)}) collective-permute-start(f32[512,128]{1,0:T(8,128)S(1)} %fusion.20), channel_id=1, source_target_pairs={{0,1},{1,0},{2,3},{3,2},{4,5},{5,4},{6,7},{7,6},{8,9},{9,8},{10,11... | collective-permute-start | bytes 786440 | tf_op jit(solution)/shard_map/ppermute | solution.py:29
  92.8 5.6 %collective-permute-start.13 = (f32[128,128]{1,0:T(8,128)S(1)}, f32[128,128]{1,0:T(8,128)S(1)}, u32[]{:S(2)}, u32[]{:S(2)}) collective-permute-start(f32[128,128]{1,0:T(8,128)S(1)} %fusion.25), channel_id=1, source_target_pairs={{0,1},{1,0},{2,3},{3,2},{4,5},{5,4},{6,7},{7,6},{8,9},{9,8},{10,11... | collective-permute-start | bytes 196616 | tf_op jit(solution)/shard_map/ppermute | solution.py:29
  98.4 5.1 %collective-permute-start.14 = (f32[128,128]{1,0:T(8,128)S(1)}, f32[128,128]{1,0:T(8,128)S(1)}, u32[]{:S(2)}, u32[]{:S(2)}) collective-permute-start(f32[128,128]{1,0:T(8,128)S(1)} %add.129), channel_id=1, source_target_pairs={{0,2},{1,3},{2,0},{3,1},{4,6},{5,7},{6,4},{7,5},{8,10},{9,11},{10,... | collective-permute-start | bytes 196616 | tf_op jit(solution)/shard_map/ppermute | solution.py:29
  100.7 14.6 %collective-permute-start.12 = (f32[512,128]{1,0:T(8,128)}, f32[512,128]{1,0:T(8,128)}, u32[]{:S(2)}, u32[]{:S(2)}) collective-permute-start(f32[512,128]{1,0:T(8,128)} %add.127), channel_id=1, source_target_pairs={{0,2},{1,3},{2,0},{3,1},{4,6},{5,7},{6,4},{7,5},{8,10},{9,11},{10,... | collective-permute-start | bytes 786440 | tf_op jit(solution)/shard_map/ppermute | solution.py:29
  116.8 29.9 %copy-start.5 = (f32[512,128]{1,0:T(8,128)}, f32[512,128]{1,0:T(8,128)S(1)}, u32[]{:S(2)}) copy-start(f32[512,128]{1,0:T(8,128)S(1)} %fusion.14) | copy-start | bytes 786436
  122.0 1.8 collective-permute-start.18
  123.9 7.4 %collective-permute-start.19 = (f32[416,128]{1,0:T(8,128)S(1)}, f32[416,128]{1,0:T(8,128)S(1)}, u32[]{:S(2)}, u32[]{:S(2)}) collective-permute-start(f32[416,128]{1,0:T(8,128)S(1)} %constant_dynamic-slice_fusion.1), channel_id=1, source_target_pairs={{0,8},{4,12},{8,0},{12,4},{16,24},{20,28},{24,16},{28,20},{1,9},{5... | collective-permute-start | bytes 638984 | tf_op jit(solution)/shard_map/ppermute | solution.py:29
  131.3 7.4 %collective-permute-start.20 = (f32[208,128]{1,0:T(8,128)S(1)}, f32[208,128]{1,0:T(8,128)S(1)}, u32[]{:S(2)}, u32[]{:S(2)}) collective-permute-start(f32[208,128]{1,0:T(8,128)S(1)} %constant_dynamic-slice_fusion), channel_id=1, source_target_pairs={{0,16},{4,20},{8,24},{12,28},{16,0},{20,4},{24,8},{28,12},{1,17},{... | collective-permute-start | bytes 319496 | tf_op jit(solution)/shard_map/ppermute | solution.py:29
  138.7 7.8 %collective-permute-start.21 = (f32[208,128]{1,0:T(8,128)S(1)}, f32[208,128]{1,0:T(8,128)S(1)}, u32[]{:S(2)}, u32[]{:S(2)}) collective-permute-start(f32[208,128]{1,0:T(8,128)S(1)} %dynamic-slice_add_fusion.4), channel_id=1, source_target_pairs={{0,16},{4,20},{8,24},{12,28},{16,0},{20,4},{24,8},{28,12},{1,17},{... | collective-permute-start | bytes 319496 | tf_op jit(solution)/shard_map/ppermute | solution.py:29
  146.6 6.9 %collective-permute-start.22 = (f32[416,128]{1,0:T(8,128)S(1)}, f32[416,128]{1,0:T(8,128)S(1)}, u32[]{:S(2)}, u32[]{:S(2)}) collective-permute-start(f32[416,128]{1,0:T(8,128)S(1)} %pad_maximum_fusion.3), channel_id=1, source_target_pairs={{0,8},{4,12},{8,0},{12,4},{16,24},{20,28},{24,16},{28,20},{1,9},{5... | collective-permute-start | bytes 638984 | tf_op jit(solution)/shard_map/ppermute | solution.py:29
  147.3 7.7 %collective-permute-start.15 = (f32[128,128]{1,0:T(8,128)S(1)}, f32[128,128]{1,0:T(8,128)S(1)}, u32[]{:S(2)}, u32[]{:S(2)}) collective-permute-start(f32[128,128]{1,0:T(8,128)S(1)} %fusion.26), channel_id=1, source_target_pairs={{0,4},{4,0},{8,12},{12,8},{16,20},{20,16},{24,28},{28,24},{1,5},{5... | collective-permute-start | bytes 196616 | tf_op jit(solution)/shard_map/ppermute | solution.py:29
  154.9 22.2 %collective-permute-start.23 = (f32[832,128]{1,0:T(8,128)}, f32[832,128]{1,0:T(8,128)}, u32[]{:S(2)}, u32[]{:S(2)}) collective-permute-start(f32[832,128]{1,0:T(8,128)} %pad_maximum_fusion.1), channel_id=1, source_target_pairs={{0,4},{4,0},{8,12},{12,8},{16,20},{20,16},{24,28},{28,24},{1,5},{5... | collective-permute-start | bytes 1277960 | tf_op jit(solution)/shard_map/ppermute | solution.py:29
  155.0 4.6 %collective-permute-start.16 = (f32[128,128]{1,0:T(8,128)S(1)}, f32[128,128]{1,0:T(8,128)S(1)}, u32[]{:S(2)}, u32[]{:S(2)}) collective-permute-start(f32[128,128]{1,0:T(8,128)S(1)} %add.131), channel_id=1, source_target_pairs={{0,8},{4,12},{8,0},{12,4},{16,24},{20,28},{24,16},{28,20},{1,9},{5... | collective-permute-start | bytes 196616 | tf_op jit(solution)/shard_map/ppermute | solution.py:29
  159.5 5.8 %collective-permute-start.17 = (f32[128,128]{1,0:T(8,128)S(1)}, f32[128,128]{1,0:T(8,128)S(1)}, u32[]{:S(2)}, u32[]{:S(2)}) collective-permute-start(f32[128,128]{1,0:T(8,128)S(1)} %add.132), channel_id=1, source_target_pairs={{0,16},{4,20},{8,24},{12,28},{16,0},{20,4},{24,8},{28,12},{1,17},{... | collective-permute-start | bytes 196616 | tf_op jit(solution)/shard_map/ppermute | solution.py:29
  175.8 8.0 %copy-start.8 = (f32[512,128]{0,1:T(8,128)S(1)}, f32[512,128]{0,1:T(8,128)}, u32[]{:S(2)}) copy-start(f32[512,128]{0,1:T(8,128)} %fusion.24) | copy-start | bytes 786436
  182.1 4.5 %collective-permute-start.24 = (f32[128,128]{1,0:T(8,128)S(1)}, f32[128,128]{1,0:T(8,128)S(1)}, u32[]{:S(2)}, u32[]{:S(2)}) collective-permute-start(f32[128,128]{1,0:T(8,128)S(1)} %fusion.29), channel_id=1, source_target_pairs={{0,1},{1,0},{2,3},{3,2},{4,5},{5,4},{6,7},{7,6},{8,9},{9,8},{10,11... | collective-permute-start | bytes 196616 | tf_op jit(solution)/shard_map/ppermute | solution.py:29
  186.6 7.1 %collective-permute-start.25 = (f32[128,128]{1,0:T(8,128)S(1)}, f32[128,128]{1,0:T(8,128)S(1)}, u32[]{:S(2)}, u32[]{:S(2)}) collective-permute-start(f32[128,128]{1,0:T(8,128)S(1)} %add.137), channel_id=1, source_target_pairs={{0,2},{1,3},{2,0},{3,1},{4,6},{5,7},{6,4},{7,5},{8,10},{9,11},{10,... | collective-permute-start | bytes 196616 | tf_op jit(solution)/shard_map/ppermute | solution.py:29
  (8 other events, 20.0 us)
where the time goes:
time: 208 us
  waiting for transfers between devices  90.4 us (43%)
  Pallas kernels  38.5 us (19%)
  matrix products  37.6 us (18%)
  starting transfers between devices  22.4 us (11%)
  other arithmetic  11.6 us (6%)
  local copies, waits for them, and re-layouts  5.85 us (3%)
    ppermute x26, waiting for transfers between devices, swap(): lax.ppermute(x, axis, [(i, i ^ mask) for i in range(lax.axis_size(axis))])  90.4 us
    pallas_call x4, Pallas kernels, factor(): pl.pallas_call(factor_body, out_shape=jax.ShapeDtypeStruct(gram.shape, gr...  38.5 us
    dot_general x18, matrix products, mm(): lax.dot_general(a, b, ((dims[0], dims[1]), ((), ())), precision=precision)  37.6 us
    ppermute x26, starting transfers between devices, swap(): lax.ppermute(x, axis, [(i, i ^ mask) for i in range(lax.axis_size(axis))])  22.4 us
    unnamed x29, local copies, waits for them, and re-layouts  5.7 us
  transfers between devices with their start and end apart: 26, of which 19 were waited for; matrix products, arithmetic and copies ran while one was open for 9% of the time, Pallas kernels for 14%

commit v1 on v0

v1 whole, which is shorter than its diff:
```python
import jax
import jax.numpy as jnp
from jax import lax
from jax.experimental import pallas as pl
from jax.experimental.pallas import tpu as pltpu
from jax.sharding import PartitionSpec as P

F32 = jnp.float32
BF16 = jnp.bfloat16
HIGHEST = lax.Precision.HIGHEST
VMEM = pl.BlockSpec(memory_space=pltpu.VMEM)
SMEM = pl.BlockSpec(memory_space=pltpu.SMEM)
NN = (((1,), (0,)), ((), ()))
NT = (((1,), (1,)), ((), ()))
KEEP = 0.95


def masks_of(axis):
    size = lax.axis_size(axis)
    masks = []
    mask = 1
    while mask < size:
        masks.append(mask)
        mask *= 2
    assert mask == size
    return masks


def swap(x, axis, mask):
    return lax.ppermute(x, axis, [(i, i ^ mask) for i in range(lax.axis_size(axis))])


def sum_whole(x, axis):
    for mask in masks_of(axis):
        x = x + swap(x, axis, mask)
    return x


def split(x):
    high = x.astype(BF16)
    return high, (x - high.astype(F32)).astype(BF16)


def dot(a, b, dims=NN):
    return lax.dot_general(a, b, dims, preferred_element_type=F32)


def exact(a, b, dims=NN):
    return lax.dot_general(a, b, dims, precision=HIGHEST, preferred_element_type=F32)


def tiles(width, most=256):
    return [(start, min(most, width - start)) for start in range(0, width, most)]


def struct(*shape, dtype=F32):
    return jax.ShapeDtypeStruct(shape, dtype)


def call(body, name, out, ins, scratch=(), flops=0, nbytes=0, **kw):
    return pl.pallas_call(
        body,
        out_shape=out,
        in_specs=[SMEM if x.dtype == jnp.int32 else VMEM for x in ins],
        out_specs=jax.tree.map(lambda _: VMEM, out),
        scratch_shapes=list(scratch),
        name=name,
        compiler_params=pltpu.CompilerParams(vmem_limit_bytes=24 * 2**20),
        cost_estimate=pl.CostEstimate(flops=flops, bytes_accessed=nbytes, transcendentals=0),
        **kw,
    )(*ins)


def start_body(momentum_ref, grad_ref, basis_ref, high_ref, low_ref, top_ref, bottom_ref, both_ref):
    step = pl.program_id(0)
    rank = basis_ref.shape[1]
    rows = momentum_ref.shape[0]
    half = top_ref.shape[0] // rows

    @pl.when(step == 0)
    def _():
        high, low = split(basis_ref[...])
        both_ref[:, :rank] = high
        both_ref[:, rank:] = low

    high, low = split(momentum_ref[...] + grad_ref[...].astype(F32))
    high_ref[...] = high
    low_ref[...] = low
    wide = dot(high, both_ref[...])
    proj = wide[:, :rank] + wide[:, rank:] + dot(low, both_ref[:, :rank])

    @pl.when(step < half)
    def _():
        top_ref[pl.ds(pl.multiple_of(step * rows, rows), rows), :] = proj

    @pl.when(step >= half)
    def _():
        bottom_ref[pl.ds(pl.multiple_of((step - half) * rows, rows), rows), :] = proj


def start(momentum, grad, basis):
    rows, cols = momentum.shape
    rank = basis.shape[1]
    block = rows // 4
    tile = pl.BlockSpec((block, cols), lambda i: (i, 0))
    whole = pl.BlockSpec((rows // 2, rank), lambda i: (0, 0))
    return pl.pallas_call(
        start_body,
        grid=(4,),
        in_specs=[tile, tile, pl.BlockSpec((cols, rank), lambda i: (0, 0))],
        out_specs=[tile, tile, whole, whole],
        out_shape=[struct(rows, cols, dtype=BF16)] * 2 + [struct(rows // 2, rank)] * 2,
        scratch_shapes=[pltpu.VMEM((cols, 2 * rank), BF16)],
        name="start",
        compiler_params=pltpu.CompilerParams(vmem_limit_bytes=24 * 2**20),
    )(momentum, grad, basis)


def pull_core(place_ref, proj, high_ref, low_ref, gram_ref, keep_ref, send_ref, turned_ref, extra=None):
    rank = proj.shape[1]
    width = high_ref.shape[1]
    turned = proj.T
    gram_ref[...] = exact(turned, proj)
    turned_ref[...] = turned
    place = place_ref[0]
    half = keep_ref.shape[0]
    count = extra[0]
    chunk = rank // count
    order = [j for j in range(count) if j % 2 == 0] + [j for j in range(count) if j % 2 == 1]
    parts = [turned_ref[pl.ds(pl.multiple_of((place ^ j) * chunk, chunk), chunk), :] for j in order]
    turned = jnp.concatenate(parts, axis=0)
    high, low = split(turned)
    both = jnp.concatenate([high, low], axis=0)
    if len(extra) > 1:
        left_ref, right_ref = extra[1:]
        cross_high, cross_low = split(-KEEP * exact(turned, left_ref[...]))
        cross = jnp.concatenate([cross_high, cross_low], axis=0)
    for at, size in tiles(width):
        wide = dot(both, high_ref[:, at:at + size])
        out = wide[:rank] + wide[rank:] + dot(high, low_ref[:, at:at + size])
        if len(extra) > 1:
            right_high, right_low = split(right_ref[:, at:at + size])
            wide = dot(cross, right_high)
            out = out + (wide[:rank] + wide[rank:] + dot(cross_high, right_low))
        keep_ref[:, at:at + size] = out[:half]
        send_ref[:, at:at + size] = out[half:]


def pull(count, place, halves, high, low, before=None):
    rows, width = high.shape
    rank = halves[0].shape[1]

    def body(place_ref, a, b, c, d, high_ref, low_ref, *rest):
        total = jnp.concatenate([a[...] + b[...], c[...] + d[...]], axis=0)
        if before is None:
            proj_ref, gram_ref, keep_ref, send_ref, turned_ref = rest
            extra = (count,)
        else:
            left_ref, right_ref, gram_in, inv_ref, proj_ref, gram_ref, keep_ref, send_ref, turned_ref = rest
            total = total - KEEP * exact(left_ref[...], gram_in[...])
            total = exact(total, inv_ref[...], NT)
            extra = (count, left_ref, right_ref)
        proj_ref[...] = total
        pull_core(place_ref, total, high_ref, low_ref, gram_ref, keep_ref, send_ref, turned_ref, extra)

    out = [struct(rows, rank), struct(rank, rank), struct(rank // 2, width), struct(rank // 2, width)]
    ins = [place, *halves, high, low] + list(before or [])
    return call(body, "pull", out, ins, [pltpu.VMEM((rank, rows), F32)], flops=1_000_000_000, nbytes=5_000_000)


def push_body(count, last, place_ref, inv_ref, proj_ref, high_ref, low_ref, *rest):
    pieces = rest[:count]
    if last:
        left_ref, right_ref, gram_ref, raw_ref = rest[count:]
    else:
        left_ref, right_ref, gram_ref, top_ref, bottom_ref, raw_ref = rest[count:]
    rank, width = right_ref.shape
    chunk = rank // count
    place = place_ref[0]
    for j, piece in enumerate(pieces):
        raw_ref[pl.ds(pl.multiple_of((place ^ j) * chunk, chunk), chunk), :] = piece[...]
    inv = inv_ref[...]
    inv_high, inv_low = split(inv)
    inv_both = jnp.concatenate([inv_high, inv_low], axis=0)
    gram = jnp.zeros((rank, rank), F32)
    image = None
    for at, size in tiles(width):
        raw_high, raw_low = split(raw_ref[:, at:at + size])
        wide = dot(inv_both, raw_high)
        right = wide[:rank] + wide[rank:] + dot(inv_high, raw_low)
        right_ref[:, at:at + size] = right
        high, low = split(right)
        both = jnp.concatenate([high, low], axis=0)
        wide = dot(both, high, NT)
        gram = gram + (wide[:rank] + wide[rank:] + dot(high, low, NT))
        if not last:
            wide = dot(high_ref[:, at:at + size], both, NT)
            part = wide[:, :rank] + wide[:, rank:] + dot(low_ref[:, at:at + size], high, NT)
            image = part if image is None else image + part
    gram_ref[...] = gram
    if not last:
        half = top_ref.shape[0]
        top_ref[...] = image[:half]
        bottom_ref[...] = image[half:]
    left_ref[...] = exact(proj_ref[...], inv, NT)


def push(count, place, inv, proj, high, low, pieces, last):
    rows, width = high.shape
    rank = inv.shape[0]
    out = [struct(rows, rank), struct(rank, width), struct(rank, rank)]
    if not last:
        out += [struct(rows // 2, rank)] * 2

    def body(*refs):
        push_body(count, last, *refs)

    ins = [place, inv, proj, high, low, *pieces]
    return call(body, "push", out, ins, [pltpu.VMEM((rank, width), F32)], flops=1_000_000_000, nbytes=5_000_000)


def finish_body(scale, momentum_ref, grad_ref, left_a, left_b, right_a, right_b, out_ref, lefts_ref, high_ref, low_ref):
    rank, width = right_a.shape

    @pl.when(pl.program_id(0) == 0)
    def _():
        for i, ref in enumerate((right_a, right_b)):
            high, low = split(KEEP * ref[...])
            high_ref[i * rank:(i + 1) * rank, :] = high
            low_ref[i * rank:(i + 1) * rank, :] = low

    lefts_ref[0] = scale * left_a[...]
    lefts_ref[1] = scale * left_b[...]
    high, low = split(jnp.concatenate([left_a[...], left_b[...]], axis=1))
    for at, size in tiles(width):
        right_high = high_ref[:, at:at + size]
        outer = dot(high, right_high) + dot(low, right_high) + dot(high, low_ref[:, at:at + size])
        work = momentum_ref[:, at:at + size] + grad_ref[:, at:at + size].astype(F32)
        out_ref[:, at:at + size] = work - outer


def finish(momentum, grad, left_a, left_b, right_a, right_b, scale):
    rows, cols = momentum.shape
    rank = left_a.shape[1]
    block = rows // 4
    tile = pl.BlockSpec((block, cols), lambda i: (i, 0))
    left_tile = pl.BlockSpec((block, rank), lambda i: (i, 0))
    right_tile = pl.BlockSpec((rank, cols), lambda i: (0, 0))

    def body(*refs):
        finish_body(scale, *refs)

    return pl.pallas_call(
        body,
        grid=(4,),
        in_specs=[tile, tile, left_tile, left_tile, right_tile, right_tile],
        out_specs=[tile, pl.BlockSpec((2, block, rank), lambda i: (0, i, 0))],
        out_shape=[struct(rows, cols), struct(2, rows, rank)],
        scratch_shapes=[pltpu.VMEM((2 * rank, cols), BF16)] * 2,
        name="finish",
        compiler_params=pltpu.CompilerParams(vmem_limit_bytes=24 * 2**20),
        cost_estimate=pl.CostEstimate(flops=1_500_000_000, bytes_accessed=12_000_000, transcendentals=0),
    )(momentum, grad, left_a, left_b, right_a, right_b)


def eliminate(full, first):
    rank = full.shape[1]
    sub = lax.broadcasted_iota(jnp.int32, (8, rank), 0)
    lane = lax.broadcasted_iota(jnp.int32, (8, rank), 1)
    rolled = pltpu.roll(full, lax.rem(rank - first, rank), 1)
    cols = [jnp.broadcast_to(rolled[:, j:j + 1], (8, rank)) for j in range(8)]
    for j in range(8):
        pivot = jnp.broadcast_to(cols[j][j:j + 1], (8, rank))
        mult = jnp.where(sub > j, cols[j] * (1.0 / pivot), 0.0)
        for k in range(j + 1, 8):
            cols[k] = cols[k] - mult * cols[k][j:j + 1]
        here = lane == first + j
        row = jnp.where(here[:1], 1.0, full[j:j + 1])
        rest = jnp.where(here & (sub > j), 0.0, full) - mult * row
        full = jnp.where(sub == j, row * lax.rsqrt(pivot), rest)
    return full

def factor_body(gram_ref, out_ref):
    rank = gram_ref.shape[0]
    out_ref[...] = gram_ref[...]
    row = lax.broadcasted_iota(jnp.int32, (rank, rank), 0)
    col = lax.broadcasted_iota(jnp.int32, (rank, rank), 1)

    def panel(p, carry):
        first = pl.multiple_of(p * 8, 8)
        done = eliminate(out_ref[pl.ds(first, 8), :], first)
        sub = lax.broadcasted_iota(jnp.int32, (8, rank), 0)
        lane = lax.broadcasted_iota(jnp.int32, (8, rank), 1)
        lower = jnp.where((lane > first + sub) & (lane < first + 8), 0.0, done)
        step = lax.dot_general(done, lower, (((0,), (0,)), ((), ())), precision=HIGHEST, preferred_element_type=jnp.float32)
        old = out_ref[...]
        old = jnp.where(row >= first + 8, jnp.where((col >= first) & (col < first + 8), 0.0, old) - step, old)
        out_ref[...] = old
        out_ref[pl.ds(first, 8), :] = done
        return carry

    lax.fori_loop(0, rank // 8, panel, 0)
    out_ref[...] = jnp.where(row >= col, out_ref[...], 0.0)

def factor(gram):
    return call(factor_body, "factor", struct(*gram.shape), [gram], flops=2_000_000_000, nbytes=131072)


def last_factor(gram, right, scale):
    def body(gram_ref, right_ref, out_ref, inv_ref):
        factor_body(gram_ref, inv_ref)
        turned = right_ref[...].T
        high, low = split(turned)
        inv_high, inv_low = split(scale * inv_ref[...])
        both = jnp.concatenate([inv_high, inv_low], axis=0)
        rank = inv_high.shape[0]
        wide = dot(high, both, NT)
        out_ref[...] = wide[:, :rank] + wide[:, rank:] + dot(low, inv_high, NT)

    rank, width = right.shape
    return call(body, "last_factor", struct(width, rank), [gram, right], [pltpu.VMEM((rank, rank), F32)],
                flops=2_000_000_000, nbytes=2_000_000)


def sum_halves(top, bottom, axis):
    masks = masks_of(axis)
    for one, two in zip(masks[:-1], masks[:0:-1]):
        other_top, other_bottom = swap(top, axis, one), swap(bottom, axis, two)
        top, bottom = top + other_top, bottom + other_bottom
    return top, swap(top, axis, masks[-1]), bottom, swap(bottom, axis, masks[0])


def sum_rows(keep, send, count):
    rows = 2 * keep.shape[0] // count
    keep = keep + swap(send, "row", 1)
    chunks = [keep[i * rows:(i + 1) * rows] for i in range(count // 2)]
    own = chunks[0]
    for i in range(1, count // 2):
        own = own + swap(chunks[i], "row", 2 * i)
    even = [own] + [swap(own, "row", 2 * i) for i in range(1, count // 2)]
    odd = [swap(x, "row", 1) for x in even]
    return [x for pair in zip(even, odd) for x in pair]


def shards(momentum, grad, basis):
    count = lax.axis_size("row")
    row_scale = float(momentum.shape[0] * count) ** 0.5
    col_scale = float(momentum.shape[1] * lax.axis_size("col")) ** 0.5
    place = lax.axis_index("row").astype(jnp.int32).reshape(1)
    high, low, top, bottom = start(momentum, grad, basis)
    halves = sum_halves(top, bottom, "col")
    proj, gram, keep, send = pull(count, place, halves, high, low)
    inv = factor(sum_whole(gram, "row"))
    pieces = sum_rows(keep, send, count)
    left_a, right_a, gram, top, bottom = push(count, place, inv, proj, high, low, pieces, False)
    gram = sum_whole(gram, "col")
    halves = sum_halves(top, bottom, "col")
    inv = factor(gram)
    proj, gram, keep, send = pull(count, place, halves, high, low, (left_a, right_a, gram, inv))
    inv = factor(sum_whole(gram, "row"))
    pieces = sum_rows(keep, send, count)
    left_b, right_b, gram = push(count, place, inv, proj, high, low, pieces, True)
    gram = sum_whole(gram, "col")
    momentum_out, lefts = finish(momentum, grad, left_a, left_b, right_a, right_b, row_scale)
    return momentum_out, lefts, last_factor(gram, right_b, col_scale)


def solution(mesh):
    in_specs = (P("row", "col"), P("row", "col"), P("col", None))
    out_specs = (P("row", "col"), P(None, "row", None), P("col", None))
    return jax.shard_map(shards, mesh=mesh, in_specs=in_specs, out_specs=out_specs, check_vma=False)
```

time: 208 us -> 148 us (0.71)
  waiting for transfers between devices: 90.4 us -> 52.4 us
  matrix products: 37.6 us -> 0 us
  starting transfers between devices: 22.4 us -> 39.2 us
  Pallas kernels: 38.5 us -> 49.2 us
  other arithmetic: 11.6 us -> 0.98 us
    ppermute x26 -> x40, waiting for transfers between devices: 90.4 us -> 52.4 us  [swap(): lax.ppermute(x, axis, [(i, i ^ mask) for i in range(lax.axis_size(axis))])]
    dot_general x18 -> x0, matrix products: 37.6 us -> none  [mm(): lax.dot_general(a, b, ((dims[0], dims[1]), ((), ())), precision=precision)]
    ppermute x26 -> x40, starting transfers between devices: 22.4 us -> 39.2 us  [swap(): lax.ppermute(x, axis, [(i, i ^ mask) for i in range(lax.axis_size(axis))])]
    pallas_call x4 -> x10, Pallas kernels: 38.5 us -> 49.2 us  [the longest x8 43.5 us: call(): pl.pallas_call(body, out_shape=out, in_specs=[SMEM if x.dtype == jnp.int3...]
    select_n x6 -> x0, other arithmetic: 3.57 us -> none  [sum_halving(): low = jnp.where(bit == 0, x, other)]
    add x13 -> x10, other arithmetic: 3.4 us -> 0.09 us  [sum_whole(): x = x + swap(x, axis, mask)]
    unnamed x29 -> x10, local copies, waits for them, and re-layouts: 5.7 us -> 4.58 us
  transfers between devices with their start and end apart: 26 -> 40, of which waited for: 19 -> 16; matrix products, arithmetic and copies ran while one was open for 9% -> 1% of each run, Pallas kernels for 14% -> 19%
where the time goes in v1:
time: 148 us; the launch traced here: 147 us
  waiting for transfers between devices  52.4 us (35%)
  Pallas kernels  49.2 us (33%)
  starting transfers between devices  39.2 us (26%)
  local copies, waits for them, and re-layouts  4.62 us (3%)
    ppermute x40, waiting for transfers between devices, swap(): lax.ppermute(x, axis, [(i, i ^ mask) for i in range(lax.axis_size(axis))])  52.4 us
    pallas_call x8, Pallas kernels, call(): pl.pallas_call(body, out_shape=out, in_specs=[SMEM if x.dtype == jnp.int3...  43.5 us
    ppermute x40, starting transfers between devices, swap(): lax.ppermute(x, axis, [(i, i ^ mask) for i in range(lax.axis_size(axis))])  39.2 us
    unnamed x10, local copies, waits for them, and re-layouts  4.58 us
    pallas_call x1, Pallas kernels, finish(): pl.pallas_call(body, grid=(4,), in_specs=[tile, tile, left_tile, left_til...  3.95 us
  transfers between devices with their start and end apart: 40, of which 16 were waited for; matrix products, arithmetic and copies ran while one was open for 1% of the time, Pallas kernels for 19%

profile of v1, /device:TPU:0, one launch (start us, length us, event | category | flops | bytes accessed | tf_op | source)
XLA Modules:
  0.0 147.3 jit_solution(13745064526104828057)
XLA Ops:
  0.6 2.0 %copy-done = f32[512,1664]{1,0:T(8,128)S(1)} copy-done((f32[512,1664]{1,0:T(8,128)S(1)}, f32[512,1664]{1,0:T(8,128)}, u32[]{:S(2)}) %copy-start) | copy-done | bytes 3407896
  5.2 1.8 %start.1 = (bf16[512,1664]{1,0:T(8,128)(2,1)S(1)}, bf16[512,1664]{1,0:T(8,128)(2,1)S(1)}, f32[256,128]{1,0:T(8,128)S(1)}, f32[256,128]{1,0:T(8,128)S(1)}) custom-call(f32[512,1664]{1,0:T(8,128)S(1)} %copy-done, bf16[512,1664]{1,0:T(8,128)(2,1)S(1)} %copy-done.2, f32[1664,128]{1,0:T(8,128)S(1)} %copy-done.4), custom_call_target="tpu_custom_call" | custom-call | tf_op jit(solution)/shard_map/start/pallas_call | solution.py:107
  7.0 3.0 %collective-permute-start = (f32[256,128]{1,0:T(8,128)S(1)}, f32[256,128]{1,0:T(8,128)S(1)}, u32[]{:S(2)}, u32[]{:S(2)}) collective-permute-start(f32[256,128]{1,0:T(8,128)S(1)} %get-tuple-element.25), channel_id=1, source_target_pairs={{0,1},{1,0},{2,3},{3,2},{4,5},{5,4},{6,7},{7,6},{8,9},{9,8},{10,11... | collective-permute-start | bytes 393224 | tf_op jit(solution)/shard_map/ppermute | solution.py:30
  10.0 1.5 %collective-permute-start.2 = (f32[256,128]{1,0:T(8,128)S(1)}, f32[256,128]{1,0:T(8,128)S(1)}, u32[]{:S(2)}, u32[]{:S(2)}) collective-permute-start(f32[256,128]{1,0:T(8,128)S(1)} %get-tuple-element.26), channel_id=1, source_target_pairs={{0,2},{1,3},{2,0},{3,1},{4,6},{5,7},{6,4},{7,5},{8,10},{9,11},{10,... | collective-permute-start | bytes 393224 | tf_op jit(solution)/shard_map/ppermute | solution.py:30
  11.5 2.0 %collective-permute-done = f32[256,128]{1,0:T(8,128)S(1)} collective-permute-done((f32[256,128]{1,0:T(8,128)S(1)}, f32[256,128]{1,0:T(8,128)S(1)}, u32[]{:S(2)}, u32[]{:S(2)}) %collective-permute-start) | collective-permute-done | bytes 131104 | tf_op jit(solution)/shard_map/ppermute | solution.py:30
  13.5 1.8 %collective-permute-start.1 = (f32[256,128]{1,0:T(8,128)S(1)}, f32[256,128]{1,0:T(8,128)}, u32[]{:S(2)}, u32[]{:S(2)}) collective-permute-start(f32[256,128]{1,0:T(8,128)S(1)} %add.66.a), channel_id=1, source_target_pairs={{0,2},{1,3},{2,0},{3,1},{4,6},{5,7},{6,4},{7,5},{8,10},{9,11},{10,... | collective-permute-start | bytes 393224 | tf_op jit(solution)/shard_map/ppermute | solution.py:30
  16.0 1.5 %collective-permute-start.3 = (f32[256,128]{1,0:T(8,128)}, f32[256,128]{1,0:T(8,128)}, u32[]{:S(2)}, u32[]{:S(2)}) collective-permute-start(f32[256,128]{1,0:T(8,128)} %add.67.c), channel_id=1, source_target_pairs={{0,1},{1,0},{2,3},{3,2},{4,5},{5,4},{6,7},{7,6},{8,9},{9,8},{10,11... | collective-permute-start | bytes 393224 | tf_op jit(solution)/shard_map/ppermute | solution.py:30
  18.7 2.7 %collective-permute-done.3.d = f32[256,128]{1,0:T(8,128)} collective-permute-done((f32[256,128]{1,0:T(8,128)}, f32[256,128]{1,0:T(8,128)}, u32[]{:S(2)}, u32[]{:S(2)}) %collective-permute-start.3) | collective-permute-done | bytes 131104 | tf_op jit(solution)/shard_map/ppermute | solution.py:30
  21.3 2.2 %pull.2 = (f32[512,128]{1,0:T(8,128)S(1)}, f32[128,128]{1,0:T(8,128)S(1)}, f32[64,1664]{1,0:T(8,128)S(1)}, f32[64,1664]{1,0:T(8,128)S(1)}) custom-call(s32[1]{0:T(128)} %bitcast.place_ref.refs_0_, f32[256,128]{1,0:T(8,128)S(1)} %add.66.a, f32[256,128]{1,0:T(8,128)} %collective-permute-done.1.b, f32[256,128]{1,0:T(8,128)} %add.67.c, ...), custom_call_target="tpu_custom_call" | custom-call | flops 1000000000 | bytes 5000000 | tf_op jit(solution)/shard_map/pull/pallas_call | solution.py:61
  23.6 1.8 %collective-permute-done.7 = f32[64,1664]{1,0:T(8,128)S(1)} collective-permute-done((f32[64,1664]{1,0:T(8,128)S(1)}, f32[64,1664]{1,0:T(8,128)S(1)}, u32[]{:S(2)}, u32[]{:S(2)}) %collective-permute-start.7) | collective-permute-done | bytes 426016 | tf_op jit(solution)/shard_map/ppermute | solution.py:30
  25.4 3.7 %collective-permute-start.10 = (f32[16,1664]{1,0:T(8,128)S(1)}, f32[16,1664]{1,0:T(8,128)S(1)}, u32[]{:S(2)}, u32[]{:S(2)}) collective-permute-start(f32[16,1664]{1,0:T(8,128)S(1)} %get-tuple-element.51), channel_id=1, source_target_pairs={{0,24},{4,28},{8,16},{12,20},{16,8},{20,12},{24,0},{28,4},{1,25},{... | collective-permute-start | bytes 319496 | tf_op jit(solution)/shard_map/ppermute | solution.py:30
  33.2 5.2 %collective-permute-done.9 = f32[16,1664]{1,0:T(8,128)S(1)} collective-permute-done((f32[16,1664]{1,0:T(8,128)S(1)}, f32[16,1664]{1,0:T(8,128)S(1)}, u32[]{:S(2)}, u32[]{:S(2)}) %collective-permute-start.9) | collective-permute-done | bytes 106528 | tf_op jit(solution)/shard_map/ppermute | solution.py:30
  39.5 2.1 %collective-permute-start.14 = (f32[16,1664]{1,0:T(8,128)S(1)}, f32[16,1664]{1,0:T(8,128)S(1)}, u32[]{:S(2)}, u32[]{:S(2)}) collective-permute-start(f32[16,1664]{1,0:T(8,128)S(1)} %fusion.3.refs_5_), channel_id=1, source_target_pairs={{0,16},{4,20},{8,24},{12,28},{16,0},{20,4},{24,8},{28,12},{1,17},{... | collective-permute-start | bytes 319496 | tf_op jit(solution)/shard_map/ppermute | solution.py:30
  43.2 10.1 %collective-permute-done.6 = f32[128,128]{1,0:T(8,128)S(1)} collective-permute-done((f32[128,128]{1,0:T(8,128)S(1)}, f32[128,128]{1,0:T(8,128)S(1)}, u32[]{:S(2)}, u32[]{:S(2)}) %collective-permute-start.6) | collective-permute-done | bytes 65568 | tf_op jit(solution)/shard_map/ppermute | solution.py:30
  54.5 8.1 %factor.3.refs_1_ = f32[128,128]{1,0:T(8,128)S(1)} custom-call(f32[128,128]{1,0:T(8,128)S(1)} %add.70.gram_ref), custom_call_target="tpu_custom_call" | custom-call | flops 2000000000 | bytes 131072 | tf_op jit(solution)/shard_map/factor/pallas_call | solution.py:61
  62.6 3.2 %push.2 = (f32[512,128]{1,0:T(8,128)S(1)}, f32[128,1664]{1,0:T(8,128)S(1)}, f32[128,128]{1,0:T(8,128)S(1)}, f32[256,128]{1,0:T(8,128)S(1)}, f32[256,128]{1,0:T(8,128)S(1)}) custom-call(s32[1]{0:T(128)} %bitcast.place_ref.refs_0_, f32[128,128]{1,0:T(8,128)S(1)} %factor.3.refs_1_, f32[512,128]{1,0:T(8,128)S(1)} %get-tuple-element.30.refs_2_, ...), custom_call_target="tpu_custom_call" | custom-call | flops 1000000000 | bytes 5000000 | tf_op jit(solution)/shard_map/push/pallas_call | solution.py:61
  65.9 1.6 %collective-permute-start.18 = (f32[256,128]{1,0:T(8,128)S(1)}, f32[256,128]{1,0:T(8,128)S(1)}, u32[]{:S(2)}, u32[]{:S(2)}) collective-permute-start(f32[256,128]{1,0:T(8,128)S(1)} %get-tuple-element.34), channel_id=1, source_target_pairs={{0,1},{1,0},{2,3},{3,2},{4,5},{5,4},{6,7},{7,6},{8,9},{9,8},{10,11... | collective-permute-start | bytes 393224 | tf_op jit(solution)/shard_map/ppermute | solution.py:30
  69.1 3.7 %collective-permute-done.22 = f32[128,128]{1,0:T(8,128)S(1)} collective-permute-done((f32[128,128]{1,0:T(8,128)S(1)}, f32[128,128]{1,0:T(8,128)S(1)}, u32[]{:S(2)}, u32[]{:S(2)}) %collective-permute-start.22) | collective-permute-done | bytes 65568 | tf_op jit(solution)/shard_map/ppermute | solution.py:30
  75.1 1.6 %collective-permute-start.21 = (f32[256,128]{1,0:T(8,128)S(1)}, f32[256,128]{1,0:T(8,128)S(1)}, u32[]{:S(2)}, u32[]{:S(2)}) collective-permute-start(f32[256,128]{1,0:T(8,128)S(1)} %add.76.c), channel_id=1, source_target_pairs={{0,1},{1,0},{2,3},{3,2},{4,5},{5,4},{6,7},{7,6},{8,9},{9,8},{10,11... | collective-permute-start | bytes 393224 | tf_op jit(solution)/shard_map/ppermute | solution.py:30
  77.8 8.1 %factor.4.rest_3_ = f32[128,128]{1,0:T(8,128)S(1)} custom-call(f32[128,128]{1,0:T(8,128)S(1)} %add.78.gram_ref.rest_2_), custom_call_target="tpu_custom_call" | custom-call | flops 2000000000 | bytes 131072 | tf_op jit(solution)/shard_map/factor/pallas_call | solution.py:61
  86.0 2.6 %pull.3 = (f32[512,128]{1,0:T(8,128)S(1)}, f32[128,128]{1,0:T(8,128)S(1)}, f32[64,1664]{1,0:T(8,128)S(1)}, f32[64,1664]{1,0:T(8,128)S(1)}) custom-call(s32[1]{0:T(128)} %bitcast.place_ref.refs_0_, f32[256,128]{1,0:T(8,128)S(1)} %add.75.a, f32[256,128]{1,0:T(8,128)S(1)} %collective-permute-done.19.b, f32[256,128]{1,0:T(8,128)S(1)} %add.76.c, ...), custom_call_target="tpu_custom_call" | custom-call | flops 1000000000 | bytes 5000000 | tf_op jit(solution)/shard_map/pull/pallas_call | solution.py:61
  88.7 1.8 %collective-permute-done.27 = f32[64,1664]{1,0:T(8,128)S(1)} collective-permute-done((f32[64,1664]{1,0:T(8,128)S(1)}, f32[64,1664]{1,0:T(8,128)S(1)}, u32[]{:S(2)}, u32[]{:S(2)}) %collective-permute-start.27) | collective-permute-done | bytes 426016 | tf_op jit(solution)/shard_map/ppermute | solution.py:30
  90.6 2.5 %collective-permute-start.30 = (f32[16,1664]{1,0:T(8,128)S(1)}, f32[16,1664]{1,0:T(8,128)S(1)}, u32[]{:S(2)}, u32[]{:S(2)}) collective-permute-start(f32[16,1664]{1,0:T(8,128)S(1)} %get-tuple-element.48), channel_id=1, source_target_pairs={{0,24},{4,28},{8,16},{12,20},{16,8},{20,12},{24,0},{28,4},{1,25},{... | collective-permute-start | bytes 319496 | tf_op jit(solution)/shard_map/ppermute | solution.py:30
  93.0 2.0 %collective-permute-start.28 = (f32[16,1664]{1,0:T(8,128)S(1)}, f32[16,1664]{1,0:T(8,128)S(1)}, u32[]{:S(2)}, u32[]{:S(2)}) collective-permute-start(f32[16,1664]{1,0:T(8,128)S(1)} %get-tuple-element.47), channel_id=1, source_target_pairs={{0,8},{4,12},{8,0},{12,4},{16,24},{20,28},{24,16},{28,20},{1,9},{5... | collective-permute-start | bytes 319496 | tf_op jit(solution)/shard_map/ppermute | solution.py:30
  96.4 1.9 %collective-permute-done.30 = f32[16,1664]{1,0:T(8,128)S(1)} collective-permute-done((f32[16,1664]{1,0:T(8,128)S(1)}, f32[16,1664]{1,0:T(8,128)S(1)}, u32[]{:S(2)}, u32[]{:S(2)}) %collective-permute-start.30) | collective-permute-done | bytes 106528 | tf_op jit(solution)/shard_map/ppermute | solution.py:30
  98.3 3.8 %collective-permute-done.29 = f32[16,1664]{1,0:T(8,128)S(1)} collective-permute-done((f32[16,1664]{1,0:T(8,128)S(1)}, f32[16,1664]{1,0:T(8,128)S(1)}, u32[]{:S(2)}, u32[]{:S(2)}) %collective-permute-start.29) | collective-permute-done | bytes 106528 | tf_op jit(solution)/shard_map/ppermute | solution.py:30
  103.5 1.7 %collective-permute-start.34 = (f32[16,1664]{1,0:T(8,128)S(1)}, f32[16,1664]{1,0:T(8,128)S(1)}, u32[]{:S(2)}, u32[]{:S(2)}) collective-permute-start(f32[16,1664]{1,0:T(8,128)S(1)} %fusion.1.refs_5_), channel_id=1, source_target_pairs={{0,16},{4,20},{8,24},{12,28},{16,0},{20,4},{24,8},{28,12},{1,17},{... | collective-permute-start | bytes 319496 | tf_op jit(solution)/shard_map/ppermute | solution.py:30
  107.0 10.7 %collective-permute-done.26 = f32[128,128]{1,0:T(8,128)S(1)} collective-permute-done((f32[128,128]{1,0:T(8,128)S(1)}, f32[128,128]{1,0:T(8,128)S(1)}, u32[]{:S(2)}, u32[]{:S(2)}) %collective-permute-start.26) | collective-permute-done | bytes 65568 | tf_op jit(solution)/shard_map/ppermute | solution.py:30
  118.8 8.1 %factor.5.refs_1_ = f32[128,128]{1,0:T(8,128)S(1)} custom-call(f32[128,128]{1,0:T(8,128)S(1)} %add.81.gram_ref), custom_call_target="tpu_custom_call" | custom-call | flops 2000000000 | bytes 131072 | tf_op jit(solution)/shard_map/factor/pallas_call | solution.py:61
  129.8 3.0 %collective-permute-done.38 = f32[128,128]{1,0:T(8,128)S(1)} collective-permute-done((f32[128,128]{1,0:T(8,128)S(1)}, f32[128,128]{1,0:T(8,128)S(1)}, u32[]{:S(2)}, u32[]{:S(2)}) %collective-permute-start.38) | collective-permute-done | bytes 65568 | tf_op jit(solution)/shard_map/ppermute | solution.py:30
  133.8 4.0 %finish.1 = (f32[512,1664]{1,0:T(8,128)}, f32[2,512,128]{2,1,0:T(8,128)}) custom-call(f32[512,1664]{1,0:T(8,128)S(1)} %copy-done.1, bf16[512,1664]{1,0:T(8,128)(2,1)S(1)} %copy-done.3, f32[512,128]{1,0:T(8,128)S(1)} %get-tuple-element.33.rest_0_.refs_2_, f32[512,128]{1,0:T(8,128)S(1)} %get-tuple-element.42.refs_3_, ...), custom_call_target="tpu_custom_call" | custom-call | flops 1500000000 | bytes 12000000 | tf_op jit(solution)/shard_map/finish/pallas_call | solution.py:253
  137.7 9.6 %last_factor.1 = f32[1664,128]{1,0:T(8,128)} custom-call(f32[128,128]{1,0:T(8,128)S(1)} %add.87.gram_ref, f32[128,1664]{1,0:T(8,128)S(1)} %get-tuple-element.43.refs_5_.right_ref), custom_call_target="tpu_custom_call" | custom-call | flops 2000000000 | bytes 2000000 | tf_op jit(solution)/shard_map/last_factor/pallas_call | solution.py:61
  (88 shorter events, 27.1 us)
Async XLA Ops:
  7.0 6.5 %collective-permute-start = (f32[256,128]{1,0:T(8,128)S(1)}, f32[256,128]{1,0:T(8,128)S(1)}, u32[]{:S(2)}, u32[]{:S(2)}) collective-permute-start(f32[256,128]{1,0:T(8,128)S(1)} %get-tuple-element.25), channel_id=1, source_target_pairs={{0,1},{1,0},{2,3},{3,2},{4,5},{5,4},{6,7},{7,6},{8,9},{9,8},{10,11... | collective-permute-start | bytes 393224 | tf_op jit(solution)/shard_map/ppermute | solution.py:30
  10.0 5.4 %collective-permute-start.2 = (f32[256,128]{1,0:T(8,128)S(1)}, f32[256,128]{1,0:T(8,128)S(1)}, u32[]{:S(2)}, u32[]{:S(2)}) collective-permute-start(f32[256,128]{1,0:T(8,128)S(1)} %get-tuple-element.26), channel_id=1, source_target_pairs={{0,2},{1,3},{2,0},{3,1},{4,6},{5,7},{6,4},{7,5},{8,10},{9,11},{10,... | collective-permute-start | bytes 393224 | tf_op jit(solution)/shard_map/ppermute | solution.py:30
  13.5 5.1 %collective-permute-start.1 = (f32[256,128]{1,0:T(8,128)S(1)}, f32[256,128]{1,0:T(8,128)}, u32[]{:S(2)}, u32[]{:S(2)}) collective-permute-start(f32[256,128]{1,0:T(8,128)S(1)} %add.66.a), channel_id=1, source_target_pairs={{0,2},{1,3},{2,0},{3,1},{4,6},{5,7},{6,4},{7,5},{8,10},{9,11},{10,... | collective-permute-start | bytes 393224 | tf_op jit(solution)/shard_map/ppermute | solution.py:30
  16.0 5.3 %collective-permute-start.3 = (f32[256,128]{1,0:T(8,128)}, f32[256,128]{1,0:T(8,128)}, u32[]{:S(2)}, u32[]{:S(2)}) collective-permute-start(f32[256,128]{1,0:T(8,128)} %add.67.c), channel_id=1, source_target_pairs={{0,1},{1,0},{2,3},{3,2},{4,5},{5,4},{6,7},{7,6},{8,9},{9,8},{10,11... | collective-permute-start | bytes 393224 | tf_op jit(solution)/shard_map/ppermute | solution.py:30
  25.4 7.8 %collective-permute-start.10 = (f32[16,1664]{1,0:T(8,128)S(1)}, f32[16,1664]{1,0:T(8,128)S(1)}, u32[]{:S(2)}, u32[]{:S(2)}) collective-permute-start(f32[16,1664]{1,0:T(8,128)S(1)} %get-tuple-element.51), channel_id=1, source_target_pairs={{0,24},{4,28},{8,16},{12,20},{16,8},{20,12},{24,0},{28,4},{1,25},{... | collective-permute-start | bytes 319496 | tf_op jit(solution)/shard_map/ppermute | solution.py:30
  29.1 9.3 %collective-permute-start.9 = (f32[16,1664]{1,0:T(8,128)S(1)}, f32[16,1664]{1,0:T(8,128)S(1)}, u32[]{:S(2)}, u32[]{:S(2)}) collective-permute-start(f32[16,1664]{1,0:T(8,128)S(1)} %get-tuple-element.52), channel_id=1, source_target_pairs={{0,16},{4,20},{8,24},{12,28},{16,0},{20,4},{24,8},{28,12},{1,17},{... | collective-permute-start | bytes 319496 | tf_op jit(solution)/shard_map/ppermute | solution.py:30
  29.1 9.3 %collective-permute-start.8 = (f32[16,1664]{1,0:T(8,128)S(1)}, f32[16,1664]{1,0:T(8,128)S(1)}, u32[]{:S(2)}, u32[]{:S(2)}) collective-permute-start(f32[16,1664]{1,0:T(8,128)S(1)} %get-tuple-element.50), channel_id=1, source_target_pairs={{0,8},{4,12},{8,0},{12,4},{16,24},{20,28},{24,16},{28,20},{1,9},{5... | collective-permute-start | bytes 319496 | tf_op jit(solution)/shard_map/ppermute | solution.py:30
  31.1 11.8 %collective-permute-start.5 = (f32[128,128]{1,0:T(8,128)S(1)}, f32[128,128]{1,0:T(8,128)S(1)}, u32[]{:S(2)}, u32[]{:S(2)}) collective-permute-start(f32[128,128]{1,0:T(8,128)S(1)} %add.68), channel_id=1, source_target_pairs={{0,8},{4,12},{8,0},{12,4},{16,24},{20,28},{24,16},{28,20},{1,9},{5... | collective-permute-start | bytes 196616 | tf_op jit(solution)/shard_map/ppermute | solution.py:30
  38.5 15.0 %collective-permute-start.12 = (f32[16,1664]{1,0:T(8,128)S(1)}, f32[16,1664]{1,0:T(8,128)S(1)}, u32[]{:S(2)}, u32[]{:S(2)}) collective-permute-start(f32[16,1664]{1,0:T(8,128)S(1)} %fusion.3.refs_5_), channel_id=1, source_target_pairs={{0,8},{4,12},{8,0},{12,4},{16,24},{20,28},{24,16},{28,20},{1,9},{5... | collective-permute-start | bytes 319496 | tf_op jit(solution)/shard_map/ppermute | solution.py:30
  39.5 14.4 %collective-permute-start.14 = (f32[16,1664]{1,0:T(8,128)S(1)}, f32[16,1664]{1,0:T(8,128)S(1)}, u32[]{:S(2)}, u32[]{:S(2)}) collective-permute-start(f32[16,1664]{1,0:T(8,128)S(1)} %fusion.3.refs_5_), channel_id=1, source_target_pairs={{0,16},{4,20},{8,24},{12,28},{16,0},{20,4},{24,8},{28,12},{1,17},{... | collective-permute-start | bytes 319496 | tf_op jit(solution)/shard_map/ppermute | solution.py:30
  41.6 12.4 %collective-permute-start.16 = (f32[16,1664]{1,0:T(8,128)S(1)}, f32[16,1664]{1,0:T(8,128)S(1)}, u32[]{:S(2)}, u32[]{:S(2)}) collective-permute-start(f32[16,1664]{1,0:T(8,128)S(1)} %fusion.3.refs_5_), channel_id=1, source_target_pairs={{0,24},{4,28},{8,16},{12,20},{16,8},{20,12},{24,0},{28,4},{1,25},{... | collective-permute-start | bytes 319496 | tf_op jit(solution)/shard_map/ppermute | solution.py:30
  42.9 10.4 %collective-permute-start.6 = (f32[128,128]{1,0:T(8,128)S(1)}, f32[128,128]{1,0:T(8,128)S(1)}, u32[]{:S(2)}, u32[]{:S(2)}) collective-permute-start(f32[128,128]{1,0:T(8,128)S(1)} %add.69), channel_id=1, source_target_pairs={{0,16},{4,20},{8,24},{12,28},{16,0},{20,4},{24,8},{28,12},{1,17},{... | collective-permute-start | bytes 196616 | tf_op jit(solution)/shard_map/ppermute | solution.py:30
  53.4 9.2 %collective-permute-start.11 = (f32[16,1664]{1,0:T(8,128)S(1)}, f32[16,1664]{1,0:T(8,128)S(1)}, u32[]{:S(2)}, u32[]{:S(2)}) collective-permute-start(f32[16,1664]{1,0:T(8,128)S(1)} %fusion.3.refs_5_), channel_id=1, source_target_pairs={{0,4},{4,0},{8,12},{12,8},{16,20},{20,16},{24,28},{28,24},{1,5},{5... | collective-permute-start | bytes 319496 | tf_op jit(solution)/shard_map/ppermute | solution.py:30
  53.4 9.2 %collective-permute-start.13 = (f32[16,1664]{1,0:T(8,128)S(1)}, f32[16,1664]{1,0:T(8,128)S(1)}, u32[]{:S(2)}, u32[]{:S(2)}) collective-permute-start(f32[16,1664]{1,0:T(8,128)S(1)} %collective-permute-done.12.refs_7_), channel_id=1, source_target_pairs={{0,4},{4,0},{8,12},{12,8},{16,20},{20,16},{24,28},{28,24},{1,5},{5... | collective-permute-start | bytes 319496 | tf_op jit(solution)/shard_map/ppermute | solution.py:30
  53.9 8.7 %collective-permute-start.15 = (f32[16,1664]{1,0:T(8,128)S(1)}, f32[16,1664]{1,0:T(8,128)S(1)}, u32[]{:S(2)}, u32[]{:S(2)}) collective-permute-start(f32[16,1664]{1,0:T(8,128)S(1)} %collective-permute-done.14.refs_9_), channel_id=1, source_target_pairs={{0,4},{4,0},{8,12},{12,8},{16,20},{20,16},{24,28},{28,24},{1,5},{5... | collective-permute-start | bytes 319496 | tf_op jit(solution)/shard_map/ppermute | solution.py:30
  54.0 8.6 %collective-permute-start.17 = (f32[16,1664]{1,0:T(8,128)S(1)}, f32[16,1664]{1,0:T(8,128)S(1)}, u32[]{:S(2)}, u32[]{:S(2)}) collective-permute-start(f32[16,1664]{1,0:T(8,128)S(1)} %collective-permute-done.16.refs_11_), channel_id=1, source_target_pairs={{0,4},{4,0},{8,12},{12,8},{16,20},{20,16},{24,28},{28,24},{1,5},{5... | collective-permute-start | bytes 319496 | tf_op jit(solution)/shard_map/ppermute | solution.py:30
  65.9 8.2 %collective-permute-start.18 = (f32[256,128]{1,0:T(8,128)S(1)}, f32[256,128]{1,0:T(8,128)S(1)}, u32[]{:S(2)}, u32[]{:S(2)}) collective-permute-start(f32[256,128]{1,0:T(8,128)S(1)} %get-tuple-element.34), channel_id=1, source_target_pairs={{0,1},{1,0},{2,3},{3,2},{4,5},{5,4},{6,7},{7,6},{8,9},{9,8},{10,11... | collective-permute-start | bytes 393224 | tf_op jit(solution)/shard_map/ppermute | solution.py:30
  67.4 7.6 %collective-permute-start.20 = (f32[256,128]{1,0:T(8,128)S(1)}, f32[256,128]{1,0:T(8,128)S(1)}, u32[]{:S(2)}, u32[]{:S(2)}) collective-permute-start(f32[256,128]{1,0:T(8,128)S(1)} %get-tuple-element.35), channel_id=1, source_target_pairs={{0,2},{1,3},{2,0},{3,1},{4,6},{5,7},{6,4},{7,5},{8,10},{9,11},{10,... | collective-permute-start | bytes 393224 | tf_op jit(solution)/shard_map/ppermute | solution.py:30
  74.1 11.9 %collective-permute-start.19 = (f32[256,128]{1,0:T(8,128)S(1)}, f32[256,128]{1,0:T(8,128)S(1)}, u32[]{:S(2)}, u32[]{:S(2)}) collective-permute-start(f32[256,128]{1,0:T(8,128)S(1)} %add.75.a), channel_id=1, source_target_pairs={{0,2},{1,3},{2,0},{3,1},{4,6},{5,7},{6,4},{7,5},{8,10},{9,11},{10,... | collective-permute-start | bytes 393224 | tf_op jit(solution)/shard_map/ppermute | solution.py:30
  75.1 10.9 %collective-permute-start.21 = (f32[256,128]{1,0:T(8,128)S(1)}, f32[256,128]{1,0:T(8,128)S(1)}, u32[]{:S(2)}, u32[]{:S(2)}) collective-permute-start(f32[256,128]{1,0:T(8,128)S(1)} %add.76.c), channel_id=1, source_target_pairs={{0,1},{1,0},{2,3},{3,2},{4,5},{5,4},{6,7},{7,6},{8,9},{9,8},{10,11... | collective-permute-start | bytes 393224 | tf_op jit(solution)/shard_map/ppermute | solution.py:30
  90.6 7.8 %collective-permute-start.30 = (f32[16,1664]{1,0:T(8,128)S(1)}, f32[16,1664]{1,0:T(8,128)S(1)}, u32[]{:S(2)}, u32[]{:S(2)}) collective-permute-start(f32[16,1664]{1,0:T(8,128)S(1)} %get-tuple-element.48), channel_id=1, source_target_pairs={{0,24},{4,28},{8,16},{12,20},{16,8},{20,12},{24,0},{28,4},{1,25},{... | collective-permute-start | bytes 319496 | tf_op jit(solution)/shard_map/ppermute | solution.py:30
  93.0 9.1 %collective-permute-start.29 = (f32[16,1664]{1,0:T(8,128)S(1)}, f32[16,1664]{1,0:T(8,128)S(1)}, u32[]{:S(2)}, u32[]{:S(2)}) collective-permute-start(f32[16,1664]{1,0:T(8,128)S(1)} %get-tuple-element.49), channel_id=1, source_target_pairs={{0,16},{4,20},{8,24},{12,28},{16,0},{20,4},{24,8},{28,12},{1,17},{... | collective-permute-start | bytes 319496 | tf_op jit(solution)/shard_map/ppermute | solution.py:30
  93.0 9.1 %collective-permute-start.28 = (f32[16,1664]{1,0:T(8,128)S(1)}, f32[16,1664]{1,0:T(8,128)S(1)}, u32[]{:S(2)}, u32[]{:S(2)}) collective-permute-start(f32[16,1664]{1,0:T(8,128)S(1)} %get-tuple-element.47), channel_id=1, source_target_pairs={{0,8},{4,12},{8,0},{12,4},{16,24},{20,28},{24,16},{28,20},{1,9},{5... | collective-permute-start | bytes 319496 | tf_op jit(solution)/shard_map/ppermute | solution.py:30
  96.3 10.3 %collective-permute-start.25 = (f32[128,128]{1,0:T(8,128)S(1)}, f32[128,128]{1,0:T(8,128)S(1)}, u32[]{:S(2)}, u32[]{:S(2)}) collective-permute-start(f32[128,128]{1,0:T(8,128)S(1)} %add.79), channel_id=1, source_target_pairs={{0,8},{4,12},{8,0},{12,4},{16,24},{20,28},{24,16},{28,20},{1,9},{5... | collective-permute-start | bytes 196616 | tf_op jit(solution)/shard_map/ppermute | solution.py:30
  102.1 15.7 %collective-permute-start.32 = (f32[16,1664]{1,0:T(8,128)S(1)}, f32[16,1664]{1,0:T(8,128)S(1)}, u32[]{:S(2)}, u32[]{:S(2)}) collective-permute-start(f32[16,1664]{1,0:T(8,128)S(1)} %fusion.1.refs_5_), channel_id=1, source_target_pairs={{0,8},{4,12},{8,0},{12,4},{16,24},{20,28},{24,16},{28,20},{1,9},{5... | collective-permute-start | bytes 319496 | tf_op jit(solution)/shard_map/ppermute | solution.py:30
  103.5 14.8 %collective-permute-start.34 = (f32[16,1664]{1,0:T(8,128)S(1)}, f32[16,1664]{1,0:T(8,128)S(1)}, u32[]{:S(2)}, u32[]{:S(2)}) collective-permute-start(f32[16,1664]{1,0:T(8,128)S(1)} %fusion.1.refs_5_), channel_id=1, source_target_pairs={{0,16},{4,20},{8,24},{12,28},{16,0},{20,4},{24,8},{28,12},{1,17},{... | collective-permute-start | bytes 319496 | tf_op jit(solution)/shard_map/ppermute | solution.py:30
  105.2 13.2 %collective-permute-start.36 = (f32[16,1664]{1,0:T(8,128)S(1)}, f32[16,1664]{1,0:T(8,128)S(1)}, u32[]{:S(2)}, u32[]{:S(2)}) collective-permute-start(f32[16,1664]{1,0:T(8,128)S(1)} %fusion.1.refs_5_), channel_id=1, source_target_pairs={{0,24},{4,28},{8,16},{12,20},{16,8},{20,12},{24,0},{28,4},{1,25},{... | collective-permute-start | bytes 319496 | tf_op jit(solution)/shard_map/ppermute | solution.py:30
  106.6 11.1 %collective-permute-start.26 = (f32[128,128]{1,0:T(8,128)S(1)}, f32[128,128]{1,0:T(8,128)S(1)}, u32[]{:S(2)}, u32[]{:S(2)}) collective-permute-start(f32[128,128]{1,0:T(8,128)S(1)} %add.80), channel_id=1, source_target_pairs={{0,16},{4,20},{8,24},{12,28},{16,0},{20,4},{24,8},{28,12},{1,17},{... | collective-permute-start | bytes 196616 | tf_op jit(solution)/shard_map/ppermute | solution.py:30
  117.7 9.2 %collective-permute-start.31 = (f32[16,1664]{1,0:T(8,128)S(1)}, f32[16,1664]{1,0:T(8,128)S(1)}, u32[]{:S(2)}, u32[]{:S(2)}) collective-permute-start(f32[16,1664]{1,0:T(8,128)S(1)} %fusion.1.refs_5_), channel_id=1, source_target_pairs={{0,4},{4,0},{8,12},{12,8},{16,20},{20,16},{24,28},{28,24},{1,5},{5... | collective-permute-start | bytes 319496 | tf_op jit(solution)/shard_map/ppermute | solution.py:30
  117.8 9.2 %collective-permute-start.33 = (f32[16,1664]{1,0:T(8,128)S(1)}, f32[16,1664]{1,0:T(8,128)S(1)}, u32[]{:S(2)}, u32[]{:S(2)}) collective-permute-start(f32[16,1664]{1,0:T(8,128)S(1)} %collective-permute-done.32.refs_7_), channel_id=1, source_target_pairs={{0,4},{4,0},{8,12},{12,8},{16,20},{20,16},{24,28},{28,24},{1,5},{5... | collective-permute-start | bytes 319496 | tf_op jit(solution)/shard_map/ppermute | solution.py:30
  118.3 8.7 %collective-permute-start.35 = (f32[16,1664]{1,0:T(8,128)S(1)}, f32[16,1664]{1,0:T(8,128)S(1)}, u32[]{:S(2)}, u32[]{:S(2)}) collective-permute-start(f32[16,1664]{1,0:T(8,128)S(1)} %collective-permute-done.34.refs_9_), channel_id=1, source_target_pairs={{0,4},{4,0},{8,12},{12,8},{16,20},{20,16},{24,28},{28,24},{1,5},{5... | collective-permute-start | bytes 319496 | tf_op jit(solution)/shard_map/ppermute | solution.py:30
  118.4 8.6 %collective-permute-start.37 = (f32[16,1664]{1,0:T(8,128)S(1)}, f32[16,1664]{1,0:T(8,128)S(1)}, u32[]{:S(2)}, u32[]{:S(2)}) collective-permute-start(f32[16,1664]{1,0:T(8,128)S(1)} %collective-permute-done.36.refs_11_), channel_id=1, source_target_pairs={{0,4},{4,0},{8,12},{12,8},{16,20},{20,16},{24,28},{28,24},{1,5},{5... | collective-permute-start | bytes 319496 | tf_op jit(solution)/shard_map/ppermute | solution.py:30
  (13 other events, 51.6 us)

commit v2 on v1

v2 whole, which is shorter than its diff:
```python
import jax
import jax.numpy as jnp
from jax import lax
from jax.experimental import pallas as pl
from jax.experimental.pallas import tpu as pltpu
from jax.sharding import PartitionSpec as P

F32 = jnp.float32
BF16 = jnp.bfloat16
HIGHEST = lax.Precision.HIGHEST
VMEM = pl.BlockSpec(memory_space=pltpu.VMEM)
SMEM = pl.BlockSpec(memory_space=pltpu.SMEM)
NN = (((1,), (0,)), ((), ()))
NT = (((1,), (1,)), ((), ()))
TN = (((0,), (0,)), ((), ()))
KEEP = 0.95
PANEL = 16
FACTOR = 1_500_000_000


def masks_of(axis):
    size = lax.axis_size(axis)
    masks = []
    mask = 1
    while mask < size:
        masks.append(mask)
        mask *= 2
    assert mask == size
    return masks


def swap(x, axis, mask):
    return lax.ppermute(x, axis, [(i, i ^ mask) for i in range(lax.axis_size(axis))])


def sum_part(x, axis):
    masks = masks_of(axis)
    for mask in masks[:-1]:
        x = x + swap(x, axis, mask)
    return x, swap(x, axis, masks[-1])


def split(x):
    high = x.astype(BF16)
    return high, (x - high.astype(F32)).astype(BF16)


def dot(a, b, dims=NN):
    return lax.dot_general(a, b, dims, preferred_element_type=F32)


def exact(a, b, dims=NN):
    return lax.dot_general(a, b, dims, precision=HIGHEST, preferred_element_type=F32)


def tiles(width, most=256):
    return [(start, min(most, width - start)) for start in range(0, width, most)]


def struct(*shape, dtype=F32):
    return jax.ShapeDtypeStruct(shape, dtype)


def call(body, name, out, ins, scratch=(), flops=0, nbytes=0, **kw):
    return pl.pallas_call(
        body,
        out_shape=out,
        in_specs=[SMEM if x.dtype == jnp.int32 else VMEM for x in ins],
        out_specs=jax.tree.map(lambda _: VMEM, out),
        scratch_shapes=list(scratch),
        name=name,
        compiler_params=pltpu.CompilerParams(vmem_limit_bytes=24 * 2**20),
        cost_estimate=pl.CostEstimate(flops=flops, bytes_accessed=nbytes, transcendentals=0),
        **kw,
    )(*ins)


def start_body(momentum_ref, grad_ref, basis_ref, high_ref, low_ref, top_ref, bottom_ref, both_ref):
    step = pl.program_id(0)
    rank = basis_ref.shape[1]
    rows = momentum_ref.shape[0]
    half = top_ref.shape[0] // rows

    @pl.when(step == 0)
    def _():
        high, low = split(basis_ref[...])
        both_ref[:, :rank] = high
        both_ref[:, rank:] = low

    high, low = split(momentum_ref[...] + grad_ref[...].astype(F32))
    high_ref[...] = high
    low_ref[...] = low
    wide = dot(high, both_ref[...])
    proj = wide[:, :rank] + wide[:, rank:] + dot(low, both_ref[:, :rank])

    @pl.when(step < half)
    def _():
        top_ref[pl.ds(pl.multiple_of(step * rows, rows), rows), :] = proj

    @pl.when(step >= half)
    def _():
        bottom_ref[pl.ds(pl.multiple_of((step - half) * rows, rows), rows), :] = proj


def start(momentum, grad, basis):
    rows, cols = momentum.shape
    rank = basis.shape[1]
    block = rows // 4
    tile = pl.BlockSpec((block, cols), lambda i: (i, 0))
    whole = pl.BlockSpec((rows // 2, rank), lambda i: (0, 0))
    return pl.pallas_call(
        start_body,
        grid=(4,),
        in_specs=[tile, tile, pl.BlockSpec((cols, rank), lambda i: (0, 0))],
        out_specs=[tile, tile, whole, whole],
        out_shape=[struct(rows, cols, dtype=BF16)] * 2 + [struct(rows // 2, rank)] * 2,
        scratch_shapes=[pltpu.VMEM((cols, 2 * rank), BF16)],
        name="start",
        compiler_params=pltpu.CompilerParams(vmem_limit_bytes=24 * 2**20),
    )(momentum, grad, basis)


def pull(count, place, halves, high, low, before=None):
    rows, width = high.shape
    rank = halves[0].shape[1]
    chunk = rank // count
    order = [*range(0, count, 2), *range(1, count, 2)]

    def body(place_ref, a, b, c, d, high_ref, low_ref, *rest):
        proj = jnp.concatenate([a[...] + b[...], c[...] + d[...]], axis=0)
        if before is None:
            proj_ref, keep_ref, send_ref, turned_ref = rest
        else:
            left_ref, right_ref, gram_ref, inv_ref, proj_ref, keep_ref, send_ref, turned_ref = rest
            proj = proj - KEEP * exact(left_ref[...], gram_ref[...])
            proj = exact(proj, inv_ref[...], NT)
        proj_ref[...] = proj
        turned_ref[...] = proj.T
        place = place_ref[0]
        parts = [turned_ref[pl.ds(pl.multiple_of((place ^ j) * chunk, chunk), chunk), :] for j in order]
        turned = jnp.concatenate(parts, axis=0)
        gram = exact(turned, proj)
        half = rank // 2
        keep_ref[:, width:] = gram[:half]
        send_ref[:, width:] = gram[half:]
        high, low = split(turned)
        both = jnp.concatenate([high, low], axis=0)
        if before is not None:
            cross_high, cross_low = split(-KEEP * exact(turned, left_ref[...]))
            cross = jnp.concatenate([cross_high, cross_low], axis=0)
        for at, size in tiles(width):
            wide = dot(both, high_ref[:, at:at + size])
            out = wide[:rank] + wide[rank:] + dot(high, low_ref[:, at:at + size])
            if before is not None:
                right_high, right_low = split(right_ref[:, at:at + size])
                wide = dot(cross, right_high)
                out = out + (wide[:rank] + wide[rank:] + dot(cross_high, right_low))
            keep_ref[:, at:at + size] = out[:half]
            send_ref[:, at:at + size] = out[half:]

    out = [struct(rows, rank), struct(rank // 2, width + rank), struct(rank // 2, width + rank)]
    ins = [place, *halves, high, low] + list(before or [])
    return call(body, "pull", out, ins, [pltpu.VMEM((rank, rows), F32)], flops=1_000_000_000, nbytes=5_000_000)


def normal(count, place, inv, pieces, width):
    rank = inv.shape[0]
    chunk = rank // count

    def body(place_ref, inv_ref, *rest):
        right_ref, gram_ref, raw_ref = rest[len(pieces):]
        place = place_ref[0]
        for (lane, order, _), piece in zip(pieces, rest):
            size = piece.shape[1]
            for i, j in enumerate(order):
                rows = pl.ds(pl.multiple_of((place ^ j) * chunk, chunk), chunk)
                raw_ref[rows, lane:lane + size] = piece[i * chunk:(i + 1) * chunk, :]
        inv_high, inv_low = split(inv_ref[...])
        inv_both = jnp.concatenate([inv_high, inv_low], axis=0)
        gram = jnp.zeros((rank, rank), F32)
        for at, size in tiles(width):
            raw_high, raw_low = split(raw_ref[:, at:at + size])
            wide = dot(inv_both, raw_high)
            right = wide[:rank] + wide[rank:] + dot(inv_high, raw_low)
            right_ref[:, at:at + size] = right
            high, low = split(right)
            wide = dot(jnp.concatenate([high, low], axis=0), high, NT)
            gram = gram + (wide[:rank] + wide[rank:] + dot(high, low, NT))
        gram_ref[...] = gram

    ins = [place, inv, *(piece for _, _, piece in pieces)]
    return call(body, "normal", [struct(rank, width), struct(rank, rank)], ins, [pltpu.VMEM((rank, width), F32)],
                flops=500_000_000, nbytes=2_000_000)


def push(inv, proj, high, low, right):
    rows, width = high.shape
    rank = inv.shape[0]

    def body(inv_ref, proj_ref, high_ref, low_ref, right_ref, left_ref, top_ref, bottom_ref):
        image = None
        for at, size in tiles(width):
            right_high, right_low = split(right_ref[:, at:at + size])
            wide = dot(high_ref[:, at:at + size], jnp.concatenate([right_high, right_low], axis=0), NT)
            part = wide[:, :rank] + wide[:, rank:] + dot(low_ref[:, at:at + size], right_high, NT)
            image = part if image is None else image + part
        top_ref[...] = image[:rows // 2]
        bottom_ref[...] = image[rows // 2:]
        left_ref[...] = exact(proj_ref[...], inv_ref[...], NT)

    out = [struct(rows, rank)] + [struct(rows // 2, rank)] * 2
    return call(body, "push", out, [inv, proj, high, low, right], flops=700_000_000, nbytes=5_000_000)


def finish_body(scale, momentum_ref, grad_ref, left_a, proj_b, inv_b, right_a, right_b, out_ref, lefts_ref, high_ref, low_ref):
    rank, width = right_a.shape
    left_b = exact(proj_b[...], inv_b[...], NT)

    @pl.when(pl.program_id(0) == 0)
    def _():
        for i, ref in enumerate((right_a, right_b)):
            high, low = split(KEEP * ref[...])
            high_ref[i * rank:(i + 1) * rank, :] = high
            low_ref[i * rank:(i + 1) * rank, :] = low

    lefts_ref[0] = scale * left_a[...]
    lefts_ref[1] = scale * left_b
    high, low = split(jnp.concatenate([left_a[...], left_b], axis=1))
    for at, size in tiles(width):
        right_high = high_ref[:, at:at + size]
        outer = dot(high, right_high) + dot(low, right_high) + dot(high, low_ref[:, at:at + size])
        work = momentum_ref[:, at:at + size] + grad_ref[:, at:at + size].astype(F32)
        out_ref[:, at:at + size] = work - outer


def finish(momentum, grad, left_a, proj_b, inv_b, right_a, right_b, scale):
    rows, cols = momentum.shape
    rank = left_a.shape[1]
    block = rows // 4
    tile = pl.BlockSpec((block, cols), lambda i: (i, 0))
    left_tile = pl.BlockSpec((block, rank), lambda i: (i, 0))
    right_tile = pl.BlockSpec((rank, cols), lambda i: (0, 0))

    def body(*refs):
        finish_body(scale, *refs)

    return pl.pallas_call(
        body,
        grid=(4,),
        in_specs=[tile, tile, left_tile, left_tile, pl.BlockSpec((rank, rank), lambda i: (0, 0)), right_tile, right_tile],
        out_specs=[tile, pl.BlockSpec((2, block, rank), lambda i: (0, i, 0))],
        out_shape=[struct(rows, cols), struct(2, rows, rank)],
        scratch_shapes=[pltpu.VMEM((2 * rank, cols), BF16)] * 2,
        name="finish",
        compiler_params=pltpu.CompilerParams(vmem_limit_bytes=24 * 2**20),
        cost_estimate=pl.CostEstimate(flops=1_500_000_000, bytes_accessed=12_000_000, transcendentals=0),
    )(momentum, grad, left_a, proj_b, inv_b, right_a, right_b)


def eliminate(full, first):
    rank = full.shape[1]
    groups = PANEL // 8
    sub = lax.broadcasted_iota(jnp.int32, (8, rank), 0)
    lane = lax.broadcasted_iota(jnp.int32, (8, rank), 1)
    rolled = pltpu.roll(full, lax.rem(rank - first, rank), 1)
    rows = [full[8 * g:8 * g + 8] for g in range(groups)]
    cols = [
        [jnp.broadcast_to(rolled[8 * g:8 * g + 8, j:j + 1], (8, rank)) for g in range(groups)] for j in range(PANEL)
    ]

    def spread(x, j):
        return jnp.broadcast_to(x[j // 8][j % 8:j % 8 + 1], (8, rank))

    pivot = spread(cols[0], 0)
    for j in range(PANEL):
        at = j // 8
        root = lax.rsqrt(pivot)
        if j + 1 < PANEL:
            above = spread(cols[j + 1], j) * root
            pivot = spread(cols[j + 1], j + 1) - above * above
        below = sub > j % 8
        here = lane == first + j
        row = jnp.where(here, 1.0, spread(rows, j)) * root
        for g in range(at, groups):
            mult = cols[j][g] * root
            rest = jnp.where(here, 0.0, rows[g])
            if g == at:
                mult = jnp.where(below, mult, 0.0)
                rest = jnp.where(below, rest, rows[g])
            rest = rest - mult * row
            rows[g] = jnp.where(sub == j % 8, row, rest) if g == at else rest
            cols[j][g] = mult
        for k in range(j + 1, PANEL):
            across = spread(cols[k], j) * root
            for g in range(at, groups):
                cols[k][g] = cols[k][g] - cols[j][g] * across
    return jnp.concatenate(rows, axis=0)


def thirds(x):
    high = x.astype(BF16)
    rest = x - high.astype(F32)
    middle = rest.astype(BF16)
    return high, middle, (rest - middle.astype(F32)).astype(BF16)


def factor_panels(state_ref, begin, end):
    rank = state_ref.shape[0]
    row = lax.broadcasted_iota(jnp.int32, (rank, rank), 0)
    col = lax.broadcasted_iota(jnp.int32, (rank, rank), 1)
    sub = lax.broadcasted_iota(jnp.int32, (PANEL, rank), 0)
    lane = lax.broadcasted_iota(jnp.int32, (PANEL, rank), 1)

    def panel(p, carry):
        first = pl.multiple_of(p * PANEL, PANEL)
        done = eliminate(state_ref[pl.ds(first, PANEL), :], first)
        lower = jnp.where((lane > first + sub) & (lane < first + PANEL), 0.0, done)
        a, b, c = thirds(done)
        d, e, f = thirds(lower)
        step = dot(
            jnp.concatenate([a, a, b, b, a, c], axis=0), jnp.concatenate([d, e, d, e, f, d], axis=0), TN
        )
        old = state_ref[...]
        fresh = jnp.where((col >= first) & (col < first + PANEL), 0.0, old) - step
        state_ref[...] = jnp.where(row >= first + PANEL, fresh, old)
        state_ref[pl.ds(first, PANEL), :] = done
        return carry

    lax.fori_loop(begin, end, panel, 0)


def factor_left(count, place, own, other):
    rank = own.shape[1]
    chunk = rank // count

    def first(place_ref, own_ref, other_ref, state_ref):
        for j in range(count):
            part = (other_ref if j % 2 else own_ref)[j // 2 * chunk:(j // 2 + 1) * chunk, :]
            state_ref[pl.ds(pl.multiple_of((place_ref[0] ^ j) * chunk, chunk), chunk), :] = part
        factor_panels(state_ref, 0, rank // PANEL // 2)

    return call(first, "factor_first", struct(rank, rank), [place, own, other], flops=FACTOR, nbytes=131072)


def factor_rest(state):
    rank = state.shape[0]

    def rest(in_ref, out_ref):
        out_ref[...] = in_ref[...]
        factor_panels(out_ref, rank // PANEL // 2, rank // PANEL)
        out_ref[...] = lower_part(out_ref[...])

    return call(rest, "factor_rest", struct(rank, rank), [state], flops=FACTOR, nbytes=131072)


def factor_right(one, two):
    rank = one.shape[0]

    def first(one_ref, two_ref, gram_ref, state_ref):
        gram = one_ref[...] + two_ref[...]
        gram_ref[...] = gram
        state_ref[...] = gram
        factor_panels(state_ref, 0, rank // PANEL // 2)

    return call(first, "factor_first", [struct(rank, rank)] * 2, [one, two], flops=FACTOR, nbytes=131072)


def lower_part(x):
    row = lax.broadcasted_iota(jnp.int32, x.shape, 0)
    col = lax.broadcasted_iota(jnp.int32, x.shape, 1)
    return jnp.where(row >= col, x, 0.0)


def last_factor(one, two, right, scale):
    def body(one_ref, two_ref, right_ref, out_ref, state_ref):
        rank = state_ref.shape[0]
        state_ref[...] = one_ref[...] + two_ref[...]
        factor_panels(state_ref, 0, rank // PANEL)
        inv_high, inv_low = split(scale * lower_part(state_ref[...]))
        high, low = split(right_ref[...].T)
        both = jnp.concatenate([inv_high, inv_low], axis=0)
        wide = dot(high, both, NT)
        out_ref[...] = wide[:, :rank] + wide[:, rank:] + dot(low, inv_high, NT)

    rank, width = right.shape
    return call(body, "last_factor", struct(width, rank), [one, two, right], [pltpu.VMEM((rank, rank), F32)],
                flops=2 * FACTOR, nbytes=2_000_000)


def sum_halves(top, bottom, axis, beside=None):
    masks = masks_of(axis)
    for one, two in zip(masks[:-1], masks[:0:-1]):
        other_top, other_bottom = swap(top, axis, one), swap(bottom, axis, two)
        top, bottom = top + other_top, bottom + other_bottom
    if beside is not None:
        top, bottom, beside = lax.optimization_barrier((top, bottom, beside))
    return (top, swap(top, axis, masks[-1]), bottom, swap(bottom, axis, masks[0])), beside


class Share:
    def __init__(self, x, order, lane):
        self.x, self.order, self.lane = x, order, lane

    def halve(self, mask, extra=None):
        rows = self.x.shape[0] // len(self.order)
        pick = [[i for i, j in enumerate(self.order) if bool(j & mask) == bit] for bit in (False, True)]
        keep, send = [
            jnp.concatenate([self.x[i * rows:(i + 1) * rows] for i in at], axis=0) for at in pick
        ]
        order = [self.order[i] for i in pick[0]]
        if extra is None:
            return Share(keep + swap(send, "row", mask), order, self.lane), None
        size = send.shape[0]
        step = mask // 2 * rows
        turned = [extra[i ^ step:(i ^ step) + rows] for i in range(0, extra.shape[0], rows)]
        turned = jnp.concatenate(turned, axis=0)
        cuts = [turned[i:i + size] for i in range(0, turned.shape[0], size)]
        got = swap(jnp.concatenate([send, *cuts], axis=1), "row", mask)
        width, wide = send.shape[1], extra.shape[1]
        back = [got[:, width + i * wide:width + (i + 1) * wide] for i in range(len(cuts))]
        return Share(keep + got[:, :width], order, self.lane), extra + jnp.concatenate(back, axis=0)

    def fetch(self, mask):
        got = swap(self.x, "row", mask)
        return Share(got, [j ^ mask for j in self.order], self.lane)

    def join(self, other):
        return Share(jnp.concatenate([self.x, other.x], axis=0), self.order + other.order, self.lane)


def sum_rows(keep, send, count, rank):
    both = keep + swap(send, "row", 1)
    width = both.shape[1] - rank
    cut = width // rank // 2 * rank
    order = list(range(0, count, 2))
    one, two = Share(both[:, :cut], order, 0), Share(both[:, cut:width], order, cut)
    gram = both[:, width:]
    masks = masks_of("row")[1:]
    for up, down in zip(masks, reversed(masks)):
        one, gram = one.halve(up, gram)
        two, _ = two.halve(down)
    one.x, two.x, gram = lax.optimization_barrier((one.x, two.x, gram))
    return one, two, gram, swap(gram, "row", 1)


def gather_rows(one, two, beside):
    masks = masks_of("row")[1:]
    pieces = [one, two]
    state = beside[0]
    steps = list(beside[1:])
    for down, up in zip(reversed(masks), masks):
        more = [one.fetch(down), two.fetch(up)]
        if steps:
            state = steps.pop(0)(state)
        one, two = one.join(more[0]), two.join(more[1])
        one.x, two.x, state = lax.optimization_barrier((one.x, two.x, state))
        pieces += more
    pieces += [one.fetch(1), two.fetch(1)]
    return [(p.lane, p.order, p.x) for p in pieces], state


def shards(momentum, grad, basis):
    count = lax.axis_size("row")
    rank = basis.shape[1]
    width = momentum.shape[1]
    row_scale = float(momentum.shape[0] * count) ** 0.5
    col_scale = float(width * lax.axis_size("col")) ** 0.5
    place = lax.axis_index("row").astype(jnp.int32).reshape(1)
    high, low, top, bottom = start(momentum, grad, basis)
    halves, _ = sum_halves(top, bottom, "col")
    proj, keep, send = pull(count, place, halves, high, low)
    one, two, own, other = sum_rows(keep, send, count, rank)
    first = lambda grams: factor_left(count, place, *grams)
    pieces, inv = gather_rows(one, two, [(own, other), first, factor_rest])
    right_a, gram = normal(count, place, inv, pieces, width)
    left_a, top, bottom = push(inv, proj, high, low, right_a)
    masks = masks_of("col")
    for mask in masks[:-1]:
        gram = gram + swap(gram, "col", mask)
    top, bottom, gram = lax.optimization_barrier((top, bottom, gram))
    gram, state = factor_right(gram, swap(gram, "col", masks[-1]))
    halves, state = sum_halves(top, bottom, "col", state)
    inv = factor_rest(state)
    proj, keep, send = pull(count, place, halves, high, low, (left_a, right_a, gram, inv))
    one, two, own, other = sum_rows(keep, send, count, rank)
    pieces, inv = gather_rows(one, two, [(own, other), first, factor_rest])
    right_b, gram = normal(count, place, inv, pieces, width)
    gram = sum_part(gram, "col")
    momentum_out, lefts = finish(momentum, grad, left_a, proj, inv, right_a, right_b, row_scale)
    return momentum_out, lefts, last_factor(*gram, right_b, col_scale)


def solution(mesh):
    in_specs = (P("row", "col"), P("row", "col"), P("col", None))
    out_specs = (P("row", "col"), P(None, "row", None), P("col", None))
    return jax.shard_map(shards, mesh=mesh, in_specs=in_specs, out_specs=out_specs, check_vma=False)
```

time: 148 us -> 133 us (0.90)
  Pallas kernels: 49.2 us -> 33.9 us
  starting transfers between devices: 39.2 us -> 41.5 us
  waiting for transfers between devices: 52.4 us -> 50.2 us
    pallas_call x8 -> x12, Pallas kernels: 43.5 us -> 26.7 us  [call(): pl.pallas_call(body, out_shape=out, in_specs=[SMEM if x.dtype == jnp.int3...]
    ppermute x40 -> x36, starting transfers between devices: 39.2 us -> 41.5 us  [swap(): lax.ppermute(x, axis, [(i, i ^ mask) for i in range(lax.axis_size(axis))])]
    ppermute x40 -> x36, waiting for transfers between devices: 52.4 us -> 50.2 us  [swap(): lax.ppermute(x, axis, [(i, i ^ mask) for i in range(lax.axis_size(axis))])]
    unnamed x10 -> x18, local copies, waits for them, and re-layouts: 4.58 us -> 4.61 us
  transfers between devices with their start and end apart: 40 -> 36, of which waited for: 16 -> 27; matrix products, arithmetic and copies ran while one was open for 1% -> 1% of each run, Pallas kernels for 19% -> 15%
where the time goes in v2:
time: 133 us; the launch traced here: 132 us
  waiting for transfers between devices  50.2 us (38%)
  starting transfers between devices  41.5 us (31%)
  Pallas kernels  33.9 us (25%)
  local copies, waits for them, and re-layouts  4.7 us (4%)
    ppermute x36, waiting for transfers between devices, swap(): lax.ppermute(x, axis, [(i, i ^ mask) for i in range(lax.axis_size(axis))])  50.2 us
    ppermute x36, starting transfers between devices, swap(): lax.ppermute(x, axis, [(i, i ^ mask) for i in range(lax.axis_size(axis))])  41.5 us
    pallas_call x12, Pallas kernels, call(): pl.pallas_call(body, out_shape=out, in_specs=[SMEM if x.dtype == jnp.int3...  26.7 us
    pallas_call x1, Pallas kernels, finish(): pl.pallas_call(body, grid=(4,), in_specs=[tile, tile, left_tile, left_til...  5.31 us
    unnamed x18, local copies, waits for them, and re-layouts  4.61 us
  transfers between devices with their start and end apart: 36, of which 27 were waited for; matrix products, arithmetic and copies ran while one was open for 1% of the time, Pallas kernels for 15%

profile of v2, /device:TPU:0, one launch (start us, length us, event | category | flops | bytes accessed | tf_op | source)
XLA Modules:
  0.0 132.5 jit_solution(8111581251086348004)
XLA Ops:
  0.6 2.0 %copy-done = f32[512,1664]{1,0:T(8,128)S(1)} copy-done((f32[512,1664]{1,0:T(8,128)S(1)}, f32[512,1664]{1,0:T(8,128)}, u32[]{:S(2)}) %copy-start) | copy-done | bytes 3407896
  5.2 1.8 %start.1 = (bf16[512,1664]{1,0:T(8,128)(2,1)S(1)}, bf16[512,1664]{1,0:T(8,128)(2,1)S(1)}, f32[256,128]{1,0:T(8,128)S(1)}, f32[256,128]{1,0:T(8,128)S(1)}) custom-call(f32[512,1664]{1,0:T(8,128)S(1)} %copy-done, bf16[512,1664]{1,0:T(8,128)(2,1)S(1)} %copy-done.2, f32[1664,128]{1,0:T(8,128)S(1)} %copy-done.4), custom_call_target="tpu_custom_call" | custom-call | tf_op jit(solution)/shard_map/start/pallas_call | solution.py:111
  7.0 3.0 %collective-permute-start = (f32[256,128]{1,0:T(8,128)S(1)}, f32[256,128]{1,0:T(8,128)S(1)}, u32[]{:S(2)}, u32[]{:S(2)}) collective-permute-start(f32[256,128]{1,0:T(8,128)S(1)} %get-tuple-element.48), channel_id=1, source_target_pairs={{0,1},{1,0},{2,3},{3,2},{4,5},{5,4},{6,7},{7,6},{8,9},{9,8},{10,11... | collective-permute-start | bytes 393224 | tf_op jit(solution)/shard_map/ppermute | solution.py:33
  11.5 2.0 %collective-permute-done = f32[256,128]{1,0:T(8,128)S(1)} collective-permute-done((f32[256,128]{1,0:T(8,128)S(1)}, f32[256,128]{1,0:T(8,128)S(1)}, u32[]{:S(2)}, u32[]{:S(2)}) %collective-permute-start) | collective-permute-done | bytes 131104 | tf_op jit(solution)/shard_map/ppermute | solution.py:33
  13.5 1.8 %collective-permute-start.1 = (f32[256,128]{1,0:T(8,128)S(1)}, f32[256,128]{1,0:T(8,128)}, u32[]{:S(2)}, u32[]{:S(2)}) collective-permute-start(f32[256,128]{1,0:T(8,128)S(1)} %add.60.a), channel_id=1, source_target_pairs={{0,2},{1,3},{2,0},{3,1},{4,6},{5,7},{6,4},{7,5},{8,10},{9,11},{10,... | collective-permute-start | bytes 393224 | tf_op jit(solution)/shard_map/ppermute | solution.py:33
  18.7 2.7 %collective-permute-done.3.d = f32[256,128]{1,0:T(8,128)} collective-permute-done((f32[256,128]{1,0:T(8,128)}, f32[256,128]{1,0:T(8,128)}, u32[]{:S(2)}, u32[]{:S(2)}) %collective-permute-start.3) | collective-permute-done | bytes 131104 | tf_op jit(solution)/shard_map/ppermute | solution.py:33
  21.3 2.2 %pull.2 = (f32[512,128]{1,0:T(8,128)S(1)}, f32[64,1792]{1,0:T(8,128)S(1)}, f32[64,1792]{1,0:T(8,128)S(1)}) custom-call(s32[1]{0:T(128)} %bitcast.place_ref, f32[256,128]{1,0:T(8,128)S(1)} %add.60.a, f32[256,128]{1,0:T(8,128)} %collective-permute-done.1.b, f32[256,128]{1,0:T(8,128)} %add.61.c, f32[256,128]{1,0:T(8,128)} %collective-permute-done.3.d, ...), custom_call_target="tpu_custom_call" | custom-call | flops 1000000000 | bytes 5000000 | tf_op jit(solution)/shard_map/pull/pallas_call | solution.py:65
  23.6 1.8 %collective-permute-done.4 = f32[64,1792]{1,0:T(8,128)S(1)} collective-permute-done((f32[64,1792]{1,0:T(8,128)S(1)}, f32[64,1792]{1,0:T(8,128)S(1)}, u32[]{:S(2)}, u32[]{:S(2)}) %collective-permute-start.4) | collective-permute-done | bytes 458784 | tf_op jit(solution)/shard_map/ppermute | solution.py:33
  25.6 2.7 %collective-permute-start.7 = (f32[32,896]{1,0:T(8,128)S(1)}, f32[32,896]{1,0:T(8,128)S(1)}, u32[]{:S(2)}, u32[]{:S(2)}) collective-permute-start(f32[32,896]{1,0:T(8,128)S(1)} %concatenate.115), channel_id=1, source_target_pairs={{0,16},{4,20},{8,24},{12,28},{16,0},{20,4},{24,8},{28,12},{1,17},{... | collective-permute-start | bytes 344072 | tf_op jit(solution)/shard_map/ppermute | solution.py:33
  29.9 4.4 %collective-permute-done.7 = f32[32,896]{1,0:T(8,128)S(1)} collective-permute-done((f32[32,896]{1,0:T(8,128)S(1)}, f32[32,896]{1,0:T(8,128)S(1)}, u32[]{:S(2)}, u32[]{:S(2)}) %collective-permute-start.7) | collective-permute-done | bytes 114720 | tf_op jit(solution)/shard_map/ppermute | solution.py:33
  35.0 3.4 %collective-permute-start.6 = (f32[16,1280]{1,0:T(8,128)S(1)}, f32[16,1280]{1,0:T(8,128)S(1)}, u32[]{:S(2)}, u32[]{:S(2)}) collective-permute-start(f32[16,1280]{1,0:T(8,128)S(1)} %constant_dynamic-update-slice_fusion), channel_id=1, source_target_pairs={{0,16},{4,20},{8,24},{12,28},{16,0},{20,4},{24,8},{28,12},{1,17},{... | collective-permute-start | bytes 245768 | tf_op jit(solution)/shard_map/ppermute | solution.py:33
  38.6 4.0 %collective-permute-done.6 = f32[16,1280]{1,0:T(8,128)S(1)} collective-permute-done((f32[16,1280]{1,0:T(8,128)S(1)}, f32[16,1280]{1,0:T(8,128)S(1)}, u32[]{:S(2)}, u32[]{:S(2)}) %collective-permute-start.6) | collective-permute-done | bytes 81952 | tf_op jit(solution)/shard_map/ppermute | solution.py:33
  44.0 1.8 %collective-permute-start.10 = (f32[16,896]{1,0:T(8,128)S(1)}, f32[16,896]{1,0:T(8,128)S(1)}, u32[]{:S(2)}, u32[]{:S(2)}) collective-permute-start(f32[16,896]{1,0:T(8,128)S(1)} %slice_add_fusion.5.rest_1_), channel_id=1, source_target_pairs={{0,8},{4,12},{8,0},{12,4},{16,24},{20,28},{24,16},{28,20},{1,9},{5... | collective-permute-start | bytes 172040 | tf_op jit(solution)/shard_map/ppermute | solution.py:33
  45.8 2.1 %factor_first.3.in_ref = f32[128,128]{1,0:T(8,128)S(1)} custom-call(s32[1]{0:T(128)} %bitcast.place_ref, f32[64,128]{1,0:T(8,128)S(1)} %maximum_add_fusion.own_ref, f32[64,128]{1,0:T(8,128)S(1)} %collective-permute-done.11.other_ref), custom_call_target="tpu_custom_call" | custom-call | flops 1500000000 | bytes 131072 | tf_op jit(solution)/shard_map/factor_first/pallas_call | solution.py:65
  51.6 2.1 %factor_rest.3.inv_ref = f32[128,128]{1,0:T(8,128)S(1)} custom-call(f32[128,128]{1,0:T(8,128)S(1)} %factor_first.3.in_ref), custom_call_target="tpu_custom_call" | custom-call | flops 1500000000 | bytes 131072 | tf_op jit(solution)/shard_map/factor_rest/pallas_call | solution.py:65
  54.9 2.8 %collective-permute-done.13.rest_5_ = f32[32,896]{1,0:T(8,128)S(1)} collective-permute-done((f32[32,896]{1,0:T(8,128)S(1)}, f32[32,896]{1,0:T(8,128)S(1)}, u32[]{:S(2)}, u32[]{:S(2)}) %collective-permute-start.13) | collective-permute-done | bytes 114720 | tf_op jit(solution)/shard_map/ppermute | solution.py:33
  69.9 2.1 %factor_first.4 = (f32[128,128]{1,0:T(8,128)S(1)}, f32[128,128]{1,0:T(8,128)S(1)}) custom-call(f32[128,128]{1,0:T(8,128)S(1)} %add.69.one_ref, f32[128,128]{1,0:T(8,128)S(1)} %collective-permute-done.19.two_ref), custom_call_target="tpu_custom_call" | custom-call | flops 1500000000 | bytes 131072 | tf_op jit(solution)/shard_map/factor_first/pallas_call | solution.py:65
  74.1 2.1 %factor_rest.4.rest_3_ = f32[128,128]{1,0:T(8,128)S(1)} custom-call(f32[128,128]{1,0:T(8,128)S(1)} %get-tuple-element.76.in_ref), custom_call_target="tpu_custom_call" | custom-call | flops 1500000000 | bytes 131072 | tf_op jit(solution)/shard_map/factor_rest/pallas_call | solution.py:65
  78.5 2.7 %pull.3 = (f32[512,128]{1,0:T(8,128)S(1)}, f32[64,1792]{1,0:T(8,128)S(1)}, f32[64,1792]{1,0:T(8,128)S(1)}) custom-call(s32[1]{0:T(128)} %bitcast.place_ref, f32[256,128]{1,0:T(8,128)S(1)} %add.70.a, f32[256,128]{1,0:T(8,128)S(1)} %collective-permute-done.20.b, f32[256,128]{1,0:T(8,128)S(1)} %add.71.c, f32[256,128]{1,0:T(8,128)S(1)} %collective-permute-done.21.d, ...), custom_call_target="tpu_custom_call" | custom-call | flops 1000000000 | bytes 5000000 | tf_op jit(solution)/shard_map/pull/pallas_call | solution.py:65
  81.3 1.8 %collective-permute-done.22 = f32[64,1792]{1,0:T(8,128)S(1)} collective-permute-done((f32[64,1792]{1,0:T(8,128)S(1)}, f32[64,1792]{1,0:T(8,128)S(1)}, u32[]{:S(2)}, u32[]{:S(2)}) %collective-permute-start.22) | collective-permute-done | bytes 458784 | tf_op jit(solution)/shard_map/ppermute | solution.py:33
  83.7 2.3 %collective-permute-start.23 = (f32[32,1024]{1,0:T(8,128)S(1)}, f32[32,1024]{1,0:T(8,128)S(1)}, u32[]{:S(2)}, u32[]{:S(2)}) collective-permute-start(f32[32,1024]{1,0:T(8,128)S(1)} %maximum_maximum_fusion.1), channel_id=1, source_target_pairs={{0,8},{4,12},{8,0},{12,4},{16,24},{20,28},{24,16},{28,20},{1,9},{5... | collective-permute-start | bytes 393224 | tf_op jit(solution)/shard_map/ppermute | solution.py:33
  86.0 5.4 %collective-permute-done.25 = f32[32,896]{1,0:T(8,128)S(1)} collective-permute-done((f32[32,896]{1,0:T(8,128)S(1)}, f32[32,896]{1,0:T(8,128)S(1)}, u32[]{:S(2)}, u32[]{:S(2)}) %collective-permute-start.25) | collective-permute-done | bytes 114720 | tf_op jit(solution)/shard_map/ppermute | solution.py:33
  92.0 2.0 %collective-permute-start.24 = (f32[16,1280]{1,0:T(8,128)S(1)}, f32[16,1280]{1,0:T(8,128)S(1)}, u32[]{:S(2)}, u32[]{:S(2)}) collective-permute-start(f32[16,1280]{1,0:T(8,128)S(1)} %constant_dynamic-update-slice_fusion.4), channel_id=1, source_target_pairs={{0,16},{4,20},{8,24},{12,28},{16,0},{20,4},{24,8},{28,12},{1,17},{... | collective-permute-start | bytes 245768 | tf_op jit(solution)/shard_map/ppermute | solution.py:33
  94.1 2.4 %collective-permute-done.26 = f32[16,896]{1,0:T(8,128)S(1)} collective-permute-done((f32[16,896]{1,0:T(8,128)S(1)}, f32[16,896]{1,0:T(8,128)S(1)}, u32[]{:S(2)}, u32[]{:S(2)}) %collective-permute-start.26) | collective-permute-done | bytes 57376 | tf_op jit(solution)/shard_map/ppermute | solution.py:33
  96.5 2.4 %collective-permute-done.24 = f32[16,1280]{1,0:T(8,128)S(1)} collective-permute-done((f32[16,1280]{1,0:T(8,128)S(1)}, f32[16,1280]{1,0:T(8,128)S(1)}, u32[]{:S(2)}, u32[]{:S(2)}) %collective-permute-start.24) | collective-permute-done | bytes 81952 | tf_op jit(solution)/shard_map/ppermute | solution.py:33
  99.6 1.9 %collective-permute-start.28 = (f32[16,896]{1,0:T(8,128)S(1)}, f32[16,896]{1,0:T(8,128)S(1)}, u32[]{:S(2)}, u32[]{:S(2)}) collective-permute-start(f32[16,896]{1,0:T(8,128)S(1)} %slice_add_fusion.4.rest_1_), channel_id=1, source_target_pairs={{0,8},{4,12},{8,0},{12,4},{16,24},{20,28},{24,16},{28,20},{1,9},{5... | collective-permute-start | bytes 172040 | tf_op jit(solution)/shard_map/ppermute | solution.py:33
  101.5 2.1 %factor_first.5.in_ref = f32[128,128]{1,0:T(8,128)S(1)} custom-call(s32[1]{0:T(128)} %bitcast.place_ref, f32[64,128]{1,0:T(8,128)S(1)} %maximum_add_fusion.1.own_ref, f32[64,128]{1,0:T(8,128)S(1)} %collective-permute-done.29.other_ref), custom_call_target="tpu_custom_call" | custom-call | flops 1500000000 | bytes 131072 | tf_op jit(solution)/shard_map/factor_first/pallas_call | solution.py:65
  107.4 2.1 %factor_rest.5.inv_ref.refs_4_ = f32[128,128]{1,0:T(8,128)S(1)} custom-call(f32[128,128]{1,0:T(8,128)S(1)} %factor_first.5.in_ref), custom_call_target="tpu_custom_call" | custom-call | flops 1500000000 | bytes 131072 | tf_op jit(solution)/shard_map/factor_rest/pallas_call | solution.py:65
  111.2 2.4 %collective-permute-done.31.rest_5_ = f32[32,896]{1,0:T(8,128)S(1)} collective-permute-done((f32[32,896]{1,0:T(8,128)S(1)}, f32[32,896]{1,0:T(8,128)S(1)}, u32[]{:S(2)}, u32[]{:S(2)}) %collective-permute-start.31) | collective-permute-done | bytes 114720 | tf_op jit(solution)/shard_map/ppermute | solution.py:33
  117.1 3.7 %collective-permute-done.34 = f32[128,128]{1,0:T(8,128)S(1)} collective-permute-done((f32[128,128]{1,0:T(8,128)S(1)}, f32[128,128]{1,0:T(8,128)S(1)}, u32[]{:S(2)}, u32[]{:S(2)}) %collective-permute-start.34) | collective-permute-done | bytes 65568 | tf_op jit(solution)/shard_map/ppermute | solution.py:33
  121.5 5.3 %finish.1 = (f32[512,1664]{1,0:T(8,128)}, f32[2,512,128]{2,1,0:T(8,128)}) custom-call(f32[512,1664]{1,0:T(8,128)S(1)} %copy-done.1, bf16[512,1664]{1,0:T(8,128)(2,1)S(1)} %copy-done.3, f32[512,128]{1,0:T(8,128)S(1)} %get-tuple-element.65.rest_0_.refs_2_, f32[512,128]{1,0:T(8,128)S(1)} %get-tuple-element.77.refs_3_, ...), custom_call_target="tpu_custom_call" | custom-call | flops 1500000000 | bytes 12000000 | tf_op jit(solution)/shard_map/finish/pallas_call | solution.py:247
  126.8 5.7 %last_factor.1 = f32[1664,128]{1,0:T(8,128)} custom-call(f32[128,128]{1,0:T(8,128)S(1)} %add.79.one_ref, f32[128,128]{1,0:T(8,128)S(1)} %collective-permute-done.35.two_ref, f32[128,1664]{1,0:T(8,128)S(1)} %get-tuple-element.89.refs_6_.right_ref), custom_call_target="tpu_custom_call" | custom-call | flops 3000000000 | bytes 2000000 | tf_op jit(solution)/shard_map/last_factor/pallas_call | solution.py:65
  (116 shorter events, 44.4 us)
Async XLA Ops:
  7.0 6.5 %collective-permute-start = (f32[256,128]{1,0:T(8,128)S(1)}, f32[256,128]{1,0:T(8,128)S(1)}, u32[]{:S(2)}, u32[]{:S(2)}) collective-permute-start(f32[256,128]{1,0:T(8,128)S(1)} %get-tuple-element.48), channel_id=1, source_target_pairs={{0,1},{1,0},{2,3},{3,2},{4,5},{5,4},{6,7},{7,6},{8,9},{9,8},{10,11... | collective-permute-start | bytes 393224 | tf_op jit(solution)/shard_map/ppermute | solution.py:33
  10.0 5.4 %collective-permute-start.2 = (f32[256,128]{1,0:T(8,128)S(1)}, f32[256,128]{1,0:T(8,128)S(1)}, u32[]{:S(2)}, u32[]{:S(2)}) collective-permute-start(f32[256,128]{1,0:T(8,128)S(1)} %get-tuple-element.49), channel_id=1, source_target_pairs={{0,2},{1,3},{2,0},{3,1},{4,6},{5,7},{6,4},{7,5},{8,10},{9,11},{10,... | collective-permute-start | bytes 393224 | tf_op jit(solution)/shard_map/ppermute | solution.py:33
  13.5 5.1 %collective-permute-start.1 = (f32[256,128]{1,0:T(8,128)S(1)}, f32[256,128]{1,0:T(8,128)}, u32[]{:S(2)}, u32[]{:S(2)}) collective-permute-start(f32[256,128]{1,0:T(8,128)S(1)} %add.60.a), channel_id=1, source_target_pairs={{0,2},{1,3},{2,0},{3,1},{4,6},{5,7},{6,4},{7,5},{8,10},{9,11},{10,... | collective-permute-start | bytes 393224 | tf_op jit(solution)/shard_map/ppermute | solution.py:33
  16.0 5.3 %collective-permute-start.3 = (f32[256,128]{1,0:T(8,128)}, f32[256,128]{1,0:T(8,128)}, u32[]{:S(2)}, u32[]{:S(2)}) collective-permute-start(f32[256,128]{1,0:T(8,128)} %add.61.c), channel_id=1, source_target_pairs={{0,1},{1,0},{2,3},{3,2},{4,5},{5,4},{6,7},{7,6},{8,9},{9,8},{10,11... | collective-permute-start | bytes 393224 | tf_op jit(solution)/shard_map/ppermute | solution.py:33
  23.6 1.9 %collective-permute-start.4 = (f32[64,1792]{1,0:T(8,128)S(1)}, f32[64,1792]{1,0:T(8,128)S(1)}, u32[]{:S(2)}, u32[]{:S(2)}) collective-permute-start(f32[64,1792]{1,0:T(8,128)S(1)} %get-tuple-element.53), channel_id=1, source_target_pairs={{0,4},{4,0},{8,12},{12,8},{16,20},{20,16},{24,28},{28,24},{1,5},{5... | collective-permute-start | bytes 1376264 | tf_op jit(solution)/shard_map/ppermute | solution.py:33
  25.6 8.7 %collective-permute-start.7 = (f32[32,896]{1,0:T(8,128)S(1)}, f32[32,896]{1,0:T(8,128)S(1)}, u32[]{:S(2)}, u32[]{:S(2)}) collective-permute-start(f32[32,896]{1,0:T(8,128)S(1)} %concatenate.115), channel_id=1, source_target_pairs={{0,16},{4,20},{8,24},{12,28},{16,0},{20,4},{24,8},{28,12},{1,17},{... | collective-permute-start | bytes 344072 | tf_op jit(solution)/shard_map/ppermute | solution.py:33
  28.2 6.7 %collective-permute-start.5 = (f32[32,1024]{1,0:T(8,128)S(1)}, f32[32,1024]{1,0:T(8,128)S(1)}, u32[]{:S(2)}, u32[]{:S(2)}) collective-permute-start(f32[32,1024]{1,0:T(8,128)S(1)} %maximum_maximum_fusion), channel_id=1, source_target_pairs={{0,8},{4,12},{8,0},{12,4},{16,24},{20,28},{24,16},{28,20},{1,9},{5... | collective-permute-start | bytes 393224 | tf_op jit(solution)/shard_map/ppermute | solution.py:33
  34.3 4.2 %collective-permute-start.8 = (f32[16,896]{1,0:T(8,128)S(1)}, f32[16,896]{1,0:T(8,128)S(1)}, u32[]{:S(2)}, u32[]{:S(2)}) collective-permute-start(f32[16,896]{1,0:T(8,128)S(1)} %slice.268), channel_id=1, source_target_pairs={{0,8},{4,12},{8,0},{12,4},{16,24},{20,28},{24,16},{28,20},{1,9},{5... | collective-permute-start | bytes 172040 | tf_op jit(solution)/shard_map/ppermute | solution.py:33
  35.0 7.6 %collective-permute-start.6 = (f32[16,1280]{1,0:T(8,128)S(1)}, f32[16,1280]{1,0:T(8,128)S(1)}, u32[]{:S(2)}, u32[]{:S(2)}) collective-permute-start(f32[16,1280]{1,0:T(8,128)S(1)} %constant_dynamic-update-slice_fusion), channel_id=1, source_target_pairs={{0,16},{4,20},{8,24},{12,28},{16,0},{20,4},{24,8},{28,12},{1,17},{... | collective-permute-start | bytes 245768 | tf_op jit(solution)/shard_map/ppermute | solution.py:33
  42.6 3.2 %collective-permute-start.11 = (f32[64,128]{1,0:T(8,128)S(1)}, f32[64,128]{1,0:T(8,128)S(1)}, u32[]{:S(2)}, u32[]{:S(2)}) collective-permute-start(f32[64,128]{1,0:T(8,128)S(1)} %maximum_add_fusion.own_ref), channel_id=1, source_target_pairs={{0,4},{4,0},{8,12},{12,8},{16,20},{20,16},{24,28},{28,24},{1,5},{5... | collective-permute-start | bytes 98312 | tf_op jit(solution)/shard_map/ppermute | solution.py:33
  42.7 6.0 %collective-permute-start.9 = (f32[16,768]{1,0:T(8,128)S(1)}, f32[16,768]{1,0:T(8,128)S(1)}, u32[]{:S(2)}, u32[]{:S(2)}) collective-permute-start(f32[16,768]{1,0:T(8,128)S(1)} %slice_add_fusion.7.rest_0_), channel_id=1, source_target_pairs={{0,16},{4,20},{8,24},{12,28},{16,0},{20,4},{24,8},{28,12},{1,17},{... | collective-permute-start | bytes 147464 | tf_op jit(solution)/shard_map/ppermute | solution.py:33
  44.0 5.1 %collective-permute-start.10 = (f32[16,896]{1,0:T(8,128)S(1)}, f32[16,896]{1,0:T(8,128)S(1)}, u32[]{:S(2)}, u32[]{:S(2)}) collective-permute-start(f32[16,896]{1,0:T(8,128)S(1)} %slice_add_fusion.5.rest_1_), channel_id=1, source_target_pairs={{0,8},{4,12},{8,0},{12,4},{16,24},{20,28},{24,16},{28,20},{1,9},{5... | collective-permute-start | bytes 172040 | tf_op jit(solution)/shard_map/ppermute | solution.py:33
  49.2 5.7 %collective-permute-start.12 = (f32[32,768]{1,0:T(8,128)S(1)}, f32[32,768]{1,0:T(8,128)S(1)}, u32[]{:S(2)}, u32[]{:S(2)}) collective-permute-start(f32[32,768]{1,0:T(8,128)S(1)} %pad_maximum_fusion.6), channel_id=1, source_target_pairs={{0,8},{4,12},{8,0},{12,4},{16,24},{20,28},{24,16},{28,20},{1,9},{5... | collective-permute-start | bytes 294920 | tf_op jit(solution)/shard_map/ppermute | solution.py:33
  50.0 7.6 %collective-permute-start.13 = (f32[32,896]{1,0:T(8,128)S(1)}, f32[32,896]{1,0:T(8,128)S(1)}, u32[]{:S(2)}, u32[]{:S(2)}) collective-permute-start(f32[32,896]{1,0:T(8,128)S(1)} %pad_maximum_fusion.4), channel_id=1, source_target_pairs={{0,16},{4,20},{8,24},{12,28},{16,0},{20,4},{24,8},{28,12},{1,17},{... | collective-permute-start | bytes 344072 | tf_op jit(solution)/shard_map/ppermute | solution.py:33
  60.6 4.3 %collective-permute-start.16 = (f32[128,128]{1,0:T(8,128)S(1)}, f32[128,128]{1,0:T(8,128)S(1)}, u32[]{:S(2)}, u32[]{:S(2)}) collective-permute-start(f32[128,128]{1,0:T(8,128)S(1)} %get-tuple-element.68), channel_id=1, source_target_pairs={{0,1},{1,0},{2,3},{3,2},{4,5},{5,4},{6,7},{7,6},{8,9},{9,8},{10,11... | collective-permute-start | bytes 196616 | tf_op jit(solution)/shard_map/ppermute | solution.py:33
  64.9 5.0 %collective-permute-start.19 = (f32[128,128]{1,0:T(8,128)S(1)}, f32[128,128]{1,0:T(8,128)S(1)}, u32[]{:S(2)}, u32[]{:S(2)}) collective-permute-start(f32[128,128]{1,0:T(8,128)S(1)} %add.69.one_ref), channel_id=1, source_target_pairs={{0,2},{1,3},{2,0},{3,1},{4,6},{5,7},{6,4},{7,5},{8,10},{9,11},{10,... | collective-permute-start | bytes 196616 | tf_op jit(solution)/shard_map/ppermute | solution.py:33
  66.1 5.9 %collective-permute-start.17 = (f32[256,128]{1,0:T(8,128)S(1)}, f32[256,128]{1,0:T(8,128)S(1)}, u32[]{:S(2)}, u32[]{:S(2)}) collective-permute-start(f32[256,128]{1,0:T(8,128)S(1)} %get-tuple-element.69), channel_id=1, source_target_pairs={{0,1},{1,0},{2,3},{3,2},{4,5},{5,4},{6,7},{7,6},{8,9},{9,8},{10,11... | collective-permute-start | bytes 393224 | tf_op jit(solution)/shard_map/ppermute | solution.py:33
  67.0 5.1 %collective-permute-start.18 = (f32[256,128]{1,0:T(8,128)S(1)}, f32[256,128]{1,0:T(8,128)S(1)}, u32[]{:S(2)}, u32[]{:S(2)}) collective-permute-start(f32[256,128]{1,0:T(8,128)S(1)} %get-tuple-element.70), channel_id=1, source_target_pairs={{0,2},{1,3},{2,0},{3,1},{4,6},{5,7},{6,4},{7,5},{8,10},{9,11},{10,... | collective-permute-start | bytes 393224 | tf_op jit(solution)/shard_map/ppermute | solution.py:33
  72.1 5.0 %collective-permute-start.20 = (f32[256,128]{1,0:T(8,128)S(1)}, f32[256,128]{1,0:T(8,128)S(1)}, u32[]{:S(2)}, u32[]{:S(2)}) collective-permute-start(f32[256,128]{1,0:T(8,128)S(1)} %add.70.a), channel_id=1, source_target_pairs={{0,2},{1,3},{2,0},{3,1},{4,6},{5,7},{6,4},{7,5},{8,10},{9,11},{10,... | collective-permute-start | bytes 393224 | tf_op jit(solution)/shard_map/ppermute | solution.py:33
  73.6 5.0 %collective-permute-start.21 = (f32[256,128]{1,0:T(8,128)S(1)}, f32[256,128]{1,0:T(8,128)S(1)}, u32[]{:S(2)}, u32[]{:S(2)}) collective-permute-start(f32[256,128]{1,0:T(8,128)S(1)} %add.71.c), channel_id=1, source_target_pairs={{0,1},{1,0},{2,3},{3,2},{4,5},{5,4},{6,7},{7,6},{8,9},{9,8},{10,11... | collective-permute-start | bytes 393224 | tf_op jit(solution)/shard_map/ppermute | solution.py:33
  81.2 1.9 %collective-permute-start.22 = (f32[64,1792]{1,0:T(8,128)S(1)}, f32[64,1792]{1,0:T(8,128)S(1)}, u32[]{:S(2)}, u32[]{:S(2)}) collective-permute-start(f32[64,1792]{1,0:T(8,128)S(1)} %get-tuple-element.79), channel_id=1, source_target_pairs={{0,4},{4,0},{8,12},{12,8},{16,20},{20,16},{24,28},{28,24},{1,5},{5... | collective-permute-start | bytes 1376264 | tf_op jit(solution)/shard_map/ppermute | solution.py:33
  83.2 8.1 %collective-permute-start.25 = (f32[32,896]{1,0:T(8,128)S(1)}, f32[32,896]{1,0:T(8,128)S(1)}, u32[]{:S(2)}, u32[]{:S(2)}) collective-permute-start(f32[32,896]{1,0:T(8,128)S(1)} %concatenate.117), channel_id=1, source_target_pairs={{0,16},{4,20},{8,24},{12,28},{16,0},{20,4},{24,8},{28,12},{1,17},{... | collective-permute-start | bytes 344072 | tf_op jit(solution)/shard_map/ppermute | solution.py:33
  83.7 8.2 %collective-permute-start.23 = (f32[32,1024]{1,0:T(8,128)S(1)}, f32[32,1024]{1,0:T(8,128)S(1)}, u32[]{:S(2)}, u32[]{:S(2)}) collective-permute-start(f32[32,1024]{1,0:T(8,128)S(1)} %maximum_maximum_fusion.1), channel_id=1, source_target_pairs={{0,8},{4,12},{8,0},{12,4},{16,24},{20,28},{24,16},{28,20},{1,9},{5... | collective-permute-start | bytes 393224 | tf_op jit(solution)/shard_map/ppermute | solution.py:33
  91.4 5.1 %collective-permute-start.26 = (f32[16,896]{1,0:T(8,128)S(1)}, f32[16,896]{1,0:T(8,128)S(1)}, u32[]{:S(2)}, u32[]{:S(2)}) collective-permute-start(f32[16,896]{1,0:T(8,128)S(1)} %slice.293), channel_id=1, source_target_pairs={{0,8},{4,12},{8,0},{12,4},{16,24},{20,28},{24,16},{28,20},{1,9},{5... | collective-permute-start | bytes 172040 | tf_op jit(solution)/shard_map/ppermute | solution.py:33
  92.0 6.8 %collective-permute-start.24 = (f32[16,1280]{1,0:T(8,128)S(1)}, f32[16,1280]{1,0:T(8,128)S(1)}, u32[]{:S(2)}, u32[]{:S(2)}) collective-permute-start(f32[16,1280]{1,0:T(8,128)S(1)} %constant_dynamic-update-slice_fusion.4), channel_id=1, source_target_pairs={{0,16},{4,20},{8,24},{12,28},{16,0},{20,4},{24,8},{28,12},{1,17},{... | collective-permute-start | bytes 245768 | tf_op jit(solution)/shard_map/ppermute | solution.py:33
  98.9 2.6 %collective-permute-start.29 = (f32[64,128]{1,0:T(8,128)S(1)}, f32[64,128]{1,0:T(8,128)S(1)}, u32[]{:S(2)}, u32[]{:S(2)}) collective-permute-start(f32[64,128]{1,0:T(8,128)S(1)} %maximum_add_fusion.1.own_ref), channel_id=1, source_target_pairs={{0,4},{4,0},{8,12},{12,8},{16,20},{20,16},{24,28},{28,24},{1,5},{5... | collective-permute-start | bytes 98312 | tf_op jit(solution)/shard_map/ppermute | solution.py:33
  99.0 5.7 %collective-permute-start.27 = (f32[16,768]{1,0:T(8,128)S(1)}, f32[16,768]{1,0:T(8,128)S(1)}, u32[]{:S(2)}, u32[]{:S(2)}) collective-permute-start(f32[16,768]{1,0:T(8,128)S(1)} %slice_add_fusion.6.rest_0_), channel_id=1, source_target_pairs={{0,16},{4,20},{8,24},{12,28},{16,0},{20,4},{24,8},{28,12},{1,17},{... | collective-permute-start | bytes 147464 | tf_op jit(solution)/shard_map/ppermute | solution.py:33
  99.6 5.2 %collective-permute-start.28 = (f32[16,896]{1,0:T(8,128)S(1)}, f32[16,896]{1,0:T(8,128)S(1)}, u32[]{:S(2)}, u32[]{:S(2)}) collective-permute-start(f32[16,896]{1,0:T(8,128)S(1)} %slice_add_fusion.4.rest_1_), channel_id=1, source_target_pairs={{0,8},{4,12},{8,0},{12,4},{16,24},{20,28},{24,16},{28,20},{1,9},{5... | collective-permute-start | bytes 172040 | tf_op jit(solution)/shard_map/ppermute | solution.py:33
  104.8 6.3 %collective-permute-start.30 = (f32[32,768]{1,0:T(8,128)S(1)}, f32[32,768]{1,0:T(8,128)S(1)}, u32[]{:S(2)}, u32[]{:S(2)}) collective-permute-start(f32[32,768]{1,0:T(8,128)S(1)} %pad_maximum_fusion.7), channel_id=1, source_target_pairs={{0,8},{4,12},{8,0},{12,4},{16,24},{20,28},{24,16},{28,20},{1,9},{5... | collective-permute-start | bytes 294920 | tf_op jit(solution)/shard_map/ppermute | solution.py:33
  105.8 7.8 %collective-permute-start.31 = (f32[32,896]{1,0:T(8,128)S(1)}, f32[32,896]{1,0:T(8,128)S(1)}, u32[]{:S(2)}, u32[]{:S(2)}) collective-permute-start(f32[32,896]{1,0:T(8,128)S(1)} %pad_maximum_fusion.5), channel_id=1, source_target_pairs={{0,16},{4,20},{8,24},{12,28},{16,0},{20,4},{24,8},{28,12},{1,17},{... | collective-permute-start | bytes 344072 | tf_op jit(solution)/shard_map/ppermute | solution.py:33
  116.5 4.3 %collective-permute-start.34 = (f32[128,128]{1,0:T(8,128)S(1)}, f32[128,128]{1,0:T(8,128)S(1)}, u32[]{:S(2)}, u32[]{:S(2)}) collective-permute-start(f32[128,128]{1,0:T(8,128)S(1)} %get-tuple-element.92), channel_id=1, source_target_pairs={{0,1},{1,0},{2,3},{3,2},{4,5},{5,4},{6,7},{7,6},{8,9},{9,8},{10,11... | collective-permute-start | bytes 196616 | tf_op jit(solution)/shard_map/ppermute | solution.py:33
  120.8 6.0 %collective-permute-start.35 = (f32[128,128]{1,0:T(8,128)S(1)}, f32[128,128]{1,0:T(8,128)S(1)}, u32[]{:S(2)}, u32[]{:S(2)}) collective-permute-start(f32[128,128]{1,0:T(8,128)S(1)} %add.79.one_ref), channel_id=1, source_target_pairs={{0,2},{1,3},{2,0},{3,1},{4,6},{5,7},{6,4},{7,5},{8,10},{9,11},{10,... | collective-permute-start | bytes 196616 | tf_op jit(solution)/shard_map/ppermute | solution.py:33
  (9 other events, 37.9 us)

commit v3 on v2

v3 whole, which is shorter than its diff:
```python
import jax
import jax.numpy as jnp
from jax import lax
from jax.experimental import pallas as pl
from jax.experimental.pallas import tpu as pltpu
from jax.sharding import PartitionSpec as P

F32 = jnp.float32
BF16 = jnp.bfloat16
HIGHEST = lax.Precision.HIGHEST
VMEM = pl.BlockSpec(memory_space=pltpu.VMEM)
SMEM = pl.BlockSpec(memory_space=pltpu.SMEM)
NN = (((1,), (0,)), ((), ()))
NT = (((1,), (1,)), ((), ()))
TN = (((0,), (0,)), ((), ()))
KEEP = 0.95
PANEL = 16
FACTOR = 1_500_000_000


def masks_of(axis):
    size = lax.axis_size(axis)
    masks = []
    mask = 1
    while mask < size:
        masks.append(mask)
        mask *= 2
    assert mask == size
    return masks


def swap(x, axis, even, odd):
    row_count, col_count = lax.axis_size("row"), lax.axis_size("col")
    pairs = []
    for row in range(row_count):
        mask = odd if row % 2 else even
        for col in range(col_count):
            to = (row ^ mask) * col_count + col if axis == "row" else row * col_count + (col ^ mask)
            pairs.append((row * col_count + col, to))
    return lax.ppermute(x, ("row", "col"), pairs)


def backward(slot, count):
    out, bit = 0, 1
    while bit < count:
        out = out * 2 + (slot // bit) % 2
        bit *= 2
    return out


def chunk_at(place, slot, count, other=False):
    if other:
        place = place ^ 1
    half = count // 2
    return place ^ jnp.where(place % 2 == 0, 2 * backward(slot, half), 2 * slot)


def split(x):
    high = x.astype(BF16)
    return high, (x - high.astype(F32)).astype(BF16)


def dot(a, b, dims=NN):
    return lax.dot_general(a, b, dims, preferred_element_type=F32)


def exact(a, b, dims=NN):
    return lax.dot_general(a, b, dims, precision=HIGHEST, preferred_element_type=F32)


def tiles(width, most=256):
    return [(start, min(most, width - start)) for start in range(0, width, most)]


def struct(*shape, dtype=F32):
    return jax.ShapeDtypeStruct(shape, dtype)


def call(body, name, out, ins, scratch=(), flops=0, nbytes=0, **kw):
    return pl.pallas_call(
        body,
        out_shape=out,
        in_specs=[SMEM if x.dtype == jnp.int32 else VMEM for x in ins],
        out_specs=jax.tree.map(lambda _: VMEM, out),
        scratch_shapes=list(scratch),
        name=name,
        compiler_params=pltpu.CompilerParams(vmem_limit_bytes=24 * 2**20),
        cost_estimate=pl.CostEstimate(flops=flops, bytes_accessed=nbytes, transcendentals=0),
        **kw,
    )(*ins)


def start(momentum, grad, basis):
    rows, cols = momentum.shape
    rank = basis.shape[1]
    steps = 4
    block = rows // steps

    def body(momentum_hbm, grad_hbm, basis_hbm, high_ref, low_ref, proj_ref, momentum_ref, grad_ref, basis_ref, both_ref, sems):
        whole = pltpu.make_async_copy(basis_hbm, basis_ref, sems.at[0])
        whole.start()
        copies = []
        for i in range(steps):
            at = pl.ds(i * block, block)
            pair = (
                pltpu.make_async_copy(momentum_hbm.at[at], momentum_ref.at[at], sems.at[1 + 2 * i]),
                pltpu.make_async_copy(grad_hbm.at[at], grad_ref.at[at], sems.at[2 + 2 * i]),
            )
            for copy in pair:
                copy.start()
            copies.append(pair)
        whole.wait()
        high, low = split(basis_ref[...])
        both_ref[:, :rank] = high
        both_ref[:, rank:] = low
        for i in range(steps):
            for copy in copies[i]:
                copy.wait()
            at = pl.ds(i * block, block)
            high, low = split(momentum_ref[at, :] + grad_ref[at, :].astype(F32))
            high_ref[at, :] = high
            low_ref[at, :] = low
            wide = dot(high, both_ref[...])
            proj_ref[at, :] = wide[:, :rank] + wide[:, rank:] + dot(low, both_ref[:, :rank])

    return pl.pallas_call(
        body,
        in_specs=[pl.BlockSpec(memory_space=pltpu.HBM)] * 3,
        out_specs=[VMEM] * 3,
        out_shape=[struct(rows, cols, dtype=BF16)] * 2 + [struct(rows, rank)],
        scratch_shapes=[
            pltpu.VMEM((rows, cols), F32),
            pltpu.VMEM((rows, cols), BF16),
            pltpu.VMEM((cols, rank), F32),
            pltpu.VMEM((cols, 2 * rank), BF16),
            pltpu.SemaphoreType.DMA((1 + 2 * steps,)),
        ],
        name="start",
        compiler_params=pltpu.CompilerParams(vmem_limit_bytes=24 * 2**20),
    )(*(pltpu.with_memory_space_constraint(x, pltpu.HBM) for x in (momentum, grad, basis)))


def pull_rows(turned, proj, high_ref, low_ref, cross, right_ref, out_ref):
    half = turned.shape[0]
    width = high_ref.shape[1]
    high, low = split(turned)
    both = jnp.concatenate([high, low], axis=0)
    for at, size in tiles(width):
        wide = dot(both, high_ref[:, at:at + size])
        out = wide[:half] + wide[half:] + dot(high, low_ref[:, at:at + size])
        if cross is not None:
            right_high, right_low = split(right_ref[:, at:at + size])
            wide = dot(jnp.concatenate(cross, axis=0), right_high)
            out = out + (wide[:half] + wide[half:] + dot(cross[0], right_low))
        out_ref[:, at:at + size] = out
    out_ref[:, width:] = exact(turned, proj)


def pull_send(count, place, one, two, high, low, before=None):
    rows, width = high.shape
    rank = one.shape[1]
    chunk = rank // count

    def body(place_ref, one_ref, two_ref, high_ref, low_ref, *rest):
        proj = one_ref[...] + two_ref[...]
        left_ref = right_ref = None
        if before is not None:
            left_ref, right_ref, gram_ref, inv_ref = rest[:4]
            proj = proj - KEEP * exact(left_ref[...], gram_ref[...])
            proj = exact(proj, inv_ref[...], NT)
        proj_ref, keep_ref, send_ref, turned_ref = rest[-4:]
        proj_ref[...] = proj
        turned_ref[...] = proj.T

        def pick(other):
            at = [chunk_at(place_ref[0], t, count, other) * chunk for t in range(count // 2)]
            return jnp.concatenate([turned_ref[pl.ds(pl.multiple_of(x, chunk), chunk), :] for x in at], axis=0)

        keep_ref[...] = pick(False)
        turned = pick(True)
        cross = None if before is None else split(-KEEP * exact(turned, left_ref[...]))
        pull_rows(turned, proj, high_ref, low_ref, cross, right_ref, send_ref)

    out = [struct(rows, rank), struct(rank // 2, rows), struct(rank // 2, width + rank)]
    ins = [place, one, two, high, low] + list(before or [])
    return call(body, "pull_send", out, ins, [pltpu.VMEM((rank, rows), F32)], flops=500_000_000, nbytes=5_000_000)


def pull_keep(turned, proj, high, low, before=None):
    rows, width = high.shape
    rank = proj.shape[1]

    def body(turned_ref, proj_ref, high_ref, low_ref, *rest):
        turned = turned_ref[...]
        cross = right_ref = None
        if before is not None:
            left_ref, right_ref = rest[:2]
            cross = split(-KEEP * exact(turned, left_ref[...]))
        pull_rows(turned, proj_ref[...], high_ref, low_ref, cross, right_ref, rest[-1])

    ins = [turned, proj, high, low] + list(before or [])[:2]
    return call(body, "pull_keep", struct(rank // 2, width + rank), ins, flops=500_000_000, nbytes=5_000_000)


def normal(count, place, inv, own, other):
    rank = inv.shape[0]
    width = other.shape[1]
    chunk = rank // count

    def body(place_ref, inv_ref, other_ref, *rest):
        right_ref, gram_ref, raw_ref = rest[len(own):]
        place = place_ref[0]

        def put(piece, first, is_other):
            for i in range(piece.shape[0] // chunk):
                at = chunk_at(place, first + i, count, is_other) * chunk
                raw_ref[pl.ds(pl.multiple_of(at, chunk), chunk), :] = piece[i * chunk:(i + 1) * chunk, :]
            return first + piece.shape[0] // chunk

        slot = 0
        for piece in rest[:len(own)]:
            slot = put(piece, slot, False)
        put(other_ref, 0, True)
        inv_high, inv_low = split(inv_ref[...])
        inv_both = jnp.concatenate([inv_high, inv_low], axis=0)
        gram = jnp.zeros((rank, rank), F32)
        for at, size in tiles(width):
            raw_high, raw_low = split(raw_ref[:, at:at + size])
            wide = dot(inv_both, raw_high)
            right = wide[:rank] + wide[rank:] + dot(inv_high, raw_low)
            right_ref[:, at:at + size] = right
            high, low = split(right)
            wide = dot(jnp.concatenate([high, low], axis=0), high, NT)
            gram = gram + (wide[:rank] + wide[rank:] + dot(high, low, NT))
        gram_ref[...] = gram

    return call(body, "normal", [struct(rank, width), struct(rank, rank)], [place, inv, other, *own],
                [pltpu.VMEM((rank, width), F32)], flops=500_000_000, nbytes=2_000_000)


def push(high, low, right):
    rows, width = high.shape
    rank = right.shape[0]

    def body(high_ref, low_ref, right_ref, out_ref):
        image = None
        for at, size in tiles(width):
            right_high, right_low = split(right_ref[:, at:at + size])
            wide = dot(high_ref[:, at:at + size], jnp.concatenate([right_high, right_low], axis=0), NT)
            part = wide[:, :rank] + wide[:, rank:] + dot(low_ref[:, at:at + size], right_high, NT)
            image = part if image is None else image + part
        out_ref[...] = image

    return call(body, "push", struct(rows, rank), [high, low, right], flops=700_000_000, nbytes=5_000_000)


def left_of(proj, inv):
    def body(proj_ref, inv_ref, out_ref):
        out_ref[...] = exact(proj_ref[...], inv_ref[...], NT)

    return call(body, "left", struct(*proj.shape), [proj, inv], flops=100_000_000, nbytes=600_000)


def deflate(base, left, right, name, last=None):
    rows, cols = base[0].shape
    rank = left.shape[1]
    block = rows // 4
    tile = pl.BlockSpec((block, cols), lambda i: (i, 0))
    left_tile = pl.BlockSpec((block, rank), lambda i: (i, 0))
    right_tile = pl.BlockSpec((rank, cols), lambda i: (0, 0))

    def body(*refs):
        base_refs = refs[:len(base)]
        left_ref, right_ref = refs[len(base):len(base) + 2]
        high_ref, low_ref = refs[-2:]
        out_ref = refs[-3] if last is None else refs[-4]

        @pl.when(pl.program_id(0) == 0)
        def _():
            high, low = split(KEEP * right_ref[...])
            high_ref[...] = high
            low_ref[...] = low

        left = left_ref[...]
        if last is not None:
            refs[-3][0] = last[1] * refs[len(base) + 2][...]
            refs[-3][1] = last[1] * left
        high, low = split(left)
        for at, size in tiles(cols):
            right_high = high_ref[:, at:at + size]
            wide = dot(jnp.concatenate([high, low], axis=0), right_high)
            outer = wide[:block] + wide[block:] + dot(high, low_ref[:, at:at + size])
            total = base_refs[0][:, at:at + size]
            for ref in base_refs[1:]:
                total = total + ref[:, at:at + size].astype(F32)
            out_ref[:, at:at + size] = total - outer

    ins, in_specs = [*base, left, right], [tile] * len(base) + [left_tile, right_tile]
    out, out_specs = [struct(rows, cols)], [tile]
    if last is not None:
        ins.append(last[0])
        in_specs.append(left_tile)
        out.append(struct(2, rows, rank))
        out_specs.append(pl.BlockSpec((2, block, rank), lambda i: (0, i, 0)))
    return pl.pallas_call(
        body,
        grid=(4,),
        in_specs=in_specs,
        out_specs=out_specs,
        out_shape=out,
        scratch_shapes=[pltpu.VMEM((rank, cols), BF16)] * 2,
        name=name,
        compiler_params=pltpu.CompilerParams(vmem_limit_bytes=24 * 2**20),
        cost_estimate=pl.CostEstimate(flops=1_500_000_000, bytes_accessed=12_000_000, transcendentals=0),
    )(*ins)


def eliminate(full, first):
    rank = full.shape[1]
    groups = PANEL // 8
    sub = lax.broadcasted_iota(jnp.int32, (8, rank), 0)
    lane = lax.broadcasted_iota(jnp.int32, (8, rank), 1)
    rolled = pltpu.roll(full, lax.rem(rank - first, rank), 1)
    rows = [full[8 * g:8 * g + 8] for g in range(groups)]
    cols = [
        [jnp.broadcast_to(rolled[8 * g:8 * g + 8, j:j + 1], (8, rank)) for g in range(groups)] for j in range(PANEL)
    ]

    def spread(x, j):
        return jnp.broadcast_to(x[j // 8][j % 8:j % 8 + 1], (8, rank))

    pivot = spread(cols[0], 0)
    for j in range(PANEL):
        at = j // 8
        root = lax.rsqrt(pivot)
        if j + 1 < PANEL:
            above = spread(cols[j + 1], j) * root
            pivot = spread(cols[j + 1], j + 1) - above * above
        below = sub > j % 8
        here = lane == first + j
        row = jnp.where(here, 1.0, spread(rows, j)) * root
        for g in range(at, groups):
            mult = cols[j][g] * root
            rest = jnp.where(here, 0.0, rows[g])
            if g == at:
                mult = jnp.where(below, mult, 0.0)
                rest = jnp.where(below, rest, rows[g])
            rest = rest - mult * row
            rows[g] = jnp.where(sub == j % 8, row, rest) if g == at else rest
            cols[j][g] = mult
        for k in range(j + 1, PANEL):
            across = spread(cols[k], j) * root
            for g in range(at, groups):
                cols[k][g] = cols[k][g] - cols[j][g] * across
    return jnp.concatenate(rows, axis=0)


def thirds(x):
    high = x.astype(BF16)
    rest = x - high.astype(F32)
    middle = rest.astype(BF16)
    return high, middle, (rest - middle.astype(F32)).astype(BF16)


def factor_panels(state_ref, begin, end):
    rank = state_ref.shape[0]
    row = lax.broadcasted_iota(jnp.int32, (rank, rank), 0)
    col = lax.broadcasted_iota(jnp.int32, (rank, rank), 1)
    sub = lax.broadcasted_iota(jnp.int32, (PANEL, rank), 0)
    lane = lax.broadcasted_iota(jnp.int32, (PANEL, rank), 1)

    def panel(p, carry):
        first = pl.multiple_of(p * PANEL, PANEL)
        done = eliminate(state_ref[pl.ds(first, PANEL), :], first)
        lower = jnp.where((lane > first + sub) & (lane < first + PANEL), 0.0, done)
        a, b, c = thirds(done)
        d, e, f = thirds(lower)
        step = dot(
            jnp.concatenate([a, a, b, b, a, c], axis=0), jnp.concatenate([d, e, d, e, f, d], axis=0), TN
        )
        old = state_ref[...]
        fresh = jnp.where((col >= first) & (col < first + PANEL), 0.0, old) - step
        state_ref[...] = jnp.where(row >= first + PANEL, fresh, old)
        state_ref[pl.ds(first, PANEL), :] = done
        return carry

    lax.fori_loop(begin, end, panel, 0)


def factor_left(count, place, own, other):
    rank = own.shape[1]
    chunk = rank // count

    def first(place_ref, own_ref, other_ref, state_ref):
        for ref, is_other in ((own_ref, False), (other_ref, True)):
            for t in range(count // 2):
                at = chunk_at(place_ref[0], t, count, is_other) * chunk
                state_ref[pl.ds(pl.multiple_of(at, chunk), chunk), :] = ref[t * chunk:(t + 1) * chunk, :]
        factor_panels(state_ref, 0, rank // PANEL // 2)

    return call(first, "factor_first", struct(rank, rank), [place, own, other], flops=FACTOR, nbytes=131072)


def factor_rest(state):
    rank = state.shape[0]

    def rest(in_ref, out_ref):
        out_ref[...] = in_ref[...]
        factor_panels(out_ref, rank // PANEL // 2, rank // PANEL)
        out_ref[...] = lower_part(out_ref[...])

    return call(rest, "factor_rest", struct(rank, rank), [state], flops=FACTOR, nbytes=131072)


def factor_right(one, two):
    rank = one.shape[0]

    def first(one_ref, two_ref, gram_ref, state_ref):
        gram = one_ref[...] + two_ref[...]
        gram_ref[...] = gram
        state_ref[...] = gram
        factor_panels(state_ref, 0, rank // PANEL // 2)

    return call(first, "factor_first", [struct(rank, rank)] * 2, [one, two], flops=FACTOR, nbytes=131072)


def lower_part(x):
    row = lax.broadcasted_iota(jnp.int32, x.shape, 0)
    col = lax.broadcasted_iota(jnp.int32, x.shape, 1)
    return jnp.where(row >= col, x, 0.0)


def turn(right):
    rank, width = right.shape

    def body(right_ref, high_ref, low_ref):
        high, low = split(right_ref[...].T)
        high_ref[...] = high
        low_ref[...] = low

    return call(body, "turn", [struct(width, rank, dtype=BF16)] * 2, [right], flops=100_000_000, nbytes=2_000_000)


def last_factor(one, two, high, low, scale):
    def body(one_ref, two_ref, high_ref, low_ref, out_ref, state_ref):
        rank = state_ref.shape[0]
        state_ref[...] = one_ref[...] + two_ref[...]
        factor_panels(state_ref, 0, rank // PANEL)
        inv_high, inv_low = split(scale * lower_part(state_ref[...]))
        both = jnp.concatenate([inv_high, inv_low], axis=0)
        wide = dot(high_ref[...], both, NT)
        out_ref[...] = wide[:, :rank] + wide[:, rank:] + dot(low_ref[...], inv_high, NT)

    width, rank = high.shape
    return call(body, "last_factor", struct(width, rank), [one, two, high, low], [pltpu.VMEM((rank, rank), F32)],
                flops=2 * FACTOR, nbytes=2_000_000)


def sum_cols(x):
    masks = masks_of("col")
    for even, odd in zip(masks[:-1], masks[:0:-1]):
        x = x + swap(x, "col", even, odd)
    return x, lambda y: swap(y, "col", masks[-1], masks[0])


def sum_rows(keep, send, count, rank, beside=None):
    x = keep + swap(send, "row", 1, 1)
    width = x.shape[1] - rank
    gram = x[:, width:]
    x = x[:, :width]
    chunk = rank // count
    slots = count // 2
    masks = masks_of("row")[1:]
    bit = slots // 2
    for even, odd in zip(masks, reversed(masks)):
        size = bit * chunk
        cuts = [gram[(t ^ bit) * chunk:((t ^ bit) + 1) * chunk] for t in range(slots)]
        cuts = [jnp.concatenate(cuts[i:i + bit], axis=0) for i in range(0, slots, bit)]
        got = swap(jnp.concatenate([x[size:], *cuts], axis=1), "row", even, odd)
        back = [got[:, width + i * rank:width + (i + 1) * rank] for i in range(slots // bit)]
        x = x[:size] + got[:, :width]
        gram = gram + jnp.concatenate(back, axis=0)
        if beside is not None:
            x, gram, beside = lax.optimization_barrier((x, gram, beside))
        bit //= 2
    x, gram = lax.optimization_barrier((x, gram))
    return x, gram, swap(gram, "row", 1, 1), beside


def gather_rows(x, state, steps):
    masks = masks_of("row")[1:]
    own = [x]
    steps = list(steps)
    for even, odd in zip(reversed(masks), masks):
        more = swap(x, "row", even, odd)
        if steps:
            state = steps.pop(0)(state)
        x = jnp.concatenate([x, more], axis=0)
        x, state = lax.optimization_barrier((x, state))
        own.append(more)
    return own, swap(x, "row", 1, 1), state


def shards(momentum, grad, basis):
    count = lax.axis_size("row")
    rank = basis.shape[1]
    width = momentum.shape[1]
    row_scale = float(momentum.shape[0] * count) ** 0.5
    col_scale = float(width * lax.axis_size("col")) ** 0.5
    place = lax.axis_index("row").astype(jnp.int32).reshape(1)

    def left_side(one, two, before, beside):
        proj, turned, send = pull_send(count, place, one, two, high, low, before)
        keep = pull_keep(turned, proj, high, low, before)
        raw, own, other, beside = sum_rows(keep, send, count, rank, beside)

        def first(grams):
            return factor_left(count, place, *grams)

        def rest(state):
            inv = factor_rest(state)
            return inv, left_of(proj, inv)

        own, other, (inv, left) = gather_rows(raw, (own, other), (first, rest))
        return left, *normal(count, place, inv, own, other), beside

    high, low, proj = start(momentum, grad, basis)
    one, last_swap = sum_cols(proj)
    left_a, right_a, gram, _ = left_side(one, last_swap(one), None, None)

    image = push(high, low, right_a)
    gram, last_swap = sum_cols(gram)
    image, gram = lax.optimization_barrier((image, gram))
    gram, state = factor_right(gram, last_swap(gram))
    one, last_swap = sum_cols(image)
    one, state = lax.optimization_barrier((one, state))
    two = last_swap(one)
    inv = factor_rest(state)

    base = deflate([momentum, grad], left_a, right_a, "deflate")
    left_b, right_b, gram, base = left_side(one, two, (left_a, right_a, gram, inv), base)

    gram, last_swap = sum_cols(gram)
    momentum_out, lefts = deflate(base, left_b, right_b, "finish", (left_a, row_scale))
    gram, momentum_out = lax.optimization_barrier((gram, momentum_out))
    turned = turn(right_b)
    return momentum_out, lefts, last_factor(gram, last_swap(gram), *turned, col_scale)


def solution(mesh):
    in_specs = (P("row", "col"), P("row", "col"), P("col", None))
    out_specs = (P("row", "col"), P(None, "row", None), P("col", None))
    return jax.shard_map(shards, mesh=mesh, in_specs=in_specs, out_specs=out_specs, check_vma=False)
```

time: 133 us -> 125 us (0.940)
  starting transfers between devices: 41.5 us -> 34.6 us
  local copies, waits for them, and re-layouts: 4.7 us -> 0.11 us
  Pallas kernels: 33.9 us -> 37.9 us
    ppermute x36 -> x22, starting transfers between devices: 41.5 us -> 34.6 us  [swap(): return lax.ppermute(x, ('row', 'col'), pairs)]
    unnamed x18 -> x12, local copies, waits for them, and re-layouts: 4.61 us -> 0.05 us
    pallas_call x12 -> x17, Pallas kernels: 26.7 us -> 28.9 us  [call(): pl.pallas_call(body, out_shape=out, in_specs=[SMEM if x.dtype == jnp.int3...]
    pallas_call x2 -> x3, Pallas kernels: 7.11 us -> 9.02 us  [the longest x2 5.81 us: deflate(): pl.pallas_call(body, grid=(4,), in_specs=in_specs, out_specs=out_specs, o...]
    ppermute x36 -> x22, waiting for transfers between devices: 50.2 us -> 50 us  [swap(): return lax.ppermute(x, ('row', 'col'), pairs)]
  transfers between devices with their start and end apart: 36 -> 22, of which waited for: 27 -> 18; matrix products, arithmetic and copies ran while one was open for 1% -> 0% of each run, Pallas kernels for 15% -> 18%
where the time goes in v3:
time: 125 us
  waiting for transfers between devices  50 us (40%)
  Pallas kernels  37.9 us (30%)
  starting transfers between devices  34.6 us (28%)
    ppermute x22, waiting for transfers between devices, swap(): return lax.ppermute(x, ('row', 'col'), pairs)  50 us
    ppermute x22, starting transfers between devices, swap(): return lax.ppermute(x, ('row', 'col'), pairs)  34.6 us
    pallas_call x17, Pallas kernels, call(): pl.pallas_call(body, out_shape=out, in_specs=[SMEM if x.dtype == jnp.int3...  28.9 us
    pallas_call x2, Pallas kernels, deflate(): pl.pallas_call(body, grid=(4,), in_specs=in_specs, out_specs=out_specs, o...  5.81 us
    pallas_call x1, Pallas kernels, start(): pl.pallas_call(body, in_specs=[pl.BlockSpec(memory_space=pltpu.HBM)] * 3,...  3.21 us
  transfers between devices with their start and end apart: 22, of which 18 were waited for; matrix products, arithmetic and copies ran while one was open for 0% of the time, Pallas kernels for 18%

profile of v3, /device:TPU:0, one launch (start us, length us, event | category | flops | bytes accessed | tf_op | source)
XLA Modules:
  0.0 124.8 jit_solution(1190241948079326697)
XLA Ops:
  0.6 3.2 %start.1 = (bf16[512,1664]{1,0:T(8,128)(2,1)S(1)}, bf16[512,1664]{1,0:T(8,128)(2,1)S(1)}, f32[512,128]{1,0:T(8,128)S(1)}) custom-call(f32[512,1664]{1,0:T(8,128)} %refs_0_.1, bf16[512,1664]{1,0:T(8,128)(2,1)} %refs_1_.1, f32[1664,128]{1,0:T(8,128)} %basis_hbm.1), custom_call_target="tpu_custom_call" | custom-call | tf_op jit(solution)/shard_map/start/pallas_call | solution.py:126
  3.8 3.0 %collective-permute-start = (f32[512,128]{1,0:T(8,128)S(1)}, f32[512,128]{1,0:T(8,128)S(1)}, u32[]{:S(2)}, u32[]{:S(2)}) collective-permute-start(f32[512,128]{1,0:T(8,128)S(1)} %get-tuple-element.50), channel_id=1, source_target_pairs={{0,1},{1,0},{2,3},{3,2},{4,6},{5,7},{6,4},{7,5},{8,9},{9,8},{10,11... | collective-permute-start | bytes 786440 | tf_op jit(solution)/shard_map/ppermute | solution.py:40
  6.8 4.4 %collective-permute-done = f32[512,128]{1,0:T(8,128)S(1)} collective-permute-done((f32[512,128]{1,0:T(8,128)S(1)}, f32[512,128]{1,0:T(8,128)S(1)}, u32[]{:S(2)}, u32[]{:S(2)}) %collective-permute-start) | collective-permute-done | bytes 262176 | tf_op jit(solution)/shard_map/ppermute | solution.py:40
  11.9 2.0 %collective-permute-start.1 = (f32[512,128]{1,0:T(8,128)}, f32[512,128]{1,0:T(8,128)}, u32[]{:S(2)}, u32[]{:S(2)}) collective-permute-start(f32[512,128]{1,0:T(8,128)} %add.42.one_ref), channel_id=1, source_target_pairs={{0,2},{1,3},{2,0},{3,1},{4,5},{5,4},{6,7},{7,6},{8,10},{9,11},{10,... | collective-permute-start | bytes 786440 | tf_op jit(solution)/shard_map/ppermute | solution.py:40
  14.0 4.7 %collective-permute-done.1.two_ref = f32[512,128]{1,0:T(8,128)} collective-permute-done((f32[512,128]{1,0:T(8,128)}, f32[512,128]{1,0:T(8,128)}, u32[]{:S(2)}, u32[]{:S(2)}) %collective-permute-start.1) | collective-permute-done | bytes 262176 | tf_op jit(solution)/shard_map/ppermute | solution.py:40
  18.7 2.0 %pull_send.2 = (f32[512,128]{1,0:T(8,128)S(1)}, f32[64,512]{1,0:T(8,128)S(1)}, f32[64,1792]{1,0:T(8,128)S(1)}) custom-call(s32[1]{0:T(128)} %bitcast.place_ref, f32[512,128]{1,0:T(8,128)} %add.42.one_ref, f32[512,128]{1,0:T(8,128)} %collective-permute-done.1.two_ref, bf16[512,1664]{1,0:T(8,128)(2,1)S(1)} %get-tuple-element.48.high_ref, ...), custom_call_target="tpu_custom_call" | custom-call | flops 500000000 | bytes 5000000 | tf_op jit(solution)/shard_map/pull_send/pallas_call | solution.py:80
  22.7 2.1 %collective-permute-start.3 = (f32[32,1920]{1,0:T(8,128)S(1)}, f32[32,1920]{1,0:T(8,128)S(1)}, u32[]{:S(2)}, u32[]{:S(2)}) collective-permute-start(f32[32,1920]{1,0:T(8,128)S(1)} %pad_maximum_fusion.2), channel_id=1, source_target_pairs={{0,8},{1,9},{2,10},{3,11},{4,20},{5,21},{6,22},{7,23},{8,0},{9,1},... | collective-permute-start | bytes 737288 | tf_op jit(solution)/shard_map/ppermute | solution.py:40
  24.8 6.4 %collective-permute-done.3 = f32[32,1920]{1,0:T(8,128)S(1)} collective-permute-done((f32[32,1920]{1,0:T(8,128)S(1)}, f32[32,1920]{1,0:T(8,128)S(1)}, u32[]{:S(2)}, u32[]{:S(2)}) %collective-permute-start.3) | collective-permute-done | bytes 245792 | tf_op jit(solution)/shard_map/ppermute | solution.py:40
  31.3 2.6 %collective-permute-start.4 = (f32[16,2176]{1,0:T(8,128)S(1)}, f32[16,2176]{1,0:T(8,128)S(1)}, u32[]{:S(2)}, u32[]{:S(2)}) collective-permute-start(f32[16,2176]{1,0:T(8,128)S(1)} %constant_dynamic-update-slice_fusion), channel_id=1, source_target_pairs={{0,16},{1,17},{2,18},{3,19},{4,12},{5,13},{6,14},{7,15},{8,24},{9,... | collective-permute-start | bytes 417800 | tf_op jit(solution)/shard_map/ppermute | solution.py:40
  33.9 3.6 %collective-permute-done.4 = f32[16,2176]{1,0:T(8,128)S(1)} collective-permute-done((f32[16,2176]{1,0:T(8,128)S(1)}, f32[16,2176]{1,0:T(8,128)S(1)}, u32[]{:S(2)}, u32[]{:S(2)}) %collective-permute-start.4) | collective-permute-done | bytes 139296 | tf_op jit(solution)/shard_map/ppermute | solution.py:40
  37.6 2.5 %collective-permute-start.5 = (f32[16,1664]{1,0:T(8,128)S(1)}, f32[16,1664]{1,0:T(8,128)S(1)}, u32[]{:S(2)}, u32[]{:S(2)}) collective-permute-start(f32[16,1664]{1,0:T(8,128)S(1)} %slice_add_fusion.3.rest_0_), channel_id=1, source_target_pairs={{0,16},{1,17},{2,18},{3,19},{4,12},{5,13},{6,14},{7,15},{8,24},{9,... | collective-permute-start | bytes 319496 | tf_op jit(solution)/shard_map/ppermute | solution.py:40
  40.1 2.3 %factor_first.3.in_ref = f32[128,128]{1,0:T(8,128)S(1)} custom-call(s32[1]{0:T(128)} %bitcast.place_ref, f32[64,128]{1,0:T(8,128)S(1)} %maximum_add_fusion.own_ref, f32[64,128]{1,0:T(8,128)S(1)} %collective-permute-done.6.other_ref), custom_call_target="tpu_custom_call" | custom-call | flops 1500000000 | bytes 131072 | tf_op jit(solution)/shard_map/factor_first/pallas_call | solution.py:80
  43.4 3.3 %collective-permute-start.7 = (f32[32,1664]{1,0:T(8,128)S(1)}, f32[32,1664]{1,0:T(8,128)S(1)}, u32[]{:S(2)}, u32[]{:S(2)}) collective-permute-start(f32[32,1664]{1,0:T(8,128)S(1)} %pad_maximum_fusion.4), channel_id=1, source_target_pairs={{0,8},{1,9},{2,10},{3,11},{4,20},{5,21},{6,22},{7,23},{8,0},{9,1},... | collective-permute-start | bytes 638984 | tf_op jit(solution)/shard_map/ppermute | solution.py:40
  46.6 2.1 %factor_rest.3.inv_ref = f32[128,128]{1,0:T(8,128)S(1)} custom-call(f32[128,128]{1,0:T(8,128)S(1)} %factor_first.3.in_ref), custom_call_target="tpu_custom_call" | custom-call | flops 1500000000 | bytes 131072 | tf_op jit(solution)/shard_map/factor_rest/pallas_call | solution.py:80
  49.1 2.6 %collective-permute-done.7.rest_2_ = f32[32,1664]{1,0:T(8,128)S(1)} collective-permute-done((f32[32,1664]{1,0:T(8,128)S(1)}, f32[32,1664]{1,0:T(8,128)S(1)}, u32[]{:S(2)}, u32[]{:S(2)}) %collective-permute-start.7) | collective-permute-done | bytes 213024 | tf_op jit(solution)/shard_map/ppermute | solution.py:40
  62.0 2.7 %collective-permute-done.11.two_ref = f32[128,128]{1,0:T(8,128)S(1)} collective-permute-done((f32[128,128]{1,0:T(8,128)S(1)}, f32[128,128]{1,0:T(8,128)S(1)}, u32[]{:S(2)}, u32[]{:S(2)}) %collective-permute-start.11) | collective-permute-done | bytes 65568 | tf_op jit(solution)/shard_map/ppermute | solution.py:40
  64.7 2.1 %factor_first.4 = (f32[128,128]{1,0:T(8,128)S(1)}, f32[128,128]{1,0:T(8,128)S(1)}) custom-call(f32[128,128]{1,0:T(8,128)S(1)} %add.48.one_ref, f32[128,128]{1,0:T(8,128)S(1)} %collective-permute-done.11.two_ref), custom_call_target="tpu_custom_call" | custom-call | flops 1500000000 | bytes 131072 | tf_op jit(solution)/shard_map/factor_first/pallas_call | solution.py:80
  68.5 2.1 %factor_rest.4.rest_3_ = f32[128,128]{1,0:T(8,128)S(1)} custom-call(f32[128,128]{1,0:T(8,128)S(1)} %get-tuple-element.68.in_ref), custom_call_target="tpu_custom_call" | custom-call | flops 1500000000 | bytes 131072 | tf_op jit(solution)/shard_map/factor_rest/pallas_call | solution.py:80
  70.6 2.7 %collective-permute-done.12.two_ref = f32[512,128]{1,0:T(8,128)S(1)} collective-permute-done((f32[512,128]{1,0:T(8,128)S(1)}, f32[512,128]{1,0:T(8,128)S(1)}, u32[]{:S(2)}, u32[]{:S(2)}) %collective-permute-start.12) | collective-permute-done | bytes 262176 | tf_op jit(solution)/shard_map/ppermute | solution.py:40
  73.4 2.1 %pull_send.3 = (f32[512,128]{1,0:T(8,128)S(1)}, f32[64,512]{1,0:T(8,128)S(1)}, f32[64,1792]{1,0:T(8,128)S(1)}) custom-call(s32[1]{0:T(128)} %bitcast.place_ref, f32[512,128]{1,0:T(8,128)S(1)} %add.49.one_ref, f32[512,128]{1,0:T(8,128)S(1)} %collective-permute-done.12.two_ref, bf16[512,1664]{1,0:T(8,128)(2,1)S(1)} %get-tuple-element.48.high_ref, ...), custom_call_target="tpu_custom_call" | custom-call | flops 500000000 | bytes 5000000 | tf_op jit(solution)/shard_map/pull_send/pallas_call | solution.py:80
  79.4 2.2 %deflate.1.refs_0_ = f32[512,1664]{1,0:T(8,128)S(1)} custom-call(f32[512,1664]{1,0:T(8,128)S(1)} %copy-done, bf16[512,1664]{1,0:T(8,128)(2,1)S(1)} %copy-done.1, f32[512,128]{1,0:T(8,128)S(1)} %left.2.rest_0_.refs_2_.refs_3_, f32[128,1664]{1,0:T(8,128)S(1)} %get-tuple-element.60.right_ref.rest_1_.refs_3_), custom_call_target="tpu_custom_call" | custom-call | flops 1500000000 | bytes 12000000 | tf_op jit(solution)/shard_map/deflate/pallas_call | solution.py:305
  81.6 4.8 %collective-permute-done.14 = f32[32,1920]{1,0:T(8,128)S(1)} collective-permute-done((f32[32,1920]{1,0:T(8,128)S(1)}, f32[32,1920]{1,0:T(8,128)S(1)}, u32[]{:S(2)}, u32[]{:S(2)}) %collective-permute-start.14) | collective-permute-done | bytes 245792 | tf_op jit(solution)/shard_map/ppermute | solution.py:40
  86.5 2.5 %collective-permute-start.15 = (f32[16,2176]{1,0:T(8,128)S(1)}, f32[16,2176]{1,0:T(8,128)S(1)}, u32[]{:S(2)}, u32[]{:S(2)}) collective-permute-start(f32[16,2176]{1,0:T(8,128)S(1)} %constant_dynamic-update-slice_fusion.4), channel_id=1, source_target_pairs={{0,16},{1,17},{2,18},{3,19},{4,12},{5,13},{6,14},{7,15},{8,24},{9,... | collective-permute-start | bytes 417800 | tf_op jit(solution)/shard_map/ppermute | solution.py:40
  89.0 3.6 %collective-permute-done.15 = f32[16,2176]{1,0:T(8,128)S(1)} collective-permute-done((f32[16,2176]{1,0:T(8,128)S(1)}, f32[16,2176]{1,0:T(8,128)S(1)}, u32[]{:S(2)}, u32[]{:S(2)}) %collective-permute-start.15) | collective-permute-done | bytes 139296 | tf_op jit(solution)/shard_map/ppermute | solution.py:40
  92.7 2.5 %collective-permute-start.16 = (f32[16,1664]{1,0:T(8,128)S(1)}, f32[16,1664]{1,0:T(8,128)S(1)}, u32[]{:S(2)}, u32[]{:S(2)}) collective-permute-start(f32[16,1664]{1,0:T(8,128)S(1)} %slice_add_fusion.2.rest_0_), channel_id=1, source_target_pairs={{0,16},{1,17},{2,18},{3,19},{4,12},{5,13},{6,14},{7,15},{8,24},{9,... | collective-permute-start | bytes 319496 | tf_op jit(solution)/shard_map/ppermute | solution.py:40
  95.2 2.1 %factor_first.5.in_ref = f32[128,128]{1,0:T(8,128)S(1)} custom-call(s32[1]{0:T(128)} %bitcast.place_ref, f32[64,128]{1,0:T(8,128)S(1)} %maximum_add_fusion.1.own_ref, f32[64,128]{1,0:T(8,128)S(1)} %collective-permute-done.17.other_ref), custom_call_target="tpu_custom_call" | custom-call | flops 1500000000 | bytes 131072 | tf_op jit(solution)/shard_map/factor_first/pallas_call | solution.py:80
  98.4 3.3 %collective-permute-start.18 = (f32[32,1664]{1,0:T(8,128)S(1)}, f32[32,1664]{1,0:T(8,128)S(1)}, u32[]{:S(2)}, u32[]{:S(2)}) collective-permute-start(f32[32,1664]{1,0:T(8,128)S(1)} %pad_maximum_fusion.5), channel_id=1, source_target_pairs={{0,8},{1,9},{2,10},{3,11},{4,20},{5,21},{6,22},{7,23},{8,0},{9,1},... | collective-permute-start | bytes 638984 | tf_op jit(solution)/shard_map/ppermute | solution.py:40
  101.7 2.1 %factor_rest.5.inv_ref = f32[128,128]{1,0:T(8,128)S(1)} custom-call(f32[128,128]{1,0:T(8,128)S(1)} %factor_first.5.in_ref), custom_call_target="tpu_custom_call" | custom-call | flops 1500000000 | bytes 131072 | tf_op jit(solution)/shard_map/factor_rest/pallas_call | solution.py:80
  104.2 3.2 %collective-permute-done.18.rest_2_ = f32[32,1664]{1,0:T(8,128)S(1)} collective-permute-done((f32[32,1664]{1,0:T(8,128)S(1)}, f32[32,1664]{1,0:T(8,128)S(1)}, u32[]{:S(2)}, u32[]{:S(2)}) %collective-permute-start.18) | collective-permute-done | bytes 213024 | tf_op jit(solution)/shard_map/ppermute | solution.py:40
  111.2 3.6 %finish.1 = (f32[512,1664]{1,0:T(8,128)}, f32[2,512,128]{2,1,0:T(8,128)}) custom-call(f32[512,1664]{1,0:T(8,128)S(1)} %deflate.1.refs_0_, f32[512,128]{1,0:T(8,128)S(1)} %left.3.refs_1_, f32[128,1664]{1,0:T(8,128)S(1)} %get-tuple-element.86.refs_2_.right_ref, f32[512,128]{1,0:T(8,128)S(1)} %left.2.rest_0_.refs_2_.refs_3_), custom_call_target="tpu_custom_call" | custom-call | flops 1500000000 | bytes 12000000 | tf_op jit(solution)/shard_map/finish/pallas_call | solution.py:305
  116.8 2.4 %collective-permute-done.21.two_ref = f32[128,128]{1,0:T(8,128)S(1)} collective-permute-done((f32[128,128]{1,0:T(8,128)S(1)}, f32[128,128]{1,0:T(8,128)S(1)}, u32[]{:S(2)}, u32[]{:S(2)}) %collective-permute-start.21) | collective-permute-done | bytes 65568 | tf_op jit(solution)/shard_map/ppermute | solution.py:40
  119.2 5.6 %last_factor.1 = f32[1664,128]{1,0:T(8,128)} custom-call(f32[128,128]{1,0:T(8,128)S(1)} %add.55.one_ref, f32[128,128]{1,0:T(8,128)S(1)} %collective-permute-done.21.two_ref, bf16[1664,128]{1,0:T(8,128)(2,1)S(1)} %get-tuple-element.91.high_ref, bf16[1664,128]{1,0:T(8,128)(2,1)S(1)} %get-tuple-element.92.low_ref), custom_call_target="tpu_custom_call" | custom-call | flops 3000000000 | bytes 2000000 | tf_op jit(solution)/shard_map/last_factor/pallas_call | solution.py:80
  (74 shorter events, 27.3 us)
Async XLA Ops:
  3.8 7.4 %collective-permute-start = (f32[512,128]{1,0:T(8,128)S(1)}, f32[512,128]{1,0:T(8,128)S(1)}, u32[]{:S(2)}, u32[]{:S(2)}) collective-permute-start(f32[512,128]{1,0:T(8,128)S(1)} %get-tuple-element.50), channel_id=1, source_target_pairs={{0,1},{1,0},{2,3},{3,2},{4,6},{5,7},{6,4},{7,5},{8,9},{9,8},{10,11... | collective-permute-start | bytes 786440 | tf_op jit(solution)/shard_map/ppermute | solution.py:40
  11.9 6.7 %collective-permute-start.1 = (f32[512,128]{1,0:T(8,128)}, f32[512,128]{1,0:T(8,128)}, u32[]{:S(2)}, u32[]{:S(2)}) collective-permute-start(f32[512,128]{1,0:T(8,128)} %add.42.one_ref), channel_id=1, source_target_pairs={{0,2},{1,3},{2,0},{3,1},{4,5},{5,4},{6,7},{7,6},{8,10},{9,11},{10,... | collective-permute-start | bytes 786440 | tf_op jit(solution)/shard_map/ppermute | solution.py:40
  20.7 1.9 %collective-permute-start.2 = (f32[64,1792]{1,0:T(8,128)S(1)}, f32[64,1792]{1,0:T(8,128)S(1)}, u32[]{:S(2)}, u32[]{:S(2)}) collective-permute-start(f32[64,1792]{1,0:T(8,128)S(1)} %get-tuple-element.53), channel_id=1, source_target_pairs={{0,4},{1,5},{2,6},{3,7},{4,0},{5,1},{6,2},{7,3},{8,12},{9,13},{10,... | collective-permute-start | bytes 1376264 | tf_op jit(solution)/shard_map/ppermute | solution.py:40
  22.7 8.6 %collective-permute-start.3 = (f32[32,1920]{1,0:T(8,128)S(1)}, f32[32,1920]{1,0:T(8,128)S(1)}, u32[]{:S(2)}, u32[]{:S(2)}) collective-permute-start(f32[32,1920]{1,0:T(8,128)S(1)} %pad_maximum_fusion.2), channel_id=1, source_target_pairs={{0,8},{1,9},{2,10},{3,11},{4,20},{5,21},{6,22},{7,23},{8,0},{9,1},... | collective-permute-start | bytes 737288 | tf_op jit(solution)/shard_map/ppermute | solution.py:40
  31.3 6.1 %collective-permute-start.4 = (f32[16,2176]{1,0:T(8,128)S(1)}, f32[16,2176]{1,0:T(8,128)S(1)}, u32[]{:S(2)}, u32[]{:S(2)}) collective-permute-start(f32[16,2176]{1,0:T(8,128)S(1)} %constant_dynamic-update-slice_fusion), channel_id=1, source_target_pairs={{0,16},{1,17},{2,18},{3,19},{4,12},{5,13},{6,14},{7,15},{8,24},{9,... | collective-permute-start | bytes 417800 | tf_op jit(solution)/shard_map/ppermute | solution.py:40
  37.5 2.6 %collective-permute-start.6 = (f32[64,128]{1,0:T(8,128)S(1)}, f32[64,128]{1,0:T(8,128)S(1)}, u32[]{:S(2)}, u32[]{:S(2)}) collective-permute-start(f32[64,128]{1,0:T(8,128)S(1)} %maximum_add_fusion.own_ref), channel_id=1, source_target_pairs={{0,4},{1,5},{2,6},{3,7},{4,0},{5,1},{6,2},{7,3},{8,12},{9,13},{10,... | collective-permute-start | bytes 98312 | tf_op jit(solution)/shard_map/ppermute | solution.py:40
  37.6 5.7 %collective-permute-start.5 = (f32[16,1664]{1,0:T(8,128)S(1)}, f32[16,1664]{1,0:T(8,128)S(1)}, u32[]{:S(2)}, u32[]{:S(2)}) collective-permute-start(f32[16,1664]{1,0:T(8,128)S(1)} %slice_add_fusion.3.rest_0_), channel_id=1, source_target_pairs={{0,16},{1,17},{2,18},{3,19},{4,12},{5,13},{6,14},{7,15},{8,24},{9,... | collective-permute-start | bytes 319496 | tf_op jit(solution)/shard_map/ppermute | solution.py:40
  43.4 8.3 %collective-permute-start.7 = (f32[32,1664]{1,0:T(8,128)S(1)}, f32[32,1664]{1,0:T(8,128)S(1)}, u32[]{:S(2)}, u32[]{:S(2)}) collective-permute-start(f32[32,1664]{1,0:T(8,128)S(1)} %pad_maximum_fusion.4), channel_id=1, source_target_pairs={{0,8},{1,9},{2,10},{3,11},{4,20},{5,21},{6,22},{7,23},{8,0},{9,1},... | collective-permute-start | bytes 638984 | tf_op jit(solution)/shard_map/ppermute | solution.py:40
  51.8 1.8 %collective-permute-start.8 = (f32[64,1664]{1,0:T(8,128)S(1)}, f32[64,1664]{1,0:T(8,128)S(1)}, u32[]{:S(2)}, u32[]{:S(2)}) collective-permute-start(f32[64,1664]{1,0:T(8,128)S(1)} %pad_maximum_fusion), channel_id=1, source_target_pairs={{0,4},{1,5},{2,6},{3,7},{4,0},{5,1},{6,2},{7,3},{8,12},{9,13},{10,... | collective-permute-start | bytes 1277960 | tf_op jit(solution)/shard_map/ppermute | solution.py:40
  54.7 4.3 %collective-permute-start.9 = (f32[128,128]{1,0:T(8,128)S(1)}, f32[128,128]{1,0:T(8,128)S(1)}, u32[]{:S(2)}, u32[]{:S(2)}) collective-permute-start(f32[128,128]{1,0:T(8,128)S(1)} %get-tuple-element.61), channel_id=1, source_target_pairs={{0,1},{1,0},{2,3},{3,2},{4,6},{5,7},{6,4},{7,5},{8,9},{9,8},{10,11... | collective-permute-start | bytes 196616 | tf_op jit(solution)/shard_map/ppermute | solution.py:40
  59.0 7.9 %collective-permute-start.10 = (f32[512,128]{1,0:T(8,128)S(1)}, f32[512,128]{1,0:T(8,128)S(1)}, u32[]{:S(2)}, u32[]{:S(2)}) collective-permute-start(f32[512,128]{1,0:T(8,128)S(1)} %push.1), channel_id=1, source_target_pairs={{0,1},{1,0},{2,3},{3,2},{4,6},{5,7},{6,4},{7,5},{8,9},{9,8},{10,11... | collective-permute-start | bytes 786440 | tf_op jit(solution)/shard_map/ppermute | solution.py:40
  60.5 4.3 %collective-permute-start.11 = (f32[128,128]{1,0:T(8,128)S(1)}, f32[128,128]{1,0:T(8,128)S(1)}, u32[]{:S(2)}, u32[]{:S(2)}) collective-permute-start(f32[128,128]{1,0:T(8,128)S(1)} %add.48.one_ref), channel_id=1, source_target_pairs={{0,2},{1,3},{2,0},{3,1},{4,5},{5,4},{6,7},{7,6},{8,10},{9,11},{10,... | collective-permute-start | bytes 196616 | tf_op jit(solution)/shard_map/ppermute | solution.py:40
  66.9 6.4 %collective-permute-start.12 = (f32[512,128]{1,0:T(8,128)S(1)}, f32[512,128]{1,0:T(8,128)S(1)}, u32[]{:S(2)}, u32[]{:S(2)}) collective-permute-start(f32[512,128]{1,0:T(8,128)S(1)} %add.49.one_ref), channel_id=1, source_target_pairs={{0,2},{1,3},{2,0},{3,1},{4,5},{5,4},{6,7},{7,6},{8,10},{9,11},{10,... | collective-permute-start | bytes 786440 | tf_op jit(solution)/shard_map/ppermute | solution.py:40
  75.5 1.9 %collective-permute-start.13 = (f32[64,1792]{1,0:T(8,128)S(1)}, f32[64,1792]{1,0:T(8,128)S(1)}, u32[]{:S(2)}, u32[]{:S(2)}) collective-permute-start(f32[64,1792]{1,0:T(8,128)S(1)} %get-tuple-element.71), channel_id=1, source_target_pairs={{0,4},{1,5},{2,6},{3,7},{4,0},{5,1},{6,2},{7,3},{8,12},{9,13},{10,... | collective-permute-start | bytes 1376264 | tf_op jit(solution)/shard_map/ppermute | solution.py:40
  75.6 3.8 %copy-start = (f32[512,1664]{1,0:T(8,128)S(1)}, f32[512,1664]{1,0:T(8,128)}, u32[]{:S(2)}) copy-start(f32[512,1664]{1,0:T(8,128)} %refs_0_.1) | copy-start | bytes 10223620
  75.6 3.8 %copy-start.1 = (bf16[512,1664]{1,0:T(8,128)(2,1)S(1)}, bf16[512,1664]{1,0:T(8,128)(2,1)}, u32[]{:S(2)}) copy-start(bf16[512,1664]{1,0:T(8,128)(2,1)} %refs_1_.1) | copy-start | bytes 5111812
  77.5 8.9 %collective-permute-start.14 = (f32[32,1920]{1,0:T(8,128)S(1)}, f32[32,1920]{1,0:T(8,128)S(1)}, u32[]{:S(2)}, u32[]{:S(2)}) collective-permute-start(f32[32,1920]{1,0:T(8,128)S(1)} %pad_maximum_fusion.3), channel_id=1, source_target_pairs={{0,8},{1,9},{2,10},{3,11},{4,20},{5,21},{6,22},{7,23},{8,0},{9,1},... | collective-permute-start | bytes 737288 | tf_op jit(solution)/shard_map/ppermute | solution.py:40
  86.5 6.1 %collective-permute-start.15 = (f32[16,2176]{1,0:T(8,128)S(1)}, f32[16,2176]{1,0:T(8,128)S(1)}, u32[]{:S(2)}, u32[]{:S(2)}) collective-permute-start(f32[16,2176]{1,0:T(8,128)S(1)} %constant_dynamic-update-slice_fusion.4), channel_id=1, source_target_pairs={{0,16},{1,17},{2,18},{3,19},{4,12},{5,13},{6,14},{7,15},{8,24},{9,... | collective-permute-start | bytes 417800 | tf_op jit(solution)/shard_map/ppermute | solution.py:40
  92.6 2.6 %collective-permute-start.17 = (f32[64,128]{1,0:T(8,128)S(1)}, f32[64,128]{1,0:T(8,128)S(1)}, u32[]{:S(2)}, u32[]{:S(2)}) collective-permute-start(f32[64,128]{1,0:T(8,128)S(1)} %maximum_add_fusion.1.own_ref), channel_id=1, source_target_pairs={{0,4},{1,5},{2,6},{3,7},{4,0},{5,1},{6,2},{7,3},{8,12},{9,13},{10,... | collective-permute-start | bytes 98312 | tf_op jit(solution)/shard_map/ppermute | solution.py:40
  92.7 5.7 %collective-permute-start.16 = (f32[16,1664]{1,0:T(8,128)S(1)}, f32[16,1664]{1,0:T(8,128)S(1)}, u32[]{:S(2)}, u32[]{:S(2)}) collective-permute-start(f32[16,1664]{1,0:T(8,128)S(1)} %slice_add_fusion.2.rest_0_), channel_id=1, source_target_pairs={{0,16},{1,17},{2,18},{3,19},{4,12},{5,13},{6,14},{7,15},{8,24},{9,... | collective-permute-start | bytes 319496 | tf_op jit(solution)/shard_map/ppermute | solution.py:40
  98.4 9.0 %collective-permute-start.18 = (f32[32,1664]{1,0:T(8,128)S(1)}, f32[32,1664]{1,0:T(8,128)S(1)}, u32[]{:S(2)}, u32[]{:S(2)}) collective-permute-start(f32[32,1664]{1,0:T(8,128)S(1)} %pad_maximum_fusion.5), channel_id=1, source_target_pairs={{0,8},{1,9},{2,10},{3,11},{4,20},{5,21},{6,22},{7,23},{8,0},{9,1},... | collective-permute-start | bytes 638984 | tf_op jit(solution)/shard_map/ppermute | solution.py:40
  107.4 1.8 %collective-permute-start.19 = (f32[64,1664]{1,0:T(8,128)S(1)}, f32[64,1664]{1,0:T(8,128)S(1)}, u32[]{:S(2)}, u32[]{:S(2)}) collective-permute-start(f32[64,1664]{1,0:T(8,128)S(1)} %pad_maximum_fusion.1), channel_id=1, source_target_pairs={{0,4},{1,5},{2,6},{3,7},{4,0},{5,1},{6,2},{7,3},{8,12},{9,13},{10,... | collective-permute-start | bytes 1277960 | tf_op jit(solution)/shard_map/ppermute | solution.py:40
  110.4 4.5 %collective-permute-start.20 = (f32[128,128]{1,0:T(8,128)S(1)}, f32[128,128]{1,0:T(8,128)S(1)}, u32[]{:S(2)}, u32[]{:S(2)}) collective-permute-start(f32[128,128]{1,0:T(8,128)S(1)} %get-tuple-element.83), channel_id=1, source_target_pairs={{0,1},{1,0},{2,3},{3,2},{4,6},{5,7},{6,4},{7,5},{8,9},{9,8},{10,11... | collective-permute-start | bytes 196616 | tf_op jit(solution)/shard_map/ppermute | solution.py:40
  114.9 4.3 %collective-permute-start.21 = (f32[128,128]{1,0:T(8,128)S(1)}, f32[128,128]{1,0:T(8,128)S(1)}, u32[]{:S(2)}, u32[]{:S(2)}) collective-permute-start(f32[128,128]{1,0:T(8,128)S(1)} %add.55.one_ref), channel_id=1, source_target_pairs={{0,2},{1,3},{2,0},{3,1},{4,5},{5,4},{6,7},{7,6},{8,10},{9,11},{10,... | collective-permute-start | bytes 196616 | tf_op jit(solution)/shard_map/ppermute | solution.py:40

commit v4 on v3

v4 whole, which is shorter than its diff:
```python
import jax
import jax.numpy as jnp
from jax import lax
from jax.experimental import pallas as pl
from jax.experimental.pallas import tpu as pltpu
from jax.sharding import PartitionSpec as P

F32 = jnp.float32
BF16 = jnp.bfloat16
HIGHEST = lax.Precision.HIGHEST
VMEM = pl.BlockSpec(memory_space=pltpu.VMEM)
SMEM = pl.BlockSpec(memory_space=pltpu.SMEM)
NN = (((1,), (0,)), ((), ()))
NT = (((1,), (1,)), ((), ()))
TN = (((0,), (0,)), ((), ()))
KEEP = 0.95
PANEL = 16
FACTOR = 1_500_000_000


def masks_of(axis):
    size = lax.axis_size(axis)
    masks = []
    mask = 1
    while mask < size:
        masks.append(mask)
        mask *= 2
    assert mask == size
    return masks


def swap(x, axis, even, odd):
    row_count, col_count = lax.axis_size("row"), lax.axis_size("col")
    pairs = []
    for row in range(row_count):
        mask = odd if row % 2 else even
        for col in range(col_count):
            to = (row ^ mask) * col_count + col if axis == "row" else row * col_count + (col ^ mask)
            pairs.append((row * col_count + col, to))
    return lax.ppermute(x, ("row", "col"), pairs)


def chunk_at(place, slot, other=False):
    return place ^ (2 * slot + (1 if other else 0))


def split(x):
    high = x.astype(BF16)
    return high, (x - high.astype(F32)).astype(BF16)


def dot(a, b, dims=NN):
    return lax.dot_general(a, b, dims, preferred_element_type=F32)


def exact(a, b, dims=NN):
    return lax.dot_general(a, b, dims, precision=HIGHEST, preferred_element_type=F32)


def tiles(width, most=256):
    return [(start, min(most, width - start)) for start in range(0, width, most)]


def struct(*shape, dtype=F32):
    return jax.ShapeDtypeStruct(shape, dtype)


def call(body, name, out, ins, scratch=(), flops=0, nbytes=0, **kw):
    return pl.pallas_call(
        body,
        out_shape=out,
        in_specs=[SMEM if x.dtype == jnp.int32 else VMEM for x in ins],
        out_specs=jax.tree.map(lambda _: VMEM, out),
        scratch_shapes=list(scratch),
        name=name,
        compiler_params=pltpu.CompilerParams(vmem_limit_bytes=24 * 2**20),
        cost_estimate=pl.CostEstimate(flops=flops, bytes_accessed=nbytes, transcendentals=0),
        **kw,
    )(*ins)


def start(momentum, grad, basis):
    rows, cols = momentum.shape
    rank = basis.shape[1]
    steps = 4
    block = rows // steps

    def body(momentum_hbm, grad_hbm, basis_hbm, high_ref, low_ref, proj_ref, momentum_ref, grad_ref, basis_ref, both_ref, sems):
        whole = pltpu.make_async_copy(basis_hbm, basis_ref, sems.at[0])
        whole.start()
        copies = []
        for i in range(steps):
            at = pl.ds(i * block, block)
            pair = (
                pltpu.make_async_copy(momentum_hbm.at[at], momentum_ref.at[at], sems.at[1 + 2 * i]),
                pltpu.make_async_copy(grad_hbm.at[at], grad_ref.at[at], sems.at[2 + 2 * i]),
            )
            for copy in pair:
                copy.start()
            copies.append(pair)
        whole.wait()
        high, low = split(basis_ref[...])
        both_ref[:, :rank] = high
        both_ref[:, rank:] = low
        for i in range(steps):
            for copy in copies[i]:
                copy.wait()
            at = pl.ds(i * block, block)
            high, low = split(momentum_ref[at, :] + grad_ref[at, :].astype(F32))
            high_ref[at, :] = high
            low_ref[at, :] = low
            wide = dot(high, both_ref[...])
            proj_ref[at, :] = wide[:, :rank] + wide[:, rank:] + dot(low, both_ref[:, :rank])

    return pl.pallas_call(
        body,
        in_specs=[pl.BlockSpec(memory_space=pltpu.HBM)] * 3,
        out_specs=[VMEM] * 3,
        out_shape=[struct(rows, cols, dtype=BF16)] * 2 + [struct(rows, rank)],
        scratch_shapes=[
            pltpu.VMEM((rows, cols), F32),
            pltpu.VMEM((rows, cols), BF16),
            pltpu.VMEM((cols, rank), F32),
            pltpu.VMEM((cols, 2 * rank), BF16),
            pltpu.SemaphoreType.DMA((1 + 2 * steps,)),
        ],
        name="start",
        compiler_params=pltpu.CompilerParams(vmem_limit_bytes=24 * 2**20),
    )(*(pltpu.with_memory_space_constraint(x, pltpu.HBM) for x in (momentum, grad, basis)))


def pull_rows(turned, proj, high_ref, low_ref, cross, right_ref, out_ref):
    half = turned.shape[0]
    width = high_ref.shape[1]
    high, low = split(turned)
    both = jnp.concatenate([high, low], axis=0)
    for at, size in tiles(width):
        wide = dot(both, high_ref[:, at:at + size])
        out = wide[:half] + wide[half:] + dot(high, low_ref[:, at:at + size])
        if cross is not None:
            right_high, right_low = split(right_ref[:, at:at + size])
            wide = dot(jnp.concatenate(cross, axis=0), right_high)
            out = out + (wide[:half] + wide[half:] + dot(cross[0], right_low))
        out_ref[:, at:at + size] = out
    return gram_rows(high, low, both, proj)


def gram_rows(high, low, both, proj):
    half, rank = high.shape[0], proj.shape[1]
    proj_high, proj_low = split(proj)
    wide = dot(both, jnp.concatenate([proj_high, proj_low], axis=1))
    return wide[:half, :rank] + wide[:half, rank:] + wide[half:, :rank]


def put_gram(place, gram, out_ref, width, chunk):
    for t in range(gram.shape[0] // chunk):
        at = pl.multiple_of((place // 2 ^ t) * chunk, chunk)
        out_ref[pl.ds(at, chunk), width:] = gram[t * chunk:(t + 1) * chunk]


def pull_send(count, place, one, two, high, low, before=None):
    rows, width = high.shape
    rank = before[0].shape[1] if before is not None else one.shape[1]
    chunk = rank // count

    def body(place_ref, one_ref, two_ref, high_ref, low_ref, *rest):
        place = place_ref[0]
        proj = one_ref[:rows, :] + two_ref[...]
        left_ref = right_ref = None
        if before is not None:
            left_ref, right_ref, gram_ref, inv_ref = rest[:4]
            proj = proj - KEEP * exact(left_ref[...], gram_ref[...])
            proj = exact(proj, inv_ref[...], NT)
        proj_ref, keep_ref, send_ref, turned_ref = rest[-4:]
        proj_ref[...] = proj
        turned_ref[...] = proj.T

        def pick(other):
            at = [chunk_at(place, t, other) * chunk for t in range(count // 2)]
            return jnp.concatenate([turned_ref[pl.ds(pl.multiple_of(x, chunk), chunk), :] for x in at], axis=0)

        keep_ref[...] = pick(False)
        turned = pick(True)
        cross = None if before is None else split(-KEEP * exact(turned, left_ref[...]))
        gram = pull_rows(turned, proj, high_ref, low_ref, cross, right_ref, send_ref)
        put_gram(place, gram, send_ref, width, chunk)

    out = [struct(rows, rank), struct(rank // 2, rows), struct(rank // 2, width + rank)]
    ins = [place, one, two, high, low] + list(before or [])
    return call(body, "pull_send", out, ins, [pltpu.VMEM((rank, rows), F32)], flops=500_000_000, nbytes=5_000_000)


def pull_keep(count, place, turned, proj, high, low, before=None):
    rows, width = high.shape
    rank = proj.shape[1]
    chunk = rank // count

    def body(place_ref, turned_ref, proj_ref, high_ref, low_ref, *rest):
        place = place_ref[0]
        turned = turned_ref[...]
        cross = right_ref = None
        if before is not None:
            left_ref, right_ref = rest[:2]
            cross = split(-KEEP * exact(turned, left_ref[...]))
        gram = pull_rows(turned, proj_ref[...], high_ref, low_ref, cross, right_ref, rest[-1])
        put_gram(place, gram, rest[-1], width, chunk)

    ins = [place, turned, proj, high, low] + list(before or [])[:2]
    return call(body, "pull_keep", struct(rank // 2, width + rank), ins, flops=500_000_000, nbytes=5_000_000)


def normal(count, place, inv, own, other, high=None, low=None):
    rank = inv.shape[0]
    width = own[0].shape[1]
    chunk = rank // count
    push = high is not None
    rows = high.shape[0] if push else 0

    def body(place_ref, inv_ref, *rest):
        pieces, rest = rest[:count], rest[count:]
        if push:
            work_high, work_low, right_ref, out_ref, raw_ref = rest
        else:
            right_ref, out_ref, raw_ref = rest
        place = place_ref[0]
        for i, piece in enumerate(pieces):
            at = chunk_at(place, i % (count // 2), i >= count // 2) * chunk
            raw_ref[pl.ds(pl.multiple_of(at, chunk), chunk), :] = piece[...]
        inv_high, inv_low = split(inv_ref[...])
        inv_both = jnp.concatenate([inv_high, inv_low], axis=0)
        gram = jnp.zeros((rank, rank), F32)
        image = jnp.zeros((rows, rank), F32) if push else None
        for at, size in tiles(width):
            raw_high, raw_low = split(raw_ref[:, at:at + size])
            wide = dot(inv_both, raw_high)
            right = wide[:rank] + wide[rank:] + dot(inv_high, raw_low)
            right_ref[:, at:at + size] = right
            high, low = split(right)
            both = jnp.concatenate([high, low], axis=0)
            wide = dot(both, high, NT)
            gram = gram + (wide[:rank] + wide[rank:] + dot(high, low, NT))
            if push:
                wide = dot(work_high[:, at:at + size], both, NT)
                image = image + (wide[:, :rank] + wide[:, rank:] + dot(work_low[:, at:at + size], high, NT))
        if push:
            out_ref[:rows, :] = image
        out_ref[rows:, :] = gram

    ins = [place, inv, *own, *other] + ([high, low] if push else [])
    return call(body, "normal", [struct(rank, width), struct(rows + rank, rank)], ins,
                [pltpu.VMEM((rank, width), F32)], flops=1_000_000_000, nbytes=5_000_000)


def left_of(proj, inv):
    def body(proj_ref, inv_ref, out_ref):
        out_ref[...] = exact(proj_ref[...], inv_ref[...], NT)

    return call(body, "left", struct(*proj.shape), [proj, inv], flops=100_000_000, nbytes=600_000)


def outer_tile(left, right_high, right_low):
    high, low = split(left)
    rows = left.shape[0]
    wide = dot(jnp.concatenate([high, low], axis=0), right_high)
    return wide[:rows] + wide[rows:] + dot(high, right_low)


def deflate(momentum, grad, left, right):
    rows, cols = momentum.shape
    block = rows // 4

    def body(momentum_ref, grad_ref, left_ref, right_ref, out_ref):
        for at, size in tiles(cols):
            lanes = slice(at, at + size)
            right_high, right_low = split(KEEP * right_ref[:, lanes])
            for i in range(4):
                row = slice(i * block, (i + 1) * block)
                work = momentum_ref[row, lanes] + grad_ref[row, lanes].astype(F32)
                out_ref[row, lanes] = work - outer_tile(left_ref[row, :], right_high, right_low)

    return call(body, "deflate", struct(rows, cols), [momentum, grad, left, right], flops=1_500_000_000, nbytes=9_000_000)


def finish(base, left, right, before=None, scale=None, part=0):
    rows, cols = base.shape
    rank = left.shape[1]
    half = rows // 2
    block = half // 2
    first = part * half

    def body(base_ref, left_ref, right_ref, *rest):
        if part == 0:
            other_ref, out_ref, lefts_ref, stage_ref, high_ref, low_ref, sems = rest
            lefts_ref[0] = scale * other_ref[...]
            lefts_ref[1] = scale * left_ref[...]
        else:
            _, out_ref, stage_ref, high_ref, low_ref, sems = rest
        for at, size in tiles(cols):
            lanes = slice(at, at + size)
            high_ref[:, lanes], low_ref[:, lanes] = split(KEEP * right_ref[:, lanes])
        copies = []
        for i in range(2):
            row = slice(first + i * block, first + (i + 1) * block)
            for at, size in tiles(cols):
                lanes = slice(at, at + size)
                outer = outer_tile(left_ref[row, :], high_ref[:, lanes], low_ref[:, lanes])
                stage_ref[i, :, lanes] = base_ref[row, lanes] - outer
            copy = pltpu.make_async_copy(stage_ref.at[i], out_ref.at[pl.ds(first + i * block, block)], sems.at[i])
            copy.start()
            copies.append(copy)
        for copy in copies:
            copy.wait()

    hbm = pl.BlockSpec(memory_space=pltpu.HBM)
    out, out_specs = [struct(rows, cols)], [hbm]
    if part == 0:
        ins, in_specs, alias = [base, left, right, before], [VMEM] * 4, {}
        out.append(struct(2, rows, rank))
        out_specs.append(VMEM)
    else:
        ins, in_specs, alias = [base, left, right, before], [VMEM] * 3 + [hbm], {3: 0}
    return pl.pallas_call(
        body,
        in_specs=in_specs,
        out_specs=out_specs,
        out_shape=out,
        scratch_shapes=[pltpu.VMEM((2, block, cols), F32)] + [pltpu.VMEM((rank, cols), BF16)] * 2
        + [pltpu.SemaphoreType.DMA((2,))],
        input_output_aliases=alias,
        name="finish",
        compiler_params=pltpu.CompilerParams(vmem_limit_bytes=24 * 2**20),
        cost_estimate=pl.CostEstimate(flops=800_000_000, bytes_accessed=6_000_000, transcendentals=0),
    )(*ins)


def eliminate(full, first):
    rank = full.shape[1]
    groups = PANEL // 8
    sub = lax.broadcasted_iota(jnp.int32, (8, rank), 0)
    lane = lax.broadcasted_iota(jnp.int32, (8, rank), 1)
    rolled = pltpu.roll(full, lax.rem(rank - first, rank), 1)
    rows = [full[8 * g:8 * g + 8] for g in range(groups)]
    cols = [
        [jnp.broadcast_to(rolled[8 * g:8 * g + 8, j:j + 1], (8, rank)) for g in range(groups)] for j in range(PANEL)
    ]

    def spread(x, j):
        return jnp.broadcast_to(x[j // 8][j % 8:j % 8 + 1], (8, rank))

    pivot = spread(cols[0], 0)
    for j in range(PANEL):
        at = j // 8
        root = lax.rsqrt(pivot)
        if j + 1 < PANEL:
            above = spread(cols[j + 1], j) * root
            pivot = spread(cols[j + 1], j + 1) - above * above
        below = sub > j % 8
        here = lane == first + j
        row = jnp.where(here, 1.0, spread(rows, j)) * root
        for g in range(at, groups):
            mult = cols[j][g] * root
            rest = jnp.where(here, 0.0, rows[g])
            if g == at:
                mult = jnp.where(below, mult, 0.0)
                rest = jnp.where(below, rest, rows[g])
            rest = rest - mult * row
            rows[g] = jnp.where(sub == j % 8, row, rest) if g == at else rest
            cols[j][g] = mult
        for k in range(j + 1, PANEL):
            across = spread(cols[k], j) * root
            for g in range(at, groups):
                cols[k][g] = cols[k][g] - cols[j][g] * across
    return jnp.concatenate(rows, axis=0)


def thirds(x):
    high = x.astype(BF16)
    rest = x - high.astype(F32)
    middle = rest.astype(BF16)
    return high, middle, (rest - middle.astype(F32)).astype(BF16)


def factor_panels(state_ref):
    rank = state_ref.shape[0]
    row = lax.broadcasted_iota(jnp.int32, (rank, rank), 0)
    col = lax.broadcasted_iota(jnp.int32, (rank, rank), 1)
    sub = lax.broadcasted_iota(jnp.int32, (PANEL, rank), 0)
    lane = lax.broadcasted_iota(jnp.int32, (PANEL, rank), 1)

    def panel(p, carry):
        first = pl.multiple_of(p * PANEL, PANEL)
        done = eliminate(state_ref[pl.ds(first, PANEL), :], first)
        lower = jnp.where((lane > first + sub) & (lane < first + PANEL), 0.0, done)
        a, b, c = thirds(done)
        d, e, f = thirds(lower)
        step = dot(
            jnp.concatenate([a, a, b, b, a, c], axis=0), jnp.concatenate([d, e, d, e, f, d], axis=0), TN
        )
        old = state_ref[...]
        fresh = jnp.where((col >= first) & (col < first + PANEL), 0.0, old) - step
        state_ref[...] = jnp.where(row >= first + PANEL, fresh, old)
        state_ref[pl.ds(first, PANEL), :] = done
        return carry

    lax.fori_loop(0, rank // PANEL, panel, 0)


def factor_left(count, place, own, other):
    chunk, rank = own.shape[0], 2 * own.shape[1] // count

    def body(place_ref, own_ref, other_ref, out_ref):
        core = place_ref[0] % 2
        for t in range(count // 2):
            for ref, at in ((own_ref, 2 * t + core), (other_ref, 2 * t + 1 - core)):
                out_ref[pl.ds(pl.multiple_of(at * chunk, chunk), chunk), :] = ref[:, t * rank:(t + 1) * rank]
        factor_panels(out_ref)
        out_ref[...] = lower_part(out_ref[...])

    return call(body, "factor", struct(rank, rank), [place, own, other], flops=2 * FACTOR, nbytes=131072)


def factor_right(one, two, first):
    rank = one.shape[1]

    def body(one_ref, two_ref, gram_ref, out_ref):
        gram = one_ref[first:, :] + two_ref[...]
        gram_ref[...] = gram
        out_ref[...] = gram
        factor_panels(out_ref)
        out_ref[...] = lower_part(out_ref[...])

    return call(body, "factor", [struct(rank, rank)] * 2, [one, two], flops=2 * FACTOR, nbytes=131072)


def lower_part(x):
    row = lax.broadcasted_iota(jnp.int32, x.shape, 0)
    col = lax.broadcasted_iota(jnp.int32, x.shape, 1)
    return jnp.where(row >= col, x, 0.0)


def turn(right):
    rank, width = right.shape

    def body(right_ref, high_ref, low_ref):
        high, low = split(right_ref[...].T)
        high_ref[...] = high
        low_ref[...] = low

    return call(body, "turn", [struct(width, rank, dtype=BF16)] * 2, [right], flops=100_000_000, nbytes=2_000_000)


def last_factor(one, two, high, low, scale):
    def body(one_ref, two_ref, high_ref, low_ref, out_ref, state_ref):
        rank = state_ref.shape[0]
        state_ref[...] = one_ref[...] + two_ref[...]
        factor_panels(state_ref)
        inv_high, inv_low = split(scale * lower_part(state_ref[...]))
        both = jnp.concatenate([inv_high, inv_low], axis=0)
        wide = dot(high_ref[...], both, NT)
        out_ref[...] = wide[:, :rank] + wide[:, rank:] + dot(low_ref[...], inv_high, NT)

    width, rank = high.shape
    return call(body, "last_factor", struct(width, rank), [one, two, high, low], [pltpu.VMEM((rank, rank), F32)],
                flops=2 * FACTOR, nbytes=2_000_000)


def sum_cols(x):
    masks = masks_of("col")
    for even, odd in zip(masks[:-1], masks[:0:-1]):
        x = x + swap(x, "col", even, odd)
    return x, lambda y: swap(y, "col", masks[-1], masks[0])


def sum_rows(keep, send, count, rank, beside=None):
    x = keep + swap(send, "row", 1, 1)
    width = x.shape[1] - rank
    chunk = rank // count
    parts = [x[i * chunk:(i + 1) * chunk] for i in range(count // 2)]
    gram = jnp.concatenate([part[:, width:] for part in parts], axis=1)
    own = jnp.concatenate([parts[0][:, :width], gram], axis=1)
    gots = []
    for i in reversed(range(1, count // 2)):
        gots.append(swap(jnp.concatenate([parts[i][:, :width], gram], axis=1), "row", 2 * i, 2 * i))
    if beside is not None:
        gots[0], beside = lax.optimization_barrier((gots[0], beside))
    for got in gots:
        own = own + got
    own, gram = lax.optimization_barrier((own[:, :width], own[:, width:]))
    return own, gram, swap(gram, "row", 1, 1), beside


def gather_rows(x, count, meanwhile):
    own = [x] + [swap(x, "row", 2 * i, 2 * i) for i in range(1, count // 2)]
    done = meanwhile()
    other = [swap(x, "row", 1, 1)]
    for piece in own[1:]:
        piece, done = lax.optimization_barrier((piece, done))
        other.append(swap(piece, "row", 1, 1))
    return own, other, done


def shards(momentum, grad, basis):
    count = lax.axis_size("row")
    rank = basis.shape[1]
    rows, width = momentum.shape
    row_scale = float(rows * count) ** 0.5
    col_scale = float(width * lax.axis_size("col")) ** 0.5
    place = lax.axis_index("row").astype(jnp.int32).reshape(1)

    def left_side(one, two, before, beside=None):
        proj, turned, send = pull_send(count, place, one, two, high, low, before)
        keep = pull_keep(count, place, turned, proj, high, low, before)
        raw, own, other, beside = sum_rows(keep, send, count, rank, beside)
        first, second, inv = gather_rows(raw, count, lambda: factor_left(count, place, own, other))
        return left_of(proj, inv), inv, (first, second), beside

    high, low, proj = start(momentum, grad, basis)
    one, last_swap = sum_cols(proj)
    left_a, inv, pieces, _ = left_side(one, last_swap(one), None)
    right_a, image = normal(count, place, inv, *pieces, high, low)

    one, last_swap = sum_cols(image)
    gram, inv = factor_right(one, last_swap(one[rows:]), rows)
    two = last_swap(one[:rows])

    base = deflate(momentum, grad, left_a, right_a)
    left_b, inv, pieces, base = left_side(one, two, (left_a, right_a, gram, inv), base)
    right_b, gram = normal(count, place, inv, *pieces)

    gram, last_swap = sum_cols(gram)
    momentum_out, lefts = finish(base, left_b, right_b, left_a, row_scale)
    gram, momentum_out = lax.optimization_barrier((gram, momentum_out))
    momentum_out, = finish(base, left_b, right_b, momentum_out, part=1)
    turned = turn(right_b)
    return momentum_out, lefts, last_factor(gram, last_swap(gram), *turned, col_scale)


def solution(mesh):
    in_specs = (P("row", "col"), P("row", "col"), P("col", None))
    out_specs = (P("row", "col"), P(None, "row", None), P("col", None))
    return jax.shard_map(shards, mesh=mesh, in_specs=in_specs, out_specs=out_specs, check_vma=False)
```

time: 125 us -> 121 us (0.968)
  starting transfers between devices: 34.6 us -> 31.4 us
  waiting for transfers between devices: 50 us -> 48.6 us
    ppermute x22 -> x31, starting transfers between devices: 34.6 us -> 31.4 us  [swap(): return lax.ppermute(x, ('row', 'col'), pairs)]
    pallas_call x17 -> x14, Pallas kernels: 28.9 us -> 30.7 us  [call(): pl.pallas_call(body, out_shape=out, in_specs=[SMEM if x.dtype == jnp.int3...]
    pallas_call x2, Pallas kernels: 5.81 us -> 4.38 us  [finish(): pl.pallas_call(body, in_specs=in_specs, out_specs=out_specs, out_shape=ou...]
    ppermute x22 -> x31, waiting for transfers between devices: 50 us -> 48.6 us  [swap(): return lax.ppermute(x, ('row', 'col'), pairs)]
  transfers between devices with their start and end apart: 22 -> 31, of which waited for: 18 -> 22; matrix products, arithmetic and copies ran while one was open for 0% -> 0% of each run, Pallas kernels for 18% -> 18%
where the time goes in v4:
time: 121 us; the launch traced here: 120 us
  waiting for transfers between devices  48.6 us (40%)
  Pallas kernels  38.3 us (32%)
  starting transfers between devices  31.4 us (26%)
    ppermute x31, waiting for transfers between devices, swap(): return lax.ppermute(x, ('row', 'col'), pairs)  48.6 us
    ppermute x31, starting transfers between devices, swap(): return lax.ppermute(x, ('row', 'col'), pairs)  31.4 us
    pallas_call x14, Pallas kernels, call(): pl.pallas_call(body, out_shape=out, in_specs=[SMEM if x.dtype == jnp.int3...  30.7 us
    pallas_call x2, Pallas kernels, finish(): pl.pallas_call(body, in_specs=in_specs, out_specs=out_specs, out_shape=ou...  4.38 us
    pallas_call x1, Pallas kernels, start(): pl.pallas_call(body, in_specs=[pl.BlockSpec(memory_space=pltpu.HBM)] * 3,...  3.21 us
  transfers between devices with their start and end apart: 31, of which 22 were waited for; matrix products, arithmetic and copies ran while one was open for 0% of the time, Pallas kernels for 18%

profile of v4, /device:TPU:0, one launch (start us, length us, event | category | flops | bytes accessed | tf_op | source)
XLA Modules:
  0.0 120.4 jit_solution(1836373390870142440)
XLA Ops:
  0.6 3.2 %start.1 = (bf16[512,1664]{1,0:T(8,128)(2,1)S(1)}, bf16[512,1664]{1,0:T(8,128)(2,1)S(1)}, f32[512,128]{1,0:T(8,128)S(1)}) custom-call(f32[512,1664]{1,0:T(8,128)} %momentum_ref.1, bf16[512,1664]{1,0:T(8,128)(2,1)} %grad_ref.1, f32[1664,128]{1,0:T(8,128)} %basis_hbm.1), custom_call_target="tpu_custom_call" | custom-call | tf_op jit(solution)/shard_map/start/pallas_call | solution.py:115
  3.8 3.0 %collective-permute-start = (f32[512,128]{1,0:T(8,128)S(1)}, f32[512,128]{1,0:T(8,128)S(1)}, u32[]{:S(2)}, u32[]{:S(2)}) collective-permute-start(f32[512,128]{1,0:T(8,128)S(1)} %get-tuple-element.42), channel_id=1, source_target_pairs={{0,1},{1,0},{2,3},{3,2},{4,6},{5,7},{6,4},{7,5},{8,9},{9,8},{10,11... | collective-permute-start | bytes 786440 | tf_op jit(solution)/shard_map/ppermute | solution.py:40
  6.8 4.4 %collective-permute-done = f32[512,128]{1,0:T(8,128)S(1)} collective-permute-done((f32[512,128]{1,0:T(8,128)S(1)}, f32[512,128]{1,0:T(8,128)S(1)}, u32[]{:S(2)}, u32[]{:S(2)}) %collective-permute-start) | collective-permute-done | bytes 262176 | tf_op jit(solution)/shard_map/ppermute | solution.py:40
  11.9 2.0 %collective-permute-start.1 = (f32[512,128]{1,0:T(8,128)}, f32[512,128]{1,0:T(8,128)}, u32[]{:S(2)}, u32[]{:S(2)}) collective-permute-start(f32[512,128]{1,0:T(8,128)} %add.33.one_ref), channel_id=1, source_target_pairs={{0,2},{1,3},{2,0},{3,1},{4,5},{5,4},{6,7},{7,6},{8,10},{9,11},{10,... | collective-permute-start | bytes 786440 | tf_op jit(solution)/shard_map/ppermute | solution.py:40
  14.0 4.7 %collective-permute-done.1.two_ref = f32[512,128]{1,0:T(8,128)} collective-permute-done((f32[512,128]{1,0:T(8,128)}, f32[512,128]{1,0:T(8,128)}, u32[]{:S(2)}, u32[]{:S(2)}) %collective-permute-start.1) | collective-permute-done | bytes 262176 | tf_op jit(solution)/shard_map/ppermute | solution.py:40
  18.7 1.9 %pull_send.2 = (f32[512,128]{1,0:T(8,128)S(1)}, f32[64,512]{1,0:T(8,128)S(1)}, f32[64,1792]{1,0:T(8,128)S(1)}) custom-call(s32[1]{0:T(128)} %bitcast.place_ref, f32[512,128]{1,0:T(8,128)} %add.33.one_ref, f32[512,128]{1,0:T(8,128)} %collective-permute-done.1.two_ref, bf16[512,1664]{1,0:T(8,128)(2,1)S(1)} %get-tuple-element.43.high_ref.rest_8_, ...), custom_call_target="tpu_custom_call" | custom-call | flops 500000000 | bytes 5000000 | tf_op jit(solution)/shard_map/pull_send/pallas_call | solution.py:69
  22.6 2.1 %collective-permute-start.5 = (f32[16,2176]{1,0:T(8,128)S(1)}, f32[16,2176]{1,0:T(8,128)S(1)}, u32[]{:S(2)}, u32[]{:S(2)}) collective-permute-start(f32[16,2176]{1,0:T(8,128)S(1)} %get-tuple-element.114), channel_id=1, source_target_pairs={{0,8},{1,9},{2,10},{3,11},{4,12},{5,13},{6,14},{7,15},{8,0},{9,1},... | collective-permute-start | bytes 417800 | tf_op jit(solution)/shard_map/ppermute | solution.py:40
  24.7 2.6 %collective-permute-start.4 = (f32[16,2176]{1,0:T(8,128)S(1)}, f32[16,2176]{1,0:T(8,128)S(1)}, u32[]{:S(2)}, u32[]{:S(2)}) collective-permute-start(f32[16,2176]{1,0:T(8,128)S(1)} %get-tuple-element.113), channel_id=1, source_target_pairs={{0,16},{1,17},{2,18},{3,19},{4,20},{5,21},{6,22},{7,23},{8,24},{9,... | collective-permute-start | bytes 417800 | tf_op jit(solution)/shard_map/ppermute | solution.py:40
  27.3 3.5 %collective-permute-done.5 = f32[16,2176]{1,0:T(8,128)S(1)} collective-permute-done((f32[16,2176]{1,0:T(8,128)S(1)}, f32[16,2176]{1,0:T(8,128)S(1)}, u32[]{:S(2)}, u32[]{:S(2)}) %collective-permute-start.5) | collective-permute-done | bytes 139296 | tf_op jit(solution)/shard_map/ppermute | solution.py:40
  30.8 7.3 %collective-permute-done.4 = f32[16,2176]{1,0:T(8,128)S(1)} collective-permute-done((f32[16,2176]{1,0:T(8,128)S(1)}, f32[16,2176]{1,0:T(8,128)S(1)}, u32[]{:S(2)}, u32[]{:S(2)}) %collective-permute-start.4) | collective-permute-done | bytes 139296 | tf_op jit(solution)/shard_map/ppermute | solution.py:40
  38.3 2.5 %collective-permute-start.6 = (f32[16,1664]{1,0:T(8,128)S(1)}, f32[16,1664]{1,0:T(8,128)S(1)}, u32[]{:S(2)}, u32[]{:S(2)}) collective-permute-start(f32[16,1664]{1,0:T(8,128)S(1)} %slice.122.rest_0_), channel_id=1, source_target_pairs={{0,24},{1,25},{2,26},{3,27},{4,28},{5,29},{6,30},{7,31},{8,16},{9,... | collective-permute-start | bytes 319496 | tf_op jit(solution)/shard_map/ppermute | solution.py:40
  42.7 4.4 %factor.3.inv_ref = f32[128,128]{1,0:T(8,128)S(1)} custom-call(s32[1]{0:T(128)} %bitcast.place_ref, f32[16,512]{1,0:T(8,128)S(1)} %slice.123.own_ref, f32[16,512]{1,0:T(8,128)S(1)} %collective-permute-done.9.other_ref), custom_call_target="tpu_custom_call" | custom-call | flops 3000000000 | bytes 131072 | tf_op jit(solution)/shard_map/factor/pallas_call | solution.py:69
  48.3 4.1 %collective-permute-done.7.rest_2_ = f32[16,1664]{1,0:T(8,128)S(1)} collective-permute-done((f32[16,1664]{1,0:T(8,128)S(1)}, f32[16,1664]{1,0:T(8,128)S(1)}, u32[]{:S(2)}, u32[]{:S(2)}) %collective-permute-start.7) | collective-permute-done | bytes 106528 | tf_op jit(solution)/shard_map/ppermute | solution.py:40
  54.1 3.0 %normal.2 = (f32[128,1664]{1,0:T(8,128)S(1)}, f32[640,128]{1,0:T(8,128)S(1)}) custom-call(s32[1]{0:T(128)} %bitcast.place_ref, f32[128,128]{1,0:T(8,128)S(1)} %factor.3.inv_ref, f32[16,1664]{1,0:T(8,128)S(1)} %slice.122.rest_0_, f32[16,1664]{1,0:T(8,128)S(1)} %collective-permute-done.8.rest_1_, f32[16,1664]{1,0:T(8,128)S(1)} %collective-permute-done.7.rest_2_, ...), custom_call_target="tpu_custom_call" | custom-call | flops 1000000000 | bytes 5000000 | tf_op jit(solution)/shard_map/normal/pallas_call | solution.py:69
  57.1 1.6 %collective-permute-start.14 = (f32[640,128]{1,0:T(8,128)S(1)}, f32[640,128]{1,0:T(8,128)S(1)}, u32[]{:S(2)}, u32[]{:S(2)}) collective-permute-start(f32[640,128]{1,0:T(8,128)S(1)} %get-tuple-element.56), channel_id=1, source_target_pairs={{0,1},{1,0},{2,3},{3,2},{4,6},{5,7},{6,4},{7,5},{8,9},{9,8},{10,11... | collective-permute-start | bytes 983048 | tf_op jit(solution)/shard_map/ppermute | solution.py:40
  58.7 5.6 %collective-permute-done.14 = f32[640,128]{1,0:T(8,128)S(1)} collective-permute-done((f32[640,128]{1,0:T(8,128)S(1)}, f32[640,128]{1,0:T(8,128)S(1)}, u32[]{:S(2)}, u32[]{:S(2)}) %collective-permute-start.14) | collective-permute-done | bytes 327712 | tf_op jit(solution)/shard_map/ppermute | solution.py:40
  64.3 1.6 %collective-permute-start.16 = (f32[128,128]{1,0:T(8,128)S(1)}, f32[128,128]{1,0:T(8,128)S(1)}, u32[]{:S(2)}, u32[]{:S(2)}) collective-permute-start(f32[128,128]{1,0:T(8,128)S(1)} %slice.125), channel_id=1, source_target_pairs={{0,2},{1,3},{2,0},{3,1},{4,5},{5,4},{6,7},{7,6},{8,10},{9,11},{10,... | collective-permute-start | bytes 196616 | tf_op jit(solution)/shard_map/ppermute | solution.py:40
  66.9 1.8 %collective-permute-done.16.two_ref = f32[128,128]{1,0:T(8,128)S(1)} collective-permute-done((f32[128,128]{1,0:T(8,128)S(1)}, f32[128,128]{1,0:T(8,128)S(1)}, u32[]{:S(2)}, u32[]{:S(2)}) %collective-permute-start.16) | collective-permute-done | bytes 65568 | tf_op jit(solution)/shard_map/ppermute | solution.py:40
  68.7 4.2 %factor.4 = (f32[128,128]{1,0:T(8,128)S(1)}, f32[128,128]{1,0:T(8,128)S(1)}) custom-call(f32[640,128]{1,0:T(8,128)S(1)} %add.38.one_ref, f32[128,128]{1,0:T(8,128)S(1)} %collective-permute-done.16.two_ref), custom_call_target="tpu_custom_call" | custom-call | flops 3000000000 | bytes 131072 | tf_op jit(solution)/shard_map/factor/pallas_call | solution.py:69
  72.9 2.1 %pull_send.3 = (f32[512,128]{1,0:T(8,128)S(1)}, f32[64,512]{1,0:T(8,128)S(1)}, f32[64,1792]{1,0:T(8,128)S(1)}) custom-call(s32[1]{0:T(128)} %bitcast.place_ref, f32[640,128]{1,0:T(8,128)S(1)} %add.38.one_ref, f32[512,128]{1,0:T(8,128)S(1)} %collective-permute-done.15.two_ref, bf16[512,1664]{1,0:T(8,128)(2,1)S(1)} %get-tuple-element.43.high_ref.rest_8_, ...), custom_call_target="tpu_custom_call" | custom-call | flops 500000000 | bytes 5000000 | tf_op jit(solution)/shard_map/pull_send/pallas_call | solution.py:69
  77.0 2.5 %collective-permute-start.18 = (f32[16,2176]{1,0:T(8,128)S(1)}, f32[16,2176]{1,0:T(8,128)S(1)}, u32[]{:S(2)}, u32[]{:S(2)}) collective-permute-start(f32[16,2176]{1,0:T(8,128)S(1)} %get-tuple-element.97), channel_id=1, source_target_pairs={{0,24},{1,25},{2,26},{3,27},{4,28},{5,29},{6,30},{7,31},{8,16},{9,... | collective-permute-start | bytes 417800 | tf_op jit(solution)/shard_map/ppermute | solution.py:40
  79.5 1.9 %collective-permute-start.19 = (f32[16,2176]{1,0:T(8,128)S(1)}, f32[16,2176]{1,0:T(8,128)S(1)}, u32[]{:S(2)}, u32[]{:S(2)}) collective-permute-start(f32[16,2176]{1,0:T(8,128)S(1)} %get-tuple-element.87), channel_id=1, source_target_pairs={{0,16},{1,17},{2,18},{3,19},{4,20},{5,21},{6,22},{7,23},{8,24},{9,... | collective-permute-start | bytes 417800 | tf_op jit(solution)/shard_map/ppermute | solution.py:40
  83.0 2.5 %collective-permute-done.18 = f32[16,2176]{1,0:T(8,128)S(1)} collective-permute-done((f32[16,2176]{1,0:T(8,128)S(1)}, f32[16,2176]{1,0:T(8,128)S(1)}, u32[]{:S(2)}, u32[]{:S(2)}) %collective-permute-start.18) | collective-permute-done | bytes 139296 | tf_op jit(solution)/shard_map/ppermute | solution.py:40
  85.5 5.0 %collective-permute-done.20 = f32[16,2176]{1,0:T(8,128)S(1)} collective-permute-done((f32[16,2176]{1,0:T(8,128)S(1)}, f32[16,2176]{1,0:T(8,128)S(1)}, u32[]{:S(2)}, u32[]{:S(2)}) %collective-permute-start.20) | collective-permute-done | bytes 139296 | tf_op jit(solution)/shard_map/ppermute | solution.py:40
  92.9 2.5 %collective-permute-start.23 = (f32[16,1664]{1,0:T(8,128)S(1)}, f32[16,1664]{1,0:T(8,128)S(1)}, u32[]{:S(2)}, u32[]{:S(2)}) collective-permute-start(f32[16,1664]{1,0:T(8,128)S(1)} %slice.134.rest_0_), channel_id=1, source_target_pairs={{0,8},{1,9},{2,10},{3,11},{4,12},{5,13},{6,14},{7,15},{8,0},{9,1},... | collective-permute-start | bytes 319496 | tf_op jit(solution)/shard_map/ppermute | solution.py:40
  95.4 4.2 %factor.5.inv_ref = f32[128,128]{1,0:T(8,128)S(1)} custom-call(s32[1]{0:T(128)} %bitcast.place_ref, f32[16,512]{1,0:T(8,128)S(1)} %slice.135.own_ref, f32[16,512]{1,0:T(8,128)S(1)} %collective-permute-done.24.other_ref), custom_call_target="tpu_custom_call" | custom-call | flops 3000000000 | bytes 131072 | tf_op jit(solution)/shard_map/factor/pallas_call | solution.py:69
  100.6 2.4 %collective-permute-done.22.rest_2_ = f32[16,1664]{1,0:T(8,128)S(1)} collective-permute-done((f32[16,1664]{1,0:T(8,128)S(1)}, f32[16,1664]{1,0:T(8,128)S(1)}, u32[]{:S(2)}, u32[]{:S(2)}) %collective-permute-start.22) | collective-permute-done | bytes 106528 | tf_op jit(solution)/shard_map/ppermute | solution.py:40
  106.0 1.5 %collective-permute-start.29 = (f32[128,128]{1,0:T(8,128)S(1)}, f32[128,128]{1,0:T(8,128)S(1)}, u32[]{:S(2)}, u32[]{:S(2)}) collective-permute-start(f32[128,128]{1,0:T(8,128)S(1)} %get-tuple-element.74), channel_id=1, source_target_pairs={{0,1},{1,0},{2,3},{3,2},{4,6},{5,7},{6,4},{7,5},{8,9},{9,8},{10,11... | collective-permute-start | bytes 196616 | tf_op jit(solution)/shard_map/ppermute | solution.py:40
  107.8 2.6 %finish.2 = (f32[512,1664]{1,0:T(8,128)}, f32[2,512,128]{2,1,0:T(8,128)}) custom-call(f32[512,1664]{1,0:T(8,128)S(1)} %deflate.1.base_ref, f32[512,128]{1,0:T(8,128)S(1)} %left.3.left_ref, f32[128,1664]{1,0:T(8,128)S(1)} %get-tuple-element.73.right_ref, f32[512,128]{1,0:T(8,128)S(1)} %left.2.rest_0_.left_ref), custom_call_target="tpu_custom_call" | custom-call | flops 800000000 | bytes 6000000 | tf_op jit(solution)/shard_map/finish/pallas_call | solution.py:322
  110.5 1.6 %collective-permute-start.30 = (f32[128,128]{1,0:T(8,128)S(1)}, f32[128,128]{1,0:T(8,128)S(1)}, u32[]{:S(2)}, u32[]{:S(2)}) collective-permute-start(f32[128,128]{1,0:T(8,128)S(1)} %add.43.one_ref), channel_id=1, source_target_pairs={{0,2},{1,3},{2,0},{3,1},{4,5},{5,4},{6,7},{7,6},{8,10},{9,11},{10,... | collective-permute-start | bytes 196616 | tf_op jit(solution)/shard_map/ppermute | solution.py:40
  112.1 1.8 %finish.3 = f32[512,1664]{1,0:T(8,128)} custom-call(f32[512,1664]{1,0:T(8,128)S(1)} %deflate.1.base_ref, f32[512,128]{1,0:T(8,128)S(1)} %left.3.left_ref, f32[128,1664]{1,0:T(8,128)S(1)} %get-tuple-element.73.right_ref, f32[512,1664]{1,0:T(8,128)} %get-tuple-element.76.rest_0_), custom_call_target="tpu_custom_call", output_to_operand_aliasing={{}: (3, {})} | custom-call | flops 800000000 | bytes 6000000 | tf_op jit(solution)/shard_map/finish/pallas_call | solution.py:322
  114.8 5.6 %last_factor.1 = f32[1664,128]{1,0:T(8,128)} custom-call(f32[128,128]{1,0:T(8,128)S(1)} %add.43.one_ref, f32[128,128]{1,0:T(8,128)S(1)} %collective-permute-done.30.two_ref, bf16[1664,128]{1,0:T(8,128)(2,1)S(1)} %get-tuple-element.79.high_ref, bf16[1664,128]{1,0:T(8,128)(2,1)S(1)} %get-tuple-element.80.low_ref), custom_call_target="tpu_custom_call" | custom-call | flops 3000000000 | bytes 2000000 | tf_op jit(solution)/shard_map/last_factor/pallas_call | solution.py:69
  (78 shorter events, 19.7 us)
Async XLA Ops:
  3.8 7.4 %collective-permute-start = (f32[512,128]{1,0:T(8,128)S(1)}, f32[512,128]{1,0:T(8,128)S(1)}, u32[]{:S(2)}, u32[]{:S(2)}) collective-permute-start(f32[512,128]{1,0:T(8,128)S(1)} %get-tuple-element.42), channel_id=1, source_target_pairs={{0,1},{1,0},{2,3},{3,2},{4,6},{5,7},{6,4},{7,5},{8,9},{9,8},{10,11... | collective-permute-start | bytes 786440 | tf_op jit(solution)/shard_map/ppermute | solution.py:40
  11.9 6.7 %collective-permute-start.1 = (f32[512,128]{1,0:T(8,128)}, f32[512,128]{1,0:T(8,128)}, u32[]{:S(2)}, u32[]{:S(2)}) collective-permute-start(f32[512,128]{1,0:T(8,128)} %add.33.one_ref), channel_id=1, source_target_pairs={{0,2},{1,3},{2,0},{3,1},{4,5},{5,4},{6,7},{7,6},{8,10},{9,11},{10,... | collective-permute-start | bytes 786440 | tf_op jit(solution)/shard_map/ppermute | solution.py:40
  20.5 1.9 %collective-permute-start.2 = (f32[64,1792]{1,0:T(8,128)S(1)}, f32[64,1792]{1,0:T(8,128)S(1)}, u32[]{:S(2)}, u32[]{:S(2)}) collective-permute-start(f32[64,1792]{1,0:T(8,128)S(1)} %get-tuple-element.47), channel_id=1, source_target_pairs={{0,4},{1,5},{2,6},{3,7},{4,0},{5,1},{6,2},{7,3},{8,12},{9,13},{10,... | collective-permute-start | bytes 1376264 | tf_op jit(solution)/shard_map/ppermute | solution.py:40
  22.6 8.2 %collective-permute-start.5 = (f32[16,2176]{1,0:T(8,128)S(1)}, f32[16,2176]{1,0:T(8,128)S(1)}, u32[]{:S(2)}, u32[]{:S(2)}) collective-permute-start(f32[16,2176]{1,0:T(8,128)S(1)} %get-tuple-element.114), channel_id=1, source_target_pairs={{0,8},{1,9},{2,10},{3,11},{4,12},{5,13},{6,14},{7,15},{8,0},{9,1},... | collective-permute-start | bytes 417800 | tf_op jit(solution)/shard_map/ppermute | solution.py:40
  24.7 13.4 %collective-permute-start.4 = (f32[16,2176]{1,0:T(8,128)S(1)}, f32[16,2176]{1,0:T(8,128)S(1)}, u32[]{:S(2)}, u32[]{:S(2)}) collective-permute-start(f32[16,2176]{1,0:T(8,128)S(1)} %get-tuple-element.113), channel_id=1, source_target_pairs={{0,16},{1,17},{2,18},{3,19},{4,20},{5,21},{6,22},{7,23},{8,24},{9,... | collective-permute-start | bytes 417800 | tf_op jit(solution)/shard_map/ppermute | solution.py:40
  27.3 10.8 %collective-permute-start.3 = (f32[16,2176]{1,0:T(8,128)S(1)}, f32[16,2176]{1,0:T(8,128)S(1)}, u32[]{:S(2)}, u32[]{:S(2)}) collective-permute-start(f32[16,2176]{1,0:T(8,128)S(1)} %get-tuple-element.104), channel_id=1, source_target_pairs={{0,24},{1,25},{2,26},{3,27},{4,28},{5,29},{6,30},{7,31},{8,16},{9,... | collective-permute-start | bytes 417800 | tf_op jit(solution)/shard_map/ppermute | solution.py:40
  38.2 4.5 %collective-permute-start.9 = (f32[16,512]{1,0:T(8,128)S(1)}, f32[16,512]{1,0:T(8,128)S(1)}, u32[]{:S(2)}, u32[]{:S(2)}) collective-permute-start(f32[16,512]{1,0:T(8,128)S(1)} %slice.123.own_ref), channel_id=1, source_target_pairs={{0,4},{1,5},{2,6},{3,7},{4,0},{5,1},{6,2},{7,3},{8,12},{9,13},{10,... | collective-permute-start | bytes 98312 | tf_op jit(solution)/shard_map/ppermute | solution.py:40
  38.3 14.0 %collective-permute-start.6 = (f32[16,1664]{1,0:T(8,128)S(1)}, f32[16,1664]{1,0:T(8,128)S(1)}, u32[]{:S(2)}, u32[]{:S(2)}) collective-permute-start(f32[16,1664]{1,0:T(8,128)S(1)} %slice.122.rest_0_), channel_id=1, source_target_pairs={{0,24},{1,25},{2,26},{3,27},{4,28},{5,29},{6,30},{7,31},{8,16},{9,... | collective-permute-start | bytes 319496 | tf_op jit(solution)/shard_map/ppermute | solution.py:40
  40.8 11.5 %collective-permute-start.7 = (f32[16,1664]{1,0:T(8,128)S(1)}, f32[16,1664]{1,0:T(8,128)S(1)}, u32[]{:S(2)}, u32[]{:S(2)}) collective-permute-start(f32[16,1664]{1,0:T(8,128)S(1)} %slice.122.rest_0_), channel_id=1, source_target_pairs={{0,16},{1,17},{2,18},{3,19},{4,20},{5,21},{6,22},{7,23},{8,24},{9,... | collective-permute-start | bytes 319496 | tf_op jit(solution)/shard_map/ppermute | solution.py:40
  42.3 6.0 %collective-permute-start.8 = (f32[16,1664]{1,0:T(8,128)S(1)}, f32[16,1664]{1,0:T(8,128)S(1)}, u32[]{:S(2)}, u32[]{:S(2)}) collective-permute-start(f32[16,1664]{1,0:T(8,128)S(1)} %slice.122.rest_0_), channel_id=1, source_target_pairs={{0,8},{1,9},{2,10},{3,11},{4,12},{5,13},{6,14},{7,15},{8,0},{9,1},... | collective-permute-start | bytes 319496 | tf_op jit(solution)/shard_map/ppermute | solution.py:40
  42.7 10.2 %collective-permute-start.10 = (f32[16,1664]{1,0:T(8,128)S(1)}, f32[16,1664]{1,0:T(8,128)S(1)}, u32[]{:S(2)}, u32[]{:S(2)}) collective-permute-start(f32[16,1664]{1,0:T(8,128)S(1)} %slice.122.rest_0_), channel_id=1, source_target_pairs={{0,4},{1,5},{2,6},{3,7},{4,0},{5,1},{6,2},{7,3},{8,12},{9,13},{10,... | collective-permute-start | bytes 319496 | tf_op jit(solution)/shard_map/ppermute | solution.py:40
  52.3 1.3 %collective-permute-start.11 = (f32[16,1664]{1,0:T(8,128)S(1)}, f32[16,1664]{1,0:T(8,128)S(1)}, u32[]{:S(2)}, u32[]{:S(2)}) collective-permute-start(f32[16,1664]{1,0:T(8,128)S(1)} %collective-permute-done.8.rest_1_), channel_id=1, source_target_pairs={{0,4},{1,5},{2,6},{3,7},{4,0},{5,1},{6,2},{7,3},{8,12},{9,13},{10,... | collective-permute-start | bytes 319496 | tf_op jit(solution)/shard_map/ppermute | solution.py:40
  52.4 1.4 %collective-permute-start.12 = (f32[16,1664]{1,0:T(8,128)S(1)}, f32[16,1664]{1,0:T(8,128)S(1)}, u32[]{:S(2)}, u32[]{:S(2)}) collective-permute-start(f32[16,1664]{1,0:T(8,128)S(1)} %collective-permute-done.7.rest_2_), channel_id=1, source_target_pairs={{0,4},{1,5},{2,6},{3,7},{4,0},{5,1},{6,2},{7,3},{8,12},{9,13},{10,... | collective-permute-start | bytes 319496 | tf_op jit(solution)/shard_map/ppermute | solution.py:40
  52.8 1.3 %collective-permute-start.13 = (f32[16,1664]{1,0:T(8,128)S(1)}, f32[16,1664]{1,0:T(8,128)S(1)}, u32[]{:S(2)}, u32[]{:S(2)}) collective-permute-start(f32[16,1664]{1,0:T(8,128)S(1)} %collective-permute-done.6.rest_3_), channel_id=1, source_target_pairs={{0,4},{1,5},{2,6},{3,7},{4,0},{5,1},{6,2},{7,3},{8,12},{9,13},{10,... | collective-permute-start | bytes 319496 | tf_op jit(solution)/shard_map/ppermute | solution.py:40
  57.1 7.1 %collective-permute-start.14 = (f32[640,128]{1,0:T(8,128)S(1)}, f32[640,128]{1,0:T(8,128)S(1)}, u32[]{:S(2)}, u32[]{:S(2)}) collective-permute-start(f32[640,128]{1,0:T(8,128)S(1)} %get-tuple-element.56), channel_id=1, source_target_pairs={{0,1},{1,0},{2,3},{3,2},{4,6},{5,7},{6,4},{7,5},{8,9},{9,8},{10,11... | collective-permute-start | bytes 983048 | tf_op jit(solution)/shard_map/ppermute | solution.py:40
  64.3 4.3 %collective-permute-start.16 = (f32[128,128]{1,0:T(8,128)S(1)}, f32[128,128]{1,0:T(8,128)S(1)}, u32[]{:S(2)}, u32[]{:S(2)}) collective-permute-start(f32[128,128]{1,0:T(8,128)S(1)} %slice.125), channel_id=1, source_target_pairs={{0,2},{1,3},{2,0},{3,1},{4,5},{5,4},{6,7},{7,6},{8,10},{9,11},{10,... | collective-permute-start | bytes 196616 | tf_op jit(solution)/shard_map/ppermute | solution.py:40
  66.3 6.6 %collective-permute-start.15 = (f32[512,128]{1,0:T(8,128)S(1)}, f32[512,128]{1,0:T(8,128)S(1)}, u32[]{:S(2)}, u32[]{:S(2)}) collective-permute-start(f32[512,128]{1,0:T(8,128)S(1)} %slice.124), channel_id=1, source_target_pairs={{0,2},{1,3},{2,0},{3,1},{4,5},{5,4},{6,7},{7,6},{8,10},{9,11},{10,... | collective-permute-start | bytes 786440 | tf_op jit(solution)/shard_map/ppermute | solution.py:40
  75.0 1.9 %collective-permute-start.17 = (f32[64,1792]{1,0:T(8,128)S(1)}, f32[64,1792]{1,0:T(8,128)S(1)}, u32[]{:S(2)}, u32[]{:S(2)}) collective-permute-start(f32[64,1792]{1,0:T(8,128)S(1)} %get-tuple-element.62), channel_id=1, source_target_pairs={{0,4},{1,5},{2,6},{3,7},{4,0},{5,1},{6,2},{7,3},{8,12},{9,13},{10,... | collective-permute-start | bytes 1376264 | tf_op jit(solution)/shard_map/ppermute | solution.py:40
  75.0 6.4 %copy-start = (f32[512,1664]{1,0:T(8,128)S(1)}, f32[512,1664]{1,0:T(8,128)}, u32[]{:S(2)}) copy-start(f32[512,1664]{1,0:T(8,128)} %momentum_ref.1) | copy-start | bytes 10223620
  77.0 8.5 %collective-permute-start.18 = (f32[16,2176]{1,0:T(8,128)S(1)}, f32[16,2176]{1,0:T(8,128)S(1)}, u32[]{:S(2)}, u32[]{:S(2)}) collective-permute-start(f32[16,2176]{1,0:T(8,128)S(1)} %get-tuple-element.97), channel_id=1, source_target_pairs={{0,24},{1,25},{2,26},{3,27},{4,28},{5,29},{6,30},{7,31},{8,16},{9,... | collective-permute-start | bytes 417800 | tf_op jit(solution)/shard_map/ppermute | solution.py:40
  79.5 11.0 %collective-permute-start.20 = (f32[16,2176]{1,0:T(8,128)S(1)}, f32[16,2176]{1,0:T(8,128)S(1)}, u32[]{:S(2)}, u32[]{:S(2)}) collective-permute-start(f32[16,2176]{1,0:T(8,128)S(1)} %get-tuple-element.96), channel_id=1, source_target_pairs={{0,8},{1,9},{2,10},{3,11},{4,12},{5,13},{6,14},{7,15},{8,0},{9,1},... | collective-permute-start | bytes 417800 | tf_op jit(solution)/shard_map/ppermute | solution.py:40
  79.5 11.3 %collective-permute-start.19 = (f32[16,2176]{1,0:T(8,128)S(1)}, f32[16,2176]{1,0:T(8,128)S(1)}, u32[]{:S(2)}, u32[]{:S(2)}) collective-permute-start(f32[16,2176]{1,0:T(8,128)S(1)} %get-tuple-element.87), channel_id=1, source_target_pairs={{0,16},{1,17},{2,18},{3,19},{4,20},{5,21},{6,22},{7,23},{8,24},{9,... | collective-permute-start | bytes 417800 | tf_op jit(solution)/shard_map/ppermute | solution.py:40
  90.9 4.5 %collective-permute-start.24 = (f32[16,512]{1,0:T(8,128)S(1)}, f32[16,512]{1,0:T(8,128)S(1)}, u32[]{:S(2)}, u32[]{:S(2)}) collective-permute-start(f32[16,512]{1,0:T(8,128)S(1)} %slice.135.own_ref), channel_id=1, source_target_pairs={{0,4},{1,5},{2,6},{3,7},{4,0},{5,1},{6,2},{7,3},{8,12},{9,13},{10,... | collective-permute-start | bytes 98312 | tf_op jit(solution)/shard_map/ppermute | solution.py:40
  91.0 12.1 %collective-permute-start.21 = (f32[16,1664]{1,0:T(8,128)S(1)}, f32[16,1664]{1,0:T(8,128)S(1)}, u32[]{:S(2)}, u32[]{:S(2)}) collective-permute-start(f32[16,1664]{1,0:T(8,128)S(1)} %slice.134.rest_0_), channel_id=1, source_target_pairs={{0,24},{1,25},{2,26},{3,27},{4,28},{5,29},{6,30},{7,31},{8,16},{9,... | collective-permute-start | bytes 319496 | tf_op jit(solution)/shard_map/ppermute | solution.py:40
  92.5 10.6 %collective-permute-start.22 = (f32[16,1664]{1,0:T(8,128)S(1)}, f32[16,1664]{1,0:T(8,128)S(1)}, u32[]{:S(2)}, u32[]{:S(2)}) collective-permute-start(f32[16,1664]{1,0:T(8,128)S(1)} %slice.134.rest_0_), channel_id=1, source_target_pairs={{0,16},{1,17},{2,18},{3,19},{4,20},{5,21},{6,22},{7,23},{8,24},{9,... | collective-permute-start | bytes 319496 | tf_op jit(solution)/shard_map/ppermute | solution.py:40
  92.9 7.7 %collective-permute-start.23 = (f32[16,1664]{1,0:T(8,128)S(1)}, f32[16,1664]{1,0:T(8,128)S(1)}, u32[]{:S(2)}, u32[]{:S(2)}) collective-permute-start(f32[16,1664]{1,0:T(8,128)S(1)} %slice.134.rest_0_), channel_id=1, source_target_pairs={{0,8},{1,9},{2,10},{3,11},{4,12},{5,13},{6,14},{7,15},{8,0},{9,1},... | collective-permute-start | bytes 319496 | tf_op jit(solution)/shard_map/ppermute | solution.py:40
  95.4 8.5 %collective-permute-start.25 = (f32[16,1664]{1,0:T(8,128)S(1)}, f32[16,1664]{1,0:T(8,128)S(1)}, u32[]{:S(2)}, u32[]{:S(2)}) collective-permute-start(f32[16,1664]{1,0:T(8,128)S(1)} %slice.134.rest_0_), channel_id=1, source_target_pairs={{0,4},{1,5},{2,6},{3,7},{4,0},{5,1},{6,2},{7,3},{8,12},{9,13},{10,... | collective-permute-start | bytes 319496 | tf_op jit(solution)/shard_map/ppermute | solution.py:40
  103.1 1.3 %collective-permute-start.26 = (f32[16,1664]{1,0:T(8,128)S(1)}, f32[16,1664]{1,0:T(8,128)S(1)}, u32[]{:S(2)}, u32[]{:S(2)}) collective-permute-start(f32[16,1664]{1,0:T(8,128)S(1)} %collective-permute-done.23.rest_1_), channel_id=1, source_target_pairs={{0,4},{1,5},{2,6},{3,7},{4,0},{5,1},{6,2},{7,3},{8,12},{9,13},{10,... | collective-permute-start | bytes 319496 | tf_op jit(solution)/shard_map/ppermute | solution.py:40
  103.1 1.5 %collective-permute-start.27 = (f32[16,1664]{1,0:T(8,128)S(1)}, f32[16,1664]{1,0:T(8,128)S(1)}, u32[]{:S(2)}, u32[]{:S(2)}) collective-permute-start(f32[16,1664]{1,0:T(8,128)S(1)} %collective-permute-done.22.rest_2_), channel_id=1, source_target_pairs={{0,4},{1,5},{2,6},{3,7},{4,0},{5,1},{6,2},{7,3},{8,12},{9,13},{10,... | collective-permute-start | bytes 319496 | tf_op jit(solution)/shard_map/ppermute | solution.py:40
  103.6 1.3 %collective-permute-start.28 = (f32[16,1664]{1,0:T(8,128)S(1)}, f32[16,1664]{1,0:T(8,128)S(1)}, u32[]{:S(2)}, u32[]{:S(2)}) collective-permute-start(f32[16,1664]{1,0:T(8,128)S(1)} %collective-permute-done.21.rest_3_), channel_id=1, source_target_pairs={{0,4},{1,5},{2,6},{3,7},{4,0},{5,1},{6,2},{7,3},{8,12},{9,13},{10,... | collective-permute-start | bytes 319496 | tf_op jit(solution)/shard_map/ppermute | solution.py:40
  106.0 4.5 %collective-permute-start.29 = (f32[128,128]{1,0:T(8,128)S(1)}, f32[128,128]{1,0:T(8,128)S(1)}, u32[]{:S(2)}, u32[]{:S(2)}) collective-permute-start(f32[128,128]{1,0:T(8,128)S(1)} %get-tuple-element.74), channel_id=1, source_target_pairs={{0,1},{1,0},{2,3},{3,2},{4,6},{5,7},{6,4},{7,5},{8,9},{9,8},{10,11... | collective-permute-start | bytes 196616 | tf_op jit(solution)/shard_map/ppermute | solution.py:40
  110.5 4.3 %collective-permute-start.30 = (f32[128,128]{1,0:T(8,128)S(1)}, f32[128,128]{1,0:T(8,128)S(1)}, u32[]{:S(2)}, u32[]{:S(2)}) collective-permute-start(f32[128,128]{1,0:T(8,128)S(1)} %add.43.one_ref), channel_id=1, source_target_pairs={{0,2},{1,3},{2,0},{3,1},{4,5},{5,4},{6,7},{7,6},{8,10},{9,11},{10,... | collective-permute-start | bytes 196616 | tf_op jit(solution)/shard_map/ppermute | solution.py:40
  (1 other events, 6.4 us)

commit v5 on v4

--- a/solution.py
+++ b/solution.py
@@ -55,6 +55,12 @@
 
 def exact(a, b, dims=NN):
     return lax.dot_general(a, b, dims, precision=HIGHEST, preferred_element_type=F32)
+
+
+def parts3(a, b, dims=NN):
+    a_high, a_low = split(a)
+    b_high, b_low = split(b)
+    return dot(a_high, b_high, dims) + (dot(a_low, b_high, dims) + dot(a_high, b_low, dims))
 
 
 def tiles(width, most=256):
@@ -85,7 +91,7 @@
     steps = 4
     block = rows // steps
 
-    def body(momentum_hbm, grad_hbm, basis_hbm, high_ref, low_ref, proj_ref, momentum_ref, grad_ref, basis_ref, both_ref, sems):
+    def body(momentum_hbm, grad_hbm, basis_hbm, high_ref, low_ref, top_ref, bottom_ref, momentum_ref, grad_ref, basis_ref, both_ref, sems):
         whole = pltpu.make_async_copy(basis_hbm, basis_ref, sems.at[0])
         whole.start()
         copies = []
@@ -110,13 +116,15 @@
             high_ref[at, :] = high
             low_ref[at, :] = low
             wide = dot(high, both_ref[...])
-            proj_ref[at, :] = wide[:, :rank] + wide[:, rank:] + dot(low, both_ref[:, :rank])
+            out_ref = top_ref if 2 * i < steps else bottom_ref
+            at = pl.ds(i % (steps // 2) * block, block)
+            out_ref[at, :] = wide[:, :rank] + wide[:, rank:] + dot(low, both_ref[:, :rank])
 
     return pl.pallas_call(
         body,
         in_specs=[pl.BlockSpec(memory_space=pltpu.HBM)] * 3,
-        out_specs=[VMEM] * 3,
-        out_shape=[struct(rows, cols, dtype=BF16)] * 2 + [struct(rows, rank)],
+        out_specs=[VMEM] * 4,
+        out_shape=[struct(rows, cols, dtype=BF16)] * 2 + [struct(rows // 2, rank)] * 2,
         scratch_shapes=[
             pltpu.VMEM((rows, cols), F32),
             pltpu.VMEM((rows, cols), BF16),
@@ -158,19 +166,20 @@
         out_ref[pl.ds(at, chunk), width:] = gram[t * chunk:(t + 1) * chunk]
 
 
-def pull_send(count, place, one, two, high, low, before=None):
+def pull_send(count, place, halves, high, low, before=None):
     rows, width = high.shape
-    rank = before[0].shape[1] if before is not None else one.shape[1]
+    rank = halves[0].shape[1]
     chunk = rank // count
-
-    def body(place_ref, one_ref, two_ref, high_ref, low_ref, *rest):
+    skip = sum(x.shape[0] for x in halves[::2]) - rows
+
+    def body(place_ref, a, b, c, d, high_ref, low_ref, *rest):
         place = place_ref[0]
-        proj = one_ref[:rows, :] + two_ref[...]
+        proj = jnp.concatenate([a[skip:, :] + b[skip:, :], c[...] + d[...]], axis=0)
         left_ref = right_ref = None
         if before is not None:
             left_ref, right_ref, gram_ref, inv_ref = rest[:4]
-            proj = proj - KEEP * exact(left_ref[...], gram_ref[...])
-            proj = exact(proj, inv_ref[...], NT)
+            proj = proj - KEEP * parts3(left_ref[...], gram_ref[...])
+            proj = parts3(proj, inv_ref[...], NT)
         proj_ref, keep_ref, send_ref, turned_ref = rest[-4:]
         proj_ref[...] = proj
         turned_ref[...] = proj.T
@@ -181,12 +190,12 @@
 
         keep_ref[...] = pick(False)
         turned = pick(True)
-        cross = None if before is None else split(-KEEP * exact(turned, left_ref[...]))
+        cross = None if before is None else split(-KEEP * parts3(turned, left_ref[...]))
         gram = pull_rows(turned, proj, high_ref, low_ref, cross, right_ref, send_ref)
         put_gram(place, gram, send_ref, width, chunk)
 
     out = [struct(rows, rank), struct(rank // 2, rows), struct(rank // 2, width + rank)]
-    ins = [place, one, two, high, low] + list(before or [])
+    ins = [place, *halves, high, low] + list(before or [])
     return call(body, "pull_send", out, ins, [pltpu.VMEM((rank, rows), F32)], flops=500_000_000, nbytes=5_000_000)
 
 
@@ -201,7 +210,7 @@
         cross = right_ref = None
         if before is not None:
             left_ref, right_ref = rest[:2]
-            cross = split(-KEEP * exact(turned, left_ref[...]))
+            cross = split(-KEEP * parts3(turned, left_ref[...]))
         gram = pull_rows(turned, proj_ref[...], high_ref, low_ref, cross, right_ref, rest[-1])
         put_gram(place, gram, rest[-1], width, chunk)
 
@@ -215,13 +224,14 @@
     chunk = rank // count
     push = high is not None
     rows = high.shape[0] if push else 0
+    cut = rank if push else 0
 
     def body(place_ref, inv_ref, *rest):
         pieces, rest = rest[:count], rest[count:]
         if push:
-            work_high, work_low, right_ref, out_ref, raw_ref = rest
+            work_high, work_low, right_ref, one_ref, two_ref, raw_ref = rest
         else:
-            right_ref, out_ref, raw_ref = rest
+            right_ref, one_ref, raw_ref = rest
         place = place_ref[0]
         for i, piece in enumerate(pieces):
             at = chunk_at(place, i % (count // 2), i >= count // 2) * chunk
@@ -229,7 +239,6 @@
         inv_high, inv_low = split(inv_ref[...])
         inv_both = jnp.concatenate([inv_high, inv_low], axis=0)
         gram = jnp.zeros((rank, rank), F32)
-        image = jnp.zeros((rows, rank), F32) if push else None
         for at, size in tiles(width):
             raw_high, raw_low = split(raw_ref[:, at:at + size])
             wide = dot(inv_both, raw_high)
@@ -239,23 +248,38 @@
             both = jnp.concatenate([high, low], axis=0)
             wide = dot(both, high, NT)
             gram = gram + (wide[:rank] + wide[rank:] + dot(high, low, NT))
-            if push:
-                wide = dot(work_high[:, at:at + size], both, NT)
-                image = image + (wide[:, :rank] + wide[:, rank:] + dot(work_low[:, at:at + size], high, NT))
+        one_ref[:rank, :] = gram
         if push:
-            out_ref[:rows, :] = image
-        out_ref[rows:, :] = gram
+            image = None
+            for at, size in tiles(width):
+                right_high, right_low = split(right_ref[:, at:at + size])
+                wide = dot(work_high[:, at:at + size], jnp.concatenate([right_high, right_low], axis=0), NT)
+                part = wide[:, :rank] + wide[:, rank:] + dot(work_low[:, at:at + size], right_high, NT)
+                image = part if image is None else image + part
+            one_ref[rank:, :] = image[:cut]
+            two_ref[...] = image[cut:]
 
     ins = [place, inv, *own, *other] + ([high, low] if push else [])
-    return call(body, "normal", [struct(rank, width), struct(rows + rank, rank)], ins,
-                [pltpu.VMEM((rank, width), F32)], flops=1_000_000_000, nbytes=5_000_000)
-
-
-def left_of(proj, inv):
-    def body(proj_ref, inv_ref, out_ref):
-        out_ref[...] = exact(proj_ref[...], inv_ref[...], NT)
-
-    return call(body, "left", struct(*proj.shape), [proj, inv], flops=100_000_000, nbytes=600_000)
+    out = [struct(rank, width), struct(rank + cut, rank)] + ([struct(rows - cut, rank)] if push else [])
+    return call(body, "normal", out, ins, [pltpu.VMEM((rank, width), F32)], flops=1_000_000_000, nbytes=5_000_000)
+
+
+def left_of(proj, inv, before=None, scale=None):
+    def body(proj_ref, inv_ref, *rest):
+        left = parts3(proj_ref[...], inv_ref[...], NT)
+        if before is None:
+            rest[0][...] = left
+        else:
+            before_ref, left_ref, both_ref = rest
+            left_ref[...] = left
+            both_ref[0] = scale * before_ref[...]
+            both_ref[1] = scale * left
+
+    rows, rank = proj.shape
+    if before is None:
+        return call(body, "left", struct(rows, rank), [proj, inv], flops=100_000_000, nbytes=600_000)
+    return call(body, "lefts", [struct(rows, rank), struct(2, rows, rank)], [proj, inv, before],
+                flops=100_000_000, nbytes=1_200_000)
 
 
 def outer_tile(left, right_high, right_low):
@@ -281,20 +305,15 @@
     return call(body, "deflate", struct(rows, cols), [momentum, grad, left, right], flops=1_500_000_000, nbytes=9_000_000)
 
 
-def finish(base, left, right, before=None, scale=None, part=0):
+def finish(base, left, right, before=None):
     rows, cols = base.shape
     rank = left.shape[1]
     half = rows // 2
     block = half // 2
-    first = part * half
+    first = 0 if before is None else half
 
     def body(base_ref, left_ref, right_ref, *rest):
-        if part == 0:
-            other_ref, out_ref, lefts_ref, stage_ref, high_ref, low_ref, sems = rest
-            lefts_ref[0] = scale * other_ref[...]
-            lefts_ref[1] = scale * left_ref[...]
-        else:
-            _, out_ref, stage_ref, high_ref, low_ref, sems = rest
+        out_ref, stage_ref, high_ref, low_ref, sems = rest[-5:]
         for at, size in tiles(cols):
             lanes = slice(at, at + size)
             high_ref[:, lanes], low_ref[:, lanes] = split(KEEP * right_ref[:, lanes])
@@ -312,25 +331,19 @@
             copy.wait()
 
     hbm = pl.BlockSpec(memory_space=pltpu.HBM)
-    out, out_specs = [struct(rows, cols)], [hbm]
-    if part == 0:
-        ins, in_specs, alias = [base, left, right, before], [VMEM] * 4, {}
-        out.append(struct(2, rows, rank))
-        out_specs.append(VMEM)
-    else:
-        ins, in_specs, alias = [base, left, right, before], [VMEM] * 3 + [hbm], {3: 0}
+    more = [] if before is None else [before]
     return pl.pallas_call(
         body,
-        in_specs=in_specs,
-        out_specs=out_specs,
-        out_shape=out,
+        in_specs=[VMEM] * 3 + [hbm] * len(more),
+        out_specs=hbm,
+        out_shape=struct(rows, cols),
         scratch_shapes=[pltpu.VMEM((2, block, cols), F32)] + [pltpu.VMEM((rank, cols), BF16)] * 2
         + [pltpu.SemaphoreType.DMA((2,))],
-        input_output_aliases=alias,
+        input_output_aliases={3: 0} if more else {},
         name="finish",
         compiler_params=pltpu.CompilerParams(vmem_limit_bytes=24 * 2**20),
         cost_estimate=pl.CostEstimate(flops=800_000_000, bytes_accessed=6_000_000, transcendentals=0),
-    )(*ins)
+    )(base, left, right, *more)
 
 
 def eliminate(full, first):
@@ -419,11 +432,11 @@
     return call(body, "factor", struct(rank, rank), [place, own, other], flops=2 * FACTOR, nbytes=131072)
 
 
-def factor_right(one, two, first):
+def factor_right(one, two):
     rank = one.shape[1]
 
     def body(one_ref, two_ref, gram_ref, out_ref):
-        gram = one_ref[first:, :] + two_ref[...]
+        gram = one_ref[:rank, :] + two_ref[:rank, :]
         gram_ref[...] = gram
         out_ref[...] = gram
         factor_panels(out_ref)
@@ -464,28 +477,50 @@
                 flops=2 * FACTOR, nbytes=2_000_000)
 
 
-def sum_cols(x):
+def sum_cols(parts):
     masks = masks_of("col")
     for even, odd in zip(masks[:-1], masks[:0:-1]):
-        x = x + swap(x, "col", even, odd)
-    return x, lambda y: swap(y, "col", masks[-1], masks[0])
+        parts = [x + swap(x, "col", even, odd) for x in parts]
+    return [y for x in parts for y in (x, swap(x, "col", masks[-1], masks[0]))]
 
 
 def sum_rows(keep, send, count, rank, beside=None):
     x = keep + swap(send, "row", 1, 1)
+    if beside is not None:
+        work, seed = beside
+        x, seed = lax.optimization_barrier((x, seed))
+        beside = work(seed)
     width = x.shape[1] - rank
     chunk = rank // count
-    parts = [x[i * chunk:(i + 1) * chunk] for i in range(count // 2)]
+    slots = count // 2
+    cut = width // rank // 2 * rank
+    cut = width - cut
+    parts = [x[i * chunk:(i + 1) * chunk] for i in range(slots)]
     gram = jnp.concatenate([part[:, width:] for part in parts], axis=1)
-    own = jnp.concatenate([parts[0][:, :width], gram], axis=1)
-    gots = []
-    for i in reversed(range(1, count // 2)):
-        gots.append(swap(jnp.concatenate([parts[i][:, :width], gram], axis=1), "row", 2 * i, 2 * i))
-    if beside is not None:
-        gots[0], beside = lax.optimization_barrier((gots[0], beside))
-    for got in gots:
-        own = own + got
-    own, gram = lax.optimization_barrier((own[:, :width], own[:, width:]))
+    stepped = {i: part[:, cut:width] for i, part in enumerate(parts)}
+    own = parts[0][:, :cut]
+    straight = {}
+    bit = 1
+    while bit < slots:
+        sent = [i for i in stepped if i & bit]
+        kept = [i for i in stepped if not i & bit]
+        cols = [stepped[i] for i in sent] + [gram]
+        first = [parts[1][:, :cut]] if bit == 1 else []
+        got = swap(jnp.concatenate(first + cols, axis=1), "row", 2 * bit, 2 * bit)
+        if bit == 1:
+            straight[1], got = got[:, :cut], got[:, cut:]
+            for i in reversed(range(2, slots)):
+                straight[i] = swap(parts[i][:, :cut], "row", 2 * i, 2 * i)
+            if beside is not None:
+                got, beside = lax.optimization_barrier((got, beside))
+        size = width - cut
+        stepped = {i: stepped[i] + got[:, n * size:(n + 1) * size] for n, i in enumerate(kept)}
+        gram = gram + got[:, len(kept) * size:]
+        bit *= 2
+    for i in straight:
+        own = own + straight[i]
+    own = jnp.concatenate([own, stepped[0]], axis=1)
+    own, gram = lax.optimization_barrier((own, gram))
     return own, gram, swap(gram, "row", 1, 1), beside
 
 
@@ -507,32 +542,34 @@
     col_scale = float(width * lax.axis_size("col")) ** 0.5
     place = lax.axis_index("row").astype(jnp.int32).reshape(1)
 
-    def left_side(one, two, before, beside=None):
-        proj, turned, send = pull_send(count, place, one, two, high, low, before)
+    def left_side(halves, before=None, beside=None):
+        proj, turned, send = pull_send(count, place, halves, high, low, before)
         keep = pull_keep(count, place, turned, proj, high, low, before)
         raw, own, other, beside = sum_rows(keep, send, count, rank, beside)
         first, second, inv = gather_rows(raw, count, lambda: factor_left(count, place, own, other))
-        return left_of(proj, inv), inv, (first, second), beside
-
-    high, low, proj = start(momentum, grad, basis)
-    one, last_swap = sum_cols(proj)
-    left_a, inv, pieces, _ = left_side(one, last_swap(one), None)
-    right_a, image = normal(count, place, inv, *pieces, high, low)
-
-    one, last_swap = sum_cols(image)
-    gram, inv = factor_right(one, last_swap(one[rows:]), rows)
-    two = last_swap(one[:rows])
-
-    base = deflate(momentum, grad, left_a, right_a)
-    left_b, inv, pieces, base = left_side(one, two, (left_a, right_a, gram, inv), base)
+        return proj, inv, (first, second), beside
+
+    high, low, *parts = start(momentum, grad, basis)
+    proj, inv, pieces, _ = left_side(sum_cols(parts))
+    left_a = left_of(proj, inv)
+    right_a, *parts = normal(count, place, inv, *pieces, high, low)
+
+    halves = sum_cols(parts)
+    gram, inv = factor_right(*halves[:2])
+
+    beside = (lambda left: deflate(momentum, grad, left, right_a)), left_a
+    proj, inv, pieces, base = left_side(halves, (left_a, right_a, gram, inv), beside)
+    left_b, lefts = left_of(proj, inv, left_a, row_scale)
     right_b, gram = normal(count, place, inv, *pieces)
 
-    gram, last_swap = sum_cols(gram)
-    momentum_out, lefts = finish(base, left_b, right_b, left_a, row_scale)
+    masks = masks_of("col")
+    momentum_out = finish(base, left_b, right_b)
+    for even, odd in zip(masks[:-1], masks[:0:-1]):
+        gram = gram + swap(gram, "col", even, odd)
     gram, momentum_out = lax.optimization_barrier((gram, momentum_out))
-    momentum_out, = finish(base, left_b, right_b, momentum_out, part=1)
+    momentum_out = finish(base, left_b, right_b, momentum_out)
     turned = turn(right_b)
-    return momentum_out, lefts, last_factor(gram, last_swap(gram), *turned, col_scale)
+    return momentum_out, lefts, last_factor(gram, swap(gram, "col", masks[-1], masks[0]), *turned, col_scale)
 
 
 def solution(mesh):

time: 121 us -> 116 us (0.959)
  waiting for transfers between devices: 48.6 us -> 39.5 us
  starting transfers between devices: 31.4 us -> 36.9 us
  Pallas kernels: 38.3 us -> 36.9 us
    ppermute x31 -> x36, waiting for transfers between devices: 48.6 us -> 39.5 us  [swap(): return lax.ppermute(x, ('row', 'col'), pairs)]
    ppermute x31 -> x36, starting transfers between devices: 31.4 us -> 36.9 us  [swap(): return lax.ppermute(x, ('row', 'col'), pairs)]
  transfers between devices with their start and end apart: 31 -> 36, of which waited for: 22 -> 23; matrix products, arithmetic and copies ran while one was open for 0% -> 1% of each run, Pallas kernels for 18% -> 18%
where the time goes in v5:
time: 116 us; the launch traced here: 115 us
  waiting for transfers between devices  39.5 us (34%)
  Pallas kernels  36.9 us (32%)
  starting transfers between devices  36.9 us (32%)
    ppermute x36, waiting for transfers between devices, swap(): return lax.ppermute(x, ('row', 'col'), pairs)  39.5 us
    ppermute x36, starting transfers between devices, swap(): return lax.ppermute(x, ('row', 'col'), pairs)  36.9 us
    pallas_call x14, Pallas kernels, call(): pl.pallas_call(body, out_shape=out, in_specs=[SMEM if x.dtype == jnp.int3...  30.1 us
    pallas_call x2, Pallas kernels, finish(): pl.pallas_call(body, in_specs=[VMEM] * 3 + [hbm] * len(more), out_specs=h...  3.56 us
    pallas_call x1, Pallas kernels, start(): pl.pallas_call(body, in_specs=[pl.BlockSpec(memory_space=pltpu.HBM)] * 3,...  3.21 us
  transfers between devices with their start and end apart: 36, of which 23 were waited for; matrix products, arithmetic and copies ran while one was open for 1% of the time, Pallas kernels for 18%

profile of v5, /device:TPU:0, one launch (start us, length us, event | category | flops | bytes accessed | tf_op | source)
XLA Modules:
  0.0 115.4 jit_solution(1676589310936251462)
XLA Ops:
  0.6 3.2 %start.1 = (bf16[512,1664]{1,0:T(8,128)(2,1)S(1)}, bf16[512,1664]{1,0:T(8,128)(2,1)S(1)}, f32[256,128]{1,0:T(8,128)S(1)}, f32[256,128]{1,0:T(8,128)S(1)}) custom-call(f32[512,1664]{1,0:T(8,128)} %momentum_ref.1, bf16[512,1664]{1,0:T(8,128)(2,1)} %grad_ref.1, f32[1664,128]{1,0:T(8,128)} %basis_hbm.1), custom_call_target="tpu_custom_call" | custom-call | tf_op jit(solution)/shard_map/start/pallas_call | solution.py:123
  3.8 3.0 %collective-permute-start = (f32[256,128]{1,0:T(8,128)S(1)}, f32[256,128]{1,0:T(8,128)S(1)}, u32[]{:S(2)}, u32[]{:S(2)}) collective-permute-start(f32[256,128]{1,0:T(8,128)S(1)} %get-tuple-element.46), channel_id=1, source_target_pairs={{0,1},{1,0},{2,3},{3,2},{4,6},{5,7},{6,4},{7,5},{8,9},{9,8},{10,11... | collective-permute-start | bytes 393224 | tf_op jit(solution)/shard_map/ppermute | solution.py:40
  6.9 2.9 %collective-permute-done = f32[256,128]{1,0:T(8,128)S(1)} collective-permute-done((f32[256,128]{1,0:T(8,128)S(1)}, f32[256,128]{1,0:T(8,128)S(1)}, u32[]{:S(2)}, u32[]{:S(2)}) %collective-permute-start) | collective-permute-done | bytes 131104 | tf_op jit(solution)/shard_map/ppermute | solution.py:40
  9.8 2.1 %collective-permute-start.1 = (f32[256,128]{1,0:T(8,128)S(1)}, f32[256,128]{1,0:T(8,128)}, u32[]{:S(2)}, u32[]{:S(2)}) collective-permute-start(f32[256,128]{1,0:T(8,128)S(1)} %add.69.a), channel_id=1, source_target_pairs={{0,2},{1,3},{2,0},{3,1},{4,5},{5,4},{6,7},{7,6},{8,10},{9,11},{10,... | collective-permute-start | bytes 393224 | tf_op jit(solution)/shard_map/ppermute | solution.py:40
  15.0 2.9 %collective-permute-done.3.d = f32[256,128]{1,0:T(8,128)} collective-permute-done((f32[256,128]{1,0:T(8,128)}, f32[256,128]{1,0:T(8,128)}, u32[]{:S(2)}, u32[]{:S(2)}) %collective-permute-start.3) | collective-permute-done | bytes 131104 | tf_op jit(solution)/shard_map/ppermute | solution.py:40
  17.9 1.9 %pull_send.2 = (f32[512,128]{1,0:T(8,128)S(1)}, f32[64,512]{1,0:T(8,128)S(1)}, f32[64,1792]{1,0:T(8,128)S(1)}) custom-call(s32[1]{0:T(128)} %bitcast.place_ref, f32[256,128]{1,0:T(8,128)S(1)} %add.69.a, f32[256,128]{1,0:T(8,128)} %collective-permute-done.1.b, f32[256,128]{1,0:T(8,128)} %add.70.c, f32[256,128]{1,0:T(8,128)} %collective-permute-done.3.d, ...), custom_call_target="tpu_custom_call" | custom-call | flops 500000000 | bytes 5000000 | tf_op jit(solution)/shard_map/pull_send/pallas_call | solution.py:75
  21.8 1.6 %collective-permute-start.5 = (f32[16,2944]{1,0:T(8,128)S(1)}, f32[16,2944]{1,0:T(8,128)S(1)}, u32[]{:S(2)}, u32[]{:S(2)}) collective-permute-start(f32[16,2944]{1,0:T(8,128)S(1)} %constant_dynamic-update-slice_fusion), channel_id=1, source_target_pairs={{0,8},{1,9},{2,10},{3,11},{4,12},{5,13},{6,14},{7,15},{8,0},{9,1},... | collective-permute-start | bytes 565256 | tf_op jit(solution)/shard_map/ppermute | solution.py:40
  23.4 2.6 %collective-permute-start.7 = (f32[16,896]{1,0:T(8,128)S(1)}, f32[16,896]{1,0:T(8,128)S(1)}, u32[]{:S(2)}, u32[]{:S(2)}) collective-permute-start(f32[16,896]{1,0:T(8,128)S(1)} %get-tuple-element.97), channel_id=1, source_target_pairs={{0,16},{1,17},{2,18},{3,19},{4,20},{5,21},{6,22},{7,23},{8,24},{9,... | collective-permute-start | bytes 172040 | tf_op jit(solution)/shard_map/ppermute | solution.py:40
  26.3 3.5 %collective-permute-done.5 = f32[16,2944]{1,0:T(8,128)S(1)} collective-permute-done((f32[16,2944]{1,0:T(8,128)S(1)}, f32[16,2944]{1,0:T(8,128)S(1)}, u32[]{:S(2)}, u32[]{:S(2)}) %collective-permute-start.5) | collective-permute-done | bytes 188448 | tf_op jit(solution)/shard_map/ppermute | solution.py:40
  29.9 2.4 %collective-permute-start.8 = (f32[16,1280]{1,0:T(8,128)S(1)}, f32[16,1280]{1,0:T(8,128)S(1)}, u32[]{:S(2)}, u32[]{:S(2)}) collective-permute-start(f32[16,1280]{1,0:T(8,128)S(1)} %pad_maximum_fusion.2), channel_id=1, source_target_pairs={{0,16},{1,17},{2,18},{3,19},{4,20},{5,21},{6,22},{7,23},{8,24},{9,... | collective-permute-start | bytes 245768 | tf_op jit(solution)/shard_map/ppermute | solution.py:40
  33.1 2.6 %collective-permute-done.8 = f32[16,1280]{1,0:T(8,128)S(1)} collective-permute-done((f32[16,1280]{1,0:T(8,128)S(1)}, f32[16,1280]{1,0:T(8,128)S(1)}, u32[]{:S(2)}, u32[]{:S(2)}) %collective-permute-start.8) | collective-permute-done | bytes 81952 | tf_op jit(solution)/shard_map/ppermute | solution.py:40
  35.8 4.5 %collective-permute-start.9 = (f32[16,1664]{1,0:T(8,128)S(1)}, f32[16,1664]{1,0:T(8,128)S(1)}, u32[]{:S(2)}, u32[]{:S(2)}) collective-permute-start(f32[16,1664]{1,0:T(8,128)S(1)} %pad_maximum_fusion.rest_0_), channel_id=1, source_target_pairs={{0,24},{1,25},{2,26},{3,27},{4,28},{5,29},{6,30},{7,31},{8,16},{9,... | collective-permute-start | bytes 319496 | tf_op jit(solution)/shard_map/ppermute | solution.py:40
  40.9 4.4 %factor.3.inv_ref = f32[128,128]{1,0:T(8,128)S(1)} custom-call(s32[1]{0:T(128)} %bitcast.place_ref, f32[16,512]{1,0:T(8,128)S(1)} %slice_add_fusion.8.own_ref, f32[16,512]{1,0:T(8,128)S(1)} %collective-permute-done.12.other_ref), custom_call_target="tpu_custom_call" | custom-call | flops 3000000000 | bytes 131072 | tf_op jit(solution)/shard_map/factor/pallas_call | solution.py:75
  45.3 2.4 %collective-permute-done.11.rest_1_ = f32[16,1664]{1,0:T(8,128)S(1)} collective-permute-done((f32[16,1664]{1,0:T(8,128)S(1)}, f32[16,1664]{1,0:T(8,128)S(1)}, u32[]{:S(2)}, u32[]{:S(2)}) %collective-permute-start.11) | collective-permute-done | bytes 106528 | tf_op jit(solution)/shard_map/ppermute | solution.py:40
  47.8 1.8 %collective-permute-done.10.rest_2_ = f32[16,1664]{1,0:T(8,128)S(1)} collective-permute-done((f32[16,1664]{1,0:T(8,128)S(1)}, f32[16,1664]{1,0:T(8,128)S(1)}, u32[]{:S(2)}, u32[]{:S(2)}) %collective-permute-start.10) | collective-permute-done | bytes 106528 | tf_op jit(solution)/shard_map/ppermute | solution.py:40
  51.4 2.2 %normal.2 = (f32[128,1664]{1,0:T(8,128)S(1)}, f32[256,128]{1,0:T(8,128)S(1)}, f32[384,128]{1,0:T(8,128)S(1)}) custom-call(s32[1]{0:T(128)} %bitcast.place_ref, f32[128,128]{1,0:T(8,128)S(1)} %factor.3.inv_ref, f32[16,1664]{1,0:T(8,128)S(1)} %pad_maximum_fusion.rest_0_, f32[16,1664]{1,0:T(8,128)S(1)} %collective-permute-done.11.rest_1_, ...), custom_call_target="tpu_custom_call" | custom-call | flops 1000000000 | bytes 5000000 | tf_op jit(solution)/shard_map/normal/pallas_call | solution.py:75
  53.6 1.6 %collective-permute-start.17 = (f32[256,128]{1,0:T(8,128)S(1)}, f32[256,128]{1,0:T(8,128)S(1)}, u32[]{:S(2)}, u32[]{:S(2)}) collective-permute-start(f32[256,128]{1,0:T(8,128)S(1)} %get-tuple-element.61), channel_id=1, source_target_pairs={{0,1},{1,0},{2,3},{3,2},{4,6},{5,7},{6,4},{7,5},{8,9},{9,8},{10,11... | collective-permute-start | bytes 393224 | tf_op jit(solution)/shard_map/ppermute | solution.py:40
  55.7 2.9 %collective-permute-done.17 = f32[256,128]{1,0:T(8,128)S(1)} collective-permute-done((f32[256,128]{1,0:T(8,128)S(1)}, f32[256,128]{1,0:T(8,128)S(1)}, u32[]{:S(2)}, u32[]{:S(2)}) %collective-permute-start.17) | collective-permute-done | bytes 131104 | tf_op jit(solution)/shard_map/ppermute | solution.py:40
  58.6 1.5 %collective-permute-start.18 = (f32[256,128]{1,0:T(8,128)S(1)}, f32[256,128]{1,0:T(8,128)S(1)}, u32[]{:S(2)}, u32[]{:S(2)}) collective-permute-start(f32[256,128]{1,0:T(8,128)S(1)} %add.80.one_ref.a), channel_id=1, source_target_pairs={{0,2},{1,3},{2,0},{3,1},{4,5},{5,4},{6,7},{7,6},{8,10},{9,11},{10,... | collective-permute-start | bytes 393224 | tf_op jit(solution)/shard_map/ppermute | solution.py:40
  63.7 4.2 %factor.4 = (f32[128,128]{1,0:T(8,128)S(1)}, f32[128,128]{1,0:T(8,128)S(1)}) custom-call(f32[256,128]{1,0:T(8,128)S(1)} %add.80.one_ref.a, f32[256,128]{1,0:T(8,128)S(1)} %collective-permute-done.18.two_ref.b), custom_call_target="tpu_custom_call" | custom-call | flops 3000000000 | bytes 131072 | tf_op jit(solution)/shard_map/factor/pallas_call | solution.py:75
  67.9 1.6 %pull_send.3 = (f32[512,128]{1,0:T(8,128)S(1)}, f32[64,512]{1,0:T(8,128)S(1)}, f32[64,1792]{1,0:T(8,128)S(1)}) custom-call(s32[1]{0:T(128)} %bitcast.place_ref, f32[256,128]{1,0:T(8,128)S(1)} %add.80.one_ref.a, f32[256,128]{1,0:T(8,128)S(1)} %collective-permute-done.18.two_ref.b, f32[384,128]{1,0:T(8,128)S(1)} %add.81.c, ...), custom_call_target="tpu_custom_call" | custom-call | flops 500000000 | bytes 5000000 | tf_op jit(solution)/shard_map/pull_send/pallas_call | solution.py:75
  73.8 2.3 %collective-permute-start.23 = (f32[16,896]{1,0:T(8,128)S(1)}, f32[16,896]{1,0:T(8,128)S(1)}, u32[]{:S(2)}, u32[]{:S(2)}) collective-permute-start(f32[16,896]{1,0:T(8,128)S(1)} %get-tuple-element.89), channel_id=1, source_target_pairs={{0,24},{1,25},{2,26},{3,27},{4,28},{5,29},{6,30},{7,31},{8,16},{9,... | collective-permute-start | bytes 172040 | tf_op jit(solution)/shard_map/ppermute | solution.py:40
  76.1 1.5 %deflate.1.base_ref = f32[512,1664]{1,0:T(8,128)S(1)} custom-call(f32[512,1664]{1,0:T(8,128)S(1)} %copy-done, bf16[512,1664]{1,0:T(8,128)(2,1)S(1)} %copy-done.1, f32[512,128]{1,0:T(8,128)S(1)} %left.1.rest_0_.left_ref, f32[128,1664]{1,0:T(8,128)S(1)} %get-tuple-element.63.rest_1_.right_ref), custom_call_target="tpu_custom_call" | custom-call | flops 1500000000 | bytes 9000000 | tf_op jit(solution)/shard_map/deflate/pallas_call | solution.py:75
  77.6 3.2 %collective-permute-done.22 = f32[16,2944]{1,0:T(8,128)S(1)} collective-permute-done((f32[16,2944]{1,0:T(8,128)S(1)}, f32[16,2944]{1,0:T(8,128)S(1)}, u32[]{:S(2)}, u32[]{:S(2)}) %collective-permute-start.22) | collective-permute-done | bytes 188448 | tf_op jit(solution)/shard_map/ppermute | solution.py:40
  81.0 5.3 %collective-permute-done.25 = f32[16,1280]{1,0:T(8,128)S(1)} collective-permute-done((f32[16,1280]{1,0:T(8,128)S(1)}, f32[16,1280]{1,0:T(8,128)S(1)}, u32[]{:S(2)}, u32[]{:S(2)}) %collective-permute-start.25) | collective-permute-done | bytes 81952 | tf_op jit(solution)/shard_map/ppermute | solution.py:40
  87.7 3.2 %collective-permute-start.28 = (f32[16,1664]{1,0:T(8,128)S(1)}, f32[16,1664]{1,0:T(8,128)S(1)}, u32[]{:S(2)}, u32[]{:S(2)}) collective-permute-start(f32[16,1664]{1,0:T(8,128)S(1)} %pad_maximum_fusion.1.rest_0_), channel_id=1, source_target_pairs={{0,8},{1,9},{2,10},{3,11},{4,12},{5,13},{6,14},{7,15},{8,0},{9,1},... | collective-permute-start | bytes 319496 | tf_op jit(solution)/shard_map/ppermute | solution.py:40
  90.9 4.2 %factor.5.inv_ref = f32[128,128]{1,0:T(8,128)S(1)} custom-call(s32[1]{0:T(128)} %bitcast.place_ref, f32[16,512]{1,0:T(8,128)S(1)} %slice_add_fusion.7.own_ref, f32[16,512]{1,0:T(8,128)S(1)} %collective-permute-done.29.other_ref), custom_call_target="tpu_custom_call" | custom-call | flops 3000000000 | bytes 131072 | tf_op jit(solution)/shard_map/factor/pallas_call | solution.py:75
  96.4 1.8 %collective-permute-done.27.rest_2_ = f32[16,1664]{1,0:T(8,128)S(1)} collective-permute-done((f32[16,1664]{1,0:T(8,128)S(1)}, f32[16,1664]{1,0:T(8,128)S(1)}, u32[]{:S(2)}, u32[]{:S(2)}) %collective-permute-start.27) | collective-permute-done | bytes 106528 | tf_op jit(solution)/shard_map/ppermute | solution.py:40
  101.1 1.6 %collective-permute-start.34 = (f32[128,128]{1,0:T(8,128)S(1)}, f32[128,128]{1,0:T(8,128)S(1)}, u32[]{:S(2)}, u32[]{:S(2)}) collective-permute-start(f32[128,128]{1,0:T(8,128)S(1)} %get-tuple-element.83), channel_id=1, source_target_pairs={{0,1},{1,0},{2,3},{3,2},{4,6},{5,7},{6,4},{7,5},{8,9},{9,8},{10,11... | collective-permute-start | bytes 196616 | tf_op jit(solution)/shard_map/ppermute | solution.py:40
  103.0 1.8 %finish.2.rest_0_ = f32[512,1664]{1,0:T(8,128)} custom-call(f32[512,1664]{1,0:T(8,128)S(1)} %deflate.1.base_ref, f32[512,128]{1,0:T(8,128)S(1)} %get-tuple-element.78.left_ref, f32[128,1664]{1,0:T(8,128)S(1)} %get-tuple-element.82.right_ref), custom_call_target="tpu_custom_call" | custom-call | flops 800000000 | bytes 6000000 | tf_op jit(solution)/shard_map/finish/pallas_call | solution.py:335
  106.9 1.8 %finish.3 = f32[512,1664]{1,0:T(8,128)} custom-call(f32[512,1664]{1,0:T(8,128)S(1)} %deflate.1.base_ref, f32[512,128]{1,0:T(8,128)S(1)} %get-tuple-element.78.left_ref, f32[128,1664]{1,0:T(8,128)S(1)} %get-tuple-element.82.right_ref, f32[512,1664]{1,0:T(8,128)} %finish.2.rest_0_), custom_call_target="tpu_custom_call", output_to_operand_aliasing={{}: (3, {})} | custom-call | flops 800000000 | bytes 6000000 | tf_op jit(solution)/shard_map/finish/pallas_call | solution.py:335
  109.8 5.6 %last_factor.1 = f32[1664,128]{1,0:T(8,128)} custom-call(f32[128,128]{1,0:T(8,128)S(1)} %add.91.one_ref, f32[128,128]{1,0:T(8,128)S(1)} %collective-permute-done.35.two_ref, bf16[1664,128]{1,0:T(8,128)(2,1)S(1)} %get-tuple-element.87.high_ref, bf16[1664,128]{1,0:T(8,128)(2,1)S(1)} %get-tuple-element.88.low_ref), custom_call_target="tpu_custom_call" | custom-call | flops 3000000000 | bytes 2000000 | tf_op jit(solution)/shard_map/last_factor/pallas_call | solution.py:75
  (97 shorter events, 26.2 us)
Async XLA Ops:
  3.8 6.0 %collective-permute-start = (f32[256,128]{1,0:T(8,128)S(1)}, f32[256,128]{1,0:T(8,128)S(1)}, u32[]{:S(2)}, u32[]{:S(2)}) collective-permute-start(f32[256,128]{1,0:T(8,128)S(1)} %get-tuple-element.46), channel_id=1, source_target_pairs={{0,1},{1,0},{2,3},{3,2},{4,6},{5,7},{6,4},{7,5},{8,9},{9,8},{10,11... | collective-permute-start | bytes 393224 | tf_op jit(solution)/shard_map/ppermute | solution.py:40
  6.8 5.1 %collective-permute-start.2 = (f32[256,128]{1,0:T(8,128)S(1)}, f32[256,128]{1,0:T(8,128)S(1)}, u32[]{:S(2)}, u32[]{:S(2)}) collective-permute-start(f32[256,128]{1,0:T(8,128)S(1)} %get-tuple-element.47), channel_id=1, source_target_pairs={{0,1},{1,0},{2,3},{3,2},{4,6},{5,7},{6,4},{7,5},{8,9},{9,8},{10,11... | collective-permute-start | bytes 393224 | tf_op jit(solution)/shard_map/ppermute | solution.py:40
  9.8 5.2 %collective-permute-start.1 = (f32[256,128]{1,0:T(8,128)S(1)}, f32[256,128]{1,0:T(8,128)}, u32[]{:S(2)}, u32[]{:S(2)}) collective-permute-start(f32[256,128]{1,0:T(8,128)S(1)} %add.69.a), channel_id=1, source_target_pairs={{0,2},{1,3},{2,0},{3,1},{4,5},{5,4},{6,7},{7,6},{8,10},{9,11},{10,... | collective-permute-start | bytes 393224 | tf_op jit(solution)/shard_map/ppermute | solution.py:40
  12.6 5.3 %collective-permute-start.3 = (f32[256,128]{1,0:T(8,128)}, f32[256,128]{1,0:T(8,128)}, u32[]{:S(2)}, u32[]{:S(2)}) collective-permute-start(f32[256,128]{1,0:T(8,128)} %add.70.c), channel_id=1, source_target_pairs={{0,2},{1,3},{2,0},{3,1},{4,5},{5,4},{6,7},{7,6},{8,10},{9,11},{10,... | collective-permute-start | bytes 393224 | tf_op jit(solution)/shard_map/ppermute | solution.py:40
  19.8 1.9 %collective-permute-start.4 = (f32[64,1792]{1,0:T(8,128)S(1)}, f32[64,1792]{1,0:T(8,128)S(1)}, u32[]{:S(2)}, u32[]{:S(2)}) collective-permute-start(f32[64,1792]{1,0:T(8,128)S(1)} %get-tuple-element.52), channel_id=1, source_target_pairs={{0,4},{1,5},{2,6},{3,7},{4,0},{5,1},{6,2},{7,3},{8,12},{9,13},{10,... | collective-permute-start | bytes 1376264 | tf_op jit(solution)/shard_map/ppermute | solution.py:40
  21.8 8.1 %collective-permute-start.5 = (f32[16,2944]{1,0:T(8,128)S(1)}, f32[16,2944]{1,0:T(8,128)S(1)}, u32[]{:S(2)}, u32[]{:S(2)}) collective-permute-start(f32[16,2944]{1,0:T(8,128)S(1)} %constant_dynamic-update-slice_fusion), channel_id=1, source_target_pairs={{0,8},{1,9},{2,10},{3,11},{4,12},{5,13},{6,14},{7,15},{8,0},{9,1},... | collective-permute-start | bytes 565256 | tf_op jit(solution)/shard_map/ppermute | solution.py:40
  23.4 8.8 %collective-permute-start.7 = (f32[16,896]{1,0:T(8,128)S(1)}, f32[16,896]{1,0:T(8,128)S(1)}, u32[]{:S(2)}, u32[]{:S(2)}) collective-permute-start(f32[16,896]{1,0:T(8,128)S(1)} %get-tuple-element.97), channel_id=1, source_target_pairs={{0,16},{1,17},{2,18},{3,19},{4,20},{5,21},{6,22},{7,23},{8,24},{9,... | collective-permute-start | bytes 172040 | tf_op jit(solution)/shard_map/ppermute | solution.py:40
  26.1 7.0 %collective-permute-start.6 = (f32[16,896]{1,0:T(8,128)S(1)}, f32[16,896]{1,0:T(8,128)S(1)}, u32[]{:S(2)}, u32[]{:S(2)}) collective-permute-start(f32[16,896]{1,0:T(8,128)S(1)} %get-tuple-element.96), channel_id=1, source_target_pairs={{0,24},{1,25},{2,26},{3,27},{4,28},{5,29},{6,30},{7,31},{8,16},{9,... | collective-permute-start | bytes 172040 | tf_op jit(solution)/shard_map/ppermute | solution.py:40
  29.9 5.8 %collective-permute-start.8 = (f32[16,1280]{1,0:T(8,128)S(1)}, f32[16,1280]{1,0:T(8,128)S(1)}, u32[]{:S(2)}, u32[]{:S(2)}) collective-permute-start(f32[16,1280]{1,0:T(8,128)S(1)} %pad_maximum_fusion.2), channel_id=1, source_target_pairs={{0,16},{1,17},{2,18},{3,19},{4,20},{5,21},{6,22},{7,23},{8,24},{9,... | collective-permute-start | bytes 245768 | tf_op jit(solution)/shard_map/ppermute | solution.py:40
  35.8 5.2 %collective-permute-start.12 = (f32[16,512]{1,0:T(8,128)S(1)}, f32[16,512]{1,0:T(8,128)S(1)}, u32[]{:S(2)}, u32[]{:S(2)}) collective-permute-start(f32[16,512]{1,0:T(8,128)S(1)} %slice_add_fusion.8.own_ref), channel_id=1, source_target_pairs={{0,4},{1,5},{2,6},{3,7},{4,0},{5,1},{6,2},{7,3},{8,12},{9,13},{10,... | collective-permute-start | bytes 98312 | tf_op jit(solution)/shard_map/ppermute | solution.py:40
  35.8 13.7 %collective-permute-start.9 = (f32[16,1664]{1,0:T(8,128)S(1)}, f32[16,1664]{1,0:T(8,128)S(1)}, u32[]{:S(2)}, u32[]{:S(2)}) collective-permute-start(f32[16,1664]{1,0:T(8,128)S(1)} %pad_maximum_fusion.rest_0_), channel_id=1, source_target_pairs={{0,24},{1,25},{2,26},{3,27},{4,28},{5,29},{6,30},{7,31},{8,16},{9,... | collective-permute-start | bytes 319496 | tf_op jit(solution)/shard_map/ppermute | solution.py:40
  40.3 9.2 %collective-permute-start.10 = (f32[16,1664]{1,0:T(8,128)S(1)}, f32[16,1664]{1,0:T(8,128)S(1)}, u32[]{:S(2)}, u32[]{:S(2)}) collective-permute-start(f32[16,1664]{1,0:T(8,128)S(1)} %pad_maximum_fusion.rest_0_), channel_id=1, source_target_pairs={{0,16},{1,17},{2,18},{3,19},{4,20},{5,21},{6,22},{7,23},{8,24},{9,... | collective-permute-start | bytes 319496 | tf_op jit(solution)/shard_map/ppermute | solution.py:40
  40.3 7.5 %collective-permute-start.11 = (f32[16,1664]{1,0:T(8,128)S(1)}, f32[16,1664]{1,0:T(8,128)S(1)}, u32[]{:S(2)}, u32[]{:S(2)}) collective-permute-start(f32[16,1664]{1,0:T(8,128)S(1)} %pad_maximum_fusion.rest_0_), channel_id=1, source_target_pairs={{0,8},{1,9},{2,10},{3,11},{4,12},{5,13},{6,14},{7,15},{8,0},{9,1},... | collective-permute-start | bytes 319496 | tf_op jit(solution)/shard_map/ppermute | solution.py:40
  40.9 9.1 %collective-permute-start.13 = (f32[16,1664]{1,0:T(8,128)S(1)}, f32[16,1664]{1,0:T(8,128)S(1)}, u32[]{:S(2)}, u32[]{:S(2)}) collective-permute-start(f32[16,1664]{1,0:T(8,128)S(1)} %pad_maximum_fusion.rest_0_), channel_id=1, source_target_pairs={{0,4},{1,5},{2,6},{3,7},{4,0},{5,1},{6,2},{7,3},{8,12},{9,13},{10,... | collective-permute-start | bytes 319496 | tf_op jit(solution)/shard_map/ppermute | solution.py:40
  53.6 5.0 %collective-permute-start.17 = (f32[256,128]{1,0:T(8,128)S(1)}, f32[256,128]{1,0:T(8,128)S(1)}, u32[]{:S(2)}, u32[]{:S(2)}) collective-permute-start(f32[256,128]{1,0:T(8,128)S(1)} %get-tuple-element.61), channel_id=1, source_target_pairs={{0,1},{1,0},{2,3},{3,2},{4,6},{5,7},{6,4},{7,5},{8,9},{9,8},{10,11... | collective-permute-start | bytes 393224 | tf_op jit(solution)/shard_map/ppermute | solution.py:40
  55.2 5.8 %collective-permute-start.19 = (f32[384,128]{1,0:T(8,128)S(1)}, f32[384,128]{1,0:T(8,128)S(1)}, u32[]{:S(2)}, u32[]{:S(2)}) collective-permute-start(f32[384,128]{1,0:T(8,128)S(1)} %get-tuple-element.62), channel_id=1, source_target_pairs={{0,1},{1,0},{2,3},{3,2},{4,6},{5,7},{6,4},{7,5},{8,9},{9,8},{10,11... | collective-permute-start | bytes 589832 | tf_op jit(solution)/shard_map/ppermute | solution.py:40
  58.6 5.0 %collective-permute-start.18 = (f32[256,128]{1,0:T(8,128)S(1)}, f32[256,128]{1,0:T(8,128)S(1)}, u32[]{:S(2)}, u32[]{:S(2)}) collective-permute-start(f32[256,128]{1,0:T(8,128)S(1)} %add.80.one_ref.a), channel_id=1, source_target_pairs={{0,2},{1,3},{2,0},{3,1},{4,5},{5,4},{6,7},{7,6},{8,10},{9,11},{10,... | collective-permute-start | bytes 393224 | tf_op jit(solution)/shard_map/ppermute | solution.py:40
  61.0 6.9 %collective-permute-start.20 = (f32[384,128]{1,0:T(8,128)S(1)}, f32[384,128]{1,0:T(8,128)S(1)}, u32[]{:S(2)}, u32[]{:S(2)}) collective-permute-start(f32[384,128]{1,0:T(8,128)S(1)} %add.81.c), channel_id=1, source_target_pairs={{0,2},{1,3},{2,0},{3,1},{4,5},{5,4},{6,7},{7,6},{8,10},{9,11},{10,... | collective-permute-start | bytes 589832 | tf_op jit(solution)/shard_map/ppermute | solution.py:40
  69.5 1.9 %collective-permute-start.21 = (f32[64,1792]{1,0:T(8,128)S(1)}, f32[64,1792]{1,0:T(8,128)S(1)}, u32[]{:S(2)}, u32[]{:S(2)}) collective-permute-start(f32[64,1792]{1,0:T(8,128)S(1)} %get-tuple-element.68), channel_id=1, source_target_pairs={{0,4},{1,5},{2,6},{3,7},{4,0},{5,1},{6,2},{7,3},{8,12},{9,13},{10,... | collective-permute-start | bytes 1376264 | tf_op jit(solution)/shard_map/ppermute | solution.py:40
  71.6 9.3 %collective-permute-start.22 = (f32[16,2944]{1,0:T(8,128)S(1)}, f32[16,2944]{1,0:T(8,128)S(1)}, u32[]{:S(2)}, u32[]{:S(2)}) collective-permute-start(f32[16,2944]{1,0:T(8,128)S(1)} %constant_dynamic-update-slice_fusion.4), channel_id=1, source_target_pairs={{0,8},{1,9},{2,10},{3,11},{4,12},{5,13},{6,14},{7,15},{8,0},{9,1},... | collective-permute-start | bytes 565256 | tf_op jit(solution)/shard_map/ppermute | solution.py:40
  72.3 8.7 %collective-permute-start.24 = (f32[16,896]{1,0:T(8,128)S(1)}, f32[16,896]{1,0:T(8,128)S(1)}, u32[]{:S(2)}, u32[]{:S(2)}) collective-permute-start(f32[16,896]{1,0:T(8,128)S(1)} %get-tuple-element.90), channel_id=1, source_target_pairs={{0,16},{1,17},{2,18},{3,19},{4,20},{5,21},{6,22},{7,23},{8,24},{9,... | collective-permute-start | bytes 172040 | tf_op jit(solution)/shard_map/ppermute | solution.py:40
  73.8 7.2 %collective-permute-start.23 = (f32[16,896]{1,0:T(8,128)S(1)}, f32[16,896]{1,0:T(8,128)S(1)}, u32[]{:S(2)}, u32[]{:S(2)}) collective-permute-start(f32[16,896]{1,0:T(8,128)S(1)} %get-tuple-element.89), channel_id=1, source_target_pairs={{0,24},{1,25},{2,26},{3,27},{4,28},{5,29},{6,30},{7,31},{8,16},{9,... | collective-permute-start | bytes 172040 | tf_op jit(solution)/shard_map/ppermute | solution.py:40
  80.9 5.4 %collective-permute-start.25 = (f32[16,1280]{1,0:T(8,128)S(1)}, f32[16,1280]{1,0:T(8,128)S(1)}, u32[]{:S(2)}, u32[]{:S(2)}) collective-permute-start(f32[16,1280]{1,0:T(8,128)S(1)} %pad_maximum_fusion.3), channel_id=1, source_target_pairs={{0,16},{1,17},{2,18},{3,19},{4,20},{5,21},{6,22},{7,23},{8,24},{9,... | collective-permute-start | bytes 245768 | tf_op jit(solution)/shard_map/ppermute | solution.py:40
  86.4 4.5 %collective-permute-start.29 = (f32[16,512]{1,0:T(8,128)S(1)}, f32[16,512]{1,0:T(8,128)S(1)}, u32[]{:S(2)}, u32[]{:S(2)}) collective-permute-start(f32[16,512]{1,0:T(8,128)S(1)} %slice_add_fusion.7.own_ref), channel_id=1, source_target_pairs={{0,4},{1,5},{2,6},{3,7},{4,0},{5,1},{6,2},{7,3},{8,12},{9,13},{10,... | collective-permute-start | bytes 98312 | tf_op jit(solution)/shard_map/ppermute | solution.py:40
  86.4 11.8 %collective-permute-start.26 = (f32[16,1664]{1,0:T(8,128)S(1)}, f32[16,1664]{1,0:T(8,128)S(1)}, u32[]{:S(2)}, u32[]{:S(2)}) collective-permute-start(f32[16,1664]{1,0:T(8,128)S(1)} %pad_maximum_fusion.1.rest_0_), channel_id=1, source_target_pairs={{0,24},{1,25},{2,26},{3,27},{4,28},{5,29},{6,30},{7,31},{8,16},{9,... | collective-permute-start | bytes 319496 | tf_op jit(solution)/shard_map/ppermute | solution.py:40
  87.7 10.5 %collective-permute-start.27 = (f32[16,1664]{1,0:T(8,128)S(1)}, f32[16,1664]{1,0:T(8,128)S(1)}, u32[]{:S(2)}, u32[]{:S(2)}) collective-permute-start(f32[16,1664]{1,0:T(8,128)S(1)} %pad_maximum_fusion.1.rest_0_), channel_id=1, source_target_pairs={{0,16},{1,17},{2,18},{3,19},{4,20},{5,21},{6,22},{7,23},{8,24},{9,... | collective-permute-start | bytes 319496 | tf_op jit(solution)/shard_map/ppermute | solution.py:40
  87.7 8.7 %collective-permute-start.28 = (f32[16,1664]{1,0:T(8,128)S(1)}, f32[16,1664]{1,0:T(8,128)S(1)}, u32[]{:S(2)}, u32[]{:S(2)}) collective-permute-start(f32[16,1664]{1,0:T(8,128)S(1)} %pad_maximum_fusion.1.rest_0_), channel_id=1, source_target_pairs={{0,8},{1,9},{2,10},{3,11},{4,12},{5,13},{6,14},{7,15},{8,0},{9,1},... | collective-permute-start | bytes 319496 | tf_op jit(solution)/shard_map/ppermute | solution.py:40
  90.9 8.9 %collective-permute-start.30 = (f32[16,1664]{1,0:T(8,128)S(1)}, f32[16,1664]{1,0:T(8,128)S(1)}, u32[]{:S(2)}, u32[]{:S(2)}) collective-permute-start(f32[16,1664]{1,0:T(8,128)S(1)} %pad_maximum_fusion.1.rest_0_), channel_id=1, source_target_pairs={{0,4},{1,5},{2,6},{3,7},{4,0},{5,1},{6,2},{7,3},{8,12},{9,13},{10,... | collective-permute-start | bytes 319496 | tf_op jit(solution)/shard_map/ppermute | solution.py:40
  98.2 1.6 %collective-permute-start.31 = (f32[16,1664]{1,0:T(8,128)S(1)}, f32[16,1664]{1,0:T(8,128)S(1)}, u32[]{:S(2)}, u32[]{:S(2)}) collective-permute-start(f32[16,1664]{1,0:T(8,128)S(1)} %collective-permute-done.28.rest_1_), channel_id=1, source_target_pairs={{0,4},{1,5},{2,6},{3,7},{4,0},{5,1},{6,2},{7,3},{8,12},{9,13},{10,... | collective-permute-start | bytes 319496 | tf_op jit(solution)/shard_map/ppermute | solution.py:40
  98.2 1.6 %collective-permute-start.32 = (f32[16,1664]{1,0:T(8,128)S(1)}, f32[16,1664]{1,0:T(8,128)S(1)}, u32[]{:S(2)}, u32[]{:S(2)}) collective-permute-start(f32[16,1664]{1,0:T(8,128)S(1)} %collective-permute-done.27.rest_2_), channel_id=1, source_target_pairs={{0,4},{1,5},{2,6},{3,7},{4,0},{5,1},{6,2},{7,3},{8,12},{9,13},{10,... | collective-permute-start | bytes 319496 | tf_op jit(solution)/shard_map/ppermute | solution.py:40
  101.1 4.3 %collective-permute-start.34 = (f32[128,128]{1,0:T(8,128)S(1)}, f32[128,128]{1,0:T(8,128)S(1)}, u32[]{:S(2)}, u32[]{:S(2)}) collective-permute-start(f32[128,128]{1,0:T(8,128)S(1)} %get-tuple-element.83), channel_id=1, source_target_pairs={{0,1},{1,0},{2,3},{3,2},{4,6},{5,7},{6,4},{7,5},{8,9},{9,8},{10,11... | collective-permute-start | bytes 196616 | tf_op jit(solution)/shard_map/ppermute | solution.py:40
  105.5 4.3 %collective-permute-start.35 = (f32[128,128]{1,0:T(8,128)S(1)}, f32[128,128]{1,0:T(8,128)S(1)}, u32[]{:S(2)}, u32[]{:S(2)}) collective-permute-start(f32[128,128]{1,0:T(8,128)S(1)} %add.91.one_ref), channel_id=1, source_target_pairs={{0,2},{1,3},{2,0},{3,1},{4,5},{5,4},{6,7},{7,6},{8,10},{9,11},{10,... | collective-permute-start | bytes 196616 | tf_op jit(solution)/shard_map/ppermute | solution.py:40
  (6 other events, 18.3 us)

commit v6 on v5

--- a/solution.py
+++ b/solution.py
@@ -15,7 +15,7 @@
 TN = (((0,), (0,)), ((), ()))
 KEEP = 0.95
 PANEL = 16
-FACTOR = 1_500_000_000
+FACTOR = 20_000_000_000
 
 
 def masks_of(axis):
@@ -170,11 +170,14 @@
     rows, width = high.shape
     rank = halves[0].shape[1]
     chunk = rank // count
-    skip = sum(x.shape[0] for x in halves[::2]) - rows
-
-    def body(place_ref, a, b, c, d, high_ref, low_ref, *rest):
+
+    pairs = len(halves)
+
+    def body(place_ref, *rest):
         place = place_ref[0]
-        proj = jnp.concatenate([a[skip:, :] + b[skip:, :], c[...] + d[...]], axis=0)
+        sums = [one[...] + two[...] for one, two in zip(rest[0:pairs:2], rest[1:pairs:2])]
+        proj = jnp.concatenate(sums, axis=0)
+        high_ref, low_ref, *rest = rest[pairs:]
         left_ref = right_ref = None
         if before is not None:
             left_ref, right_ref, gram_ref, inv_ref = rest[:4]
@@ -218,20 +221,14 @@
     return call(body, "pull_keep", struct(rank // 2, width + rank), ins, flops=500_000_000, nbytes=5_000_000)
 
 
-def normal(count, place, inv, own, other, high=None, low=None):
+def normal(count, place, inv, own, other):
     rank = inv.shape[0]
     width = own[0].shape[1]
     chunk = rank // count
-    push = high is not None
-    rows = high.shape[0] if push else 0
-    cut = rank if push else 0
 
     def body(place_ref, inv_ref, *rest):
-        pieces, rest = rest[:count], rest[count:]
-        if push:
-            work_high, work_low, right_ref, one_ref, two_ref, raw_ref = rest
-        else:
-            right_ref, one_ref, raw_ref = rest
+        pieces = rest[:count]
+        right_ref, gram_ref, raw_ref = rest[count:]
         place = place_ref[0]
         for i, piece in enumerate(pieces):
             at = chunk_at(place, i % (count // 2), i >= count // 2) * chunk
@@ -245,23 +242,28 @@
             right = wide[:rank] + wide[rank:] + dot(inv_high, raw_low)
             right_ref[:, at:at + size] = right
             high, low = split(right)
-            both = jnp.concatenate([high, low], axis=0)
-            wide = dot(both, high, NT)
+            wide = dot(jnp.concatenate([high, low], axis=0), high, NT)
             gram = gram + (wide[:rank] + wide[rank:] + dot(high, low, NT))
-        one_ref[:rank, :] = gram
-        if push:
-            image = None
-            for at, size in tiles(width):
-                right_high, right_low = split(right_ref[:, at:at + size])
-                wide = dot(work_high[:, at:at + size], jnp.concatenate([right_high, right_low], axis=0), NT)
-                part = wide[:, :rank] + wide[:, rank:] + dot(work_low[:, at:at + size], right_high, NT)
-                image = part if image is None else image + part
-            one_ref[rank:, :] = image[:cut]
-            two_ref[...] = image[cut:]
-
-    ins = [place, inv, *own, *other] + ([high, low] if push else [])
-    out = [struct(rank, width), struct(rank + cut, rank)] + ([struct(rows - cut, rank)] if push else [])
-    return call(body, "normal", out, ins, [pltpu.VMEM((rank, width), F32)], flops=1_000_000_000, nbytes=5_000_000)
+        gram_ref[...] = gram
+
+    return call(body, "normal", [struct(rank, width), struct(rank, rank)], [place, inv, *own, *other],
+                [pltpu.VMEM((rank, width), F32)], flops=500_000_000, nbytes=2_000_000)
+
+
+def push(high, low, right):
+    rows, width = high.shape
+    rank = right.shape[0]
+
+    def body(high_ref, low_ref, right_ref, out_ref):
+        image = None
+        for at, size in tiles(width):
+            right_high, right_low = split(right_ref[:, at:at + size])
+            wide = dot(high_ref[:, at:at + size], jnp.concatenate([right_high, right_low], axis=0), NT)
+            part = wide[:, :rank] + wide[:, rank:] + dot(low_ref[:, at:at + size], right_high, NT)
+            image = part if image is None else image + part
+        out_ref[...] = image
+
+    return call(body, "push", struct(rows, rank), [high, low, right], flops=1_000_000_000, nbytes=5_000_000)
 
 
 def left_of(proj, inv, before=None, scale=None):
@@ -346,25 +348,25 @@
     )(base, left, right, *more)
 
 
-def eliminate(full, first):
+def eliminate(full, first, size):
     rank = full.shape[1]
-    groups = PANEL // 8
+    groups = size // 8
     sub = lax.broadcasted_iota(jnp.int32, (8, rank), 0)
     lane = lax.broadcasted_iota(jnp.int32, (8, rank), 1)
     rolled = pltpu.roll(full, lax.rem(rank - first, rank), 1)
     rows = [full[8 * g:8 * g + 8] for g in range(groups)]
     cols = [
-        [jnp.broadcast_to(rolled[8 * g:8 * g + 8, j:j + 1], (8, rank)) for g in range(groups)] for j in range(PANEL)
+        [jnp.broadcast_to(rolled[8 * g:8 * g + 8, j:j + 1], (8, rank)) for g in range(groups)] for j in range(size)
     ]
 
     def spread(x, j):
         return jnp.broadcast_to(x[j // 8][j % 8:j % 8 + 1], (8, rank))
 
     pivot = spread(cols[0], 0)
-    for j in range(PANEL):
+    for j in range(size):
         at = j // 8
         root = lax.rsqrt(pivot)
-        if j + 1 < PANEL:
+        if j + 1 < size:
             above = spread(cols[j + 1], j) * root
             pivot = spread(cols[j + 1], j + 1) - above * above
         below = sub > j % 8
@@ -379,7 +381,7 @@
             rest = rest - mult * row
             rows[g] = jnp.where(sub == j % 8, row, rest) if g == at else rest
             cols[j][g] = mult
-        for k in range(j + 1, PANEL):
+        for k in range(j + 1, size):
             across = spread(cols[k], j) * root
             for g in range(at, groups):
                 cols[k][g] = cols[k][g] - cols[j][g] * across
@@ -393,29 +395,29 @@
     return high, middle, (rest - middle.astype(F32)).astype(BF16)
 
 
-def factor_panels(state_ref):
+def factor_panels(state_ref, size=PANEL):
     rank = state_ref.shape[0]
     row = lax.broadcasted_iota(jnp.int32, (rank, rank), 0)
     col = lax.broadcasted_iota(jnp.int32, (rank, rank), 1)
-    sub = lax.broadcasted_iota(jnp.int32, (PANEL, rank), 0)
-    lane = lax.broadcasted_iota(jnp.int32, (PANEL, rank), 1)
+    sub = lax.broadcasted_iota(jnp.int32, (size, rank), 0)
+    lane = lax.broadcasted_iota(jnp.int32, (size, rank), 1)
 
     def panel(p, carry):
-        first = pl.multiple_of(p * PANEL, PANEL)
-        done = eliminate(state_ref[pl.ds(first, PANEL), :], first)
-        lower = jnp.where((lane > first + sub) & (lane < first + PANEL), 0.0, done)
+        first = pl.multiple_of(p * size, size)
+        done = eliminate(state_ref[pl.ds(first, size), :], first, size)
+        lower = jnp.where((lane > first + sub) & (lane < first + size), 0.0, done)
         a, b, c = thirds(done)
         d, e, f = thirds(lower)
         step = dot(
             jnp.concatenate([a, a, b, b, a, c], axis=0), jnp.concatenate([d, e, d, e, f, d], axis=0), TN
         )
         old = state_ref[...]
-        fresh = jnp.where((col >= first) & (col < first + PANEL), 0.0, old) - step
-        state_ref[...] = jnp.where(row >= first + PANEL, fresh, old)
-        state_ref[pl.ds(first, PANEL), :] = done
+        fresh = jnp.where((col >= first) & (col < first + size), 0.0, old) - step
+        state_ref[...] = jnp.where(row >= first + size, fresh, old)
+        state_ref[pl.ds(first, size), :] = done
         return carry
 
-    lax.fori_loop(0, rank // PANEL, panel, 0)
+    lax.fori_loop(0, rank // size, panel, 0)
 
 
 def factor_left(count, place, own, other):
@@ -426,7 +428,7 @@
         for t in range(count // 2):
             for ref, at in ((own_ref, 2 * t + core), (other_ref, 2 * t + 1 - core)):
                 out_ref[pl.ds(pl.multiple_of(at * chunk, chunk), chunk), :] = ref[:, t * rank:(t + 1) * rank]
-        factor_panels(out_ref)
+        factor_panels(out_ref, 32)
         out_ref[...] = lower_part(out_ref[...])
 
     return call(body, "factor", struct(rank, rank), [place, own, other], flops=2 * FACTOR, nbytes=131072)
@@ -463,18 +465,37 @@
 
 
 def last_factor(one, two, high, low, scale):
-    def body(one_ref, two_ref, high_ref, low_ref, out_ref, state_ref):
-        rank = state_ref.shape[0]
+    width, rank = high.shape
+    steps = 4
+    block = width // steps
+
+    def body(one_ref, two_ref, high_ref, low_ref, out_ref, state_ref, stage_ref, sems):
         state_ref[...] = one_ref[...] + two_ref[...]
         factor_panels(state_ref)
         inv_high, inv_low = split(scale * lower_part(state_ref[...]))
         both = jnp.concatenate([inv_high, inv_low], axis=0)
-        wide = dot(high_ref[...], both, NT)
-        out_ref[...] = wide[:, :rank] + wide[:, rank:] + dot(low_ref[...], inv_high, NT)
-
-    width, rank = high.shape
-    return call(body, "last_factor", struct(width, rank), [one, two, high, low], [pltpu.VMEM((rank, rank), F32)],
-                flops=2 * FACTOR, nbytes=2_000_000)
+        copies = []
+        for i in range(steps):
+            row = slice(i * block, (i + 1) * block)
+            wide = dot(high_ref[row, :], both, NT)
+            stage_ref[row, :] = wide[:, :rank] + wide[:, rank:] + dot(low_ref[row, :], inv_high, NT)
+            at = pl.ds(i * block, block)
+            copy = pltpu.make_async_copy(stage_ref.at[at], out_ref.at[at], sems.at[i])
+            copy.start()
+            copies.append(copy)
+        for copy in copies:
+            copy.wait()
+
+    return pl.pallas_call(
+        body,
+        in_specs=[VMEM] * 4,
+        out_specs=pl.BlockSpec(memory_space=pltpu.HBM),
+        out_shape=struct(width, rank),
+        scratch_shapes=[pltpu.VMEM((rank, rank), F32), pltpu.VMEM((width, rank), F32), pltpu.SemaphoreType.DMA((steps,))],
+        name="last_factor",
+        compiler_params=pltpu.CompilerParams(vmem_limit_bytes=24 * 2**20),
+        cost_estimate=pl.CostEstimate(flops=2 * FACTOR, bytes_accessed=2_000_000, transcendentals=0),
+    )(one, two, high, low)
 
 
 def sum_cols(parts):
@@ -493,33 +514,18 @@
     width = x.shape[1] - rank
     chunk = rank // count
     slots = count // 2
-    cut = width // rank // 2 * rank
-    cut = width - cut
     parts = [x[i * chunk:(i + 1) * chunk] for i in range(slots)]
     gram = jnp.concatenate([part[:, width:] for part in parts], axis=1)
-    stepped = {i: part[:, cut:width] for i, part in enumerate(parts)}
-    own = parts[0][:, :cut]
-    straight = {}
-    bit = 1
-    while bit < slots:
-        sent = [i for i in stepped if i & bit]
-        kept = [i for i in stepped if not i & bit]
-        cols = [stepped[i] for i in sent] + [gram]
-        first = [parts[1][:, :cut]] if bit == 1 else []
-        got = swap(jnp.concatenate(first + cols, axis=1), "row", 2 * bit, 2 * bit)
-        if bit == 1:
-            straight[1], got = got[:, :cut], got[:, cut:]
-            for i in reversed(range(2, slots)):
-                straight[i] = swap(parts[i][:, :cut], "row", 2 * i, 2 * i)
-            if beside is not None:
-                got, beside = lax.optimization_barrier((got, beside))
-        size = width - cut
-        stepped = {i: stepped[i] + got[:, n * size:(n + 1) * size] for n, i in enumerate(kept)}
-        gram = gram + got[:, len(kept) * size:]
-        bit *= 2
-    for i in straight:
-        own = own + straight[i]
-    own = jnp.concatenate([own, stepped[0]], axis=1)
+    got = swap(jnp.concatenate([parts[1][:, :width], gram], axis=1), "row", 2, 2)
+    gots = [swap(parts[i][:, :width], "row", 2 * i, 2 * i) for i in range(2, slots)]
+    gram = gram + got[:, width:]
+    if beside is not None:
+        gram, beside = lax.optimization_barrier((gram, beside))
+    for mask in masks_of("row")[2:]:
+        gram = gram + swap(gram, "row", mask, mask)
+    own = parts[0][:, :width] + got[:, :width]
+    for got in gots:
+        own = own + got
     own, gram = lax.optimization_barrier((own, gram))
     return own, gram, swap(gram, "row", 1, 1), beside
 
@@ -552,10 +558,9 @@
     high, low, *parts = start(momentum, grad, basis)
     proj, inv, pieces, _ = left_side(sum_cols(parts))
     left_a = left_of(proj, inv)
-    right_a, *parts = normal(count, place, inv, *pieces, high, low)
-
-    halves = sum_cols(parts)
-    gram, inv = factor_right(*halves[:2])
+    right_a, gram = normal(count, place, inv, *pieces)
+    gram, inv = factor_right(*sum_cols([gram]))
+    halves = sum_cols([push(high, low, right_a)])
 
     beside = (lambda left: deflate(momentum, grad, left, right_a)), left_a
     proj, inv, pieces, base = left_side(halves, (left_a, right_a, gram, inv), beside)

time: 116 us -> 116 us (level)
    pallas_call x0 -> x1, Pallas kernels: none -> 5.45 us  [last_factor(): pl.pallas_call(body, in_specs=[VMEM] * 4, out_specs=pl.BlockSpec(memory_s...]
    pallas_call x14, Pallas kernels: 30.1 us -> 25.1 us  [call(): pl.pallas_call(body, out_shape=out, in_specs=[SMEM if x.dtype == jnp.int3...]
  transfers between devices with their start and end apart: 36 -> 36, of which waited for: 23 -> 25; matrix products, arithmetic and copies ran while one was open for 1% -> 1% of each run, Pallas kernels for 18% -> 19%
where the time goes in v6:
time: 116 us
  waiting for transfers between devices  38.4 us (33%)
  starting transfers between devices  38 us (33%)
  Pallas kernels  37.3 us (32%)
    ppermute x36, waiting for transfers between devices, swap(): return lax.ppermute(x, ('row', 'col'), pairs)  38.4 us
    ppermute x36, starting transfers between devices, swap(): return lax.ppermute(x, ('row', 'col'), pairs)  38 us
    pallas_call x14, Pallas kernels, call(): pl.pallas_call(body, out_shape=out, in_specs=[SMEM if x.dtype == jnp.int3...  25.1 us
    pallas_call x1, Pallas kernels, last_factor(): pl.pallas_call(body, in_specs=[VMEM] * 4, out_specs=pl.BlockSpec(memory_s...  5.45 us
    pallas_call x2, Pallas kernels, finish(): pl.pallas_call(body, in_specs=[VMEM] * 3 + [hbm] * len(more), out_specs=h...  3.56 us
    pallas_call x1, Pallas kernels, start(): pl.pallas_call(body, in_specs=[pl.BlockSpec(memory_space=pltpu.HBM)] * 3,...  3.21 us
  transfers between devices with their start and end apart: 36, of which 25 were waited for; matrix products, arithmetic and copies ran while one was open for 1% of the time, Pallas kernels for 19%

profile of v6, /device:TPU:0, one launch (start us, length us, event | category | flops | bytes accessed | tf_op | source)
XLA Modules:
  0.0 115.9 jit_solution(13940463618190568296)
XLA Ops:
  0.6 3.2 %start.1 = (bf16[512,1664]{1,0:T(8,128)(2,1)S(1)}, bf16[512,1664]{1,0:T(8,128)(2,1)S(1)}, f32[256,128]{1,0:T(8,128)S(1)}, f32[256,128]{1,0:T(8,128)S(1)}) custom-call(f32[512,1664]{1,0:T(8,128)} %momentum_ref.1, bf16[512,1664]{1,0:T(8,128)(2,1)} %grad_ref.1, f32[1664,128]{1,0:T(8,128)} %basis_hbm.1), custom_call_target="tpu_custom_call" | custom-call | tf_op jit(solution)/shard_map/start/pallas_call | solution.py:123
  3.8 3.0 %collective-permute-start = (f32[256,128]{1,0:T(8,128)S(1)}, f32[256,128]{1,0:T(8,128)S(1)}, u32[]{:S(2)}, u32[]{:S(2)}) collective-permute-start(f32[256,128]{1,0:T(8,128)S(1)} %get-tuple-element.47), channel_id=1, source_target_pairs={{0,1},{1,0},{2,3},{3,2},{4,6},{5,7},{6,4},{7,5},{8,9},{9,8},{10,11... | collective-permute-start | bytes 393224 | tf_op jit(solution)/shard_map/ppermute | solution.py:40
  6.9 2.9 %collective-permute-done = f32[256,128]{1,0:T(8,128)S(1)} collective-permute-done((f32[256,128]{1,0:T(8,128)S(1)}, f32[256,128]{1,0:T(8,128)S(1)}, u32[]{:S(2)}, u32[]{:S(2)}) %collective-permute-start) | collective-permute-done | bytes 131104 | tf_op jit(solution)/shard_map/ppermute | solution.py:40
  9.8 2.1 %collective-permute-start.1 = (f32[256,128]{1,0:T(8,128)S(1)}, f32[256,128]{1,0:T(8,128)}, u32[]{:S(2)}, u32[]{:S(2)}) collective-permute-start(f32[256,128]{1,0:T(8,128)S(1)} %add.51.rest_0_), channel_id=1, source_target_pairs={{0,2},{1,3},{2,0},{3,1},{4,5},{5,4},{6,7},{7,6},{8,10},{9,11},{10,... | collective-permute-start | bytes 393224 | tf_op jit(solution)/shard_map/ppermute | solution.py:40
  15.0 2.9 %collective-permute-done.3.rest_3_ = f32[256,128]{1,0:T(8,128)} collective-permute-done((f32[256,128]{1,0:T(8,128)}, f32[256,128]{1,0:T(8,128)}, u32[]{:S(2)}, u32[]{:S(2)}) %collective-permute-start.3) | collective-permute-done | bytes 131104 | tf_op jit(solution)/shard_map/ppermute | solution.py:40
  17.9 1.9 %pull_send.2 = (f32[512,128]{1,0:T(8,128)S(1)}, f32[64,512]{1,0:T(8,128)S(1)}, f32[64,1792]{1,0:T(8,128)S(1)}) custom-call(s32[1]{0:T(128)} %bitcast.place_ref, f32[256,128]{1,0:T(8,128)S(1)} %add.51.rest_0_, f32[256,128]{1,0:T(8,128)} %collective-permute-done.1.rest_1_, f32[256,128]{1,0:T(8,128)} %add.52.rest_2_, ...), custom_call_target="tpu_custom_call" | custom-call | flops 500000000 | bytes 5000000 | tf_op jit(solution)/shard_map/pull_send/pallas_call | solution.py:75
  21.8 1.6 %collective-permute-start.5 = (f32[16,2176]{1,0:T(8,128)S(1)}, f32[16,2176]{1,0:T(8,128)S(1)}, u32[]{:S(2)}, u32[]{:S(2)}) collective-permute-start(f32[16,2176]{1,0:T(8,128)S(1)} %constant_dynamic-update-slice_fusion), channel_id=1, source_target_pairs={{0,8},{1,9},{2,10},{3,11},{4,12},{5,13},{6,14},{7,15},{8,0},{9,1},... | collective-permute-start | bytes 417800 | tf_op jit(solution)/shard_map/ppermute | solution.py:40
  23.4 2.5 %collective-permute-start.7 = (f32[16,1664]{1,0:T(8,128)S(1)}, f32[16,1664]{1,0:T(8,128)S(1)}, u32[]{:S(2)}, u32[]{:S(2)}) collective-permute-start(f32[16,1664]{1,0:T(8,128)S(1)} %get-tuple-element.101), channel_id=1, source_target_pairs={{0,24},{1,25},{2,26},{3,27},{4,28},{5,29},{6,30},{7,31},{8,16},{9,... | collective-permute-start | bytes 319496 | tf_op jit(solution)/shard_map/ppermute | solution.py:40
  26.0 1.6 %collective-permute-done.5 = f32[16,2176]{1,0:T(8,128)S(1)} collective-permute-done((f32[16,2176]{1,0:T(8,128)S(1)}, f32[16,2176]{1,0:T(8,128)S(1)}, u32[]{:S(2)}, u32[]{:S(2)}) %collective-permute-start.5) | collective-permute-done | bytes 139296 | tf_op jit(solution)/shard_map/ppermute | solution.py:40
  27.6 3.6 %collective-permute-start.8 = (f32[16,512]{1,0:T(8,128)S(1)}, f32[16,512]{1,0:T(8,128)S(1)}, u32[]{:S(2)}, u32[]{:S(2)}) collective-permute-start(f32[16,512]{1,0:T(8,128)S(1)} %slice_add_fusion.3), channel_id=1, source_target_pairs={{0,16},{1,17},{2,18},{3,19},{4,20},{5,21},{6,22},{7,23},{8,24},{9,... | collective-permute-start | bytes 98312 | tf_op jit(solution)/shard_map/ppermute | solution.py:40
  31.1 1.6 %collective-permute-done.7 = f32[16,1664]{1,0:T(8,128)S(1)} collective-permute-done((f32[16,1664]{1,0:T(8,128)S(1)}, f32[16,1664]{1,0:T(8,128)S(1)}, u32[]{:S(2)}, u32[]{:S(2)}) %collective-permute-start.7) | collective-permute-done | bytes 106528 | tf_op jit(solution)/shard_map/ppermute | solution.py:40
  32.8 4.1 %collective-permute-done.6 = f32[16,1664]{1,0:T(8,128)S(1)} collective-permute-done((f32[16,1664]{1,0:T(8,128)S(1)}, f32[16,1664]{1,0:T(8,128)S(1)}, u32[]{:S(2)}, u32[]{:S(2)}) %collective-permute-start.6) | collective-permute-done | bytes 106528 | tf_op jit(solution)/shard_map/ppermute | solution.py:40
  37.3 2.7 %collective-permute-start.9 = (f32[16,1664]{1,0:T(8,128)S(1)}, f32[16,1664]{1,0:T(8,128)S(1)}, u32[]{:S(2)}, u32[]{:S(2)}) collective-permute-start(f32[16,1664]{1,0:T(8,128)S(1)} %fusion.3.rest_0_), channel_id=1, source_target_pairs={{0,24},{1,25},{2,26},{3,27},{4,28},{5,29},{6,30},{7,31},{8,16},{9,... | collective-permute-start | bytes 319496 | tf_op jit(solution)/shard_map/ppermute | solution.py:40
  40.0 1.7 %collective-permute-start.11 = (f32[16,1664]{1,0:T(8,128)S(1)}, f32[16,1664]{1,0:T(8,128)S(1)}, u32[]{:S(2)}, u32[]{:S(2)}) collective-permute-start(f32[16,1664]{1,0:T(8,128)S(1)} %fusion.3.rest_0_), channel_id=1, source_target_pairs={{0,8},{1,9},{2,10},{3,11},{4,12},{5,13},{6,14},{7,15},{8,0},{9,1},... | collective-permute-start | bytes 319496 | tf_op jit(solution)/shard_map/ppermute | solution.py:40
  41.7 4.7 %factor.3.inv_ref = f32[128,128]{1,0:T(8,128)S(1)} custom-call(s32[1]{0:T(128)} %bitcast.place_ref, f32[16,512]{1,0:T(8,128)S(1)} %add.58.own_ref, f32[16,512]{1,0:T(8,128)S(1)} %collective-permute-done.12.other_ref), custom_call_target="tpu_custom_call" | custom-call | flops 40000000000 | bytes 131072 | tf_op jit(solution)/shard_map/factor/pallas_call | solution.py:75
  47.4 1.6 %collective-permute-done.10.rest_2_ = f32[16,1664]{1,0:T(8,128)S(1)} collective-permute-done((f32[16,1664]{1,0:T(8,128)S(1)}, f32[16,1664]{1,0:T(8,128)S(1)}, u32[]{:S(2)}, u32[]{:S(2)}) %collective-permute-start.10) | collective-permute-done | bytes 106528 | tf_op jit(solution)/shard_map/ppermute | solution.py:40
  53.0 1.6 %collective-permute-start.17 = (f32[512,128]{1,0:T(8,128)S(1)}, f32[512,128]{1,0:T(8,128)S(1)}, u32[]{:S(2)}, u32[]{:S(2)}) collective-permute-start(f32[512,128]{1,0:T(8,128)S(1)} %push.1), channel_id=1, source_target_pairs={{0,1},{1,0},{2,3},{3,2},{4,6},{5,7},{6,4},{7,5},{8,9},{9,8},{10,11... | collective-permute-start | bytes 786440 | tf_op jit(solution)/shard_map/ppermute | solution.py:40
  55.1 5.0 %collective-permute-done.19 = f32[128,128]{1,0:T(8,128)S(1)} collective-permute-done((f32[128,128]{1,0:T(8,128)S(1)}, f32[128,128]{1,0:T(8,128)S(1)}, u32[]{:S(2)}, u32[]{:S(2)}) %collective-permute-start.19) | collective-permute-done | bytes 65568 | tf_op jit(solution)/shard_map/ppermute | solution.py:40
  62.7 1.8 %collective-permute-done.20.two_ref = f32[128,128]{1,0:T(8,128)S(1)} collective-permute-done((f32[128,128]{1,0:T(8,128)S(1)}, f32[128,128]{1,0:T(8,128)S(1)}, u32[]{:S(2)}, u32[]{:S(2)}) %collective-permute-start.20) | collective-permute-done | bytes 65568 | tf_op jit(solution)/shard_map/ppermute | solution.py:40
  64.5 4.2 %factor.4 = (f32[128,128]{1,0:T(8,128)S(1)}, f32[128,128]{1,0:T(8,128)S(1)}) custom-call(f32[128,128]{1,0:T(8,128)S(1)} %add.60.one_ref, f32[128,128]{1,0:T(8,128)S(1)} %collective-permute-done.20.two_ref), custom_call_target="tpu_custom_call" | custom-call | flops 40000000000 | bytes 131072 | tf_op jit(solution)/shard_map/factor/pallas_call | solution.py:75
  68.8 1.6 %pull_send.3 = (f32[512,128]{1,0:T(8,128)S(1)}, f32[64,512]{1,0:T(8,128)S(1)}, f32[64,1792]{1,0:T(8,128)S(1)}) custom-call(s32[1]{0:T(128)} %bitcast.place_ref, f32[512,128]{1,0:T(8,128)S(1)} %add.59.rest_0_, f32[512,128]{1,0:T(8,128)S(1)} %collective-permute-done.18.rest_1_, bf16[512,1664]{1,0:T(8,128)(2,1)S(1)} %get-tuple-element.45.rest_4_.high_ref.rest_2_, ...), custom_call_target="tpu_custom_call" | custom-call | flops 500000000 | bytes 5000000 | tf_op jit(solution)/shard_map/pull_send/pallas_call | solution.py:75
  73.4 1.8 %collective-permute-start.24 = (f32[16,1664]{1,0:T(8,128)S(1)}, f32[16,1664]{1,0:T(8,128)S(1)}, u32[]{:S(2)}, u32[]{:S(2)}) collective-permute-start(f32[16,1664]{1,0:T(8,128)S(1)} %get-tuple-element.88), channel_id=1, source_target_pairs={{0,24},{1,25},{2,26},{3,27},{4,28},{5,29},{6,30},{7,31},{8,16},{9,... | collective-permute-start | bytes 319496 | tf_op jit(solution)/shard_map/ppermute | solution.py:40
  78.2 2.6 %collective-permute-start.25 = (f32[16,512]{1,0:T(8,128)S(1)}, f32[16,512]{1,0:T(8,128)S(1)}, u32[]{:S(2)}, u32[]{:S(2)}) collective-permute-start(f32[16,512]{1,0:T(8,128)S(1)} %slice_add_fusion.2), channel_id=1, source_target_pairs={{0,16},{1,17},{2,18},{3,19},{4,20},{5,21},{6,22},{7,23},{8,24},{9,... | collective-permute-start | bytes 98312 | tf_op jit(solution)/shard_map/ppermute | solution.py:40
  82.0 4.6 %collective-permute-done.23 = f32[16,1664]{1,0:T(8,128)S(1)} collective-permute-done((f32[16,1664]{1,0:T(8,128)S(1)}, f32[16,1664]{1,0:T(8,128)S(1)}, u32[]{:S(2)}, u32[]{:S(2)}) %collective-permute-start.23) | collective-permute-done | bytes 106528 | tf_op jit(solution)/shard_map/ppermute | solution.py:40
  86.9 2.7 %collective-permute-start.26 = (f32[16,1664]{1,0:T(8,128)S(1)}, f32[16,1664]{1,0:T(8,128)S(1)}, u32[]{:S(2)}, u32[]{:S(2)}) collective-permute-start(f32[16,1664]{1,0:T(8,128)S(1)} %fusion.1.rest_0_), channel_id=1, source_target_pairs={{0,24},{1,25},{2,26},{3,27},{4,28},{5,29},{6,30},{7,31},{8,16},{9,... | collective-permute-start | bytes 319496 | tf_op jit(solution)/shard_map/ppermute | solution.py:40
  89.6 1.7 %collective-permute-start.28 = (f32[16,1664]{1,0:T(8,128)S(1)}, f32[16,1664]{1,0:T(8,128)S(1)}, u32[]{:S(2)}, u32[]{:S(2)}) collective-permute-start(f32[16,1664]{1,0:T(8,128)S(1)} %fusion.1.rest_0_), channel_id=1, source_target_pairs={{0,8},{1,9},{2,10},{3,11},{4,12},{5,13},{6,14},{7,15},{8,0},{9,1},... | collective-permute-start | bytes 319496 | tf_op jit(solution)/shard_map/ppermute | solution.py:40
  91.4 4.5 %factor.5.inv_ref = f32[128,128]{1,0:T(8,128)S(1)} custom-call(s32[1]{0:T(128)} %bitcast.place_ref, f32[16,512]{1,0:T(8,128)S(1)} %add.66.own_ref, f32[16,512]{1,0:T(8,128)S(1)} %collective-permute-done.29.other_ref), custom_call_target="tpu_custom_call" | custom-call | flops 40000000000 | bytes 131072 | tf_op jit(solution)/shard_map/factor/pallas_call | solution.py:75
  97.1 1.6 %collective-permute-done.27.rest_2_ = f32[16,1664]{1,0:T(8,128)S(1)} collective-permute-done((f32[16,1664]{1,0:T(8,128)S(1)}, f32[16,1664]{1,0:T(8,128)S(1)}, u32[]{:S(2)}, u32[]{:S(2)}) %collective-permute-start.27) | collective-permute-done | bytes 106528 | tf_op jit(solution)/shard_map/ppermute | solution.py:40
  101.6 1.6 %collective-permute-start.34 = (f32[128,128]{1,0:T(8,128)S(1)}, f32[128,128]{1,0:T(8,128)S(1)}, u32[]{:S(2)}, u32[]{:S(2)}) collective-permute-start(f32[128,128]{1,0:T(8,128)S(1)} %get-tuple-element.81), channel_id=1, source_target_pairs={{0,1},{1,0},{2,3},{3,2},{4,6},{5,7},{6,4},{7,5},{8,9},{9,8},{10,11... | collective-permute-start | bytes 196616 | tf_op jit(solution)/shard_map/ppermute | solution.py:40
  103.5 1.8 %finish.2.rest_0_ = f32[512,1664]{1,0:T(8,128)} custom-call(f32[512,1664]{1,0:T(8,128)S(1)} %deflate.1.base_ref, f32[512,128]{1,0:T(8,128)S(1)} %get-tuple-element.76.left_ref, f32[128,1664]{1,0:T(8,128)S(1)} %get-tuple-element.80.right_ref), custom_call_target="tpu_custom_call" | custom-call | flops 800000000 | bytes 6000000 | tf_op jit(solution)/shard_map/finish/pallas_call | solution.py:337
  107.4 1.8 %finish.3 = f32[512,1664]{1,0:T(8,128)} custom-call(f32[512,1664]{1,0:T(8,128)S(1)} %deflate.1.base_ref, f32[512,128]{1,0:T(8,128)S(1)} %get-tuple-element.76.left_ref, f32[128,1664]{1,0:T(8,128)S(1)} %get-tuple-element.80.right_ref, f32[512,1664]{1,0:T(8,128)} %finish.2.rest_0_), custom_call_target="tpu_custom_call", output_to_operand_aliasing={{}: (3, {})} | custom-call | flops 800000000 | bytes 6000000 | tf_op jit(solution)/shard_map/finish/pallas_call | solution.py:337
  110.3 5.5 %last_factor.1 = f32[1664,128]{1,0:T(8,128)} custom-call(f32[128,128]{1,0:T(8,128)S(1)} %add.67.one_ref, f32[128,128]{1,0:T(8,128)S(1)} %collective-permute-done.35.two_ref, bf16[1664,128]{1,0:T(8,128)(2,1)S(1)} %get-tuple-element.85.high_ref, bf16[1664,128]{1,0:T(8,128)(2,1)S(1)} %get-tuple-element.86.low_ref), custom_call_target="tpu_custom_call" | custom-call | flops 40000000000 | bytes 2000000 | tf_op jit(solution)/shard_map/last_factor/pallas_call | solution.py:489
  (85 shorter events, 28.5 us)
Async XLA Ops:
  3.8 6.0 %collective-permute-start = (f32[256,128]{1,0:T(8,128)S(1)}, f32[256,128]{1,0:T(8,128)S(1)}, u32[]{:S(2)}, u32[]{:S(2)}) collective-permute-start(f32[256,128]{1,0:T(8,128)S(1)} %get-tuple-element.47), channel_id=1, source_target_pairs={{0,1},{1,0},{2,3},{3,2},{4,6},{5,7},{6,4},{7,5},{8,9},{9,8},{10,11... | collective-permute-start | bytes 393224 | tf_op jit(solution)/shard_map/ppermute | solution.py:40
  6.8 5.1 %collective-permute-start.2 = (f32[256,128]{1,0:T(8,128)S(1)}, f32[256,128]{1,0:T(8,128)S(1)}, u32[]{:S(2)}, u32[]{:S(2)}) collective-permute-start(f32[256,128]{1,0:T(8,128)S(1)} %get-tuple-element.48), channel_id=1, source_target_pairs={{0,1},{1,0},{2,3},{3,2},{4,6},{5,7},{6,4},{7,5},{8,9},{9,8},{10,11... | collective-permute-start | bytes 393224 | tf_op jit(solution)/shard_map/ppermute | solution.py:40
  9.8 5.2 %collective-permute-start.1 = (f32[256,128]{1,0:T(8,128)S(1)}, f32[256,128]{1,0:T(8,128)}, u32[]{:S(2)}, u32[]{:S(2)}) collective-permute-start(f32[256,128]{1,0:T(8,128)S(1)} %add.51.rest_0_), channel_id=1, source_target_pairs={{0,2},{1,3},{2,0},{3,1},{4,5},{5,4},{6,7},{7,6},{8,10},{9,11},{10,... | collective-permute-start | bytes 393224 | tf_op jit(solution)/shard_map/ppermute | solution.py:40
  12.6 5.3 %collective-permute-start.3 = (f32[256,128]{1,0:T(8,128)}, f32[256,128]{1,0:T(8,128)}, u32[]{:S(2)}, u32[]{:S(2)}) collective-permute-start(f32[256,128]{1,0:T(8,128)} %add.52.rest_2_), channel_id=1, source_target_pairs={{0,2},{1,3},{2,0},{3,1},{4,5},{5,4},{6,7},{7,6},{8,10},{9,11},{10,... | collective-permute-start | bytes 393224 | tf_op jit(solution)/shard_map/ppermute | solution.py:40
  19.8 1.9 %collective-permute-start.4 = (f32[64,1792]{1,0:T(8,128)S(1)}, f32[64,1792]{1,0:T(8,128)S(1)}, u32[]{:S(2)}, u32[]{:S(2)}) collective-permute-start(f32[64,1792]{1,0:T(8,128)S(1)} %get-tuple-element.51), channel_id=1, source_target_pairs={{0,4},{1,5},{2,6},{3,7},{4,0},{5,1},{6,2},{7,3},{8,12},{9,13},{10,... | collective-permute-start | bytes 1376264 | tf_op jit(solution)/shard_map/ppermute | solution.py:40
  21.8 5.8 %collective-permute-start.5 = (f32[16,2176]{1,0:T(8,128)S(1)}, f32[16,2176]{1,0:T(8,128)S(1)}, u32[]{:S(2)}, u32[]{:S(2)}) collective-permute-start(f32[16,2176]{1,0:T(8,128)S(1)} %constant_dynamic-update-slice_fusion), channel_id=1, source_target_pairs={{0,8},{1,9},{2,10},{3,11},{4,12},{5,13},{6,14},{7,15},{8,0},{9,1},... | collective-permute-start | bytes 417800 | tf_op jit(solution)/shard_map/ppermute | solution.py:40
  23.4 9.3 %collective-permute-start.7 = (f32[16,1664]{1,0:T(8,128)S(1)}, f32[16,1664]{1,0:T(8,128)S(1)}, u32[]{:S(2)}, u32[]{:S(2)}) collective-permute-start(f32[16,1664]{1,0:T(8,128)S(1)} %get-tuple-element.101), channel_id=1, source_target_pairs={{0,24},{1,25},{2,26},{3,27},{4,28},{5,29},{6,30},{7,31},{8,16},{9,... | collective-permute-start | bytes 319496 | tf_op jit(solution)/shard_map/ppermute | solution.py:40
  25.9 11.0 %collective-permute-start.6 = (f32[16,1664]{1,0:T(8,128)S(1)}, f32[16,1664]{1,0:T(8,128)S(1)}, u32[]{:S(2)}, u32[]{:S(2)}) collective-permute-start(f32[16,1664]{1,0:T(8,128)S(1)} %get-tuple-element.102), channel_id=1, source_target_pairs={{0,16},{1,17},{2,18},{3,19},{4,20},{5,21},{6,22},{7,23},{8,24},{9,... | collective-permute-start | bytes 319496 | tf_op jit(solution)/shard_map/ppermute | solution.py:40
  27.6 9.7 %collective-permute-start.8 = (f32[16,512]{1,0:T(8,128)S(1)}, f32[16,512]{1,0:T(8,128)S(1)}, u32[]{:S(2)}, u32[]{:S(2)}) collective-permute-start(f32[16,512]{1,0:T(8,128)S(1)} %slice_add_fusion.3), channel_id=1, source_target_pairs={{0,16},{1,17},{2,18},{3,19},{4,20},{5,21},{6,22},{7,23},{8,24},{9,... | collective-permute-start | bytes 98312 | tf_op jit(solution)/shard_map/ppermute | solution.py:40
  37.3 4.5 %collective-permute-start.12 = (f32[16,512]{1,0:T(8,128)S(1)}, f32[16,512]{1,0:T(8,128)S(1)}, u32[]{:S(2)}, u32[]{:S(2)}) collective-permute-start(f32[16,512]{1,0:T(8,128)S(1)} %add.58.own_ref), channel_id=1, source_target_pairs={{0,4},{1,5},{2,6},{3,7},{4,0},{5,1},{6,2},{7,3},{8,12},{9,13},{10,... | collective-permute-start | bytes 98312 | tf_op jit(solution)/shard_map/ppermute | solution.py:40
  37.3 11.7 %collective-permute-start.9 = (f32[16,1664]{1,0:T(8,128)S(1)}, f32[16,1664]{1,0:T(8,128)S(1)}, u32[]{:S(2)}, u32[]{:S(2)}) collective-permute-start(f32[16,1664]{1,0:T(8,128)S(1)} %fusion.3.rest_0_), channel_id=1, source_target_pairs={{0,24},{1,25},{2,26},{3,27},{4,28},{5,29},{6,30},{7,31},{8,16},{9,... | collective-permute-start | bytes 319496 | tf_op jit(solution)/shard_map/ppermute | solution.py:40
  40.0 9.0 %collective-permute-start.10 = (f32[16,1664]{1,0:T(8,128)S(1)}, f32[16,1664]{1,0:T(8,128)S(1)}, u32[]{:S(2)}, u32[]{:S(2)}) collective-permute-start(f32[16,1664]{1,0:T(8,128)S(1)} %fusion.3.rest_0_), channel_id=1, source_target_pairs={{0,16},{1,17},{2,18},{3,19},{4,20},{5,21},{6,22},{7,23},{8,24},{9,... | collective-permute-start | bytes 319496 | tf_op jit(solution)/shard_map/ppermute | solution.py:40
  40.0 7.5 %collective-permute-start.11 = (f32[16,1664]{1,0:T(8,128)S(1)}, f32[16,1664]{1,0:T(8,128)S(1)}, u32[]{:S(2)}, u32[]{:S(2)}) collective-permute-start(f32[16,1664]{1,0:T(8,128)S(1)} %fusion.3.rest_0_), channel_id=1, source_target_pairs={{0,8},{1,9},{2,10},{3,11},{4,12},{5,13},{6,14},{7,15},{8,0},{9,1},... | collective-permute-start | bytes 319496 | tf_op jit(solution)/shard_map/ppermute | solution.py:40
  41.7 7.8 %collective-permute-start.13 = (f32[16,1664]{1,0:T(8,128)S(1)}, f32[16,1664]{1,0:T(8,128)S(1)}, u32[]{:S(2)}, u32[]{:S(2)}) collective-permute-start(f32[16,1664]{1,0:T(8,128)S(1)} %fusion.3.rest_0_), channel_id=1, source_target_pairs={{0,4},{1,5},{2,6},{3,7},{4,0},{5,1},{6,2},{7,3},{8,12},{9,13},{10,... | collective-permute-start | bytes 319496 | tf_op jit(solution)/shard_map/ppermute | solution.py:40
  53.0 8.9 %collective-permute-start.17 = (f32[512,128]{1,0:T(8,128)S(1)}, f32[512,128]{1,0:T(8,128)S(1)}, u32[]{:S(2)}, u32[]{:S(2)}) collective-permute-start(f32[512,128]{1,0:T(8,128)S(1)} %push.1), channel_id=1, source_target_pairs={{0,1},{1,0},{2,3},{3,2},{4,6},{5,7},{6,4},{7,5},{8,9},{9,8},{10,11... | collective-permute-start | bytes 786440 | tf_op jit(solution)/shard_map/ppermute | solution.py:40
  54.6 5.6 %collective-permute-start.19 = (f32[128,128]{1,0:T(8,128)S(1)}, f32[128,128]{1,0:T(8,128)S(1)}, u32[]{:S(2)}, u32[]{:S(2)}) collective-permute-start(f32[128,128]{1,0:T(8,128)S(1)} %get-tuple-element.61), channel_id=1, source_target_pairs={{0,1},{1,0},{2,3},{3,2},{4,6},{5,7},{6,4},{7,5},{8,9},{9,8},{10,11... | collective-permute-start | bytes 196616 | tf_op jit(solution)/shard_map/ppermute | solution.py:40
  60.2 4.3 %collective-permute-start.20 = (f32[128,128]{1,0:T(8,128)S(1)}, f32[128,128]{1,0:T(8,128)S(1)}, u32[]{:S(2)}, u32[]{:S(2)}) collective-permute-start(f32[128,128]{1,0:T(8,128)S(1)} %add.60.one_ref), channel_id=1, source_target_pairs={{0,2},{1,3},{2,0},{3,1},{4,5},{5,4},{6,7},{7,6},{8,10},{9,11},{10,... | collective-permute-start | bytes 196616 | tf_op jit(solution)/shard_map/ppermute | solution.py:40
  62.0 6.8 %collective-permute-start.18 = (f32[512,128]{1,0:T(8,128)S(1)}, f32[512,128]{1,0:T(8,128)S(1)}, u32[]{:S(2)}, u32[]{:S(2)}) collective-permute-start(f32[512,128]{1,0:T(8,128)S(1)} %add.59.rest_0_), channel_id=1, source_target_pairs={{0,2},{1,3},{2,0},{3,1},{4,5},{5,4},{6,7},{7,6},{8,10},{9,11},{10,... | collective-permute-start | bytes 786440 | tf_op jit(solution)/shard_map/ppermute | solution.py:40
  70.4 1.9 %collective-permute-start.21 = (f32[64,1792]{1,0:T(8,128)S(1)}, f32[64,1792]{1,0:T(8,128)S(1)}, u32[]{:S(2)}, u32[]{:S(2)}) collective-permute-start(f32[64,1792]{1,0:T(8,128)S(1)} %get-tuple-element.66), channel_id=1, source_target_pairs={{0,4},{1,5},{2,6},{3,7},{4,0},{5,1},{6,2},{7,3},{8,12},{9,13},{10,... | collective-permute-start | bytes 1376264 | tf_op jit(solution)/shard_map/ppermute | solution.py:40
  72.4 5.8 %collective-permute-start.22 = (f32[16,2176]{1,0:T(8,128)S(1)}, f32[16,2176]{1,0:T(8,128)S(1)}, u32[]{:S(2)}, u32[]{:S(2)}) collective-permute-start(f32[16,2176]{1,0:T(8,128)S(1)} %constant_dynamic-update-slice_fusion.4), channel_id=1, source_target_pairs={{0,8},{1,9},{2,10},{3,11},{4,12},{5,13},{6,14},{7,15},{8,0},{9,1},... | collective-permute-start | bytes 417800 | tf_op jit(solution)/shard_map/ppermute | solution.py:40
  73.4 8.6 %collective-permute-start.24 = (f32[16,1664]{1,0:T(8,128)S(1)}, f32[16,1664]{1,0:T(8,128)S(1)}, u32[]{:S(2)}, u32[]{:S(2)}) collective-permute-start(f32[16,1664]{1,0:T(8,128)S(1)} %get-tuple-element.88), channel_id=1, source_target_pairs={{0,24},{1,25},{2,26},{3,27},{4,28},{5,29},{6,30},{7,31},{8,16},{9,... | collective-permute-start | bytes 319496 | tf_op jit(solution)/shard_map/ppermute | solution.py:40
  75.2 11.4 %collective-permute-start.23 = (f32[16,1664]{1,0:T(8,128)S(1)}, f32[16,1664]{1,0:T(8,128)S(1)}, u32[]{:S(2)}, u32[]{:S(2)}) collective-permute-start(f32[16,1664]{1,0:T(8,128)S(1)} %get-tuple-element.87), channel_id=1, source_target_pairs={{0,16},{1,17},{2,18},{3,19},{4,20},{5,21},{6,22},{7,23},{8,24},{9,... | collective-permute-start | bytes 319496 | tf_op jit(solution)/shard_map/ppermute | solution.py:40
  78.2 8.7 %collective-permute-start.25 = (f32[16,512]{1,0:T(8,128)S(1)}, f32[16,512]{1,0:T(8,128)S(1)}, u32[]{:S(2)}, u32[]{:S(2)}) collective-permute-start(f32[16,512]{1,0:T(8,128)S(1)} %slice_add_fusion.2), channel_id=1, source_target_pairs={{0,16},{1,17},{2,18},{3,19},{4,20},{5,21},{6,22},{7,23},{8,24},{9,... | collective-permute-start | bytes 98312 | tf_op jit(solution)/shard_map/ppermute | solution.py:40
  86.9 4.5 %collective-permute-start.29 = (f32[16,512]{1,0:T(8,128)S(1)}, f32[16,512]{1,0:T(8,128)S(1)}, u32[]{:S(2)}, u32[]{:S(2)}) collective-permute-start(f32[16,512]{1,0:T(8,128)S(1)} %add.66.own_ref), channel_id=1, source_target_pairs={{0,4},{1,5},{2,6},{3,7},{4,0},{5,1},{6,2},{7,3},{8,12},{9,13},{10,... | collective-permute-start | bytes 98312 | tf_op jit(solution)/shard_map/ppermute | solution.py:40
  86.9 11.7 %collective-permute-start.26 = (f32[16,1664]{1,0:T(8,128)S(1)}, f32[16,1664]{1,0:T(8,128)S(1)}, u32[]{:S(2)}, u32[]{:S(2)}) collective-permute-start(f32[16,1664]{1,0:T(8,128)S(1)} %fusion.1.rest_0_), channel_id=1, source_target_pairs={{0,24},{1,25},{2,26},{3,27},{4,28},{5,29},{6,30},{7,31},{8,16},{9,... | collective-permute-start | bytes 319496 | tf_op jit(solution)/shard_map/ppermute | solution.py:40
  89.6 9.0 %collective-permute-start.27 = (f32[16,1664]{1,0:T(8,128)S(1)}, f32[16,1664]{1,0:T(8,128)S(1)}, u32[]{:S(2)}, u32[]{:S(2)}) collective-permute-start(f32[16,1664]{1,0:T(8,128)S(1)} %fusion.1.rest_0_), channel_id=1, source_target_pairs={{0,16},{1,17},{2,18},{3,19},{4,20},{5,21},{6,22},{7,23},{8,24},{9,... | collective-permute-start | bytes 319496 | tf_op jit(solution)/shard_map/ppermute | solution.py:40
  89.6 7.5 %collective-permute-start.28 = (f32[16,1664]{1,0:T(8,128)S(1)}, f32[16,1664]{1,0:T(8,128)S(1)}, u32[]{:S(2)}, u32[]{:S(2)}) collective-permute-start(f32[16,1664]{1,0:T(8,128)S(1)} %fusion.1.rest_0_), channel_id=1, source_target_pairs={{0,8},{1,9},{2,10},{3,11},{4,12},{5,13},{6,14},{7,15},{8,0},{9,1},... | collective-permute-start | bytes 319496 | tf_op jit(solution)/shard_map/ppermute | solution.py:40
  91.4 8.9 %collective-permute-start.30 = (f32[16,1664]{1,0:T(8,128)S(1)}, f32[16,1664]{1,0:T(8,128)S(1)}, u32[]{:S(2)}, u32[]{:S(2)}) collective-permute-start(f32[16,1664]{1,0:T(8,128)S(1)} %fusion.1.rest_0_), channel_id=1, source_target_pairs={{0,4},{1,5},{2,6},{3,7},{4,0},{5,1},{6,2},{7,3},{8,12},{9,13},{10,... | collective-permute-start | bytes 319496 | tf_op jit(solution)/shard_map/ppermute | solution.py:40
  98.7 1.6 %collective-permute-start.31 = (f32[16,1664]{1,0:T(8,128)S(1)}, f32[16,1664]{1,0:T(8,128)S(1)}, u32[]{:S(2)}, u32[]{:S(2)}) collective-permute-start(f32[16,1664]{1,0:T(8,128)S(1)} %collective-permute-done.28.rest_1_), channel_id=1, source_target_pairs={{0,4},{1,5},{2,6},{3,7},{4,0},{5,1},{6,2},{7,3},{8,12},{9,13},{10,... | collective-permute-start | bytes 319496 | tf_op jit(solution)/shard_map/ppermute | solution.py:40
  98.7 1.6 %collective-permute-start.32 = (f32[16,1664]{1,0:T(8,128)S(1)}, f32[16,1664]{1,0:T(8,128)S(1)}, u32[]{:S(2)}, u32[]{:S(2)}) collective-permute-start(f32[16,1664]{1,0:T(8,128)S(1)} %collective-permute-done.27.rest_2_), channel_id=1, source_target_pairs={{0,4},{1,5},{2,6},{3,7},{4,0},{5,1},{6,2},{7,3},{8,12},{9,13},{10,... | collective-permute-start | bytes 319496 | tf_op jit(solution)/shard_map/ppermute | solution.py:40
  101.6 4.3 %collective-permute-start.34 = (f32[128,128]{1,0:T(8,128)S(1)}, f32[128,128]{1,0:T(8,128)S(1)}, u32[]{:S(2)}, u32[]{:S(2)}) collective-permute-start(f32[128,128]{1,0:T(8,128)S(1)} %get-tuple-element.81), channel_id=1, source_target_pairs={{0,1},{1,0},{2,3},{3,2},{4,6},{5,7},{6,4},{7,5},{8,9},{9,8},{10,11... | collective-permute-start | bytes 196616 | tf_op jit(solution)/shard_map/ppermute | solution.py:40
  105.9 4.3 %collective-permute-start.35 = (f32[128,128]{1,0:T(8,128)S(1)}, f32[128,128]{1,0:T(8,128)S(1)}, u32[]{:S(2)}, u32[]{:S(2)}) collective-permute-start(f32[128,128]{1,0:T(8,128)S(1)} %add.67.one_ref), channel_id=1, source_target_pairs={{0,2},{1,3},{2,0},{3,1},{4,5},{5,4},{6,7},{7,6},{8,10},{9,11},{10,... | collective-permute-start | bytes 196616 | tf_op jit(solution)/shard_map/ppermute | solution.py:40
  (6 other events, 16.3 us)

commit v7 on v6

--- a/solution.py
+++ b/solution.py
@@ -417,7 +417,8 @@
         state_ref[pl.ds(first, size), :] = done
         return carry
 
-    lax.fori_loop(0, rank // size, panel, 0)
+    lax.fori_loop(0, rank // size - 1, panel, 0)
+    state_ref[rank - size:, :] = eliminate(state_ref[rank - size:, :], rank - size, size)
 
 
 def factor_left(count, place, own, other):
@@ -428,23 +429,30 @@
         for t in range(count // 2):
             for ref, at in ((own_ref, 2 * t + core), (other_ref, 2 * t + 1 - core)):
                 out_ref[pl.ds(pl.multiple_of(at * chunk, chunk), chunk), :] = ref[:, t * rank:(t + 1) * rank]
-        factor_panels(out_ref, 32)
+        factor_panels(out_ref)
         out_ref[...] = lower_part(out_ref[...])
 
     return call(body, "factor", struct(rank, rank), [place, own, other], flops=2 * FACTOR, nbytes=131072)
 
 
-def factor_right(one, two):
-    rank = one.shape[1]
-
-    def body(one_ref, two_ref, gram_ref, out_ref):
-        gram = one_ref[:rank, :] + two_ref[:rank, :]
+def tree_sum(xs):
+    while len(xs) > 1:
+        xs = [x + y for x, y in zip(xs[::2], xs[1::2])]
+    return xs[0]
+
+
+def factor_right(grams):
+    rank = grams[0].shape[0]
+
+    def body(*refs):
+        gram_ref, out_ref = refs[-2:]
+        gram = tree_sum([ref[...] for ref in refs[:-2]])
         gram_ref[...] = gram
         out_ref[...] = gram
         factor_panels(out_ref)
         out_ref[...] = lower_part(out_ref[...])
 
-    return call(body, "factor", [struct(rank, rank)] * 2, [one, two], flops=2 * FACTOR, nbytes=131072)
+    return call(body, "factor", [struct(rank, rank)] * 2, grams, flops=2 * FACTOR, nbytes=131072)
 
 
 def lower_part(x):
@@ -464,13 +472,14 @@
     return call(body, "turn", [struct(width, rank, dtype=BF16)] * 2, [right], flops=100_000_000, nbytes=2_000_000)
 
 
-def last_factor(one, two, high, low, scale):
+def last_factor(grams, high, low, scale):
     width, rank = high.shape
     steps = 4
     block = width // steps
 
-    def body(one_ref, two_ref, high_ref, low_ref, out_ref, state_ref, stage_ref, sems):
-        state_ref[...] = one_ref[...] + two_ref[...]
+    def body(high_ref, low_ref, *rest):
+        out_ref, state_ref, stage_ref, sems = rest[-4:]
+        state_ref[...] = tree_sum([ref[...] for ref in rest[:-4]])
         factor_panels(state_ref)
         inv_high, inv_low = split(scale * lower_part(state_ref[...]))
         both = jnp.concatenate([inv_high, inv_low], axis=0)
@@ -488,14 +497,14 @@
 
     return pl.pallas_call(
         body,
-        in_specs=[VMEM] * 4,
+        in_specs=[VMEM] * (2 + len(grams)),
         out_specs=pl.BlockSpec(memory_space=pltpu.HBM),
         out_shape=struct(width, rank),
         scratch_shapes=[pltpu.VMEM((rank, rank), F32), pltpu.VMEM((width, rank), F32), pltpu.SemaphoreType.DMA((steps,))],
         name="last_factor",
         compiler_params=pltpu.CompilerParams(vmem_limit_bytes=24 * 2**20),
         cost_estimate=pl.CostEstimate(flops=2 * FACTOR, bytes_accessed=2_000_000, transcendentals=0),
-    )(one, two, high, low)
+    )(high, low, *grams)
 
 
 def sum_cols(parts):
@@ -503,6 +512,10 @@
     for even, odd in zip(masks[:-1], masks[:0:-1]):
         parts = [x + swap(x, "col", even, odd) for x in parts]
     return [y for x in parts for y in (x, swap(x, "col", masks[-1], masks[0]))]
+
+
+def share_cols(x):
+    return [x] + [swap(x, "col", mask, mask) for mask in range(1, lax.axis_size("col"))]
 
 
 def sum_rows(keep, send, count, rank, beside=None):
@@ -514,18 +527,33 @@
     width = x.shape[1] - rank
     chunk = rank // count
     slots = count // 2
+    cut = width // rank // 2 * rank
+    cut = width - cut
     parts = [x[i * chunk:(i + 1) * chunk] for i in range(slots)]
     gram = jnp.concatenate([part[:, width:] for part in parts], axis=1)
-    got = swap(jnp.concatenate([parts[1][:, :width], gram], axis=1), "row", 2, 2)
-    gots = [swap(parts[i][:, :width], "row", 2 * i, 2 * i) for i in range(2, slots)]
-    gram = gram + got[:, width:]
-    if beside is not None:
-        gram, beside = lax.optimization_barrier((gram, beside))
-    for mask in masks_of("row")[2:]:
-        gram = gram + swap(gram, "row", mask, mask)
-    own = parts[0][:, :width] + got[:, :width]
-    for got in gots:
-        own = own + got
+    stepped = {i: part[:, cut:width] for i, part in enumerate(parts)}
+    own = parts[0][:, :cut]
+    straight = {}
+    bit = 1
+    while bit < slots:
+        sent = [i for i in stepped if i & bit]
+        kept = [i for i in stepped if not i & bit]
+        cols = [stepped[i] for i in sent] + [gram]
+        first = [parts[1][:, :cut]] if bit == 1 else []
+        got = swap(jnp.concatenate(first + cols, axis=1), "row", 2 * bit, 2 * bit)
+        if bit == 1:
+            straight[1], got = got[:, :cut], got[:, cut:]
+            for i in reversed(range(2, slots)):
+                straight[i] = swap(parts[i][:, :cut], "row", 2 * i, 2 * i)
+            if beside is not None:
+                got, beside = lax.optimization_barrier((got, beside))
+        size = width - cut
+        stepped = {i: stepped[i] + got[:, n * size:(n + 1) * size] for n, i in enumerate(kept)}
+        gram = gram + got[:, len(kept) * size:]
+        bit *= 2
+    for i in straight:
+        own = own + straight[i]
+    own = jnp.concatenate([own, stepped[0]], axis=1)
     own, gram = lax.optimization_barrier((own, gram))
     return own, gram, swap(gram, "row", 1, 1), beside
 
@@ -559,7 +587,7 @@
     proj, inv, pieces, _ = left_side(sum_cols(parts))
     left_a = left_of(proj, inv)
     right_a, gram = normal(count, place, inv, *pieces)
-    gram, inv = factor_right(*sum_cols([gram]))
+    gram, inv = factor_right(share_cols(gram))
     halves = sum_cols([push(high, low, right_a)])
 
     beside = (lambda left: deflate(momentum, grad, left, right_a)), left_a
@@ -567,14 +595,10 @@
     left_b, lefts = left_of(proj, inv, left_a, row_scale)
     right_b, gram = normal(count, place, inv, *pieces)
 
-    masks = masks_of("col")
+    grams = share_cols(gram)
     momentum_out = finish(base, left_b, right_b)
-    for even, odd in zip(masks[:-1], masks[:0:-1]):
-        gram = gram + swap(gram, "col", even, odd)
-    gram, momentum_out = lax.optimization_barrier((gram, momentum_out))
     momentum_out = finish(base, left_b, right_b, momentum_out)
-    turned = turn(right_b)
-    return momentum_out, lefts, last_factor(gram, swap(gram, "col", masks[-1], masks[0]), *turned, col_scale)
+    return momentum_out, lefts, last_factor(grams, *turn(right_b), col_scale)
 
 
 def solution(mesh):

time: 116 us -> 114 us (0.983)
  Pallas kernels: 37.3 us -> 35.9 us
    pallas_call x14, Pallas kernels: 25.1 us -> 23.9 us  [call(): pl.pallas_call(body, out_shape=out, in_specs=[SMEM if x.dtype == jnp.int3...]
    ppermute x36 -> x38, waiting for transfers between devices: 38.4 us -> 37.4 us  [swap(): return lax.ppermute(x, ('row', 'col'), pairs)]
    ppermute x36 -> x38, starting transfers between devices: 38 us -> 38.6 us  [swap(): return lax.ppermute(x, ('row', 'col'), pairs)]
  transfers between devices with their start and end apart: 36 -> 38, of which waited for: 25 -> 22; matrix products, arithmetic and copies ran while one was open for 1% -> 1% of each run, Pallas kernels for 19% -> 18%
where the time goes in v7:
time: 114 us
  starting transfers between devices  38.6 us (34%)
  waiting for transfers between devices  37.4 us (33%)
  Pallas kernels  35.9 us (31%)
  between operations  1.21 us (1%)
    ppermute x38, starting transfers between devices, swap(): return lax.ppermute(x, ('row', 'col'), pairs)  38.6 us
    ppermute x38, waiting for transfers between devices, swap(): return lax.ppermute(x, ('row', 'col'), pairs)  37.4 us
    pallas_call x14, Pallas kernels, call(): pl.pallas_call(body, out_shape=out, in_specs=[SMEM if x.dtype == jnp.int3...  23.9 us
    pallas_call x1, Pallas kernels, last_factor(): pl.pallas_call(body, in_specs=[VMEM] * (2 + len(grams)), out_specs=pl.Blo...  5.24 us
    pallas_call x2, Pallas kernels, finish(): pl.pallas_call(body, in_specs=[VMEM] * 3 + [hbm] * len(more), out_specs=h...  3.56 us
    pallas_call x1, Pallas kernels, start(): pl.pallas_call(body, in_specs=[pl.BlockSpec(memory_space=pltpu.HBM)] * 3,...  3.21 us
  transfers between devices with their start and end apart: 38, of which 22 were waited for; matrix products, arithmetic and copies ran while one was open for 1% of the time, Pallas kernels for 18%

profile of v7, /device:TPU:0, one launch (start us, length us, event | category | flops | bytes accessed | tf_op | source)
XLA Modules:
  0.0 114.2 jit_solution(8019378197467664607)
XLA Ops:
  0.6 3.2 %start.1 = (bf16[512,1664]{1,0:T(8,128)(2,1)S(1)}, bf16[512,1664]{1,0:T(8,128)(2,1)S(1)}, f32[256,128]{1,0:T(8,128)S(1)}, f32[256,128]{1,0:T(8,128)S(1)}) custom-call(f32[512,1664]{1,0:T(8,128)} %momentum_ref.1, bf16[512,1664]{1,0:T(8,128)(2,1)} %grad_ref.1, f32[1664,128]{1,0:T(8,128)} %basis_hbm.1), custom_call_target="tpu_custom_call" | custom-call | tf_op jit(solution)/shard_map/start/pallas_call | solution.py:123
  3.8 3.0 %collective-permute-start = (f32[256,128]{1,0:T(8,128)S(1)}, f32[256,128]{1,0:T(8,128)S(1)}, u32[]{:S(2)}, u32[]{:S(2)}) collective-permute-start(f32[256,128]{1,0:T(8,128)S(1)} %get-tuple-element.45), channel_id=1, source_target_pairs={{0,1},{1,0},{2,3},{3,2},{4,6},{5,7},{6,4},{7,5},{8,9},{9,8},{10,11... | collective-permute-start | bytes 393224 | tf_op jit(solution)/shard_map/ppermute | solution.py:40
  6.9 2.9 %collective-permute-done = f32[256,128]{1,0:T(8,128)S(1)} collective-permute-done((f32[256,128]{1,0:T(8,128)S(1)}, f32[256,128]{1,0:T(8,128)S(1)}, u32[]{:S(2)}, u32[]{:S(2)}) %collective-permute-start) | collective-permute-done | bytes 131104 | tf_op jit(solution)/shard_map/ppermute | solution.py:40
  9.8 2.1 %collective-permute-start.1 = (f32[256,128]{1,0:T(8,128)S(1)}, f32[256,128]{1,0:T(8,128)}, u32[]{:S(2)}, u32[]{:S(2)}) collective-permute-start(f32[256,128]{1,0:T(8,128)S(1)} %add.63.rest_0_), channel_id=1, source_target_pairs={{0,2},{1,3},{2,0},{3,1},{4,5},{5,4},{6,7},{7,6},{8,10},{9,11},{10,... | collective-permute-start | bytes 393224 | tf_op jit(solution)/shard_map/ppermute | solution.py:40
  15.0 2.9 %collective-permute-done.3.rest_3_ = f32[256,128]{1,0:T(8,128)} collective-permute-done((f32[256,128]{1,0:T(8,128)}, f32[256,128]{1,0:T(8,128)}, u32[]{:S(2)}, u32[]{:S(2)}) %collective-permute-start.3) | collective-permute-done | bytes 131104 | tf_op jit(solution)/shard_map/ppermute | solution.py:40
  17.9 1.9 %pull_send.2 = (f32[512,128]{1,0:T(8,128)S(1)}, f32[64,512]{1,0:T(8,128)S(1)}, f32[64,1792]{1,0:T(8,128)S(1)}) custom-call(s32[1]{0:T(128)} %bitcast.place_ref, f32[256,128]{1,0:T(8,128)S(1)} %add.63.rest_0_, f32[256,128]{1,0:T(8,128)} %collective-permute-done.1.rest_1_, f32[256,128]{1,0:T(8,128)} %add.64.rest_2_, ...), custom_call_target="tpu_custom_call" | custom-call | flops 500000000 | bytes 5000000 | tf_op jit(solution)/shard_map/pull_send/pallas_call | solution.py:75
  21.8 1.6 %collective-permute-start.5 = (f32[16,2944]{1,0:T(8,128)S(1)}, f32[16,2944]{1,0:T(8,128)S(1)}, u32[]{:S(2)}, u32[]{:S(2)}) collective-permute-start(f32[16,2944]{1,0:T(8,128)S(1)} %constant_dynamic-update-slice_fusion), channel_id=1, source_target_pairs={{0,8},{1,9},{2,10},{3,11},{4,12},{5,13},{6,14},{7,15},{8,0},{9,1},... | collective-permute-start | bytes 565256 | tf_op jit(solution)/shard_map/ppermute | solution.py:40
  23.4 2.6 %collective-permute-start.7 = (f32[16,896]{1,0:T(8,128)S(1)}, f32[16,896]{1,0:T(8,128)S(1)}, u32[]{:S(2)}, u32[]{:S(2)}) collective-permute-start(f32[16,896]{1,0:T(8,128)S(1)} %get-tuple-element.91), channel_id=1, source_target_pairs={{0,16},{1,17},{2,18},{3,19},{4,20},{5,21},{6,22},{7,23},{8,24},{9,... | collective-permute-start | bytes 172040 | tf_op jit(solution)/shard_map/ppermute | solution.py:40
  26.3 3.5 %collective-permute-done.5 = f32[16,2944]{1,0:T(8,128)S(1)} collective-permute-done((f32[16,2944]{1,0:T(8,128)S(1)}, f32[16,2944]{1,0:T(8,128)S(1)}, u32[]{:S(2)}, u32[]{:S(2)}) %collective-permute-start.5) | collective-permute-done | bytes 188448 | tf_op jit(solution)/shard_map/ppermute | solution.py:40
  29.9 2.4 %collective-permute-start.8 = (f32[16,1280]{1,0:T(8,128)S(1)}, f32[16,1280]{1,0:T(8,128)S(1)}, u32[]{:S(2)}, u32[]{:S(2)}) collective-permute-start(f32[16,1280]{1,0:T(8,128)S(1)} %pad_maximum_fusion.2), channel_id=1, source_target_pairs={{0,16},{1,17},{2,18},{3,19},{4,20},{5,21},{6,22},{7,23},{8,24},{9,... | collective-permute-start | bytes 245768 | tf_op jit(solution)/shard_map/ppermute | solution.py:40
  33.1 2.6 %collective-permute-done.8 = f32[16,1280]{1,0:T(8,128)S(1)} collective-permute-done((f32[16,1280]{1,0:T(8,128)S(1)}, f32[16,1280]{1,0:T(8,128)S(1)}, u32[]{:S(2)}, u32[]{:S(2)}) %collective-permute-start.8) | collective-permute-done | bytes 81952 | tf_op jit(solution)/shard_map/ppermute | solution.py:40
  35.8 4.5 %collective-permute-start.9 = (f32[16,1664]{1,0:T(8,128)S(1)}, f32[16,1664]{1,0:T(8,128)S(1)}, u32[]{:S(2)}, u32[]{:S(2)}) collective-permute-start(f32[16,1664]{1,0:T(8,128)S(1)} %pad_maximum_fusion.rest_0_), channel_id=1, source_target_pairs={{0,24},{1,25},{2,26},{3,27},{4,28},{5,29},{6,30},{7,31},{8,16},{9,... | collective-permute-start | bytes 319496 | tf_op jit(solution)/shard_map/ppermute | solution.py:40
  40.9 4.2 %factor.3.inv_ref = f32[128,128]{1,0:T(8,128)S(1)} custom-call(s32[1]{0:T(128)} %bitcast.place_ref, f32[16,512]{1,0:T(8,128)S(1)} %slice_add_fusion.8.own_ref, f32[16,512]{1,0:T(8,128)S(1)} %collective-permute-done.12.other_ref), custom_call_target="tpu_custom_call" | custom-call | flops 40000000000 | bytes 131072 | tf_op jit(solution)/shard_map/factor/pallas_call | solution.py:75
  45.2 2.6 %collective-permute-done.11.rest_1_ = f32[16,1664]{1,0:T(8,128)S(1)} collective-permute-done((f32[16,1664]{1,0:T(8,128)S(1)}, f32[16,1664]{1,0:T(8,128)S(1)}, u32[]{:S(2)}, u32[]{:S(2)}) %collective-permute-start.11) | collective-permute-done | bytes 106528 | tf_op jit(solution)/shard_map/ppermute | solution.py:40
  47.8 1.8 %collective-permute-done.10.rest_2_ = f32[16,1664]{1,0:T(8,128)S(1)} collective-permute-done((f32[16,1664]{1,0:T(8,128)S(1)}, f32[16,1664]{1,0:T(8,128)S(1)}, u32[]{:S(2)}, u32[]{:S(2)}) %collective-permute-start.10) | collective-permute-done | bytes 106528 | tf_op jit(solution)/shard_map/ppermute | solution.py:40
  53.6 1.6 %collective-permute-start.17 = (f32[512,128]{1,0:T(8,128)S(1)}, f32[512,128]{1,0:T(8,128)S(1)}, u32[]{:S(2)}, u32[]{:S(2)}) collective-permute-start(f32[512,128]{1,0:T(8,128)S(1)} %push.1), channel_id=1, source_target_pairs={{0,1},{1,0},{2,3},{3,2},{4,6},{5,7},{6,4},{7,5},{8,9},{9,8},{10,11... | collective-permute-start | bytes 786440 | tf_op jit(solution)/shard_map/ppermute | solution.py:40
  57.1 1.6 %collective-permute-start.21 = (f32[128,128]{1,0:T(8,128)S(1)}, f32[128,128]{1,0:T(8,128)S(1)}, u32[]{:S(2)}, u32[]{:S(2)}) collective-permute-start(f32[128,128]{1,0:T(8,128)S(1)} %get-tuple-element.59.refs_0_), channel_id=1, source_target_pairs={{0,3},{1,2},{2,1},{3,0},{4,7},{5,6},{6,5},{7,4},{8,11},{9,10},{10,... | collective-permute-start | bytes 196616 | tf_op jit(solution)/shard_map/ppermute | solution.py:40
  58.9 2.5 %collective-permute-done.17 = f32[512,128]{1,0:T(8,128)S(1)} collective-permute-done((f32[512,128]{1,0:T(8,128)S(1)}, f32[512,128]{1,0:T(8,128)S(1)}, u32[]{:S(2)}, u32[]{:S(2)}) %collective-permute-start.17) | collective-permute-done | bytes 262176 | tf_op jit(solution)/shard_map/ppermute | solution.py:40
  63.4 4.0 %factor.4 = (f32[128,128]{1,0:T(8,128)S(1)}, f32[128,128]{1,0:T(8,128)S(1)}) custom-call(f32[128,128]{1,0:T(8,128)S(1)} %get-tuple-element.59.refs_0_, f32[128,128]{1,0:T(8,128)S(1)} %collective-permute-done.19.refs_1_, f32[128,128]{1,0:T(8,128)S(1)} %collective-permute-done.20.refs_2_, f32[128,128]{1,0:T(8,128)S(1)} %collective-permute-done.21.refs_3_), custom_call_target="tpu_custom_call" | custom-call | flops 40000000000 | bytes 131072 | tf_op jit(solution)/shard_map/factor/pallas_call | solution.py:75
  67.9 1.6 %pull_send.3 = (f32[512,128]{1,0:T(8,128)S(1)}, f32[64,512]{1,0:T(8,128)S(1)}, f32[64,1792]{1,0:T(8,128)S(1)}) custom-call(s32[1]{0:T(128)} %bitcast.place_ref, f32[512,128]{1,0:T(8,128)S(1)} %add.74.rest_0_, f32[512,128]{1,0:T(8,128)S(1)} %collective-permute-done.18.rest_1_, bf16[512,1664]{1,0:T(8,128)(2,1)S(1)} %get-tuple-element.43.rest_4_.high_ref.rest_2_, ...), custom_call_target="tpu_custom_call" | custom-call | flops 500000000 | bytes 5000000 | tf_op jit(solution)/shard_map/pull_send/pallas_call | solution.py:75
  72.3 1.5 %collective-permute-start.25 = (f32[16,896]{1,0:T(8,128)S(1)}, f32[16,896]{1,0:T(8,128)S(1)}, u32[]{:S(2)}, u32[]{:S(2)}) collective-permute-start(f32[16,896]{1,0:T(8,128)S(1)} %get-tuple-element.84), channel_id=1, source_target_pairs={{0,16},{1,17},{2,18},{3,19},{4,20},{5,21},{6,22},{7,23},{8,24},{9,... | collective-permute-start | bytes 172040 | tf_op jit(solution)/shard_map/ppermute | solution.py:40
  73.8 2.3 %collective-permute-start.24 = (f32[16,896]{1,0:T(8,128)S(1)}, f32[16,896]{1,0:T(8,128)S(1)}, u32[]{:S(2)}, u32[]{:S(2)}) collective-permute-start(f32[16,896]{1,0:T(8,128)S(1)} %get-tuple-element.83), channel_id=1, source_target_pairs={{0,24},{1,25},{2,26},{3,27},{4,28},{5,29},{6,30},{7,31},{8,16},{9,... | collective-permute-start | bytes 172040 | tf_op jit(solution)/shard_map/ppermute | solution.py:40
  76.1 1.5 %deflate.1.base_ref = f32[512,1664]{1,0:T(8,128)S(1)} custom-call(f32[512,1664]{1,0:T(8,128)S(1)} %copy-done, bf16[512,1664]{1,0:T(8,128)(2,1)S(1)} %copy-done.1, f32[512,128]{1,0:T(8,128)S(1)} %left.1.rest_4_.rest_0_.left_ref, f32[128,1664]{1,0:T(8,128)S(1)} %get-tuple-element.58.right_ref.rest_5_.rest_1_), custom_call_target="tpu_custom_call" | custom-call | flops 1500000000 | bytes 9000000 | tf_op jit(solution)/shard_map/deflate/pallas_call | solution.py:75
  77.6 3.2 %collective-permute-done.23 = f32[16,2944]{1,0:T(8,128)S(1)} collective-permute-done((f32[16,2944]{1,0:T(8,128)S(1)}, f32[16,2944]{1,0:T(8,128)S(1)}, u32[]{:S(2)}, u32[]{:S(2)}) %collective-permute-start.23) | collective-permute-done | bytes 188448 | tf_op jit(solution)/shard_map/ppermute | solution.py:40
  81.0 5.3 %collective-permute-done.26 = f32[16,1280]{1,0:T(8,128)S(1)} collective-permute-done((f32[16,1280]{1,0:T(8,128)S(1)}, f32[16,1280]{1,0:T(8,128)S(1)}, u32[]{:S(2)}, u32[]{:S(2)}) %collective-permute-start.26) | collective-permute-done | bytes 81952 | tf_op jit(solution)/shard_map/ppermute | solution.py:40
  87.7 3.2 %collective-permute-start.29 = (f32[16,1664]{1,0:T(8,128)S(1)}, f32[16,1664]{1,0:T(8,128)S(1)}, u32[]{:S(2)}, u32[]{:S(2)}) collective-permute-start(f32[16,1664]{1,0:T(8,128)S(1)} %pad_maximum_fusion.1.rest_0_), channel_id=1, source_target_pairs={{0,8},{1,9},{2,10},{3,11},{4,12},{5,13},{6,14},{7,15},{8,0},{9,1},... | collective-permute-start | bytes 319496 | tf_op jit(solution)/shard_map/ppermute | solution.py:40
  90.9 4.0 %factor.5.inv_ref = f32[128,128]{1,0:T(8,128)S(1)} custom-call(s32[1]{0:T(128)} %bitcast.place_ref, f32[16,512]{1,0:T(8,128)S(1)} %slice_add_fusion.7.own_ref, f32[16,512]{1,0:T(8,128)S(1)} %collective-permute-done.30.other_ref), custom_call_target="tpu_custom_call" | custom-call | flops 40000000000 | bytes 131072 | tf_op jit(solution)/shard_map/factor/pallas_call | solution.py:75
  96.3 1.8 %collective-permute-done.28.rest_2_ = f32[16,1664]{1,0:T(8,128)S(1)} collective-permute-done((f32[16,1664]{1,0:T(8,128)S(1)}, f32[16,1664]{1,0:T(8,128)S(1)}, u32[]{:S(2)}, u32[]{:S(2)}) %collective-permute-start.28) | collective-permute-done | bytes 106528 | tf_op jit(solution)/shard_map/ppermute | solution.py:40
  101.1 1.6 %collective-permute-start.35 = (f32[128,128]{1,0:T(8,128)S(1)}, f32[128,128]{1,0:T(8,128)S(1)}, u32[]{:S(2)}, u32[]{:S(2)}) collective-permute-start(f32[128,128]{1,0:T(8,128)S(1)} %get-tuple-element.82.rest_0_), channel_id=1, source_target_pairs={{0,1},{1,0},{2,3},{3,2},{4,5},{5,4},{6,7},{7,6},{8,9},{9,8},{10,11... | collective-permute-start | bytes 196616 | tf_op jit(solution)/shard_map/ppermute | solution.py:40
  104.9 1.8 %finish.2.rest_0_ = f32[512,1664]{1,0:T(8,128)} custom-call(f32[512,1664]{1,0:T(8,128)S(1)} %deflate.1.base_ref, f32[512,128]{1,0:T(8,128)S(1)} %get-tuple-element.74.left_ref, f32[128,1664]{1,0:T(8,128)S(1)} %get-tuple-element.78.right_ref), custom_call_target="tpu_custom_call" | custom-call | flops 800000000 | bytes 6000000 | tf_op jit(solution)/shard_map/finish/pallas_call | solution.py:337
  106.7 1.8 %finish.3 = f32[512,1664]{1,0:T(8,128)} custom-call(f32[512,1664]{1,0:T(8,128)S(1)} %deflate.1.base_ref, f32[512,128]{1,0:T(8,128)S(1)} %get-tuple-element.74.left_ref, f32[128,1664]{1,0:T(8,128)S(1)} %get-tuple-element.78.right_ref, f32[512,1664]{1,0:T(8,128)} %finish.2.rest_0_), custom_call_target="tpu_custom_call", output_to_operand_aliasing={{}: (3, {})} | custom-call | flops 800000000 | bytes 6000000 | tf_op jit(solution)/shard_map/finish/pallas_call | solution.py:337
  108.8 5.2 %last_factor.1 = f32[1664,128]{1,0:T(8,128)} custom-call(bf16[1664,128]{1,0:T(8,128)(2,1)S(1)} %get-tuple-element.80.high_ref, bf16[1664,128]{1,0:T(8,128)(2,1)S(1)} %get-tuple-element.81.low_ref, f32[128,128]{1,0:T(8,128)S(1)} %get-tuple-element.82.rest_0_, f32[128,128]{1,0:T(8,128)S(1)} %collective-permute-done.35.rest_1_, ...), custom_call_target="tpu_custom_call" | custom-call | flops 40000000000 | bytes 2000000 | tf_op jit(solution)/shard_map/last_factor/pallas_call | solution.py:498
  (100 shorter events, 26.7 us)
Async XLA Ops:
  3.8 6.0 %collective-permute-start = (f32[256,128]{1,0:T(8,128)S(1)}, f32[256,128]{1,0:T(8,128)S(1)}, u32[]{:S(2)}, u32[]{:S(2)}) collective-permute-start(f32[256,128]{1,0:T(8,128)S(1)} %get-tuple-element.45), channel_id=1, source_target_pairs={{0,1},{1,0},{2,3},{3,2},{4,6},{5,7},{6,4},{7,5},{8,9},{9,8},{10,11... | collective-permute-start | bytes 393224 | tf_op jit(solution)/shard_map/ppermute | solution.py:40
  6.8 5.1 %collective-permute-start.2 = (f32[256,128]{1,0:T(8,128)S(1)}, f32[256,128]{1,0:T(8,128)S(1)}, u32[]{:S(2)}, u32[]{:S(2)}) collective-permute-start(f32[256,128]{1,0:T(8,128)S(1)} %get-tuple-element.46), channel_id=1, source_target_pairs={{0,1},{1,0},{2,3},{3,2},{4,6},{5,7},{6,4},{7,5},{8,9},{9,8},{10,11... | collective-permute-start | bytes 393224 | tf_op jit(solution)/shard_map/ppermute | solution.py:40
  9.8 5.2 %collective-permute-start.1 = (f32[256,128]{1,0:T(8,128)S(1)}, f32[256,128]{1,0:T(8,128)}, u32[]{:S(2)}, u32[]{:S(2)}) collective-permute-start(f32[256,128]{1,0:T(8,128)S(1)} %add.63.rest_0_), channel_id=1, source_target_pairs={{0,2},{1,3},{2,0},{3,1},{4,5},{5,4},{6,7},{7,6},{8,10},{9,11},{10,... | collective-permute-start | bytes 393224 | tf_op jit(solution)/shard_map/ppermute | solution.py:40
  12.6 5.3 %collective-permute-start.3 = (f32[256,128]{1,0:T(8,128)}, f32[256,128]{1,0:T(8,128)}, u32[]{:S(2)}, u32[]{:S(2)}) collective-permute-start(f32[256,128]{1,0:T(8,128)} %add.64.rest_2_), channel_id=1, source_target_pairs={{0,2},{1,3},{2,0},{3,1},{4,5},{5,4},{6,7},{7,6},{8,10},{9,11},{10,... | collective-permute-start | bytes 393224 | tf_op jit(solution)/shard_map/ppermute | solution.py:40
  19.8 1.9 %collective-permute-start.4 = (f32[64,1792]{1,0:T(8,128)S(1)}, f32[64,1792]{1,0:T(8,128)S(1)}, u32[]{:S(2)}, u32[]{:S(2)}) collective-permute-start(f32[64,1792]{1,0:T(8,128)S(1)} %get-tuple-element.49), channel_id=1, source_target_pairs={{0,4},{1,5},{2,6},{3,7},{4,0},{5,1},{6,2},{7,3},{8,12},{9,13},{10,... | collective-permute-start | bytes 1376264 | tf_op jit(solution)/shard_map/ppermute | solution.py:40
  21.8 8.1 %collective-permute-start.5 = (f32[16,2944]{1,0:T(8,128)S(1)}, f32[16,2944]{1,0:T(8,128)S(1)}, u32[]{:S(2)}, u32[]{:S(2)}) collective-permute-start(f32[16,2944]{1,0:T(8,128)S(1)} %constant_dynamic-update-slice_fusion), channel_id=1, source_target_pairs={{0,8},{1,9},{2,10},{3,11},{4,12},{5,13},{6,14},{7,15},{8,0},{9,1},... | collective-permute-start | bytes 565256 | tf_op jit(solution)/shard_map/ppermute | solution.py:40
  23.4 8.8 %collective-permute-start.7 = (f32[16,896]{1,0:T(8,128)S(1)}, f32[16,896]{1,0:T(8,128)S(1)}, u32[]{:S(2)}, u32[]{:S(2)}) collective-permute-start(f32[16,896]{1,0:T(8,128)S(1)} %get-tuple-element.91), channel_id=1, source_target_pairs={{0,16},{1,17},{2,18},{3,19},{4,20},{5,21},{6,22},{7,23},{8,24},{9,... | collective-permute-start | bytes 172040 | tf_op jit(solution)/shard_map/ppermute | solution.py:40
  26.1 7.0 %collective-permute-start.6 = (f32[16,896]{1,0:T(8,128)S(1)}, f32[16,896]{1,0:T(8,128)S(1)}, u32[]{:S(2)}, u32[]{:S(2)}) collective-permute-start(f32[16,896]{1,0:T(8,128)S(1)} %get-tuple-element.90), channel_id=1, source_target_pairs={{0,24},{1,25},{2,26},{3,27},{4,28},{5,29},{6,30},{7,31},{8,16},{9,... | collective-permute-start | bytes 172040 | tf_op jit(solution)/shard_map/ppermute | solution.py:40
  29.9 5.8 %collective-permute-start.8 = (f32[16,1280]{1,0:T(8,128)S(1)}, f32[16,1280]{1,0:T(8,128)S(1)}, u32[]{:S(2)}, u32[]{:S(2)}) collective-permute-start(f32[16,1280]{1,0:T(8,128)S(1)} %pad_maximum_fusion.2), channel_id=1, source_target_pairs={{0,16},{1,17},{2,18},{3,19},{4,20},{5,21},{6,22},{7,23},{8,24},{9,... | collective-permute-start | bytes 245768 | tf_op jit(solution)/shard_map/ppermute | solution.py:40
  35.8 5.2 %collective-permute-start.12 = (f32[16,512]{1,0:T(8,128)S(1)}, f32[16,512]{1,0:T(8,128)S(1)}, u32[]{:S(2)}, u32[]{:S(2)}) collective-permute-start(f32[16,512]{1,0:T(8,128)S(1)} %slice_add_fusion.8.own_ref), channel_id=1, source_target_pairs={{0,4},{1,5},{2,6},{3,7},{4,0},{5,1},{6,2},{7,3},{8,12},{9,13},{10,... | collective-permute-start | bytes 98312 | tf_op jit(solution)/shard_map/ppermute | solution.py:40
  35.8 13.7 %collective-permute-start.9 = (f32[16,1664]{1,0:T(8,128)S(1)}, f32[16,1664]{1,0:T(8,128)S(1)}, u32[]{:S(2)}, u32[]{:S(2)}) collective-permute-start(f32[16,1664]{1,0:T(8,128)S(1)} %pad_maximum_fusion.rest_0_), channel_id=1, source_target_pairs={{0,24},{1,25},{2,26},{3,27},{4,28},{5,29},{6,30},{7,31},{8,16},{9,... | collective-permute-start | bytes 319496 | tf_op jit(solution)/shard_map/ppermute | solution.py:40
  40.3 9.2 %collective-permute-start.10 = (f32[16,1664]{1,0:T(8,128)S(1)}, f32[16,1664]{1,0:T(8,128)S(1)}, u32[]{:S(2)}, u32[]{:S(2)}) collective-permute-start(f32[16,1664]{1,0:T(8,128)S(1)} %pad_maximum_fusion.rest_0_), channel_id=1, source_target_pairs={{0,16},{1,17},{2,18},{3,19},{4,20},{5,21},{6,22},{7,23},{8,24},{9,... | collective-permute-start | bytes 319496 | tf_op jit(solution)/shard_map/ppermute | solution.py:40
  40.3 7.5 %collective-permute-start.11 = (f32[16,1664]{1,0:T(8,128)S(1)}, f32[16,1664]{1,0:T(8,128)S(1)}, u32[]{:S(2)}, u32[]{:S(2)}) collective-permute-start(f32[16,1664]{1,0:T(8,128)S(1)} %pad_maximum_fusion.rest_0_), channel_id=1, source_target_pairs={{0,8},{1,9},{2,10},{3,11},{4,12},{5,13},{6,14},{7,15},{8,0},{9,1},... | collective-permute-start | bytes 319496 | tf_op jit(solution)/shard_map/ppermute | solution.py:40
  40.9 9.1 %collective-permute-start.13 = (f32[16,1664]{1,0:T(8,128)S(1)}, f32[16,1664]{1,0:T(8,128)S(1)}, u32[]{:S(2)}, u32[]{:S(2)}) collective-permute-start(f32[16,1664]{1,0:T(8,128)S(1)} %pad_maximum_fusion.rest_0_), channel_id=1, source_target_pairs={{0,4},{1,5},{2,6},{3,7},{4,0},{5,1},{6,2},{7,3},{8,12},{9,13},{10,... | collective-permute-start | bytes 319496 | tf_op jit(solution)/shard_map/ppermute | solution.py:40
  53.6 7.8 %collective-permute-start.17 = (f32[512,128]{1,0:T(8,128)S(1)}, f32[512,128]{1,0:T(8,128)S(1)}, u32[]{:S(2)}, u32[]{:S(2)}) collective-permute-start(f32[512,128]{1,0:T(8,128)S(1)} %push.1), channel_id=1, source_target_pairs={{0,1},{1,0},{2,3},{3,2},{4,6},{5,7},{6,4},{7,5},{8,9},{9,8},{10,11... | collective-permute-start | bytes 786440 | tf_op jit(solution)/shard_map/ppermute | solution.py:40
  55.1 7.3 %collective-permute-start.19 = (f32[128,128]{1,0:T(8,128)S(1)}, f32[128,128]{1,0:T(8,128)S(1)}, u32[]{:S(2)}, u32[]{:S(2)}) collective-permute-start(f32[128,128]{1,0:T(8,128)S(1)} %get-tuple-element.59.refs_0_), channel_id=1, source_target_pairs={{0,1},{1,0},{2,3},{3,2},{4,5},{5,4},{6,7},{7,6},{8,9},{9,8},{10,11... | collective-permute-start | bytes 196616 | tf_op jit(solution)/shard_map/ppermute | solution.py:40
  55.7 6.8 %collective-permute-start.20 = (f32[128,128]{1,0:T(8,128)S(1)}, f32[128,128]{1,0:T(8,128)S(1)}, u32[]{:S(2)}, u32[]{:S(2)}) collective-permute-start(f32[128,128]{1,0:T(8,128)S(1)} %get-tuple-element.59.refs_0_), channel_id=1, source_target_pairs={{0,2},{1,3},{2,0},{3,1},{4,6},{5,7},{6,4},{7,5},{8,10},{9,11},{10,... | collective-permute-start | bytes 196616 | tf_op jit(solution)/shard_map/ppermute | solution.py:40
  57.1 6.4 %collective-permute-start.21 = (f32[128,128]{1,0:T(8,128)S(1)}, f32[128,128]{1,0:T(8,128)S(1)}, u32[]{:S(2)}, u32[]{:S(2)}) collective-permute-start(f32[128,128]{1,0:T(8,128)S(1)} %get-tuple-element.59.refs_0_), channel_id=1, source_target_pairs={{0,3},{1,2},{2,1},{3,0},{4,7},{5,6},{6,5},{7,4},{8,11},{9,10},{10,... | collective-permute-start | bytes 196616 | tf_op jit(solution)/shard_map/ppermute | solution.py:40
  61.5 6.4 %collective-permute-start.18 = (f32[512,128]{1,0:T(8,128)S(1)}, f32[512,128]{1,0:T(8,128)S(1)}, u32[]{:S(2)}, u32[]{:S(2)}) collective-permute-start(f32[512,128]{1,0:T(8,128)S(1)} %add.74.rest_0_), channel_id=1, source_target_pairs={{0,2},{1,3},{2,0},{3,1},{4,5},{5,4},{6,7},{7,6},{8,10},{9,11},{10,... | collective-permute-start | bytes 786440 | tf_op jit(solution)/shard_map/ppermute | solution.py:40
  69.5 1.9 %collective-permute-start.22 = (f32[64,1792]{1,0:T(8,128)S(1)}, f32[64,1792]{1,0:T(8,128)S(1)}, u32[]{:S(2)}, u32[]{:S(2)}) collective-permute-start(f32[64,1792]{1,0:T(8,128)S(1)} %get-tuple-element.64), channel_id=1, source_target_pairs={{0,4},{1,5},{2,6},{3,7},{4,0},{5,1},{6,2},{7,3},{8,12},{9,13},{10,... | collective-permute-start | bytes 1376264 | tf_op jit(solution)/shard_map/ppermute | solution.py:40
  71.5 9.3 %collective-permute-start.23 = (f32[16,2944]{1,0:T(8,128)S(1)}, f32[16,2944]{1,0:T(8,128)S(1)}, u32[]{:S(2)}, u32[]{:S(2)}) collective-permute-start(f32[16,2944]{1,0:T(8,128)S(1)} %constant_dynamic-update-slice_fusion.4), channel_id=1, source_target_pairs={{0,8},{1,9},{2,10},{3,11},{4,12},{5,13},{6,14},{7,15},{8,0},{9,1},... | collective-permute-start | bytes 565256 | tf_op jit(solution)/shard_map/ppermute | solution.py:40
  72.3 8.7 %collective-permute-start.25 = (f32[16,896]{1,0:T(8,128)S(1)}, f32[16,896]{1,0:T(8,128)S(1)}, u32[]{:S(2)}, u32[]{:S(2)}) collective-permute-start(f32[16,896]{1,0:T(8,128)S(1)} %get-tuple-element.84), channel_id=1, source_target_pairs={{0,16},{1,17},{2,18},{3,19},{4,20},{5,21},{6,22},{7,23},{8,24},{9,... | collective-permute-start | bytes 172040 | tf_op jit(solution)/shard_map/ppermute | solution.py:40
  73.8 7.2 %collective-permute-start.24 = (f32[16,896]{1,0:T(8,128)S(1)}, f32[16,896]{1,0:T(8,128)S(1)}, u32[]{:S(2)}, u32[]{:S(2)}) collective-permute-start(f32[16,896]{1,0:T(8,128)S(1)} %get-tuple-element.83), channel_id=1, source_target_pairs={{0,24},{1,25},{2,26},{3,27},{4,28},{5,29},{6,30},{7,31},{8,16},{9,... | collective-permute-start | bytes 172040 | tf_op jit(solution)/shard_map/ppermute | solution.py:40
  80.9 5.4 %collective-permute-start.26 = (f32[16,1280]{1,0:T(8,128)S(1)}, f32[16,1280]{1,0:T(8,128)S(1)}, u32[]{:S(2)}, u32[]{:S(2)}) collective-permute-start(f32[16,1280]{1,0:T(8,128)S(1)} %pad_maximum_fusion.3), channel_id=1, source_target_pairs={{0,16},{1,17},{2,18},{3,19},{4,20},{5,21},{6,22},{7,23},{8,24},{9,... | collective-permute-start | bytes 245768 | tf_op jit(solution)/shard_map/ppermute | solution.py:40
  86.3 4.5 %collective-permute-start.30 = (f32[16,512]{1,0:T(8,128)S(1)}, f32[16,512]{1,0:T(8,128)S(1)}, u32[]{:S(2)}, u32[]{:S(2)}) collective-permute-start(f32[16,512]{1,0:T(8,128)S(1)} %slice_add_fusion.7.own_ref), channel_id=1, source_target_pairs={{0,4},{1,5},{2,6},{3,7},{4,0},{5,1},{6,2},{7,3},{8,12},{9,13},{10,... | collective-permute-start | bytes 98312 | tf_op jit(solution)/shard_map/ppermute | solution.py:40
  86.4 11.8 %collective-permute-start.27 = (f32[16,1664]{1,0:T(8,128)S(1)}, f32[16,1664]{1,0:T(8,128)S(1)}, u32[]{:S(2)}, u32[]{:S(2)}) collective-permute-start(f32[16,1664]{1,0:T(8,128)S(1)} %pad_maximum_fusion.1.rest_0_), channel_id=1, source_target_pairs={{0,24},{1,25},{2,26},{3,27},{4,28},{5,29},{6,30},{7,31},{8,16},{9,... | collective-permute-start | bytes 319496 | tf_op jit(solution)/shard_map/ppermute | solution.py:40
  87.7 10.5 %collective-permute-start.28 = (f32[16,1664]{1,0:T(8,128)S(1)}, f32[16,1664]{1,0:T(8,128)S(1)}, u32[]{:S(2)}, u32[]{:S(2)}) collective-permute-start(f32[16,1664]{1,0:T(8,128)S(1)} %pad_maximum_fusion.1.rest_0_), channel_id=1, source_target_pairs={{0,16},{1,17},{2,18},{3,19},{4,20},{5,21},{6,22},{7,23},{8,24},{9,... | collective-permute-start | bytes 319496 | tf_op jit(solution)/shard_map/ppermute | solution.py:40
  87.7 8.7 %collective-permute-start.29 = (f32[16,1664]{1,0:T(8,128)S(1)}, f32[16,1664]{1,0:T(8,128)S(1)}, u32[]{:S(2)}, u32[]{:S(2)}) collective-permute-start(f32[16,1664]{1,0:T(8,128)S(1)} %pad_maximum_fusion.1.rest_0_), channel_id=1, source_target_pairs={{0,8},{1,9},{2,10},{3,11},{4,12},{5,13},{6,14},{7,15},{8,0},{9,1},... | collective-permute-start | bytes 319496 | tf_op jit(solution)/shard_map/ppermute | solution.py:40
  90.9 8.9 %collective-permute-start.31 = (f32[16,1664]{1,0:T(8,128)S(1)}, f32[16,1664]{1,0:T(8,128)S(1)}, u32[]{:S(2)}, u32[]{:S(2)}) collective-permute-start(f32[16,1664]{1,0:T(8,128)S(1)} %pad_maximum_fusion.1.rest_0_), channel_id=1, source_target_pairs={{0,4},{1,5},{2,6},{3,7},{4,0},{5,1},{6,2},{7,3},{8,12},{9,13},{10,... | collective-permute-start | bytes 319496 | tf_op jit(solution)/shard_map/ppermute | solution.py:40
  101.1 7.4 %collective-permute-start.35 = (f32[128,128]{1,0:T(8,128)S(1)}, f32[128,128]{1,0:T(8,128)S(1)}, u32[]{:S(2)}, u32[]{:S(2)}) collective-permute-start(f32[128,128]{1,0:T(8,128)S(1)} %get-tuple-element.82.rest_0_), channel_id=1, source_target_pairs={{0,1},{1,0},{2,3},{3,2},{4,5},{5,4},{6,7},{7,6},{8,9},{9,8},{10,11... | collective-permute-start | bytes 196616 | tf_op jit(solution)/shard_map/ppermute | solution.py:40
  102.6 5.9 %collective-permute-start.36 = (f32[128,128]{1,0:T(8,128)S(1)}, f32[128,128]{1,0:T(8,128)S(1)}, u32[]{:S(2)}, u32[]{:S(2)}) collective-permute-start(f32[128,128]{1,0:T(8,128)S(1)} %get-tuple-element.82.rest_0_), channel_id=1, source_target_pairs={{0,2},{1,3},{2,0},{3,1},{4,6},{5,7},{6,4},{7,5},{8,10},{9,11},{10,... | collective-permute-start | bytes 196616 | tf_op jit(solution)/shard_map/ppermute | solution.py:40
  103.6 5.2 %collective-permute-start.37 = (f32[128,128]{1,0:T(8,128)S(1)}, f32[128,128]{1,0:T(8,128)S(1)}, u32[]{:S(2)}, u32[]{:S(2)}) collective-permute-start(f32[128,128]{1,0:T(8,128)S(1)} %get-tuple-element.82.rest_0_), channel_id=1, source_target_pairs={{0,3},{1,2},{2,1},{3,0},{4,7},{5,6},{6,5},{7,4},{8,11},{9,10},{10,... | collective-permute-start | bytes 196616 | tf_op jit(solution)/shard_map/ppermute | solution.py:40
  (8 other events, 21.5 us)

commit v8 on v7

--- a/solution.py
+++ b/solution.py
@@ -353,7 +353,7 @@
     groups = size // 8
     sub = lax.broadcasted_iota(jnp.int32, (8, rank), 0)
     lane = lax.broadcasted_iota(jnp.int32, (8, rank), 1)
-    rolled = pltpu.roll(full, lax.rem(rank - first, rank), 1)
+    rolled = pltpu.roll(full, lax.rem(rank - first, rank), 1) if not isinstance(first, int) else full[:, first:first + size]
     rows = [full[8 * g:8 * g + 8] for g in range(groups)]
     cols = [
         [jnp.broadcast_to(rolled[8 * g:8 * g + 8, j:j + 1], (8, rank)) for g in range(groups)] for j in range(size)
@@ -421,6 +421,28 @@
     state_ref[rank - size:, :] = eliminate(state_ref[rank - size:, :], rank - size, size)
 
 
+def factor_unrolled(state_ref):
+    rank = state_ref.shape[0]
+    sub = lax.broadcasted_iota(jnp.int32, (PANEL, rank), 0)
+    lane = lax.broadcasted_iota(jnp.int32, (PANEL, rank), 1)
+    for first in range(0, rank, PANEL):
+        last = first + PANEL
+        done = eliminate(state_ref[first:last, :], first, PANEL)
+        state_ref[first:last, :] = done
+        if last == rank:
+            break
+        lower = jnp.where((lane > first + sub) & (lane < last), 0.0, done)
+        a, b, c = thirds(done)
+        d, e, f = thirds(lower)
+        step = dot(
+            jnp.concatenate([a, a, b, b, a, c], axis=0), jnp.concatenate([d, e, d, e, f, d], axis=0), TN
+        )
+        inside = (lane >= first) & (lane < last)
+        for row in range(last, rank, PANEL):
+            old = state_ref[row:row + PANEL, :]
+            state_ref[row:row + PANEL, :] = jnp.where(inside, 0.0, old) - step[row:row + PANEL, :]
+
+
 def factor_left(count, place, own, other):
     chunk, rank = own.shape[0], 2 * own.shape[1] // count
 
@@ -449,7 +471,7 @@
         gram = tree_sum([ref[...] for ref in refs[:-2]])
         gram_ref[...] = gram
         out_ref[...] = gram
-        factor_panels(out_ref)
+        factor_unrolled(out_ref)
         out_ref[...] = lower_part(out_ref[...])
 
     return call(body, "factor", [struct(rank, rank)] * 2, grams, flops=2 * FACTOR, nbytes=131072)
@@ -480,7 +502,7 @@
     def body(high_ref, low_ref, *rest):
         out_ref, state_ref, stage_ref, sems = rest[-4:]
         state_ref[...] = tree_sum([ref[...] for ref in rest[:-4]])
-        factor_panels(state_ref)
+        factor_unrolled(state_ref)
         inv_high, inv_low = split(scale * lower_part(state_ref[...]))
         both = jnp.concatenate([inv_high, inv_low], axis=0)
         copies = []
@@ -515,7 +537,8 @@
 
 
 def share_cols(x):
-    return [x] + [swap(x, "col", mask, mask) for mask in range(1, lax.axis_size("col"))]
+    others = [swap(x, "col", mask, mask) for mask in reversed(range(1, lax.axis_size("col")))]
+    return [x] + others[::-1]
 
 
 def sum_rows(keep, send, count, rank, beside=None):

time: 114 us -> 114 us (level)
  Pallas kernels: 35.9 us -> 34.7 us
where the time goes in v8:
time: 114 us
  starting transfers between devices  38.6 us (34%)
  waiting for transfers between devices  37.9 us (33%)
  Pallas kernels  34.7 us (30%)
  between operations  1.23 us (1%)
    ppermute x38, starting transfers between devices, swap(): return lax.ppermute(x, ('row', 'col'), pairs)  38.6 us
    ppermute x38, waiting for transfers between devices, swap(): return lax.ppermute(x, ('row', 'col'), pairs)  37.9 us
    pallas_call x14, Pallas kernels, call(): pl.pallas_call(body, out_shape=out, in_specs=[SMEM if x.dtype == jnp.int3...  23.3 us
    pallas_call x1, Pallas kernels, last_factor(): pl.pallas_call(body, in_specs=[VMEM] * (2 + len(grams)), out_specs=pl.Blo...  4.62 us
    pallas_call x2, Pallas kernels, finish(): pl.pallas_call(body, in_specs=[VMEM] * 3 + [hbm] * len(more), out_specs=h...  3.56 us
    pallas_call x1, Pallas kernels, start(): pl.pallas_call(body, in_specs=[pl.BlockSpec(memory_space=pltpu.HBM)] * 3,...  3.21 us
  transfers between devices with their start and end apart: 38, of which 22 were waited for; matrix products, arithmetic and copies ran while one was open for 1% of the time, Pallas kernels for 18%

profile of v8, /device:TPU:0, one launch (start us, length us, event | category | flops | bytes accessed | tf_op | source)
XLA Modules:
  0.0 113.5 jit_solution(6248494260308817619)
XLA Ops:
  0.6 3.2 %start.1 = (bf16[512,1664]{1,0:T(8,128)(2,1)S(1)}, bf16[512,1664]{1,0:T(8,128)(2,1)S(1)}, f32[256,128]{1,0:T(8,128)S(1)}, f32[256,128]{1,0:T(8,128)S(1)}) custom-call(f32[512,1664]{1,0:T(8,128)} %momentum_ref.1, bf16[512,1664]{1,0:T(8,128)(2,1)} %grad_ref.1, f32[1664,128]{1,0:T(8,128)} %basis_hbm.1), custom_call_target="tpu_custom_call" | custom-call | tf_op jit(solution)/shard_map/start/pallas_call | solution.py:123
  3.8 3.0 %collective-permute-start = (f32[256,128]{1,0:T(8,128)S(1)}, f32[256,128]{1,0:T(8,128)S(1)}, u32[]{:S(2)}, u32[]{:S(2)}) collective-permute-start(f32[256,128]{1,0:T(8,128)S(1)} %get-tuple-element.45), channel_id=1, source_target_pairs={{0,1},{1,0},{2,3},{3,2},{4,6},{5,7},{6,4},{7,5},{8,9},{9,8},{10,11... | collective-permute-start | bytes 393224 | tf_op jit(solution)/shard_map/ppermute | solution.py:40
  6.9 2.9 %collective-permute-done = f32[256,128]{1,0:T(8,128)S(1)} collective-permute-done((f32[256,128]{1,0:T(8,128)S(1)}, f32[256,128]{1,0:T(8,128)S(1)}, u32[]{:S(2)}, u32[]{:S(2)}) %collective-permute-start) | collective-permute-done | bytes 131104 | tf_op jit(solution)/shard_map/ppermute | solution.py:40
  9.8 2.1 %collective-permute-start.1 = (f32[256,128]{1,0:T(8,128)S(1)}, f32[256,128]{1,0:T(8,128)}, u32[]{:S(2)}, u32[]{:S(2)}) collective-permute-start(f32[256,128]{1,0:T(8,128)S(1)} %add.63.rest_0_), channel_id=1, source_target_pairs={{0,2},{1,3},{2,0},{3,1},{4,5},{5,4},{6,7},{7,6},{8,10},{9,11},{10,... | collective-permute-start | bytes 393224 | tf_op jit(solution)/shard_map/ppermute | solution.py:40
  15.0 2.9 %collective-permute-done.3.rest_3_ = f32[256,128]{1,0:T(8,128)} collective-permute-done((f32[256,128]{1,0:T(8,128)}, f32[256,128]{1,0:T(8,128)}, u32[]{:S(2)}, u32[]{:S(2)}) %collective-permute-start.3) | collective-permute-done | bytes 131104 | tf_op jit(solution)/shard_map/ppermute | solution.py:40
  17.9 1.9 %pull_send.2 = (f32[512,128]{1,0:T(8,128)S(1)}, f32[64,512]{1,0:T(8,128)S(1)}, f32[64,1792]{1,0:T(8,128)S(1)}) custom-call(s32[1]{0:T(128)} %bitcast.place_ref, f32[256,128]{1,0:T(8,128)S(1)} %add.63.rest_0_, f32[256,128]{1,0:T(8,128)} %collective-permute-done.1.rest_1_, f32[256,128]{1,0:T(8,128)} %add.64.rest_2_, ...), custom_call_target="tpu_custom_call" | custom-call | flops 500000000 | bytes 5000000 | tf_op jit(solution)/shard_map/pull_send/pallas_call | solution.py:75
  21.8 1.6 %collective-permute-start.5 = (f32[16,2944]{1,0:T(8,128)S(1)}, f32[16,2944]{1,0:T(8,128)S(1)}, u32[]{:S(2)}, u32[]{:S(2)}) collective-permute-start(f32[16,2944]{1,0:T(8,128)S(1)} %constant_dynamic-update-slice_fusion), channel_id=1, source_target_pairs={{0,8},{1,9},{2,10},{3,11},{4,12},{5,13},{6,14},{7,15},{8,0},{9,1},... | collective-permute-start | bytes 565256 | tf_op jit(solution)/shard_map/ppermute | solution.py:40
  23.4 2.6 %collective-permute-start.7 = (f32[16,896]{1,0:T(8,128)S(1)}, f32[16,896]{1,0:T(8,128)S(1)}, u32[]{:S(2)}, u32[]{:S(2)}) collective-permute-start(f32[16,896]{1,0:T(8,128)S(1)} %get-tuple-element.91), channel_id=1, source_target_pairs={{0,16},{1,17},{2,18},{3,19},{4,20},{5,21},{6,22},{7,23},{8,24},{9,... | collective-permute-start | bytes 172040 | tf_op jit(solution)/shard_map/ppermute | solution.py:40
  26.3 3.5 %collective-permute-done.5 = f32[16,2944]{1,0:T(8,128)S(1)} collective-permute-done((f32[16,2944]{1,0:T(8,128)S(1)}, f32[16,2944]{1,0:T(8,128)S(1)}, u32[]{:S(2)}, u32[]{:S(2)}) %collective-permute-start.5) | collective-permute-done | bytes 188448 | tf_op jit(solution)/shard_map/ppermute | solution.py:40
  29.9 2.4 %collective-permute-start.8 = (f32[16,1280]{1,0:T(8,128)S(1)}, f32[16,1280]{1,0:T(8,128)S(1)}, u32[]{:S(2)}, u32[]{:S(2)}) collective-permute-start(f32[16,1280]{1,0:T(8,128)S(1)} %pad_maximum_fusion.2), channel_id=1, source_target_pairs={{0,16},{1,17},{2,18},{3,19},{4,20},{5,21},{6,22},{7,23},{8,24},{9,... | collective-permute-start | bytes 245768 | tf_op jit(solution)/shard_map/ppermute | solution.py:40
  33.1 2.6 %collective-permute-done.8 = f32[16,1280]{1,0:T(8,128)S(1)} collective-permute-done((f32[16,1280]{1,0:T(8,128)S(1)}, f32[16,1280]{1,0:T(8,128)S(1)}, u32[]{:S(2)}, u32[]{:S(2)}) %collective-permute-start.8) | collective-permute-done | bytes 81952 | tf_op jit(solution)/shard_map/ppermute | solution.py:40
  35.8 4.5 %collective-permute-start.9 = (f32[16,1664]{1,0:T(8,128)S(1)}, f32[16,1664]{1,0:T(8,128)S(1)}, u32[]{:S(2)}, u32[]{:S(2)}) collective-permute-start(f32[16,1664]{1,0:T(8,128)S(1)} %pad_maximum_fusion.rest_0_), channel_id=1, source_target_pairs={{0,24},{1,25},{2,26},{3,27},{4,28},{5,29},{6,30},{7,31},{8,16},{9,... | collective-permute-start | bytes 319496 | tf_op jit(solution)/shard_map/ppermute | solution.py:40
  40.9 4.1 %factor.3.inv_ref = f32[128,128]{1,0:T(8,128)S(1)} custom-call(s32[1]{0:T(128)} %bitcast.place_ref, f32[16,512]{1,0:T(8,128)S(1)} %slice_add_fusion.8.own_ref, f32[16,512]{1,0:T(8,128)S(1)} %collective-permute-done.12.other_ref), custom_call_target="tpu_custom_call" | custom-call | flops 40000000000 | bytes 131072 | tf_op jit(solution)/shard_map/factor/pallas_call | solution.py:75
  45.1 2.7 %collective-permute-done.11.rest_1_ = f32[16,1664]{1,0:T(8,128)S(1)} collective-permute-done((f32[16,1664]{1,0:T(8,128)S(1)}, f32[16,1664]{1,0:T(8,128)S(1)}, u32[]{:S(2)}, u32[]{:S(2)}) %collective-permute-start.11) | collective-permute-done | bytes 106528 | tf_op jit(solution)/shard_map/ppermute | solution.py:40
  47.8 1.8 %collective-permute-done.10.rest_2_ = f32[16,1664]{1,0:T(8,128)S(1)} collective-permute-done((f32[16,1664]{1,0:T(8,128)S(1)}, f32[16,1664]{1,0:T(8,128)S(1)}, u32[]{:S(2)}, u32[]{:S(2)}) %collective-permute-start.10) | collective-permute-done | bytes 106528 | tf_op jit(solution)/shard_map/ppermute | solution.py:40
  53.6 1.6 %collective-permute-start.17 = (f32[512,128]{1,0:T(8,128)S(1)}, f32[512,128]{1,0:T(8,128)S(1)}, u32[]{:S(2)}, u32[]{:S(2)}) collective-permute-start(f32[512,128]{1,0:T(8,128)S(1)} %push.1), channel_id=1, source_target_pairs={{0,1},{1,0},{2,3},{3,2},{4,6},{5,7},{6,4},{7,5},{8,9},{9,8},{10,11... | collective-permute-start | bytes 786440 | tf_op jit(solution)/shard_map/ppermute | solution.py:40
  57.1 1.6 %collective-permute-start.21 = (f32[128,128]{1,0:T(8,128)S(1)}, f32[128,128]{1,0:T(8,128)S(1)}, u32[]{:S(2)}, u32[]{:S(2)}) collective-permute-start(f32[128,128]{1,0:T(8,128)S(1)} %get-tuple-element.59.refs_0_), channel_id=1, source_target_pairs={{0,3},{1,2},{2,1},{3,0},{4,7},{5,6},{6,5},{7,4},{8,11},{9,10},{10,... | collective-permute-start | bytes 196616 | tf_op jit(solution)/shard_map/ppermute | solution.py:40
  58.9 2.5 %collective-permute-done.17 = f32[512,128]{1,0:T(8,128)S(1)} collective-permute-done((f32[512,128]{1,0:T(8,128)S(1)}, f32[512,128]{1,0:T(8,128)S(1)}, u32[]{:S(2)}, u32[]{:S(2)}) %collective-permute-start.17) | collective-permute-done | bytes 262176 | tf_op jit(solution)/shard_map/ppermute | solution.py:40
  63.4 3.4 %factor.4 = (f32[128,128]{1,0:T(8,128)S(1)}, f32[128,128]{1,0:T(8,128)S(1)}) custom-call(f32[128,128]{1,0:T(8,128)S(1)} %get-tuple-element.59.refs_0_, f32[128,128]{1,0:T(8,128)S(1)} %collective-permute-done.19.refs_1_, f32[128,128]{1,0:T(8,128)S(1)} %collective-permute-done.20.refs_2_, f32[128,128]{1,0:T(8,128)S(1)} %collective-permute-done.21.refs_3_), custom_call_target="tpu_custom_call" | custom-call | flops 40000000000 | bytes 131072 | tf_op jit(solution)/shard_map/factor/pallas_call | solution.py:75
  67.9 1.6 %pull_send.3 = (f32[512,128]{1,0:T(8,128)S(1)}, f32[64,512]{1,0:T(8,128)S(1)}, f32[64,1792]{1,0:T(8,128)S(1)}) custom-call(s32[1]{0:T(128)} %bitcast.place_ref, f32[512,128]{1,0:T(8,128)S(1)} %add.74.rest_0_, f32[512,128]{1,0:T(8,128)S(1)} %collective-permute-done.18.rest_1_, bf16[512,1664]{1,0:T(8,128)(2,1)S(1)} %get-tuple-element.43.rest_4_.high_ref.rest_2_, ...), custom_call_target="tpu_custom_call" | custom-call | flops 500000000 | bytes 5000000 | tf_op jit(solution)/shard_map/pull_send/pallas_call | solution.py:75
  72.3 1.5 %collective-permute-start.25 = (f32[16,896]{1,0:T(8,128)S(1)}, f32[16,896]{1,0:T(8,128)S(1)}, u32[]{:S(2)}, u32[]{:S(2)}) collective-permute-start(f32[16,896]{1,0:T(8,128)S(1)} %get-tuple-element.84), channel_id=1, source_target_pairs={{0,16},{1,17},{2,18},{3,19},{4,20},{5,21},{6,22},{7,23},{8,24},{9,... | collective-permute-start | bytes 172040 | tf_op jit(solution)/shard_map/ppermute | solution.py:40
  73.8 2.3 %collective-permute-start.24 = (f32[16,896]{1,0:T(8,128)S(1)}, f32[16,896]{1,0:T(8,128)S(1)}, u32[]{:S(2)}, u32[]{:S(2)}) collective-permute-start(f32[16,896]{1,0:T(8,128)S(1)} %get-tuple-element.83), channel_id=1, source_target_pairs={{0,24},{1,25},{2,26},{3,27},{4,28},{5,29},{6,30},{7,31},{8,16},{9,... | collective-permute-start | bytes 172040 | tf_op jit(solution)/shard_map/ppermute | solution.py:40
  76.1 1.5 %deflate.1.base_ref = f32[512,1664]{1,0:T(8,128)S(1)} custom-call(f32[512,1664]{1,0:T(8,128)S(1)} %copy-done, bf16[512,1664]{1,0:T(8,128)(2,1)S(1)} %copy-done.1, f32[512,128]{1,0:T(8,128)S(1)} %left.1.rest_4_.rest_0_.left_ref, f32[128,1664]{1,0:T(8,128)S(1)} %get-tuple-element.58.right_ref.rest_5_.rest_1_), custom_call_target="tpu_custom_call" | custom-call | flops 1500000000 | bytes 9000000 | tf_op jit(solution)/shard_map/deflate/pallas_call | solution.py:75
  77.6 3.2 %collective-permute-done.23 = f32[16,2944]{1,0:T(8,128)S(1)} collective-permute-done((f32[16,2944]{1,0:T(8,128)S(1)}, f32[16,2944]{1,0:T(8,128)S(1)}, u32[]{:S(2)}, u32[]{:S(2)}) %collective-permute-start.23) | collective-permute-done | bytes 188448 | tf_op jit(solution)/shard_map/ppermute | solution.py:40
  81.0 5.3 %collective-permute-done.26 = f32[16,1280]{1,0:T(8,128)S(1)} collective-permute-done((f32[16,1280]{1,0:T(8,128)S(1)}, f32[16,1280]{1,0:T(8,128)S(1)}, u32[]{:S(2)}, u32[]{:S(2)}) %collective-permute-start.26) | collective-permute-done | bytes 81952 | tf_op jit(solution)/shard_map/ppermute | solution.py:40
  87.7 3.2 %collective-permute-start.29 = (f32[16,1664]{1,0:T(8,128)S(1)}, f32[16,1664]{1,0:T(8,128)S(1)}, u32[]{:S(2)}, u32[]{:S(2)}) collective-permute-start(f32[16,1664]{1,0:T(8,128)S(1)} %pad_maximum_fusion.1.rest_0_), channel_id=1, source_target_pairs={{0,8},{1,9},{2,10},{3,11},{4,12},{5,13},{6,14},{7,15},{8,0},{9,1},... | collective-permute-start | bytes 319496 | tf_op jit(solution)/shard_map/ppermute | solution.py:40
  90.9 4.2 %factor.5.inv_ref = f32[128,128]{1,0:T(8,128)S(1)} custom-call(s32[1]{0:T(128)} %bitcast.place_ref, f32[16,512]{1,0:T(8,128)S(1)} %slice_add_fusion.7.own_ref, f32[16,512]{1,0:T(8,128)S(1)} %collective-permute-done.30.other_ref), custom_call_target="tpu_custom_call" | custom-call | flops 40000000000 | bytes 131072 | tf_op jit(solution)/shard_map/factor/pallas_call | solution.py:75
  96.3 1.8 %collective-permute-done.28.rest_2_ = f32[16,1664]{1,0:T(8,128)S(1)} collective-permute-done((f32[16,1664]{1,0:T(8,128)S(1)}, f32[16,1664]{1,0:T(8,128)S(1)}, u32[]{:S(2)}, u32[]{:S(2)}) %collective-permute-start.28) | collective-permute-done | bytes 106528 | tf_op jit(solution)/shard_map/ppermute | solution.py:40
  101.1 1.6 %collective-permute-start.35 = (f32[128,128]{1,0:T(8,128)S(1)}, f32[128,128]{1,0:T(8,128)S(1)}, u32[]{:S(2)}, u32[]{:S(2)}) collective-permute-start(f32[128,128]{1,0:T(8,128)S(1)} %get-tuple-element.82.rest_0_), channel_id=1, source_target_pairs={{0,1},{1,0},{2,3},{3,2},{4,5},{5,4},{6,7},{7,6},{8,9},{9,8},{10,11... | collective-permute-start | bytes 196616 | tf_op jit(solution)/shard_map/ppermute | solution.py:40
  104.9 1.8 %finish.2.rest_0_ = f32[512,1664]{1,0:T(8,128)} custom-call(f32[512,1664]{1,0:T(8,128)S(1)} %deflate.1.base_ref, f32[512,128]{1,0:T(8,128)S(1)} %get-tuple-element.74.left_ref, f32[128,1664]{1,0:T(8,128)S(1)} %get-tuple-element.78.right_ref), custom_call_target="tpu_custom_call" | custom-call | flops 800000000 | bytes 6000000 | tf_op jit(solution)/shard_map/finish/pallas_call | solution.py:337
  106.7 1.8 %finish.3 = f32[512,1664]{1,0:T(8,128)} custom-call(f32[512,1664]{1,0:T(8,128)S(1)} %deflate.1.base_ref, f32[512,128]{1,0:T(8,128)S(1)} %get-tuple-element.74.left_ref, f32[128,1664]{1,0:T(8,128)S(1)} %get-tuple-element.78.right_ref, f32[512,1664]{1,0:T(8,128)} %finish.2.rest_0_), custom_call_target="tpu_custom_call", output_to_operand_aliasing={{}: (3, {})} | custom-call | flops 800000000 | bytes 6000000 | tf_op jit(solution)/shard_map/finish/pallas_call | solution.py:337
  108.7 4.6 %last_factor.1 = f32[1664,128]{1,0:T(8,128)} custom-call(bf16[1664,128]{1,0:T(8,128)(2,1)S(1)} %get-tuple-element.80.high_ref, bf16[1664,128]{1,0:T(8,128)(2,1)S(1)} %get-tuple-element.81.low_ref, f32[128,128]{1,0:T(8,128)S(1)} %get-tuple-element.82.rest_0_, f32[128,128]{1,0:T(8,128)S(1)} %collective-permute-done.35.rest_1_, ...), custom_call_target="tpu_custom_call" | custom-call | flops 40000000000 | bytes 2000000 | tf_op jit(solution)/shard_map/last_factor/pallas_call | solution.py:520
  (100 shorter events, 27.1 us)
Async XLA Ops:
  3.8 6.0 %collective-permute-start = (f32[256,128]{1,0:T(8,128)S(1)}, f32[256,128]{1,0:T(8,128)S(1)}, u32[]{:S(2)}, u32[]{:S(2)}) collective-permute-start(f32[256,128]{1,0:T(8,128)S(1)} %get-tuple-element.45), channel_id=1, source_target_pairs={{0,1},{1,0},{2,3},{3,2},{4,6},{5,7},{6,4},{7,5},{8,9},{9,8},{10,11... | collective-permute-start | bytes 393224 | tf_op jit(solution)/shard_map/ppermute | solution.py:40
  6.8 5.1 %collective-permute-start.2 = (f32[256,128]{1,0:T(8,128)S(1)}, f32[256,128]{1,0:T(8,128)S(1)}, u32[]{:S(2)}, u32[]{:S(2)}) collective-permute-start(f32[256,128]{1,0:T(8,128)S(1)} %get-tuple-element.46), channel_id=1, source_target_pairs={{0,1},{1,0},{2,3},{3,2},{4,6},{5,7},{6,4},{7,5},{8,9},{9,8},{10,11... | collective-permute-start | bytes 393224 | tf_op jit(solution)/shard_map/ppermute | solution.py:40
  9.8 5.2 %collective-permute-start.1 = (f32[256,128]{1,0:T(8,128)S(1)}, f32[256,128]{1,0:T(8,128)}, u32[]{:S(2)}, u32[]{:S(2)}) collective-permute-start(f32[256,128]{1,0:T(8,128)S(1)} %add.63.rest_0_), channel_id=1, source_target_pairs={{0,2},{1,3},{2,0},{3,1},{4,5},{5,4},{6,7},{7,6},{8,10},{9,11},{10,... | collective-permute-start | bytes 393224 | tf_op jit(solution)/shard_map/ppermute | solution.py:40
  12.6 5.3 %collective-permute-start.3 = (f32[256,128]{1,0:T(8,128)}, f32[256,128]{1,0:T(8,128)}, u32[]{:S(2)}, u32[]{:S(2)}) collective-permute-start(f32[256,128]{1,0:T(8,128)} %add.64.rest_2_), channel_id=1, source_target_pairs={{0,2},{1,3},{2,0},{3,1},{4,5},{5,4},{6,7},{7,6},{8,10},{9,11},{10,... | collective-permute-start | bytes 393224 | tf_op jit(solution)/shard_map/ppermute | solution.py:40
  19.8 1.9 %collective-permute-start.4 = (f32[64,1792]{1,0:T(8,128)S(1)}, f32[64,1792]{1,0:T(8,128)S(1)}, u32[]{:S(2)}, u32[]{:S(2)}) collective-permute-start(f32[64,1792]{1,0:T(8,128)S(1)} %get-tuple-element.49), channel_id=1, source_target_pairs={{0,4},{1,5},{2,6},{3,7},{4,0},{5,1},{6,2},{7,3},{8,12},{9,13},{10,... | collective-permute-start | bytes 1376264 | tf_op jit(solution)/shard_map/ppermute | solution.py:40
  21.8 8.1 %collective-permute-start.5 = (f32[16,2944]{1,0:T(8,128)S(1)}, f32[16,2944]{1,0:T(8,128)S(1)}, u32[]{:S(2)}, u32[]{:S(2)}) collective-permute-start(f32[16,2944]{1,0:T(8,128)S(1)} %constant_dynamic-update-slice_fusion), channel_id=1, source_target_pairs={{0,8},{1,9},{2,10},{3,11},{4,12},{5,13},{6,14},{7,15},{8,0},{9,1},... | collective-permute-start | bytes 565256 | tf_op jit(solution)/shard_map/ppermute | solution.py:40
  23.4 8.8 %collective-permute-start.7 = (f32[16,896]{1,0:T(8,128)S(1)}, f32[16,896]{1,0:T(8,128)S(1)}, u32[]{:S(2)}, u32[]{:S(2)}) collective-permute-start(f32[16,896]{1,0:T(8,128)S(1)} %get-tuple-element.91), channel_id=1, source_target_pairs={{0,16},{1,17},{2,18},{3,19},{4,20},{5,21},{6,22},{7,23},{8,24},{9,... | collective-permute-start | bytes 172040 | tf_op jit(solution)/shard_map/ppermute | solution.py:40
  26.1 7.0 %collective-permute-start.6 = (f32[16,896]{1,0:T(8,128)S(1)}, f32[16,896]{1,0:T(8,128)S(1)}, u32[]{:S(2)}, u32[]{:S(2)}) collective-permute-start(f32[16,896]{1,0:T(8,128)S(1)} %get-tuple-element.90), channel_id=1, source_target_pairs={{0,24},{1,25},{2,26},{3,27},{4,28},{5,29},{6,30},{7,31},{8,16},{9,... | collective-permute-start | bytes 172040 | tf_op jit(solution)/shard_map/ppermute | solution.py:40
  29.9 5.8 %collective-permute-start.8 = (f32[16,1280]{1,0:T(8,128)S(1)}, f32[16,1280]{1,0:T(8,128)S(1)}, u32[]{:S(2)}, u32[]{:S(2)}) collective-permute-start(f32[16,1280]{1,0:T(8,128)S(1)} %pad_maximum_fusion.2), channel_id=1, source_target_pairs={{0,16},{1,17},{2,18},{3,19},{4,20},{5,21},{6,22},{7,23},{8,24},{9,... | collective-permute-start | bytes 245768 | tf_op jit(solution)/shard_map/ppermute | solution.py:40
  35.8 5.2 %collective-permute-start.12 = (f32[16,512]{1,0:T(8,128)S(1)}, f32[16,512]{1,0:T(8,128)S(1)}, u32[]{:S(2)}, u32[]{:S(2)}) collective-permute-start(f32[16,512]{1,0:T(8,128)S(1)} %slice_add_fusion.8.own_ref), channel_id=1, source_target_pairs={{0,4},{1,5},{2,6},{3,7},{4,0},{5,1},{6,2},{7,3},{8,12},{9,13},{10,... | collective-permute-start | bytes 98312 | tf_op jit(solution)/shard_map/ppermute | solution.py:40
  35.8 13.7 %collective-permute-start.9 = (f32[16,1664]{1,0:T(8,128)S(1)}, f32[16,1664]{1,0:T(8,128)S(1)}, u32[]{:S(2)}, u32[]{:S(2)}) collective-permute-start(f32[16,1664]{1,0:T(8,128)S(1)} %pad_maximum_fusion.rest_0_), channel_id=1, source_target_pairs={{0,24},{1,25},{2,26},{3,27},{4,28},{5,29},{6,30},{7,31},{8,16},{9,... | collective-permute-start | bytes 319496 | tf_op jit(solution)/shard_map/ppermute | solution.py:40
  40.3 9.2 %collective-permute-start.10 = (f32[16,1664]{1,0:T(8,128)S(1)}, f32[16,1664]{1,0:T(8,128)S(1)}, u32[]{:S(2)}, u32[]{:S(2)}) collective-permute-start(f32[16,1664]{1,0:T(8,128)S(1)} %pad_maximum_fusion.rest_0_), channel_id=1, source_target_pairs={{0,16},{1,17},{2,18},{3,19},{4,20},{5,21},{6,22},{7,23},{8,24},{9,... | collective-permute-start | bytes 319496 | tf_op jit(solution)/shard_map/ppermute | solution.py:40
  40.3 7.5 %collective-permute-start.11 = (f32[16,1664]{1,0:T(8,128)S(1)}, f32[16,1664]{1,0:T(8,128)S(1)}, u32[]{:S(2)}, u32[]{:S(2)}) collective-permute-start(f32[16,1664]{1,0:T(8,128)S(1)} %pad_maximum_fusion.rest_0_), channel_id=1, source_target_pairs={{0,8},{1,9},{2,10},{3,11},{4,12},{5,13},{6,14},{7,15},{8,0},{9,1},... | collective-permute-start | bytes 319496 | tf_op jit(solution)/shard_map/ppermute | solution.py:40
  40.9 9.1 %collective-permute-start.13 = (f32[16,1664]{1,0:T(8,128)S(1)}, f32[16,1664]{1,0:T(8,128)S(1)}, u32[]{:S(2)}, u32[]{:S(2)}) collective-permute-start(f32[16,1664]{1,0:T(8,128)S(1)} %pad_maximum_fusion.rest_0_), channel_id=1, source_target_pairs={{0,4},{1,5},{2,6},{3,7},{4,0},{5,1},{6,2},{7,3},{8,12},{9,13},{10,... | collective-permute-start | bytes 319496 | tf_op jit(solution)/shard_map/ppermute | solution.py:40
  53.6 7.8 %collective-permute-start.17 = (f32[512,128]{1,0:T(8,128)S(1)}, f32[512,128]{1,0:T(8,128)S(1)}, u32[]{:S(2)}, u32[]{:S(2)}) collective-permute-start(f32[512,128]{1,0:T(8,128)S(1)} %push.1), channel_id=1, source_target_pairs={{0,1},{1,0},{2,3},{3,2},{4,6},{5,7},{6,4},{7,5},{8,9},{9,8},{10,11... | collective-permute-start | bytes 786440 | tf_op jit(solution)/shard_map/ppermute | solution.py:40
  55.1 7.3 %collective-permute-start.19 = (f32[128,128]{1,0:T(8,128)S(1)}, f32[128,128]{1,0:T(8,128)S(1)}, u32[]{:S(2)}, u32[]{:S(2)}) collective-permute-start(f32[128,128]{1,0:T(8,128)S(1)} %get-tuple-element.59.refs_0_), channel_id=1, source_target_pairs={{0,1},{1,0},{2,3},{3,2},{4,5},{5,4},{6,7},{7,6},{8,9},{9,8},{10,11... | collective-permute-start | bytes 196616 | tf_op jit(solution)/shard_map/ppermute | solution.py:40
  55.7 6.8 %collective-permute-start.20 = (f32[128,128]{1,0:T(8,128)S(1)}, f32[128,128]{1,0:T(8,128)S(1)}, u32[]{:S(2)}, u32[]{:S(2)}) collective-permute-start(f32[128,128]{1,0:T(8,128)S(1)} %get-tuple-element.59.refs_0_), channel_id=1, source_target_pairs={{0,2},{1,3},{2,0},{3,1},{4,6},{5,7},{6,4},{7,5},{8,10},{9,11},{10,... | collective-permute-start | bytes 196616 | tf_op jit(solution)/shard_map/ppermute | solution.py:40
  57.1 6.4 %collective-permute-start.21 = (f32[128,128]{1,0:T(8,128)S(1)}, f32[128,128]{1,0:T(8,128)S(1)}, u32[]{:S(2)}, u32[]{:S(2)}) collective-permute-start(f32[128,128]{1,0:T(8,128)S(1)} %get-tuple-element.59.refs_0_), channel_id=1, source_target_pairs={{0,3},{1,2},{2,1},{3,0},{4,7},{5,6},{6,5},{7,4},{8,11},{9,10},{10,... | collective-permute-start | bytes 196616 | tf_op jit(solution)/shard_map/ppermute | solution.py:40
  61.5 6.4 %collective-permute-start.18 = (f32[512,128]{1,0:T(8,128)S(1)}, f32[512,128]{1,0:T(8,128)S(1)}, u32[]{:S(2)}, u32[]{:S(2)}) collective-permute-start(f32[512,128]{1,0:T(8,128)S(1)} %add.74.rest_0_), channel_id=1, source_target_pairs={{0,2},{1,3},{2,0},{3,1},{4,5},{5,4},{6,7},{7,6},{8,10},{9,11},{10,... | collective-permute-start | bytes 786440 | tf_op jit(solution)/shard_map/ppermute | solution.py:40
  69.5 1.9 %collective-permute-start.22 = (f32[64,1792]{1,0:T(8,128)S(1)}, f32[64,1792]{1,0:T(8,128)S(1)}, u32[]{:S(2)}, u32[]{:S(2)}) collective-permute-start(f32[64,1792]{1,0:T(8,128)S(1)} %get-tuple-element.64), channel_id=1, source_target_pairs={{0,4},{1,5},{2,6},{3,7},{4,0},{5,1},{6,2},{7,3},{8,12},{9,13},{10,... | collective-permute-start | bytes 1376264 | tf_op jit(solution)/shard_map/ppermute | solution.py:40
  71.5 9.3 %collective-permute-start.23 = (f32[16,2944]{1,0:T(8,128)S(1)}, f32[16,2944]{1,0:T(8,128)S(1)}, u32[]{:S(2)}, u32[]{:S(2)}) collective-permute-start(f32[16,2944]{1,0:T(8,128)S(1)} %constant_dynamic-update-slice_fusion.4), channel_id=1, source_target_pairs={{0,8},{1,9},{2,10},{3,11},{4,12},{5,13},{6,14},{7,15},{8,0},{9,1},... | collective-permute-start | bytes 565256 | tf_op jit(solution)/shard_map/ppermute | solution.py:40
  72.3 8.7 %collective-permute-start.25 = (f32[16,896]{1,0:T(8,128)S(1)}, f32[16,896]{1,0:T(8,128)S(1)}, u32[]{:S(2)}, u32[]{:S(2)}) collective-permute-start(f32[16,896]{1,0:T(8,128)S(1)} %get-tuple-element.84), channel_id=1, source_target_pairs={{0,16},{1,17},{2,18},{3,19},{4,20},{5,21},{6,22},{7,23},{8,24},{9,... | collective-permute-start | bytes 172040 | tf_op jit(solution)/shard_map/ppermute | solution.py:40
  73.8 7.2 %collective-permute-start.24 = (f32[16,896]{1,0:T(8,128)S(1)}, f32[16,896]{1,0:T(8,128)S(1)}, u32[]{:S(2)}, u32[]{:S(2)}) collective-permute-start(f32[16,896]{1,0:T(8,128)S(1)} %get-tuple-element.83), channel_id=1, source_target_pairs={{0,24},{1,25},{2,26},{3,27},{4,28},{5,29},{6,30},{7,31},{8,16},{9,... | collective-permute-start | bytes 172040 | tf_op jit(solution)/shard_map/ppermute | solution.py:40
  80.9 5.4 %collective-permute-start.26 = (f32[16,1280]{1,0:T(8,128)S(1)}, f32[16,1280]{1,0:T(8,128)S(1)}, u32[]{:S(2)}, u32[]{:S(2)}) collective-permute-start(f32[16,1280]{1,0:T(8,128)S(1)} %pad_maximum_fusion.3), channel_id=1, source_target_pairs={{0,16},{1,17},{2,18},{3,19},{4,20},{5,21},{6,22},{7,23},{8,24},{9,... | collective-permute-start | bytes 245768 | tf_op jit(solution)/shard_map/ppermute | solution.py:40
  86.3 4.5 %collective-permute-start.30 = (f32[16,512]{1,0:T(8,128)S(1)}, f32[16,512]{1,0:T(8,128)S(1)}, u32[]{:S(2)}, u32[]{:S(2)}) collective-permute-start(f32[16,512]{1,0:T(8,128)S(1)} %slice_add_fusion.7.own_ref), channel_id=1, source_target_pairs={{0,4},{1,5},{2,6},{3,7},{4,0},{5,1},{6,2},{7,3},{8,12},{9,13},{10,... | collective-permute-start | bytes 98312 | tf_op jit(solution)/shard_map/ppermute | solution.py:40
  86.4 11.8 %collective-permute-start.27 = (f32[16,1664]{1,0:T(8,128)S(1)}, f32[16,1664]{1,0:T(8,128)S(1)}, u32[]{:S(2)}, u32[]{:S(2)}) collective-permute-start(f32[16,1664]{1,0:T(8,128)S(1)} %pad_maximum_fusion.1.rest_0_), channel_id=1, source_target_pairs={{0,24},{1,25},{2,26},{3,27},{4,28},{5,29},{6,30},{7,31},{8,16},{9,... | collective-permute-start | bytes 319496 | tf_op jit(solution)/shard_map/ppermute | solution.py:40
  87.7 10.5 %collective-permute-start.28 = (f32[16,1664]{1,0:T(8,128)S(1)}, f32[16,1664]{1,0:T(8,128)S(1)}, u32[]{:S(2)}, u32[]{:S(2)}) collective-permute-start(f32[16,1664]{1,0:T(8,128)S(1)} %pad_maximum_fusion.1.rest_0_), channel_id=1, source_target_pairs={{0,16},{1,17},{2,18},{3,19},{4,20},{5,21},{6,22},{7,23},{8,24},{9,... | collective-permute-start | bytes 319496 | tf_op jit(solution)/shard_map/ppermute | solution.py:40
  87.7 8.7 %collective-permute-start.29 = (f32[16,1664]{1,0:T(8,128)S(1)}, f32[16,1664]{1,0:T(8,128)S(1)}, u32[]{:S(2)}, u32[]{:S(2)}) collective-permute-start(f32[16,1664]{1,0:T(8,128)S(1)} %pad_maximum_fusion.1.rest_0_), channel_id=1, source_target_pairs={{0,8},{1,9},{2,10},{3,11},{4,12},{5,13},{6,14},{7,15},{8,0},{9,1},... | collective-permute-start | bytes 319496 | tf_op jit(solution)/shard_map/ppermute | solution.py:40
  90.9 8.9 %collective-permute-start.31 = (f32[16,1664]{1,0:T(8,128)S(1)}, f32[16,1664]{1,0:T(8,128)S(1)}, u32[]{:S(2)}, u32[]{:S(2)}) collective-permute-start(f32[16,1664]{1,0:T(8,128)S(1)} %pad_maximum_fusion.1.rest_0_), channel_id=1, source_target_pairs={{0,4},{1,5},{2,6},{3,7},{4,0},{5,1},{6,2},{7,3},{8,12},{9,13},{10,... | collective-permute-start | bytes 319496 | tf_op jit(solution)/shard_map/ppermute | solution.py:40
  101.1 7.4 %collective-permute-start.35 = (f32[128,128]{1,0:T(8,128)S(1)}, f32[128,128]{1,0:T(8,128)S(1)}, u32[]{:S(2)}, u32[]{:S(2)}) collective-permute-start(f32[128,128]{1,0:T(8,128)S(1)} %get-tuple-element.82.rest_0_), channel_id=1, source_target_pairs={{0,1},{1,0},{2,3},{3,2},{4,5},{5,4},{6,7},{7,6},{8,9},{9,8},{10,11... | collective-permute-start | bytes 196616 | tf_op jit(solution)/shard_map/ppermute | solution.py:40
  102.6 5.9 %collective-permute-start.36 = (f32[128,128]{1,0:T(8,128)S(1)}, f32[128,128]{1,0:T(8,128)S(1)}, u32[]{:S(2)}, u32[]{:S(2)}) collective-permute-start(f32[128,128]{1,0:T(8,128)S(1)} %get-tuple-element.82.rest_0_), channel_id=1, source_target_pairs={{0,2},{1,3},{2,0},{3,1},{4,6},{5,7},{6,4},{7,5},{8,10},{9,11},{10,... | collective-permute-start | bytes 196616 | tf_op jit(solution)/shard_map/ppermute | solution.py:40
  103.6 5.2 %collective-permute-start.37 = (f32[128,128]{1,0:T(8,128)S(1)}, f32[128,128]{1,0:T(8,128)S(1)}, u32[]{:S(2)}, u32[]{:S(2)}) collective-permute-start(f32[128,128]{1,0:T(8,128)S(1)} %get-tuple-element.82.rest_0_), channel_id=1, source_target_pairs={{0,3},{1,2},{2,1},{3,0},{4,7},{5,6},{6,5},{7,4},{8,11},{9,10},{10,... | collective-permute-start | bytes 196616 | tf_op jit(solution)/shard_map/ppermute | solution.py:40
  (8 other events, 21.5 us)
